TPU v7x, 32 devices: a whole 2x2x4 slice. The times are simulated.
32 devices in a mesh: dp: 4 (over y, core), pool: 8 (over z, x).
Axes of the slice: x: 2, y: 2, z: 4, core: 2. Of those that a mesh axis runs over, the one named last changes fastest.
Arguments:
- feats: bfloat16 [8192, 2048], P(('dp', 'pool')), may hold values from -6 to 6
- tower_w: bfloat16 [2048, 256], replicated, may hold values from -0.125 to 0.125
- partners: int32 [8192], P(('dp', 'pool')), may hold values from 0 to 2047, as said below
- popularity_buckets: int32 [8192], P(('dp', 'pool')), may hold values from 0 to 31
- row_counts: int32 [4, 8], replicated, may hold values from 64 to 256, as said below
Outputs:
- grad_w: float32 [2048, 256], P(('dp', 'pool'))
Inputs may be any that keep to these rules, and one draw needn't show every extreme that they name: row_counts[d, p] valid slots stand first in the block of 256 slots of pool member p in data group d; in every data group some member has all 256 slots valid. `partners`: each slot's partner is the position, within its data group's 2048 slots, of a valid slot other than itself.
All inputs are finite; a program needn't handle non-finite values.
Results may differ from a plain program's by a relative error of at most 0.0038.
The roundings to bfloat16 on the way count: a program that leaves them out, or rounds other values in their place, can miss the bound.
Values may be sent and summed in bfloat16 or wider, within the bound.
No kernel may reach another device: no remote copies, remote signals or barrier semaphores. Data moves between devices by JAX's collectives and lax.ppermute only.
A program may use at most 64 MiB of HBM per device.

v0:
```python
import jax
import jax.numpy as jnp
from jax import lax
from jax.sharding import PartitionSpec as P

sharpness_scaler = 0.05
epsilon = 1e-06


def contract_rows(left, right):
    return lax.dot_general(
        left, right, (((0,), (0,)), ((), ())), preferred_element_type=jnp.float32
    )


def contract_cols(left, right):
    return lax.dot_general(
        left, right, (((1,), (1,)), ((), ())), preferred_element_type=jnp.float32
    )


def per_device(feats, tower_w, partners, popularity_buckets, row_counts):
    shard_rows = feats.shape[0]
    pool_size = lax.axis_size("pool")
    member = lax.axis_index("pool")
    group_index = lax.axis_index("dp")
    projected = jnp.dot(feats, tower_w, preferred_element_type=jnp.float32)
    inv_norm = lax.rsqrt(jnp.sum(projected * projected, axis=1, keepdims=True) + epsilon)
    normed = projected * inv_norm
    embedded = normed.astype(jnp.bfloat16)
    prior_occurrence_correction = (-(popularity_buckets.astype(jnp.float32) + 0.5) / 4.0).astype(
        jnp.bfloat16
    )
    all_emb, all_logq = (
        lax.all_gather(embedded, "pool", axis=0, tiled=True),
        lax.all_gather(prior_occurrence_correction, "pool", axis=0, tiled=True),
    )
    group_counts = lax.dynamic_index_in_dim(row_counts, group_index, 0, keepdims=False)
    own_count = lax.dynamic_index_in_dim(group_counts, member, 0, keepdims=False)
    local_rows = jnp.arange(shard_rows, dtype=jnp.int32)
    source_usable = local_rows < own_count
    row_index = member * shard_rows + local_rows
    col_valid = (local_rows[None, :] < group_counts[:, None]).reshape(-1)
    shards_per = min(pool_size, max(1, 512 // shard_rows))
    while pool_size % shards_per:
        shards_per = shards_per - 1
    block_width = shard_rows * shards_per
    block_count = pool_size // shards_per
    emb_blocks = all_emb.reshape(block_count, block_width, -1)
    logq_blocks = all_logq.astype(jnp.float32).reshape(block_count, block_width)
    valid_blocks = col_valid.reshape(block_count, block_width)
    first_cols = jnp.arange(block_count, dtype=jnp.int32) * block_width
    own_logq = prior_occurrence_correction.astype(jnp.float32)

    def segment_contributions(block_emb, tile_popularity_logarithm, block_valid, first_col):
        angular_affinities = contract_cols(embedded, block_emb)
        target_ordinal = first_col + jnp.arange(block_width, dtype=jnp.int32)
        admitted_flags = block_valid[None, :] & (row_index[:, None] != target_ordinal[None, :])
        natural_powers = jnp.where(
            admitted_flags,
            jnp.exp(angular_affinities / sharpness_scaler - tile_popularity_logarithm[None, :]),
            0.0,
        )
        return (angular_affinities, target_ordinal, natural_powers)

    def add_totals(running, operand_tensors):
        return (running + jnp.sum(segment_contributions(*operand_tensors)[2], axis=1), None)

    shared = (emb_blocks, logq_blocks, valid_blocks, first_cols)
    normalizer_sums, ignored = lax.scan(add_totals, jnp.zeros((shard_rows,), jnp.float32), shared)

    def source_multiplier(target_ordinal, natural_powers):
        matched_partner = (partners[:, None] == target_ordinal[None, :]).astype(jnp.float32)
        return jnp.where(
            source_usable[:, None], natural_powers / normalizer_sums[:, None] - matched_partner, 0.0
        ).astype(jnp.bfloat16)

    zero_grad = jnp.zeros(normed.shape, jnp.float32)
    all_totals = lax.all_gather(normalizer_sums, "pool", axis=0, tiled=True)
    all_partners = lax.all_gather(partners, "pool", axis=0, tiled=True)
    extended = shared + (
        all_totals.reshape(block_count, block_width),
        all_partners.reshape(block_count, block_width),
    )

    def both_step(running, operand_tensors):
        angular_affinities, target_ordinal, natural_powers = segment_contributions(
            *operand_tensors[:4]
        )
        pair_multiplier = source_multiplier(target_ordinal, natural_powers)
        anchor_valid = operand_tensors[2]
        mirror_keep = (
            source_usable[:, None]
            & anchor_valid[None, :]
            & (row_index[:, None] != target_ordinal[None, :])
        )
        mirror_exp = jnp.where(
            mirror_keep, jnp.exp(angular_affinities / sharpness_scaler - own_logq[:, None]), 0.0
        )
        mirror_pos = (operand_tensors[5][None, :] == row_index[:, None]).astype(jnp.float32)
        mirror_coeff = jnp.where(
            anchor_valid[None, :], mirror_exp / operand_tensors[4][None, :] - mirror_pos, 0.0
        ).astype(jnp.bfloat16)
        rows_part = running[0] + jnp.dot(
            pair_multiplier, operand_tensors[0], preferred_element_type=jnp.float32
        )
        cols_part = running[1] + jnp.dot(
            mirror_coeff, operand_tensors[0], preferred_element_type=jnp.float32
        )
        return ((rows_part, cols_part), None)

    (row_term, own_term), ignored = lax.scan(both_step, (zero_grad, zero_grad), extended)
    grad_emb = row_term + own_term
    grad_proj = (
        (grad_emb - normed * jnp.sum(normed * grad_emb, axis=1, keepdims=True)) * inv_norm
    ).astype(jnp.bfloat16)
    return lax.psum_scatter(
        contract_rows(feats, grad_proj), ("dp", "pool"), scatter_dimension=0, tiled=True
    )


def solution(mesh):
    return jax.shard_map(
        per_device,
        mesh=mesh,
        in_specs=(P(("dp", "pool"), None), P(), P(("dp", "pool")), P(("dp", "pool")), P()),
        out_specs=P(("dp", "pool"), None),
        check_vma=False,
    )
```

profile of v0, /device:TPU:0, one launch (start us, length us, event | category | flops | bytes accessed | tf_op | source)
XLA Modules:
  0.0 239.1 jit_solution(7367086615403951315)
XLA Ops:
  6.6 1.2 copy-done
  7.8 1.8 multiply_reduce_fusion.1
  9.5 0.7 multiply_convert_fusion.1
  10.3 1.0 copy.23
  11.6 22.2 %all-gather = bf16[8,1,256]{2,1,0:T(2,128)(2,1)S(1)} all-gather(bf16[1,1,256]{2,1,0:T(2,128)(2,1)S(1)} %reshape.51), channel_id=1, replica_groups=mesh['dp'=4,'pool'=8] {'pool'}, dimensions={0}, use_global_device_ids=true | all-gather | bytes 4608 | tf_op jit(solution)/shard_map/all_gather | solution.py:36
  33.9 16.5 %all-gather.2 = s32[8,1,256]{2,1,0:T(1,128)S(1)} all-gather(s32[1,1,256]{2,1,0:T(1,128)S(1)} %bitcast.100), channel_id=1, replica_groups=mesh['dp'=4,'pool'=8] {'pool'}, dimensions={0}, use_global_device_ids=true | all-gather | bytes 9216 | tf_op jit(solution)/shard_map/all_gather | solution.py:80
  51.0 1.6 all-gather.5.cloned.1.call-done
  52.7 1.5 copy.29
  54.1 7.4 %while.24 = (s32[]{:T(128)}, f32[256]{0:T(256)S(1)}, pred[4,512]{1,0:T(4,128)(4,1)S(1)}, s32[4]{0:T(128)S(1)}, bf16[4,512,256]{2,1,0:T(8,128)(2,1)S(1)}, /*index...) while((s32[]{:T(128)}, f32[256]{0:T(256)S(1)}, ...), condition=%wide.region_3.4_spmd.clone, body=%wide.region_1.3_spmd.clone.sunk | while | flops 67896320 | bytes 411287 | solution.py:70
  54.1 0.7 dynamic_slice.92
  54.8 0.7 iota_add_fusion.9
  56.0 0.7 dynamic_slice.92
  56.7 0.7 iota_add_fusion.9
  57.8 0.7 dynamic_slice.92
  58.5 0.7 iota_add_fusion.9
  59.7 0.7 dynamic_slice.92
  60.4 0.7 iota_add_fusion.9
  61.5 18.4 %all-gather.1 = f32[8,1,256]{2,1,0:T(1,128)S(1)} all-gather(f32[1,1,256]{2,1,0:T(1,128)S(1)} %bitcast.97), channel_id=1, replica_groups=mesh['dp'=4,'pool'=8] {'pool'}, dimensions={0}, use_global_device_ids=true | all-gather | bytes 9216 | tf_op jit(solution)/shard_map/all_gather | solution.py:79
  80.0 14.6 %while.25 = (s32[]{:T(128)}, f32[256,256]{1,0:T(8,128)S(1)}, f32[256,256]{1,0:T(8,128)S(1)}, pred[4,512]{1,0:T(4,128)(4,1)S(1)}, s32[4]{0:T(128)S(1)}, /*index=5...) while((s32[]{:T(128)}, f32[256,256]{1,0:T(8,128)S(1)}, ...), condition=%wide.region_5.6_spmd.clone, body=%wide.region_4.5_spmd.clone.sunk | while | flops 204473344 | bytes 3573216 | solution.py:112
  80.0 0.7 dynamic_slice.99
  81.3 0.7 iota_add_fusion.11
  82.3 0.7 convolution_add_fusion.5
  83.6 0.7 dynamic_slice.99
  85.0 0.7 iota_add_fusion.11
  86.0 0.7 convolution_add_fusion.5
  87.3 0.7 dynamic_slice.99
  88.6 0.7 iota_add_fusion.11
  90.9 0.7 dynamic_slice.99
  92.3 0.7 iota_add_fusion.11
  93.3 0.7 convolution_add_fusion.5
  95.3 1.9 copy.27
  97.2 135.0 %reduce-scatter.4.cloned.1.call-done = f32[64,256]{1,0:T(8,128)} async-done(((f32[2048,256]{1,0:T(8,128)}), f32[64,256]{1,0:T(8,128)}) %reduce-scatter.4.cloned.1.call-update) | async-done | bytes 65552 | tf_op jit(solution)/shard_map/reduce_scatter | solution.py:117
  (85 shorter events, 10.5 us)
Async XLA Ops:
  6.5 1.2 copy-start
  6.5 4.8 %copy-start.3 = (s32[4,8]{1,0:T(4,128)S(1)}, s32[4,8]{1,0:T(4,128)}, u32[]{:S(2)}) copy-start(s32[4,8]{1,0:T(4,128)} %param.13) | copy-start | bytes 388
  6.5 4.9 %copy-start.2 = (s32[256]{0:T(256)S(1)}, s32[256]{0:T(256)}, u32[]{:S(2)}) copy-start(s32[256]{0:T(256)} %param.12) | copy-start | bytes 3076
  6.5 27.3 %copy-start.1 = (s32[256]{0:T(256)S(1)}, s32[256]{0:T(256)}, u32[]{:S(2)}) copy-start(s32[256]{0:T(256)} %param.11) | copy-start | bytes 3076
  6.5 46.1 %all-gather.5.cloned.1.call-start = ((), (), s32[]{:S(2)}) async-start(), calls=%async_computation.1 | async-start | bytes 1179648 | tf_op jit(solution)/shard_map/all_gather | solution.py:35
  10.2 222.0 %reduce-scatter.4.cloned.1.call-start = ((), (), s32[]{:S(2)}) async-start(), calls=%async_computation.2 | async-start | bytes 2162688 | tf_op jit(solution)/shard_map/reduce_scatter | solution.py:117
Sparse Core Ops, SparseCore 0:
  10.4 42.2 all-gather.4
  97.4 134.8 reduce-scatter.3
where the time goes:
time: 239 us
  waiting for transfers between devices  137 us (57%)
  blocking collectives  57.2 us (24%)
  between operations  13.6 us (6%)
  local copies, waits for them, and re-layouts  12.3 us (5%)
  matrix products  9.88 us (4%)
  other arithmetic  8.95 us (4%)
    reduce_scatter x1, waiting for transfers between devices, per_device(): lax.psum_scatter(contract_rows(feats, grad_proj), ('dp', 'pool'), scatter...  135 us
    all_gather x1, blocking collectives, per_device(): lax.all_gather(prior_occurrence_correction, 'pool', axis=0, tiled=True)  22.2 us
    all_gather x1, blocking collectives, per_device(): all_totals = lax.all_gather(normalizer_sums, 'pool', axis=0, tiled=True)  18.4 us
    all_gather x1, blocking collectives, per_device(): all_partners = lax.all_gather(partners, 'pool', axis=0, tiled=True)  16.5 us
    unnamed x16, local copies, waits for them, and re-layouts  5.63 us
    dynamic_slice x24, local copies, waits for them, and re-layouts, per_device(): lax.scan(add_totals, jnp.zeros((shard_rows,), jnp.float32), shared)  5.62 us
    add x8, other arithmetic, segment_contributions(): target_ordinal = first_col + jnp.arange(block_width, dtype=jnp.int32)  5.53 us
  transfers between devices with their start and end apart: 2, of which 2 were waited for; matrix products, arithmetic and copies ran while one was open for 1% of the time, Pallas kernels for 0%

commit v1 on v0

v1 whole, which is shorter than its diff:
```python
import functools
import math

import jax
import jax.numpy as jnp
from jax import lax
from jax.experimental import pallas as pl
from jax.experimental.pallas import tpu as pltpu
from jax.sharding import PartitionSpec as P

sharpness_scaler = 0.05
epsilon = 1e-06
META = 16
DIGIT_BITS = 8
DIGIT = 1 << DIGIT_BITS
EXP2_SCALE = math.log2(math.e) / sharpness_scaler
LOG2E = math.log2(math.e)
VMEM_LIMIT = 48 * 1024 * 1024

VMEM = pl.BlockSpec(memory_space=pltpu.VMEM)
SMEM = pl.BlockSpec(memory_space=pltpu.SMEM)
ANY = pl.BlockSpec(memory_space=pl.ANY)


def f32_dot(left, right, dims):
    return lax.dot_general(left, right, (dims, ((), ())), preferred_element_type=jnp.float32)


def column_of(row):
    return jnp.transpose(jnp.broadcast_to(row, (128, row.shape[1])))


def project_kernel(chunks, feats_hbm, w_hbm, partners_ref, buckets_ref, msg_ref, normed_ref, inv_ref,
                   feats_v, w_v, sems):
    rows, din = feats_v.shape
    width = w_v.shape[1]
    step = din // chunks
    copies = []
    for c in range(chunks):
        cut = pl.ds(c * step, step)
        pair = (
            pltpu.make_async_copy(feats_hbm.at[:, cut], feats_v.at[:, cut], sems.at[0, c]),
            pltpu.make_async_copy(w_hbm.at[cut, :], w_v.at[cut, :], sems.at[1, c]),
        )
        pair[0].start()
        pair[1].start()
        copies.append(pair)
    partners = partners_ref[...]
    logq = -(buckets_ref[...].astype(jnp.float32) + 0.5) / 4.0
    high = (partners >> DIGIT_BITS).astype(jnp.float32)
    low = (partners & (DIGIT - 1)).astype(jnp.float32)
    kinds = lax.broadcasted_iota(jnp.int32, (META, rows), 0)
    meta = jnp.where(kinds == 0, logq, jnp.where(kinds == 1, high, jnp.where(kinds == 2, low, 0.0)))
    msg_ref[pl.ds(rows, META), :] = meta.astype(jnp.bfloat16)
    projected = jnp.zeros((rows, width), jnp.float32)
    for c in range(chunks):
        copies[c][0].wait()
        copies[c][1].wait()
        cut = pl.ds(c * step, step)
        projected = projected + jnp.dot(feats_v[:, cut], w_v[cut, :], preferred_element_type=jnp.float32)
    inv_norm = lax.rsqrt(jnp.sum(projected * projected, axis=1, keepdims=True) + epsilon)
    normed = projected * inv_norm
    normed_ref[...] = normed
    inv_ref[...] = jnp.broadcast_to(inv_norm, inv_ref.shape)
    msg_ref[pl.ds(0, rows), :] = normed.astype(jnp.bfloat16)


def project(feats, tower_w, partners, buckets):
    rows, din = feats.shape
    width = tower_w.shape[1]
    chunks = 4
    return pl.pallas_call(
        functools.partial(project_kernel, chunks),
        out_shape=(
            jax.ShapeDtypeStruct((rows + META, width), jnp.bfloat16),
            jax.ShapeDtypeStruct((rows, width), jnp.float32),
            jax.ShapeDtypeStruct((rows, 128), jnp.float32),
        ),
        in_specs=[ANY, ANY, VMEM, VMEM],
        out_specs=(VMEM, VMEM, VMEM),
        scratch_shapes=[
            pltpu.VMEM((rows, din), jnp.bfloat16),
            pltpu.VMEM((din, width), jnp.bfloat16),
            pltpu.SemaphoreType.DMA((2, chunks)),
        ],
        compiler_params=pltpu.CompilerParams(vmem_limit_bytes=VMEM_LIMIT),
        cost_estimate=pl.CostEstimate(
            flops=2 * rows * din * width, bytes_accessed=2 * din * (rows + width), transcendentals=rows
        ),
        name="project",
    )(feats, tower_w, partners, buckets)


def cut_kernel(feats_hbm, msg_hbm, *refs):
    outs, sems = refs[:-1], refs[-1]
    width = outs[0].shape[1]
    me = lax.axis_index("dp")
    copies = []
    for k, out in enumerate(outs):
        first = pl.multiple_of((me ^ k) * width, width)
        copies.append(pltpu.make_async_copy(feats_hbm.at[:, pl.ds(first, width)], out, sems.at[k]))
    for copy in copies:
        copy.start()
    for copy in copies:
        copy.wait()


def cut_feats(feats, msg, parts):
    rows, din = feats.shape
    return pl.pallas_call(
        cut_kernel,
        out_shape=tuple(jax.ShapeDtypeStruct((rows, din // parts), feats.dtype) for _ in range(parts)),
        in_specs=[ANY, ANY],
        out_specs=tuple(ANY for _ in range(parts)),
        scratch_shapes=[pltpu.SemaphoreType.DMA((parts,))],
        cost_estimate=pl.CostEstimate(flops=0, bytes_accessed=4 * rows * din, transcendentals=0),
        name="cut_feats",
    )(feats, msg)


def grad_kernel(members, counts_ref, *refs):
    msgs = refs[:members]
    normed_ref, inv_ref, out_ref, emb, weight, recip, partner, kept = refs[members:]
    rows, width = normed_ref.shape
    group = lax.axis_index("dp")
    me = lax.axis_index("pool")
    lanes = lax.broadcasted_iota(jnp.int32, (1, rows), 1)
    for k in range(members):
        emb[k] = msgs[k][pl.ds(0, rows), :]
        meta = msgs[k][pl.ds(rows, META), :].astype(jnp.float32)
        valid = lanes < counts_ref[group, me ^ k]
        weight[k] = jnp.where(valid, jnp.exp2(meta[0:1] * -LOG2E), 0.0)
        partner[k] = jnp.where(valid, meta[1:2] * DIGIT + meta[2:3], -1.0)

    def exps(left, k):
        return jnp.exp2(f32_dot(left, emb[k], ((1,), (1,))) * EXP2_SCALE)

    def folded(terms):
        total = terms[:, 0:128]
        for at in range(128, rows, 128):
            total = total + terms[:, at:at + 128]
        return total

    off_diagonal = lax.broadcasted_iota(jnp.int32, (rows, rows), 0) != lax.broadcasted_iota(
        jnp.int32, (rows, rows), 1
    )

    def store_recip(block, sums):
        totals = jnp.sum(jnp.transpose(sums), axis=0, keepdims=True)
        recip[block] = jnp.where(weight[block] > 0.0, 1.0 / totals, 0.0)

    own_emb = emb[0]
    own_sums = jnp.zeros((rows, 128), jnp.float32)
    for k in range(members):
        powers = exps(own_emb, k)
        if k == 0:
            powers = jnp.where(off_diagonal, powers, 0.0)
        kept[k] = powers
        own_sums = own_sums + folded(powers * weight[k])
    store_recip(0, own_sums)

    def other_totals(block, carry):
        left = emb[block]
        sums = folded(jnp.where(off_diagonal, exps(left, block), 0.0) * weight[block])
        for k in range(1, members):
            sums = sums + folded(exps(left, block ^ k) * weight[block ^ k])
        store_recip(block, sums)
        return carry

    lax.fori_loop(1, members, other_totals, 0)

    own_recip = column_of(recip[0])[:, 0:1]
    own_weight = column_of(weight[0])[:, 0:1]
    own_partner = column_of(partner[0])[:, 0:1].astype(jnp.int32)
    own_rows = me * rows + lax.broadcasted_iota(jnp.int32, (rows, 1), 0)
    grad = jnp.zeros((rows, width), jnp.float32)
    for k in range(members):
        columns = (me ^ k) * rows + lanes
        powers = kept[k]
        along = powers * weight[k] * own_recip - jnp.where(own_partner == columns, 1.0, 0.0)
        across = powers * own_weight * recip[k] - jnp.where(
            partner[k].astype(jnp.int32) == own_rows, 1.0, 0.0
        )
        grad = grad + f32_dot(along.astype(jnp.bfloat16), emb[k], ((1,), (0,)))
        grad = grad + f32_dot(across.astype(jnp.bfloat16), emb[k], ((1,), (0,)))
    normed = normed_ref[...]
    inward = jnp.sum(normed * grad, axis=1, keepdims=True)
    out_ref[...] = ((grad - normed * inward) * inv_ref[:, 0:1]).astype(jnp.bfloat16)


def group_grad(counts, msgs, normed, inv):
    members = len(msgs)
    rows, width = normed.shape
    pairs = members * members * rows * rows
    return pl.pallas_call(
        functools.partial(grad_kernel, members),
        out_shape=jax.ShapeDtypeStruct((rows, width), jnp.bfloat16),
        in_specs=[SMEM] + [VMEM] * (members + 2),
        out_specs=VMEM,
        scratch_shapes=[
            pltpu.VMEM((members, rows, width), jnp.bfloat16),
            pltpu.VMEM((members, 1, rows), jnp.float32),
            pltpu.VMEM((members, 1, rows), jnp.float32),
            pltpu.VMEM((members, 1, rows), jnp.float32),
            pltpu.VMEM((members, rows, rows), jnp.float32),
        ],
        compiler_params=pltpu.CompilerParams(vmem_limit_bytes=VMEM_LIMIT),
        cost_estimate=pl.CostEstimate(
            flops=2 * pairs * width, bytes_accessed=2 * members * rows * width, transcendentals=pairs
        ),
        name="group_grad",
    )(counts, *msgs, normed, inv)


def weight_kernel(parts, members, *refs):
    feats, grads = refs[:parts], refs[parts:2 * parts]
    own_ref, outs, total = refs[2 * parts], refs[2 * parts + 1:-1], refs[-1]
    piece = own_ref.shape[0]
    me = lax.axis_index("pool")
    result = f32_dot(feats[0][...], grads[0][...], ((0,), (0,)))
    for k in range(1, parts):
        result = result + f32_dot(feats[k][...], grads[k][...], ((0,), (0,)))
    total[...] = result
    for k, out in enumerate((own_ref,) + outs):
        first = pl.multiple_of((me ^ k) * piece, piece)
        out[...] = total[pl.ds(first, piece), :].astype(out.dtype)


def weight_grad(feats, grads, members):
    parts = len(feats)
    rows, cols = feats[0].shape
    width = grads[0].shape[1]
    piece = (cols // members, width)
    return pl.pallas_call(
        functools.partial(weight_kernel, parts, members),
        out_shape=(jax.ShapeDtypeStruct(piece, jnp.float32),)
        + tuple(jax.ShapeDtypeStruct(piece, jnp.float32) for _ in range(1, members)),
        in_specs=[VMEM] * (2 * parts),
        out_specs=tuple(VMEM for _ in range(members)),
        scratch_shapes=[pltpu.VMEM((cols, width), jnp.float32)],
        compiler_params=pltpu.CompilerParams(vmem_limit_bytes=VMEM_LIMIT),
        cost_estimate=pl.CostEstimate(
            flops=2 * parts * rows * cols * width, bytes_accessed=2 * parts * rows * cols, transcendentals=0
        ),
        name="weight_grad",
    )(*feats, *grads)


def swap(value, axis, flip):
    size = lax.axis_size(axis)
    return lax.ppermute(value, axis, [(at, at ^ flip) for at in range(size)])


def per_device(feats, tower_w, partners, popularity_buckets, row_counts):
    members = lax.axis_size("pool")
    parts = lax.axis_size("dp")
    minor = 1 << ((members.bit_length() - 1) // 2)
    msg, normed, inv = project(feats, tower_w, partners[None, :], popularity_buckets[None, :])
    msgs = [msg] + [None] * (members - 1)
    for far in range(minor, members, minor):
        msgs[far] = swap(msg, "pool", far)
    for near in range(1, minor):
        for far in range(0, members, minor):
            msgs[far + near] = swap(msgs[far], "pool", near)
    cuts = cut_feats(feats, msg, parts)
    cuts = [cuts[0]] + [swap(cuts[k], "dp", k) for k in range(1, parts)]
    grad_proj = group_grad(row_counts, msgs, normed, inv)
    grads = [grad_proj] + [swap(grad_proj, "dp", k) for k in range(1, parts)]
    pieces = weight_grad(cuts, grads, members)
    total = pieces[0]
    for k in range(1, members):
        total = total + swap(pieces[k], "pool", k)
    return total


def solution(mesh):
    return jax.shard_map(
        per_device,
        mesh=mesh,
        in_specs=(P(("dp", "pool"), None), P(), P(("dp", "pool")), P(("dp", "pool")), P()),
        out_specs=P(("dp", "pool"), None),
        check_vma=False,
    )
```

time: 239 us -> 94.9 us (0.40)
  waiting for transfers between devices: 137 us -> 22.3 us
  blocking collectives: 57.2 us -> 0 us
  Pallas kernels: 0 us -> 41.1 us
  starting transfers between devices: 0.08 us -> 26.2 us
  between operations: 13.6 us -> 0.08 us
  matrix products: 9.88 us -> 0 us
  other arithmetic: 8.95 us -> 0.67 us
  local copies, waits for them, and re-layouts: 12.3 us -> 4.46 us
    reduce_scatter x1 -> x0, waiting for transfers between devices: 135 us -> none  [per_device(): lax.psum_scatter(contract_rows(feats, grad_proj), ('dp', 'pool'), scatter...]
    all_gather x3 -> x0, blocking collectives: 57.2 us -> none  [the longest x1 22.2 us: per_device(): lax.all_gather(prior_occurrence_correction, 'pool', axis=0, tiled=True)]
    pallas_call x0 -> x4, Pallas kernels: none -> 41.1 us  [the longest x1 32.9 us: cut_feats(): pl.pallas_call(cut_kernel, out_shape=tuple((jax.ShapeDtypeStruct((rows, d...]
    ppermute x0 -> x20, starting transfers between devices: none -> 26.2 us  [swap(): return lax.ppermute(value, axis, [(at, at ^ flip) for at in range(size)])]
    ppermute x0 -> x20, waiting for transfers between devices: none -> 22.3 us  [swap(): return lax.ppermute(value, axis, [(at, at ^ flip) for at in range(size)])]
    dot_general x18 -> x0, matrix products: 9.88 us -> none  [the longest x4 2.62 us: both_step(): jnp.dot(mirror_coeff, operand_tensors[0], preferred_element_type=jnp.floa...]
    dynamic_slice x30 -> x0, local copies, waits for them, and re-layouts: 6.29 us -> none  [the longest x24 5.62 us: per_device(): lax.scan(add_totals, jnp.zeros((shard_rows,), jnp.float32), shared)]
    add x20 -> x1, other arithmetic: 5.62 us -> 0.67 us  [per_device(): total = total + swap(pieces[k], 'pool', k)]
  transfers between devices with their start and end apart: 2 -> 20, of which waited for: 2 -> 8; matrix products, arithmetic and copies ran while one was open for 1% -> 0% of each run, Pallas kernels for 0% -> 41%
where the time goes in v1:
time: 94.9 us; the launch traced here: 94.7 us
  Pallas kernels  41.1 us (43%)
  starting transfers between devices  26.2 us (28%)
  waiting for transfers between devices  22.3 us (23%)
  local copies, waits for them, and re-layouts  4.46 us (5%)
    pallas_call x1, Pallas kernels, cut_feats(): pl.pallas_call(cut_kernel, out_shape=tuple((jax.ShapeDtypeStruct((rows, d...  32.9 us
    ppermute x20, starting transfers between devices, swap(): return lax.ppermute(value, axis, [(at, at ^ flip) for at in range(size)])  26.2 us
    ppermute x20, waiting for transfers between devices, swap(): return lax.ppermute(value, axis, [(at, at ^ flip) for at in range(size)])  22.3 us
    pallas_call x1, Pallas kernels, group_grad(): pl.pallas_call(functools.partial(grad_kernel, members), out_shape=jax.Sha...  6.37 us
    unnamed x16, local copies, waits for them, and re-layouts  4.46 us
  transfers between devices with their start and end apart: 20, of which 8 were waited for; matrix products, arithmetic and copies ran while one was open for 0% of the time, Pallas kernels for 41%

profile of v1, /device:TPU:0, one launch (start us, length us, event | category | flops | bytes accessed | tf_op | source)
XLA Modules:
  0.0 94.7 jit_solution(8864751654485767965)
XLA Ops:
  0.0 0.7 copy-done.6
  0.7 1.2 %copy-done = bf16[256,2048]{1,0:T(8,128)(2,1)S(1)} copy-done((bf16[256,2048]{1,0:T(8,128)(2,1)S(1)}, bf16[256,2048]{1,0:T(8,128)(2,1)}, u32[]{:S(2)}) %copy-start) | copy-done | bytes 1048600
  1.9 1.2 %copy-done.1 = bf16[2048,256]{1,0:T(8,128)(2,1)S(1)} copy-done((bf16[2048,256]{1,0:T(8,128)(2,1)S(1)}, bf16[2048,256]{1,0:T(8,128)(2,1)}, u32[]{:S(2)}) %copy-start.1) | copy-done | bytes 1048600
  3.1 1.3 %project.1 = (bf16[272,256]{1,0:T(8,128)(2,1)S(1)}, f32[256,256]{1,0:T(8,128)S(1)}, f32[256,128]{1,0:T(8,128)S(1)}) custom-call(bf16[256,2048]{1,0:T(8,128)(2,1)S(1)} %copy-done, bf16[2048,256]{1,0:T(8,128)(2,1)S(1)} %copy-done.1, s32[1,256]{1,0:T(1,128)S(1)} %bitcast.2, s32[1,256]{1,0:T(1,128)S(1)} %bitcast.3), custom_call_target="tpu_custom_call" | custom-call | flops 268435456 | bytes 2097152 | tf_op jit(solution)/shard_map/project/pallas_call | solution.py:72
  4.4 5.1 %collective-permute-start.8 = (bf16[272,256]{1,0:T(8,128)(2,1)S(1)}, bf16[272,256]{1,0:T(8,128)(2,1)S(1)}, u32[]{:S(2)}, u32[]{:S(2)}) collective-permute-start(bf16[272,256]{1,0:T(8,128)(2,1)S(1)} %get-tuple-element.20.msg_hbm.refs_0_), channel_id=1, source_target_pairs={{0,6},{1,7},{2,4},{3,5},{4,2},{5,3},{6,0},{7,1},{8,14},{9,15},{10,... | collective-permute-start | bytes 417800 | tf_op jit(solution)/shard_map/ppermute | solution.py:251
  9.6 0.6 collective-permute-start.4
  10.2 1.6 %collective-permute-start.3 = (bf16[272,256]{1,0:T(8,128)(2,1)S(1)}, bf16[272,256]{1,0:T(8,128)(2,1)S(1)}, u32[]{:S(2)}, u32[]{:S(2)}) collective-permute-start(bf16[272,256]{1,0:T(8,128)(2,1)S(1)} %get-tuple-element.20.msg_hbm.refs_0_), channel_id=1, source_target_pairs={{0,1},{1,0},{2,3},{3,2},{4,5},{5,4},{6,7},{7,6},{8,9},{9,8},{10,11... | collective-permute-start | bytes 417800 | tf_op jit(solution)/shard_map/ppermute | solution.py:251
  11.8 2.3 %collective-permute-done.8.refs_6_ = bf16[272,256]{1,0:T(8,128)(2,1)S(1)} collective-permute-done((bf16[272,256]{1,0:T(8,128)(2,1)S(1)}, bf16[272,256]{1,0:T(8,128)(2,1)S(1)}, u32[]{:S(2)}, u32[]{:S(2)}) %collective-permute-start.8) | collective-permute-done | bytes 139296 | tf_op jit(solution)/shard_map/ppermute | solution.py:251
  14.2 1.7 %collective-permute-start.9 = (bf16[272,256]{1,0:T(8,128)(2,1)S(1)}, bf16[272,256]{1,0:T(8,128)(2,1)S(1)}, u32[]{:S(2)}, u32[]{:S(2)}) collective-permute-start(bf16[272,256]{1,0:T(8,128)(2,1)S(1)} %collective-permute-done.8.refs_6_), channel_id=1, source_target_pairs={{0,1},{1,0},{2,3},{3,2},{4,5},{5,4},{6,7},{7,6},{8,9},{9,8},{10,11... | collective-permute-start | bytes 417800 | tf_op jit(solution)/shard_map/ppermute | solution.py:251
  15.8 5.5 %collective-permute-done.6.refs_4_ = bf16[272,256]{1,0:T(8,128)(2,1)S(1)} collective-permute-done((bf16[272,256]{1,0:T(8,128)(2,1)S(1)}, bf16[272,256]{1,0:T(8,128)(2,1)S(1)}, u32[]{:S(2)}, u32[]{:S(2)}) %collective-permute-start.6) | collective-permute-done | bytes 139296 | tf_op jit(solution)/shard_map/ppermute | solution.py:251
  21.3 1.5 %collective-permute-start.7 = (bf16[272,256]{1,0:T(8,128)(2,1)S(1)}, bf16[272,256]{1,0:T(8,128)(2,1)S(1)}, u32[]{:S(2)}, u32[]{:S(2)}) collective-permute-start(bf16[272,256]{1,0:T(8,128)(2,1)S(1)} %collective-permute-done.6.refs_4_), channel_id=1, source_target_pairs={{0,1},{1,0},{2,3},{3,2},{4,5},{5,4},{6,7},{7,6},{8,9},{9,8},{10,11... | collective-permute-start | bytes 417800 | tf_op jit(solution)/shard_map/ppermute | solution.py:251
  22.8 0.6 collective-permute-start.5
  23.4 32.9 %cut_feats.1 = (bf16[256,512]{1,0:T(8,128)(2,1)}, bf16[256,512]{1,0:T(8,128)(2,1)}, bf16[256,512]{1,0:T(8,128)(2,1)}, bf16[256,512]{1,0:T(8,128)(2,1)}) custom-call(bf16[256,2048]{1,0:T(8,128)(2,1)} %feats_hbm.3, bf16[272,256]{1,0:T(8,128)(2,1)} %copy-done.3), custom_call_target="tpu_custom_call" | custom-call | bytes 2097152 | tf_op jit(solution)/shard_map/cut_feats/pallas_call | solution.py:110
  56.4 1.6 %collective-permute-start.1 = (bf16[256,512]{1,0:T(8,128)(2,1)}, bf16[256,512]{1,0:T(8,128)(2,1)S(1)}, u32[]{:S(2)}, u32[]{:S(2)}) collective-permute-start(bf16[256,512]{1,0:T(8,128)(2,1)} %get-tuple-element.23), channel_id=1, source_target_pairs={{0,16},{8,24},{16,0},{24,8},{1,17},{9,25},{17,1},{25,9},{2,18},{10... | collective-permute-start | bytes 786440 | tf_op jit(solution)/shard_map/ppermute | solution.py:251
  58.2 0.4 copy-done.7
  58.6 0.9 copy-done.4
  59.6 6.4 %group_grad.1.refs_4_ = bf16[256,256]{1,0:T(8,128)(2,1)S(1)} custom-call(s32[4,8]{1,0:T(4,128)S(1)} %copy-done.7, bf16[272,256]{1,0:T(8,128)(2,1)S(1)} %copy-done.4, bf16[272,256]{1,0:T(8,128)(2,1)S(1)} %collective-permute-done.3.refs_1_, bf16[272,256]{1,0:T(8,128)(2,1)S(1)} %collective-permute-done.4.refs_2_, ...), custom_call_target="tpu_custom_call" | custom-call | flops 2147483648 | bytes 1048576 | tf_op jit(solution)/shard_map/group_grad/pallas_call | solution.py:195
  65.9 1.1 %collective-permute-start.12 = (bf16[256,256]{1,0:T(8,128)(2,1)S(1)}, bf16[256,256]{1,0:T(8,128)(2,1)S(1)}, u32[]{:S(2)}, u32[]{:S(2)}) collective-permute-start(bf16[256,256]{1,0:T(8,128)(2,1)S(1)} %group_grad.1.refs_4_), channel_id=1, source_target_pairs={{0,24},{8,16},{16,8},{24,0},{1,25},{9,17},{17,9},{25,1},{2,26},{10... | collective-permute-start | bytes 393224 | tf_op jit(solution)/shard_map/ppermute | solution.py:251
  67.1 0.7 collective-permute-start.11
  67.9 2.7 %collective-permute-done.2.refs_3_ = bf16[256,512]{1,0:T(8,128)(2,1)S(1)} collective-permute-done((bf16[256,512]{1,0:T(8,128)(2,1)}, bf16[256,512]{1,0:T(8,128)(2,1)S(1)}, u32[]{:S(2)}, u32[]{:S(2)}) %collective-permute-start.2) | collective-permute-done | bytes 262176 | tf_op jit(solution)/shard_map/ppermute | solution.py:251
  70.5 2.7 %collective-permute-done.12.refs_7_ = bf16[256,256]{1,0:T(8,128)(2,1)S(1)} collective-permute-done((bf16[256,256]{1,0:T(8,128)(2,1)S(1)}, bf16[256,256]{1,0:T(8,128)(2,1)S(1)}, u32[]{:S(2)}, u32[]{:S(2)}) %collective-permute-start.12) | collective-permute-done | bytes 131104 | tf_op jit(solution)/shard_map/ppermute | solution.py:251
  73.3 3.3 %collective-permute-done.11.refs_6_ = bf16[256,256]{1,0:T(8,128)(2,1)S(1)} collective-permute-done((bf16[256,256]{1,0:T(8,128)(2,1)S(1)}, bf16[256,256]{1,0:T(8,128)(2,1)S(1)}, u32[]{:S(2)}, u32[]{:S(2)}) %collective-permute-start.11) | collective-permute-done | bytes 131104 | tf_op jit(solution)/shard_map/ppermute | solution.py:251
  76.5 0.5 weight_grad.1
  77.1 1.5 %collective-permute-start.13 = (f32[64,256]{1,0:T(8,128)S(1)}, f32[64,256]{1,0:T(8,128)S(1)}, u32[]{:S(2)}, u32[]{:S(2)}) collective-permute-start(f32[64,256]{1,0:T(8,128)S(1)} %get-tuple-element.28), channel_id=1, source_target_pairs={{0,1},{1,0},{2,3},{3,2},{4,5},{5,4},{6,7},{7,6},{8,9},{9,8},{10,11... | collective-permute-start | bytes 196616 | tf_op jit(solution)/shard_map/ppermute | solution.py:251
  78.6 2.0 %collective-permute-start.15 = (f32[64,256]{1,0:T(8,128)S(1)}, f32[64,256]{1,0:T(8,128)S(1)}, u32[]{:S(2)}, u32[]{:S(2)}) collective-permute-start(f32[64,256]{1,0:T(8,128)S(1)} %get-tuple-element.30), channel_id=1, source_target_pairs={{0,3},{1,2},{2,1},{3,0},{4,7},{5,6},{6,5},{7,4},{8,11},{9,10},{10,... | collective-permute-start | bytes 196616 | tf_op jit(solution)/shard_map/ppermute | solution.py:251
  80.6 1.2 %collective-permute-start.16 = (f32[64,256]{1,0:T(8,128)S(1)}, f32[64,256]{1,0:T(8,128)S(1)}, u32[]{:S(2)}, u32[]{:S(2)}) collective-permute-start(f32[64,256]{1,0:T(8,128)S(1)} %get-tuple-element.31), channel_id=1, source_target_pairs={{0,4},{1,5},{2,6},{3,7},{4,0},{5,1},{6,2},{7,3},{8,12},{9,13},{10,... | collective-permute-start | bytes 196616 | tf_op jit(solution)/shard_map/ppermute | solution.py:251
  81.9 2.6 %collective-permute-start.17 = (f32[64,256]{1,0:T(8,128)S(1)}, f32[64,256]{1,0:T(8,128)S(1)}, u32[]{:S(2)}, u32[]{:S(2)}) collective-permute-start(f32[64,256]{1,0:T(8,128)S(1)} %get-tuple-element.32), channel_id=1, source_target_pairs={{0,5},{1,4},{2,7},{3,6},{4,1},{5,0},{6,3},{7,2},{8,13},{9,12},{10,... | collective-permute-start | bytes 196616 | tf_op jit(solution)/shard_map/ppermute | solution.py:251
  84.5 2.5 %collective-permute-start.18 = (f32[64,256]{1,0:T(8,128)S(1)}, f32[64,256]{1,0:T(8,128)S(1)}, u32[]{:S(2)}, u32[]{:S(2)}) collective-permute-start(f32[64,256]{1,0:T(8,128)S(1)} %get-tuple-element.33), channel_id=1, source_target_pairs={{0,6},{1,7},{2,4},{3,5},{4,2},{5,3},{6,0},{7,1},{8,14},{9,15},{10,... | collective-permute-start | bytes 196616 | tf_op jit(solution)/shard_map/ppermute | solution.py:251
  87.0 1.3 %collective-permute-start.19 = (f32[64,256]{1,0:T(8,128)S(1)}, f32[64,256]{1,0:T(8,128)S(1)}, u32[]{:S(2)}, u32[]{:S(2)}) collective-permute-start(f32[64,256]{1,0:T(8,128)S(1)} %get-tuple-element.34), channel_id=1, source_target_pairs={{0,7},{1,6},{2,5},{3,4},{4,3},{5,2},{6,1},{7,0},{8,15},{9,14},{10,... | collective-permute-start | bytes 196616 | tf_op jit(solution)/shard_map/ppermute | solution.py:251
  88.6 4.4 %collective-permute-done.17 = f32[64,256]{1,0:T(8,128)S(1)} collective-permute-done((f32[64,256]{1,0:T(8,128)S(1)}, f32[64,256]{1,0:T(8,128)S(1)}, u32[]{:S(2)}, u32[]{:S(2)}) %collective-permute-start.17) | collective-permute-done | bytes 65568 | tf_op jit(solution)/shard_map/ppermute | solution.py:251
  93.0 1.1 %collective-permute-done.19 = f32[64,256]{1,0:T(8,128)S(1)} collective-permute-done((f32[64,256]{1,0:T(8,128)S(1)}, f32[64,256]{1,0:T(8,128)S(1)}, u32[]{:S(2)}, u32[]{:S(2)}) %collective-permute-start.19) | collective-permute-done | bytes 65568 | tf_op jit(solution)/shard_map/ppermute | solution.py:251
  94.0 0.7 add_add_fusion
  (29 shorter events, 0.8 us)
Async XLA Ops:
  0.0 0.7 copy-start.6
  0.0 0.7 copy-start.5
  0.7 1.2 %copy-start = (bf16[256,2048]{1,0:T(8,128)(2,1)S(1)}, bf16[256,2048]{1,0:T(8,128)(2,1)}, u32[]{:S(2)}) copy-start(bf16[256,2048]{1,0:T(8,128)(2,1)} %feats_hbm.3) | copy-start | bytes 3145732
  1.9 1.2 %copy-start.1 = (bf16[2048,256]{1,0:T(8,128)(2,1)S(1)}, bf16[2048,256]{1,0:T(8,128)(2,1)}, u32[]{:S(2)}) copy-start(bf16[2048,256]{1,0:T(8,128)(2,1)} %w_hbm.1) | copy-start | bytes 3145732
  4.4 18.9 %copy-start.3 = (bf16[272,256]{1,0:T(8,128)(2,1)}, bf16[272,256]{1,0:T(8,128)(2,1)S(1)}, u32[]{:S(2)}) copy-start(bf16[272,256]{1,0:T(8,128)(2,1)S(1)} %get-tuple-element.20.msg_hbm.refs_0_) | copy-start | bytes 417796
  4.4 9.7 %collective-permute-start.8 = (bf16[272,256]{1,0:T(8,128)(2,1)S(1)}, bf16[272,256]{1,0:T(8,128)(2,1)S(1)}, u32[]{:S(2)}, u32[]{:S(2)}) collective-permute-start(bf16[272,256]{1,0:T(8,128)(2,1)S(1)} %get-tuple-element.20.msg_hbm.refs_0_), channel_id=1, source_target_pairs={{0,6},{1,7},{2,4},{3,5},{4,2},{5,3},{6,0},{7,1},{8,14},{9,15},{10,... | collective-permute-start | bytes 417800 | tf_op jit(solution)/shard_map/ppermute | solution.py:251
  9.6 11.8 %collective-permute-start.6 = (bf16[272,256]{1,0:T(8,128)(2,1)S(1)}, bf16[272,256]{1,0:T(8,128)(2,1)S(1)}, u32[]{:S(2)}, u32[]{:S(2)}) collective-permute-start(bf16[272,256]{1,0:T(8,128)(2,1)S(1)} %get-tuple-element.20.msg_hbm.refs_0_), channel_id=1, source_target_pairs={{0,4},{1,5},{2,6},{3,7},{4,0},{5,1},{6,2},{7,3},{8,12},{9,13},{10,... | collective-permute-start | bytes 417800 | tf_op jit(solution)/shard_map/ppermute | solution.py:251
  9.6 13.3 %collective-permute-start.4 = (bf16[272,256]{1,0:T(8,128)(2,1)S(1)}, bf16[272,256]{1,0:T(8,128)(2,1)S(1)}, u32[]{:S(2)}, u32[]{:S(2)}) collective-permute-start(bf16[272,256]{1,0:T(8,128)(2,1)S(1)} %get-tuple-element.20.msg_hbm.refs_0_), channel_id=1, source_target_pairs={{0,2},{1,3},{2,0},{3,1},{4,6},{5,7},{6,4},{7,5},{8,10},{9,11},{10,... | collective-permute-start | bytes 417800 | tf_op jit(solution)/shard_map/ppermute | solution.py:251
  10.2 46.2 %collective-permute-start.3 = (bf16[272,256]{1,0:T(8,128)(2,1)S(1)}, bf16[272,256]{1,0:T(8,128)(2,1)S(1)}, u32[]{:S(2)}, u32[]{:S(2)}) collective-permute-start(bf16[272,256]{1,0:T(8,128)(2,1)S(1)} %get-tuple-element.20.msg_hbm.refs_0_), channel_id=1, source_target_pairs={{0,1},{1,0},{2,3},{3,2},{4,5},{5,4},{6,7},{7,6},{8,9},{9,8},{10,11... | collective-permute-start | bytes 417800 | tf_op jit(solution)/shard_map/ppermute | solution.py:251
  14.2 43.8 %collective-permute-start.9 = (bf16[272,256]{1,0:T(8,128)(2,1)S(1)}, bf16[272,256]{1,0:T(8,128)(2,1)S(1)}, u32[]{:S(2)}, u32[]{:S(2)}) collective-permute-start(bf16[272,256]{1,0:T(8,128)(2,1)S(1)} %collective-permute-done.8.refs_6_), channel_id=1, source_target_pairs={{0,1},{1,0},{2,3},{3,2},{4,5},{5,4},{6,7},{7,6},{8,9},{9,8},{10,11... | collective-permute-start | bytes 417800 | tf_op jit(solution)/shard_map/ppermute | solution.py:251
  21.3 36.9 %collective-permute-start.7 = (bf16[272,256]{1,0:T(8,128)(2,1)S(1)}, bf16[272,256]{1,0:T(8,128)(2,1)S(1)}, u32[]{:S(2)}, u32[]{:S(2)}) collective-permute-start(bf16[272,256]{1,0:T(8,128)(2,1)S(1)} %collective-permute-done.6.refs_4_), channel_id=1, source_target_pairs={{0,1},{1,0},{2,3},{3,2},{4,5},{5,4},{6,7},{7,6},{8,9},{9,8},{10,11... | collective-permute-start | bytes 417800 | tf_op jit(solution)/shard_map/ppermute | solution.py:251
  22.8 35.4 %collective-permute-start.5 = (bf16[272,256]{1,0:T(8,128)(2,1)S(1)}, bf16[272,256]{1,0:T(8,128)(2,1)S(1)}, u32[]{:S(2)}, u32[]{:S(2)}) collective-permute-start(bf16[272,256]{1,0:T(8,128)(2,1)S(1)} %collective-permute-done.4.refs_2_), channel_id=1, source_target_pairs={{0,1},{1,0},{2,3},{3,2},{4,5},{5,4},{6,7},{7,6},{8,9},{9,8},{10,11... | collective-permute-start | bytes 417800 | tf_op jit(solution)/shard_map/ppermute | solution.py:251
  56.3 11.5 %collective-permute-start = (bf16[256,512]{1,0:T(8,128)(2,1)}, bf16[256,512]{1,0:T(8,128)(2,1)S(1)}, u32[]{:S(2)}, u32[]{:S(2)}) collective-permute-start(bf16[256,512]{1,0:T(8,128)(2,1)} %get-tuple-element.22), channel_id=1, source_target_pairs={{0,8},{8,0},{16,24},{24,16},{1,9},{9,1},{17,25},{25,17},{2,10},{10... | collective-permute-start | bytes 786440 | tf_op jit(solution)/shard_map/ppermute | solution.py:251
  56.4 11.5 %collective-permute-start.1 = (bf16[256,512]{1,0:T(8,128)(2,1)}, bf16[256,512]{1,0:T(8,128)(2,1)S(1)}, u32[]{:S(2)}, u32[]{:S(2)}) collective-permute-start(bf16[256,512]{1,0:T(8,128)(2,1)} %get-tuple-element.23), channel_id=1, source_target_pairs={{0,16},{8,24},{16,0},{24,8},{1,17},{9,25},{17,1},{25,9},{2,18},{10... | collective-permute-start | bytes 786440 | tf_op jit(solution)/shard_map/ppermute | solution.py:251
  58.0 0.7 copy-start.7
  58.0 12.6 %collective-permute-start.2 = (bf16[256,512]{1,0:T(8,128)(2,1)}, bf16[256,512]{1,0:T(8,128)(2,1)S(1)}, u32[]{:S(2)}, u32[]{:S(2)}) collective-permute-start(bf16[256,512]{1,0:T(8,128)(2,1)} %get-tuple-element.24), channel_id=1, source_target_pairs={{0,24},{8,16},{16,8},{24,0},{1,25},{9,17},{17,9},{25,1},{2,26},{10... | collective-permute-start | bytes 786440 | tf_op jit(solution)/shard_map/ppermute | solution.py:251
  58.6 0.9 copy-start.4
  59.5 17.0 %copy-start.2 = (bf16[256,512]{1,0:T(8,128)(2,1)S(1)}, bf16[256,512]{1,0:T(8,128)(2,1)}, u32[]{:S(2)}) copy-start(bf16[256,512]{1,0:T(8,128)(2,1)} %get-tuple-element.21.refs_0_) | copy-start | bytes 786436
  65.9 7.3 %collective-permute-start.12 = (bf16[256,256]{1,0:T(8,128)(2,1)S(1)}, bf16[256,256]{1,0:T(8,128)(2,1)S(1)}, u32[]{:S(2)}, u32[]{:S(2)}) collective-permute-start(bf16[256,256]{1,0:T(8,128)(2,1)S(1)} %group_grad.1.refs_4_), channel_id=1, source_target_pairs={{0,24},{8,16},{16,8},{24,0},{1,25},{9,17},{17,9},{25,1},{2,26},{10... | collective-permute-start | bytes 393224 | tf_op jit(solution)/shard_map/ppermute | solution.py:251
  67.1 9.5 %collective-permute-start.11 = (bf16[256,256]{1,0:T(8,128)(2,1)S(1)}, bf16[256,256]{1,0:T(8,128)(2,1)S(1)}, u32[]{:S(2)}, u32[]{:S(2)}) collective-permute-start(bf16[256,256]{1,0:T(8,128)(2,1)S(1)} %group_grad.1.refs_4_), channel_id=1, source_target_pairs={{0,16},{8,24},{16,0},{24,8},{1,17},{9,25},{17,1},{25,9},{2,18},{10... | collective-permute-start | bytes 393224 | tf_op jit(solution)/shard_map/ppermute | solution.py:251
  67.8 8.7 %collective-permute-start.10 = (bf16[256,256]{1,0:T(8,128)(2,1)S(1)}, bf16[256,256]{1,0:T(8,128)(2,1)S(1)}, u32[]{:S(2)}, u32[]{:S(2)}) collective-permute-start(bf16[256,256]{1,0:T(8,128)(2,1)S(1)} %group_grad.1.refs_4_), channel_id=1, source_target_pairs={{0,8},{8,0},{16,24},{24,16},{1,9},{9,1},{17,25},{25,17},{2,10},{10... | collective-permute-start | bytes 393224 | tf_op jit(solution)/shard_map/ppermute | solution.py:251
  77.1 7.4 %collective-permute-start.13 = (f32[64,256]{1,0:T(8,128)S(1)}, f32[64,256]{1,0:T(8,128)S(1)}, u32[]{:S(2)}, u32[]{:S(2)}) collective-permute-start(f32[64,256]{1,0:T(8,128)S(1)} %get-tuple-element.28), channel_id=1, source_target_pairs={{0,1},{1,0},{2,3},{3,2},{4,5},{5,4},{6,7},{7,6},{8,9},{9,8},{10,11... | collective-permute-start | bytes 196616 | tf_op jit(solution)/shard_map/ppermute | solution.py:251
  78.6 8.4 %collective-permute-start.14 = (f32[64,256]{1,0:T(8,128)S(1)}, f32[64,256]{1,0:T(8,128)S(1)}, u32[]{:S(2)}, u32[]{:S(2)}) collective-permute-start(f32[64,256]{1,0:T(8,128)S(1)} %get-tuple-element.29), channel_id=1, source_target_pairs={{0,2},{1,3},{2,0},{3,1},{4,6},{5,7},{6,4},{7,5},{8,10},{9,11},{10,... | collective-permute-start | bytes 196616 | tf_op jit(solution)/shard_map/ppermute | solution.py:251
  78.6 9.7 %collective-permute-start.15 = (f32[64,256]{1,0:T(8,128)S(1)}, f32[64,256]{1,0:T(8,128)S(1)}, u32[]{:S(2)}, u32[]{:S(2)}) collective-permute-start(f32[64,256]{1,0:T(8,128)S(1)} %get-tuple-element.30), channel_id=1, source_target_pairs={{0,3},{1,2},{2,1},{3,0},{4,7},{5,6},{6,5},{7,4},{8,11},{9,10},{10,... | collective-permute-start | bytes 196616 | tf_op jit(solution)/shard_map/ppermute | solution.py:251
  80.6 8.0 %collective-permute-start.16 = (f32[64,256]{1,0:T(8,128)S(1)}, f32[64,256]{1,0:T(8,128)S(1)}, u32[]{:S(2)}, u32[]{:S(2)}) collective-permute-start(f32[64,256]{1,0:T(8,128)S(1)} %get-tuple-element.31), channel_id=1, source_target_pairs={{0,4},{1,5},{2,6},{3,7},{4,0},{5,1},{6,2},{7,3},{8,12},{9,13},{10,... | collective-permute-start | bytes 196616 | tf_op jit(solution)/shard_map/ppermute | solution.py:251
  81.9 11.1 %collective-permute-start.17 = (f32[64,256]{1,0:T(8,128)S(1)}, f32[64,256]{1,0:T(8,128)S(1)}, u32[]{:S(2)}, u32[]{:S(2)}) collective-permute-start(f32[64,256]{1,0:T(8,128)S(1)} %get-tuple-element.32), channel_id=1, source_target_pairs={{0,5},{1,4},{2,7},{3,6},{4,1},{5,0},{6,3},{7,2},{8,13},{9,12},{10,... | collective-permute-start | bytes 196616 | tf_op jit(solution)/shard_map/ppermute | solution.py:251
  84.5 8.5 %collective-permute-start.18 = (f32[64,256]{1,0:T(8,128)S(1)}, f32[64,256]{1,0:T(8,128)S(1)}, u32[]{:S(2)}, u32[]{:S(2)}) collective-permute-start(f32[64,256]{1,0:T(8,128)S(1)} %get-tuple-element.33), channel_id=1, source_target_pairs={{0,6},{1,7},{2,4},{3,5},{4,2},{5,3},{6,0},{7,1},{8,14},{9,15},{10,... | collective-permute-start | bytes 196616 | tf_op jit(solution)/shard_map/ppermute | solution.py:251
  87.0 7.1 %collective-permute-start.19 = (f32[64,256]{1,0:T(8,128)S(1)}, f32[64,256]{1,0:T(8,128)S(1)}, u32[]{:S(2)}, u32[]{:S(2)}) collective-permute-start(f32[64,256]{1,0:T(8,128)S(1)} %get-tuple-element.34), channel_id=1, source_target_pairs={{0,7},{1,6},{2,5},{3,4},{4,3},{5,2},{6,1},{7,0},{8,15},{9,14},{10,... | collective-permute-start | bytes 196616 | tf_op jit(solution)/shard_map/ppermute | solution.py:251

commit v2 on v1

--- a/solution.py
+++ b/solution.py
@@ -19,7 +19,7 @@
 
 VMEM = pl.BlockSpec(memory_space=pltpu.VMEM)
 SMEM = pl.BlockSpec(memory_space=pltpu.SMEM)
-ANY = pl.BlockSpec(memory_space=pl.ANY)
+HBM = pl.BlockSpec(memory_space=pltpu.HBM)
 
 
 def f32_dot(left, right, dims):
@@ -30,17 +30,18 @@
     return jnp.transpose(jnp.broadcast_to(row, (128, row.shape[1])))
 
 
-def project_kernel(chunks, feats_hbm, w_hbm, partners_ref, buckets_ref, msg_ref, normed_ref, inv_ref,
-                   feats_v, w_v, sems):
-    rows, din = feats_v.shape
+def project_kernel(parts, feats_hbm, w_hbm, partners_ref, buckets_ref, msg_ref, normed_ref, inv_ref, *rest):
+    cuts, w_v, sems = rest[:parts], rest[parts], rest[parts + 1]
     width = w_v.shape[1]
-    step = din // chunks
+    rows, step = cuts[0].shape
+    me = lax.axis_index("dp")
     copies = []
-    for c in range(chunks):
-        cut = pl.ds(c * step, step)
+    for k in range(parts):
+        first = pl.multiple_of((me ^ k) * step, step)
+        cut = pl.ds(first, step)
         pair = (
-            pltpu.make_async_copy(feats_hbm.at[:, cut], feats_v.at[:, cut], sems.at[0, c]),
-            pltpu.make_async_copy(w_hbm.at[cut, :], w_v.at[cut, :], sems.at[1, c]),
+            pltpu.make_async_copy(feats_hbm.at[:, cut], cuts[k], sems.at[0, k]),
+            pltpu.make_async_copy(w_hbm.at[cut, :], w_v.at[pl.ds(k * step, step), :], sems.at[1, k]),
         )
         pair[0].start()
         pair[1].start()
@@ -53,11 +54,10 @@
     meta = jnp.where(kinds == 0, logq, jnp.where(kinds == 1, high, jnp.where(kinds == 2, low, 0.0)))
     msg_ref[pl.ds(rows, META), :] = meta.astype(jnp.bfloat16)
     projected = jnp.zeros((rows, width), jnp.float32)
-    for c in range(chunks):
-        copies[c][0].wait()
-        copies[c][1].wait()
-        cut = pl.ds(c * step, step)
-        projected = projected + jnp.dot(feats_v[:, cut], w_v[cut, :], preferred_element_type=jnp.float32)
+    for k in range(parts):
+        copies[k][0].wait()
+        copies[k][1].wait()
+        projected = projected + f32_dot(cuts[k][...], w_v[pl.ds(k * step, step), :], ((1,), (0,)))
     inv_norm = lax.rsqrt(jnp.sum(projected * projected, axis=1, keepdims=True) + epsilon)
     normed = projected * inv_norm
     normed_ref[...] = normed
@@ -65,23 +65,22 @@
     msg_ref[pl.ds(0, rows), :] = normed.astype(jnp.bfloat16)
 
 
-def project(feats, tower_w, partners, buckets):
+def project(feats, tower_w, partners, buckets, parts):
     rows, din = feats.shape
     width = tower_w.shape[1]
-    chunks = 4
     return pl.pallas_call(
-        functools.partial(project_kernel, chunks),
+        functools.partial(project_kernel, parts),
         out_shape=(
             jax.ShapeDtypeStruct((rows + META, width), jnp.bfloat16),
             jax.ShapeDtypeStruct((rows, width), jnp.float32),
             jax.ShapeDtypeStruct((rows, 128), jnp.float32),
-        ),
-        in_specs=[ANY, ANY, VMEM, VMEM],
-        out_specs=(VMEM, VMEM, VMEM),
+        )
+        + tuple(jax.ShapeDtypeStruct((rows, din // parts), feats.dtype) for _ in range(parts)),
+        in_specs=[HBM, HBM, VMEM, VMEM],
+        out_specs=(VMEM,) * (3 + parts),
         scratch_shapes=[
-            pltpu.VMEM((rows, din), jnp.bfloat16),
             pltpu.VMEM((din, width), jnp.bfloat16),
-            pltpu.SemaphoreType.DMA((2, chunks)),
+            pltpu.SemaphoreType.DMA((2, parts)),
         ],
         compiler_params=pltpu.CompilerParams(vmem_limit_bytes=VMEM_LIMIT),
         cost_estimate=pl.CostEstimate(
@@ -89,33 +88,6 @@
         ),
         name="project",
     )(feats, tower_w, partners, buckets)
-
-
-def cut_kernel(feats_hbm, msg_hbm, *refs):
-    outs, sems = refs[:-1], refs[-1]
-    width = outs[0].shape[1]
-    me = lax.axis_index("dp")
-    copies = []
-    for k, out in enumerate(outs):
-        first = pl.multiple_of((me ^ k) * width, width)
-        copies.append(pltpu.make_async_copy(feats_hbm.at[:, pl.ds(first, width)], out, sems.at[k]))
-    for copy in copies:
-        copy.start()
-    for copy in copies:
-        copy.wait()
-
-
-def cut_feats(feats, msg, parts):
-    rows, din = feats.shape
-    return pl.pallas_call(
-        cut_kernel,
-        out_shape=tuple(jax.ShapeDtypeStruct((rows, din // parts), feats.dtype) for _ in range(parts)),
-        in_specs=[ANY, ANY],
-        out_specs=tuple(ANY for _ in range(parts)),
-        scratch_shapes=[pltpu.SemaphoreType.DMA((parts,))],
-        cost_estimate=pl.CostEstimate(flops=0, bytes_accessed=4 * rows * din, transcendentals=0),
-        name="cut_feats",
-    )(feats, msg)
 
 
 def grad_kernel(members, counts_ref, *refs):
@@ -212,32 +184,23 @@
     )(counts, *msgs, normed, inv)
 
 
-def weight_kernel(parts, members, *refs):
-    feats, grads = refs[:parts], refs[parts:2 * parts]
-    own_ref, outs, total = refs[2 * parts], refs[2 * parts + 1:-1], refs[-1]
-    piece = own_ref.shape[0]
-    me = lax.axis_index("pool")
+def weight_kernel(parts, *refs):
+    feats, grads, out_ref = refs[:parts], refs[parts:2 * parts], refs[2 * parts]
     result = f32_dot(feats[0][...], grads[0][...], ((0,), (0,)))
     for k in range(1, parts):
         result = result + f32_dot(feats[k][...], grads[k][...], ((0,), (0,)))
-    total[...] = result
-    for k, out in enumerate((own_ref,) + outs):
-        first = pl.multiple_of((me ^ k) * piece, piece)
-        out[...] = total[pl.ds(first, piece), :].astype(out.dtype)
-
-
-def weight_grad(feats, grads, members):
+    out_ref[...] = result.astype(out_ref.dtype)
+
+
+def weight_grad(feats, grads):
     parts = len(feats)
     rows, cols = feats[0].shape
     width = grads[0].shape[1]
-    piece = (cols // members, width)
     return pl.pallas_call(
-        functools.partial(weight_kernel, parts, members),
-        out_shape=(jax.ShapeDtypeStruct(piece, jnp.float32),)
-        + tuple(jax.ShapeDtypeStruct(piece, jnp.float32) for _ in range(1, members)),
+        functools.partial(weight_kernel, parts),
+        out_shape=jax.ShapeDtypeStruct((cols, width), jnp.bfloat16),
         in_specs=[VMEM] * (2 * parts),
-        out_specs=tuple(VMEM for _ in range(members)),
-        scratch_shapes=[pltpu.VMEM((cols, width), jnp.float32)],
+        out_specs=VMEM,
         compiler_params=pltpu.CompilerParams(vmem_limit_bytes=VMEM_LIMIT),
         cost_estimate=pl.CostEstimate(
             flops=2 * parts * rows * cols * width, bytes_accessed=2 * parts * rows * cols, transcendentals=0
@@ -255,22 +218,20 @@
     members = lax.axis_size("pool")
     parts = lax.axis_size("dp")
     minor = 1 << ((members.bit_length() - 1) // 2)
-    msg, normed, inv = project(feats, tower_w, partners[None, :], popularity_buckets[None, :])
+    msg, normed, inv, *cuts = project(feats, tower_w, partners[None, :], popularity_buckets[None, :], parts)
     msgs = [msg] + [None] * (members - 1)
     for far in range(minor, members, minor):
         msgs[far] = swap(msg, "pool", far)
     for near in range(1, minor):
         for far in range(0, members, minor):
             msgs[far + near] = swap(msgs[far], "pool", near)
-    cuts = cut_feats(feats, msg, parts)
     cuts = [cuts[0]] + [swap(cuts[k], "dp", k) for k in range(1, parts)]
     grad_proj = group_grad(row_counts, msgs, normed, inv)
     grads = [grad_proj] + [swap(grad_proj, "dp", k) for k in range(1, parts)]
-    pieces = weight_grad(cuts, grads, members)
-    total = pieces[0]
-    for k in range(1, members):
-        total = total + swap(pieces[k], "pool", k)
-    return total
+    partial = weight_grad(cuts, grads)
+    pieces = partial.reshape(members, partial.shape[0] // members, partial.shape[1])
+    pieces = lax.all_to_all(pieces, "pool", split_axis=0, concat_axis=0)
+    return jnp.sum(pieces.astype(jnp.float32), axis=0)
 
 
 def solution(mesh):

time: 94.9 us -> 58.9 us (0.62)
  Pallas kernels: 41.1 us -> 8.11 us
  blocking collectives: 0 us -> 13.4 us
  starting transfers between devices: 26.2 us -> 14.9 us
  waiting for transfers between devices: 22.3 us -> 18.3 us
  local copies, waits for them, and re-layouts: 4.46 us -> 3.15 us
    pallas_call x3 -> x2, Pallas kernels: 34.7 us -> 1.71 us  [the longest x1 1.23 us: project(): pl.pallas_call(functools.partial(project_kernel, parts), out_shape=(jax.S...]
    all_to_all x0 -> x1, blocking collectives: none -> 13.4 us  [per_device(): pieces = lax.all_to_all(pieces, 'pool', split_axis=0, concat_axis=0)]
    ppermute x20 -> x13, starting transfers between devices: 26.2 us -> 14.9 us  [swap(): return lax.ppermute(value, axis, [(at, at ^ flip) for at in range(size)])]
    ppermute x20 -> x13, waiting for transfers between devices: 22.3 us -> 18.3 us  [swap(): return lax.ppermute(value, axis, [(at, at ^ flip) for at in range(size)])]
    unnamed x16 -> x10, local copies, waits for them, and re-layouts: 4.46 us -> 3.15 us
  transfers between devices with their start and end apart: 20 -> 13, of which waited for: 8 -> 6; matrix products, arithmetic and copies ran while one was open for 0% -> 0% of each run, Pallas kernels for 41% -> 11%
where the time goes in v2:
time: 58.9 us; the launch traced here: 58.7 us
  waiting for transfers between devices  18.3 us (31%)
  starting transfers between devices  14.9 us (25%)
  blocking collectives  13.4 us (23%)
  Pallas kernels  8.11 us (14%)
  local copies, waits for them, and re-layouts  3.15 us (5%)
  other arithmetic  0.67 us (1%)
    ppermute x13, waiting for transfers between devices, swap(): return lax.ppermute(value, axis, [(at, at ^ flip) for at in range(size)])  18.3 us
    ppermute x13, starting transfers between devices, swap(): return lax.ppermute(value, axis, [(at, at ^ flip) for at in range(size)])  14.9 us
    all_to_all x1, blocking collectives, per_device(): pieces = lax.all_to_all(pieces, 'pool', split_axis=0, concat_axis=0)  13.4 us
    pallas_call x1, Pallas kernels, group_grad(): pl.pallas_call(functools.partial(grad_kernel, members), out_shape=jax.Sha...  6.4 us
    unnamed x10, local copies, waits for them, and re-layouts  3.15 us
    pallas_call x1, Pallas kernels, project(): pl.pallas_call(functools.partial(project_kernel, parts), out_shape=(jax.S...  1.23 us
  transfers between devices with their start and end apart: 13, of which 6 were waited for; matrix products, arithmetic and copies ran while one was open for 0% of the time, Pallas kernels for 11%

profile of v2, /device:TPU:0, one launch (start us, length us, event | category | flops | bytes accessed | tf_op | source)
XLA Modules:
  0.0 58.7 jit_solution(18267287648548214690)
XLA Ops:
  0.0 0.7 %copy-done.3 = s32[256]{0:T(256)S(1)} copy-done((s32[256]{0:T(256)S(1)}, s32[256]{0:T(256)}, u32[]{:S(2)}) %copy-start.3) | copy-done | bytes 1048
  0.7 0.0 copy-done.2
  0.7 1.2 %copy-done = bf16[256,2048]{1,0:T(8,128)(2,1)S(1)} copy-done((bf16[256,2048]{1,0:T(8,128)(2,1)S(1)}, bf16[256,2048]{1,0:T(8,128)(2,1)}, u32[]{:S(2)}) %copy-start) | copy-done | bytes 1048600
  1.9 1.2 %copy-done.1 = bf16[2048,256]{1,0:T(8,128)(2,1)S(1)} copy-done((bf16[2048,256]{1,0:T(8,128)(2,1)S(1)}, bf16[2048,256]{1,0:T(8,128)(2,1)}, u32[]{:S(2)}) %copy-start.1) | copy-done | bytes 1048600
  3.1 1.2 %project.1 = (bf16[272,256]{1,0:T(8,128)(2,1)S(1)}, f32[256,256]{1,0:T(8,128)S(1)}, f32[256,128]{1,0:T(8,128)S(1)}, bf16[256,512]{1,0:T(8,128)(2,1)S(1)}, bf16[2...) custom-call(bf16[256,2048]{1,0:T(8,128)(2,1)S(1)} %copy-done, ...), custom_call_target="tpu_custom_call" | custom-call | flops 268435456 | bytes 2097152 | tf_op jit(solution)/shard_map/project/pallas_call | solution.py:71
  4.4 5.1 %collective-permute-start.8 = (bf16[272,256]{1,0:T(8,128)(2,1)S(1)}, bf16[272,256]{1,0:T(8,128)(2,1)S(1)}, u32[]{:S(2)}, u32[]{:S(2)}) collective-permute-start(bf16[272,256]{1,0:T(8,128)(2,1)S(1)} %get-tuple-element.16.refs_0_), channel_id=1, source_target_pairs={{0,6},{1,7},{2,4},{3,5},{4,2},{5,3},{6,0},{7,1},{8,14},{9,15},{10,... | collective-permute-start | bytes 417800 | tf_op jit(solution)/shard_map/ppermute | solution.py:214
  9.5 0.0 collective-permute-start.6
  9.5 0.6 %collective-permute-start.4 = (bf16[272,256]{1,0:T(8,128)(2,1)S(1)}, bf16[272,256]{1,0:T(8,128)(2,1)S(1)}, u32[]{:S(2)}, u32[]{:S(2)}) collective-permute-start(bf16[272,256]{1,0:T(8,128)(2,1)S(1)} %get-tuple-element.16.refs_0_), channel_id=1, source_target_pairs={{0,2},{1,3},{2,0},{3,1},{4,6},{5,7},{6,4},{7,5},{8,10},{9,11},{10,... | collective-permute-start | bytes 417800 | tf_op jit(solution)/shard_map/ppermute | solution.py:214
  10.1 1.6 %collective-permute-start.3 = (bf16[272,256]{1,0:T(8,128)(2,1)S(1)}, bf16[272,256]{1,0:T(8,128)(2,1)S(1)}, u32[]{:S(2)}, u32[]{:S(2)}) collective-permute-start(bf16[272,256]{1,0:T(8,128)(2,1)S(1)} %get-tuple-element.16.refs_0_), channel_id=1, source_target_pairs={{0,1},{1,0},{2,3},{3,2},{4,5},{5,4},{6,7},{7,6},{8,9},{9,8},{10,11... | collective-permute-start | bytes 417800 | tf_op jit(solution)/shard_map/ppermute | solution.py:214
  11.8 2.3 %collective-permute-done.8.refs_6_ = bf16[272,256]{1,0:T(8,128)(2,1)S(1)} collective-permute-done((bf16[272,256]{1,0:T(8,128)(2,1)S(1)}, bf16[272,256]{1,0:T(8,128)(2,1)S(1)}, u32[]{:S(2)}, u32[]{:S(2)}) %collective-permute-start.8) | collective-permute-done | bytes 139296 | tf_op jit(solution)/shard_map/ppermute | solution.py:214
  14.1 1.7 %collective-permute-start.9 = (bf16[272,256]{1,0:T(8,128)(2,1)S(1)}, bf16[272,256]{1,0:T(8,128)(2,1)S(1)}, u32[]{:S(2)}, u32[]{:S(2)}) collective-permute-start(bf16[272,256]{1,0:T(8,128)(2,1)S(1)} %collective-permute-done.8.refs_6_), channel_id=1, source_target_pairs={{0,1},{1,0},{2,3},{3,2},{4,5},{5,4},{6,7},{7,6},{8,9},{9,8},{10,11... | collective-permute-start | bytes 417800 | tf_op jit(solution)/shard_map/ppermute | solution.py:214
  15.8 5.5 %collective-permute-done.6.refs_4_ = bf16[272,256]{1,0:T(8,128)(2,1)S(1)} collective-permute-done((bf16[272,256]{1,0:T(8,128)(2,1)S(1)}, bf16[272,256]{1,0:T(8,128)(2,1)S(1)}, u32[]{:S(2)}, u32[]{:S(2)}) %collective-permute-start.6) | collective-permute-done | bytes 139296 | tf_op jit(solution)/shard_map/ppermute | solution.py:214
  21.3 1.5 %collective-permute-start.7 = (bf16[272,256]{1,0:T(8,128)(2,1)S(1)}, bf16[272,256]{1,0:T(8,128)(2,1)S(1)}, u32[]{:S(2)}, u32[]{:S(2)}) collective-permute-start(bf16[272,256]{1,0:T(8,128)(2,1)S(1)} %collective-permute-done.6.refs_4_), channel_id=1, source_target_pairs={{0,1},{1,0},{2,3},{3,2},{4,5},{5,4},{6,7},{7,6},{8,9},{9,8},{10,11... | collective-permute-start | bytes 417800 | tf_op jit(solution)/shard_map/ppermute | solution.py:214
  22.8 0.0 collective-permute-done.4.refs_2_
  22.8 0.6 collective-permute-start.5
  23.3 0.0 collective-permute-done.3.refs_1_
  23.3 1.5 %collective-permute-start.1 = (bf16[256,512]{1,0:T(8,128)(2,1)S(1)}, bf16[256,512]{1,0:T(8,128)(2,1)S(1)}, u32[]{:S(2)}, u32[]{:S(2)}) collective-permute-start(bf16[256,512]{1,0:T(8,128)(2,1)S(1)} %get-tuple-element.14), channel_id=1, source_target_pairs={{0,16},{8,24},{16,0},{24,8},{1,17},{9,25},{17,1},{25,9},{2,18},{10... | collective-permute-start | bytes 786440 | tf_op jit(solution)/shard_map/ppermute | solution.py:214
  24.8 0.0 collective-permute-done.9.refs_7_
  24.9 0.3 collective-permute-start.2
  25.2 2.3 %collective-permute-done.7.refs_5_ = bf16[272,256]{1,0:T(8,128)(2,1)S(1)} collective-permute-done((bf16[272,256]{1,0:T(8,128)(2,1)S(1)}, bf16[272,256]{1,0:T(8,128)(2,1)S(1)}, u32[]{:S(2)}, u32[]{:S(2)}) %collective-permute-start.7) | collective-permute-done | bytes 139296 | tf_op jit(solution)/shard_map/ppermute | solution.py:214
  27.5 1.5 %collective-permute-done.5.refs_3_ = bf16[272,256]{1,0:T(8,128)(2,1)S(1)} collective-permute-done((bf16[272,256]{1,0:T(8,128)(2,1)S(1)}, bf16[272,256]{1,0:T(8,128)(2,1)S(1)}, u32[]{:S(2)}, u32[]{:S(2)}) %collective-permute-start.5) | collective-permute-done | bytes 139296 | tf_op jit(solution)/shard_map/ppermute | solution.py:214
  29.0 6.4 %group_grad.1.refs_4_ = bf16[256,256]{1,0:T(8,128)(2,1)S(1)} custom-call(s32[4,8]{1,0:T(4,128)S(1)} %copy-done.4, bf16[272,256]{1,0:T(8,128)(2,1)S(1)} %get-tuple-element.16.refs_0_, bf16[272,256]{1,0:T(8,128)(2,1)S(1)} %collective-permute-done.3.refs_1_, bf16[272,256]{1,0:T(8,128)(2,1)S(1)} %collective-permute-done.4.refs_2_, ...), custom_call_target="tpu_custom_call" | custom-call | flops 2147483648 | bytes 1048576 | tf_op jit(solution)/shard_map/group_grad/pallas_call | solution.py:167
  35.4 0.1 collective-permute-start.12
  35.5 1.6 %collective-permute-start.11 = (bf16[256,256]{1,0:T(8,128)(2,1)S(1)}, bf16[256,256]{1,0:T(8,128)(2,1)S(1)}, u32[]{:S(2)}, u32[]{:S(2)}) collective-permute-start(bf16[256,256]{1,0:T(8,128)(2,1)S(1)} %group_grad.1.refs_4_), channel_id=1, source_target_pairs={{0,16},{8,24},{16,0},{24,8},{1,17},{9,25},{17,1},{25,9},{2,18},{10... | collective-permute-start | bytes 393224 | tf_op jit(solution)/shard_map/ppermute | solution.py:214
  37.1 0.3 collective-permute-start.10
  37.3 0.0 collective-permute-done.1.refs_2_
  37.3 3.8 %collective-permute-done.12.refs_7_ = bf16[256,256]{1,0:T(8,128)(2,1)S(1)} collective-permute-done((bf16[256,256]{1,0:T(8,128)(2,1)S(1)}, bf16[256,256]{1,0:T(8,128)(2,1)S(1)}, u32[]{:S(2)}, u32[]{:S(2)}) %collective-permute-start.12) | collective-permute-done | bytes 131104 | tf_op jit(solution)/shard_map/ppermute | solution.py:214
  41.2 2.9 %collective-permute-done.11.refs_6_ = bf16[256,256]{1,0:T(8,128)(2,1)S(1)} collective-permute-done((bf16[256,256]{1,0:T(8,128)(2,1)S(1)}, bf16[256,256]{1,0:T(8,128)(2,1)S(1)}, u32[]{:S(2)}, u32[]{:S(2)}) %collective-permute-start.11) | collective-permute-done | bytes 131104 | tf_op jit(solution)/shard_map/ppermute | solution.py:214
  44.1 0.0 collective-permute-done.10.refs_5_
  44.1 0.5 weight_grad.1
  44.6 13.4 %all_to_all.5 = bf16[8,64,256]{2,1,0:T(8,128)(2,1)S(1)} all-to-all(bf16[8,64,256]{2,1,0:T(8,128)(2,1)S(1)} %bitcast.3), channel_id=1, replica_groups=mesh['dp'=4,'pool'=8] {'pool'}, dimensions={0} | all-to-all | bytes 524288 | tf_op jit(solution)/shard_map/all_to_all | solution.py:233
  58.0 0.7 %convert_reduce_fusion = f32[64,256]{1,0:T(8,128)} fusion(bf16[8,64,256]{2,1,0:T(8,128)(2,1)S(1)} %all_to_all.5), kind=kLoop, calls=%fused_computation | loop fusion | flops 245760 | bytes 327680 | tf_op jit(solution)/shard_map/reduce_sum | solution.py:234
  (9 shorter events, 0.0 us)
Async XLA Ops:
  0.0 0.7 %copy-start.3 = (s32[256]{0:T(256)S(1)}, s32[256]{0:T(256)}, u32[]{:S(2)}) copy-start(s32[256]{0:T(256)} %param.8) | copy-start | bytes 3076
  0.0 0.7 %copy-start.2 = (s32[256]{0:T(256)S(1)}, s32[256]{0:T(256)}, u32[]{:S(2)}) copy-start(s32[256]{0:T(256)} %param.7) | copy-start | bytes 3076
  0.7 1.2 %copy-start = (bf16[256,2048]{1,0:T(8,128)(2,1)S(1)}, bf16[256,2048]{1,0:T(8,128)(2,1)}, u32[]{:S(2)}) copy-start(bf16[256,2048]{1,0:T(8,128)(2,1)} %feats_hbm.1) | copy-start | bytes 3145732
  1.9 1.2 %copy-start.1 = (bf16[2048,256]{1,0:T(8,128)(2,1)S(1)}, bf16[2048,256]{1,0:T(8,128)(2,1)}, u32[]{:S(2)}) copy-start(bf16[2048,256]{1,0:T(8,128)(2,1)} %w_hbm.1) | copy-start | bytes 3145732
  4.4 9.7 %collective-permute-start.8 = (bf16[272,256]{1,0:T(8,128)(2,1)S(1)}, bf16[272,256]{1,0:T(8,128)(2,1)S(1)}, u32[]{:S(2)}, u32[]{:S(2)}) collective-permute-start(bf16[272,256]{1,0:T(8,128)(2,1)S(1)} %get-tuple-element.16.refs_0_), channel_id=1, source_target_pairs={{0,6},{1,7},{2,4},{3,5},{4,2},{5,3},{6,0},{7,1},{8,14},{9,15},{10,... | collective-permute-start | bytes 417800 | tf_op jit(solution)/shard_map/ppermute | solution.py:214
  9.5 11.8 %collective-permute-start.6 = (bf16[272,256]{1,0:T(8,128)(2,1)S(1)}, bf16[272,256]{1,0:T(8,128)(2,1)S(1)}, u32[]{:S(2)}, u32[]{:S(2)}) collective-permute-start(bf16[272,256]{1,0:T(8,128)(2,1)S(1)} %get-tuple-element.16.refs_0_), channel_id=1, source_target_pairs={{0,4},{1,5},{2,6},{3,7},{4,0},{5,1},{6,2},{7,3},{8,12},{9,13},{10,... | collective-permute-start | bytes 417800 | tf_op jit(solution)/shard_map/ppermute | solution.py:214
  9.5 13.3 %collective-permute-start.4 = (bf16[272,256]{1,0:T(8,128)(2,1)S(1)}, bf16[272,256]{1,0:T(8,128)(2,1)S(1)}, u32[]{:S(2)}, u32[]{:S(2)}) collective-permute-start(bf16[272,256]{1,0:T(8,128)(2,1)S(1)} %get-tuple-element.16.refs_0_), channel_id=1, source_target_pairs={{0,2},{1,3},{2,0},{3,1},{4,6},{5,7},{6,4},{7,5},{8,10},{9,11},{10,... | collective-permute-start | bytes 417800 | tf_op jit(solution)/shard_map/ppermute | solution.py:214
  10.1 13.2 %collective-permute-start.3 = (bf16[272,256]{1,0:T(8,128)(2,1)S(1)}, bf16[272,256]{1,0:T(8,128)(2,1)S(1)}, u32[]{:S(2)}, u32[]{:S(2)}) collective-permute-start(bf16[272,256]{1,0:T(8,128)(2,1)S(1)} %get-tuple-element.16.refs_0_), channel_id=1, source_target_pairs={{0,1},{1,0},{2,3},{3,2},{4,5},{5,4},{6,7},{7,6},{8,9},{9,8},{10,11... | collective-permute-start | bytes 417800 | tf_op jit(solution)/shard_map/ppermute | solution.py:214
  14.1 10.7 %collective-permute-start.9 = (bf16[272,256]{1,0:T(8,128)(2,1)S(1)}, bf16[272,256]{1,0:T(8,128)(2,1)S(1)}, u32[]{:S(2)}, u32[]{:S(2)}) collective-permute-start(bf16[272,256]{1,0:T(8,128)(2,1)S(1)} %collective-permute-done.8.refs_6_), channel_id=1, source_target_pairs={{0,1},{1,0},{2,3},{3,2},{4,5},{5,4},{6,7},{7,6},{8,9},{9,8},{10,11... | collective-permute-start | bytes 417800 | tf_op jit(solution)/shard_map/ppermute | solution.py:214
  21.3 6.2 %collective-permute-start.7 = (bf16[272,256]{1,0:T(8,128)(2,1)S(1)}, bf16[272,256]{1,0:T(8,128)(2,1)S(1)}, u32[]{:S(2)}, u32[]{:S(2)}) collective-permute-start(bf16[272,256]{1,0:T(8,128)(2,1)S(1)} %collective-permute-done.6.refs_4_), channel_id=1, source_target_pairs={{0,1},{1,0},{2,3},{3,2},{4,5},{5,4},{6,7},{7,6},{8,9},{9,8},{10,11... | collective-permute-start | bytes 417800 | tf_op jit(solution)/shard_map/ppermute | solution.py:214
  22.8 6.2 %collective-permute-start.5 = (bf16[272,256]{1,0:T(8,128)(2,1)S(1)}, bf16[272,256]{1,0:T(8,128)(2,1)S(1)}, u32[]{:S(2)}, u32[]{:S(2)}) collective-permute-start(bf16[272,256]{1,0:T(8,128)(2,1)S(1)} %collective-permute-done.4.refs_2_), channel_id=1, source_target_pairs={{0,1},{1,0},{2,3},{3,2},{4,5},{5,4},{6,7},{7,6},{8,9},{9,8},{10,11... | collective-permute-start | bytes 417800 | tf_op jit(solution)/shard_map/ppermute | solution.py:214
  23.3 13.7 %collective-permute-start = (bf16[256,512]{1,0:T(8,128)(2,1)S(1)}, bf16[256,512]{1,0:T(8,128)(2,1)S(1)}, u32[]{:S(2)}, u32[]{:S(2)}) collective-permute-start(bf16[256,512]{1,0:T(8,128)(2,1)S(1)} %get-tuple-element.13), channel_id=1, source_target_pairs={{0,8},{8,0},{16,24},{24,16},{1,9},{9,1},{17,25},{25,17},{2,10},{10... | collective-permute-start | bytes 786440 | tf_op jit(solution)/shard_map/ppermute | solution.py:214
  23.3 14.0 %collective-permute-start.1 = (bf16[256,512]{1,0:T(8,128)(2,1)S(1)}, bf16[256,512]{1,0:T(8,128)(2,1)S(1)}, u32[]{:S(2)}, u32[]{:S(2)}) collective-permute-start(bf16[256,512]{1,0:T(8,128)(2,1)S(1)} %get-tuple-element.14), channel_id=1, source_target_pairs={{0,16},{8,24},{16,0},{24,8},{1,17},{9,25},{17,1},{25,9},{2,18},{10... | collective-permute-start | bytes 786440 | tf_op jit(solution)/shard_map/ppermute | solution.py:214
  24.8 4.1 %copy-start.4 = (s32[4,8]{1,0:T(4,128)S(1)}, s32[4,8]{1,0:T(4,128)}, u32[]{:S(2)}) copy-start(s32[4,8]{1,0:T(4,128)} %counts_ref.1) | copy-start | bytes 388
  24.9 12.5 %collective-permute-start.2 = (bf16[256,512]{1,0:T(8,128)(2,1)S(1)}, bf16[256,512]{1,0:T(8,128)(2,1)S(1)}, u32[]{:S(2)}, u32[]{:S(2)}) collective-permute-start(bf16[256,512]{1,0:T(8,128)(2,1)S(1)} %get-tuple-element.15), channel_id=1, source_target_pairs={{0,24},{8,16},{16,8},{24,0},{1,25},{9,17},{17,9},{25,1},{2,26},{10... | collective-permute-start | bytes 786440 | tf_op jit(solution)/shard_map/ppermute | solution.py:214
  35.4 5.8 %collective-permute-start.12 = (bf16[256,256]{1,0:T(8,128)(2,1)S(1)}, bf16[256,256]{1,0:T(8,128)(2,1)S(1)}, u32[]{:S(2)}, u32[]{:S(2)}) collective-permute-start(bf16[256,256]{1,0:T(8,128)(2,1)S(1)} %group_grad.1.refs_4_), channel_id=1, source_target_pairs={{0,24},{8,16},{16,8},{24,0},{1,25},{9,17},{17,9},{25,1},{2,26},{10... | collective-permute-start | bytes 393224 | tf_op jit(solution)/shard_map/ppermute | solution.py:214
  35.5 8.6 %collective-permute-start.11 = (bf16[256,256]{1,0:T(8,128)(2,1)S(1)}, bf16[256,256]{1,0:T(8,128)(2,1)S(1)}, u32[]{:S(2)}, u32[]{:S(2)}) collective-permute-start(bf16[256,256]{1,0:T(8,128)(2,1)S(1)} %group_grad.1.refs_4_), channel_id=1, source_target_pairs={{0,16},{8,24},{16,0},{24,8},{1,17},{9,25},{17,1},{25,9},{2,18},{10... | collective-permute-start | bytes 393224 | tf_op jit(solution)/shard_map/ppermute | solution.py:214
  37.1 7.0 %collective-permute-start.10 = (bf16[256,256]{1,0:T(8,128)(2,1)S(1)}, bf16[256,256]{1,0:T(8,128)(2,1)S(1)}, u32[]{:S(2)}, u32[]{:S(2)}) collective-permute-start(bf16[256,256]{1,0:T(8,128)(2,1)S(1)} %group_grad.1.refs_4_), channel_id=1, source_target_pairs={{0,8},{8,0},{16,24},{24,16},{1,9},{9,1},{17,25},{25,17},{2,10},{10... | collective-permute-start | bytes 393224 | tf_op jit(solution)/shard_map/ppermute | solution.py:214

commit v3 on v2

v3 whole, which is shorter than its diff:
```python
import functools
import math

import jax
import jax.numpy as jnp
from jax import lax
from jax.experimental import pallas as pl
from jax.experimental.pallas import tpu as pltpu
from jax.sharding import PartitionSpec as P

sharpness_scaler = 0.05
epsilon = 1e-06
META = 16
DIGIT_BITS = 8
DIGIT = 1 << DIGIT_BITS
EXP2_SCALE = math.log2(math.e) / sharpness_scaler
LOG2E = math.log2(math.e)
VMEM_LIMIT = 48 * 1024 * 1024

VMEM = pl.BlockSpec(memory_space=pltpu.VMEM)
SMEM = pl.BlockSpec(memory_space=pltpu.SMEM)
HBM = pl.BlockSpec(memory_space=pltpu.HBM)


def f32_dot(left, right, dims):
    return lax.dot_general(left, right, (dims, ((), ())), preferred_element_type=jnp.float32)


def column_of(row):
    return jnp.transpose(jnp.broadcast_to(row, (128, row.shape[1])))


def project_kernel(parts, feats_hbm, w_hbm, partners_hbm, buckets_hbm, msg_ref, normed_ref, inv_ref, *rest):
    cuts = rest[:parts]
    w_v, partners_ref, buckets_ref, sems, small_sems = rest[parts:]
    width = w_v.shape[1]
    rows, step = cuts[0].shape
    me = lax.axis_index("dp")
    copies = []
    for k in range(parts):
        first = pl.multiple_of((me ^ k) * step, step)
        cut = pl.ds(first, step)
        pair = (
            pltpu.make_async_copy(feats_hbm.at[:, cut], cuts[k], sems.at[0, k]),
            pltpu.make_async_copy(w_hbm.at[cut, :], w_v.at[pl.ds(k * step, step), :], sems.at[1, k]),
        )
        pair[0].start()
        pair[1].start()
        copies.append(pair)
    small = (
        pltpu.make_async_copy(partners_hbm, partners_ref, small_sems.at[0]),
        pltpu.make_async_copy(buckets_hbm, buckets_ref, small_sems.at[1]),
    )
    for copy in small:
        copy.start()
    for copy in small:
        copy.wait()
    partners = partners_ref[...]
    logq = -(buckets_ref[...].astype(jnp.float32) + 0.5) / 4.0
    high = (partners >> DIGIT_BITS).astype(jnp.float32)
    low = (partners & (DIGIT - 1)).astype(jnp.float32)
    kinds = lax.broadcasted_iota(jnp.int32, (META, rows), 0)
    meta = jnp.where(kinds == 0, logq, jnp.where(kinds == 1, high, jnp.where(kinds == 2, low, 0.0)))
    msg_ref[pl.ds(rows, META), :] = meta.astype(jnp.bfloat16)
    projected = jnp.zeros((rows, width), jnp.float32)
    for k in range(parts):
        copies[k][0].wait()
        copies[k][1].wait()
        projected = projected + f32_dot(cuts[k][...], w_v[pl.ds(k * step, step), :], ((1,), (0,)))
    inv_norm = lax.rsqrt(jnp.sum(projected * projected, axis=1, keepdims=True) + epsilon)
    normed = projected * inv_norm
    normed_ref[...] = normed
    inv_ref[...] = jnp.broadcast_to(inv_norm, inv_ref.shape)
    msg_ref[pl.ds(0, rows), :] = normed.astype(jnp.bfloat16)


def project(feats, tower_w, partners, buckets, parts):
    rows, din = feats.shape
    width = tower_w.shape[1]
    return pl.pallas_call(
        functools.partial(project_kernel, parts),
        out_shape=(
            jax.ShapeDtypeStruct((rows + META, width), jnp.bfloat16),
            jax.ShapeDtypeStruct((rows, width), jnp.float32),
            jax.ShapeDtypeStruct((rows, 128), jnp.float32),
        )
        + tuple(jax.ShapeDtypeStruct((rows, din // parts), feats.dtype) for _ in range(parts)),
        in_specs=[HBM, HBM, HBM, HBM],
        out_specs=(VMEM,) * (3 + parts),
        scratch_shapes=[
            pltpu.VMEM((din, width), jnp.bfloat16),
            pltpu.VMEM((1, rows), jnp.int32),
            pltpu.VMEM((1, rows), jnp.int32),
            pltpu.SemaphoreType.DMA((2, parts)),
            pltpu.SemaphoreType.DMA((2,)),
        ],
        compiler_params=pltpu.CompilerParams(vmem_limit_bytes=VMEM_LIMIT),
        cost_estimate=pl.CostEstimate(
            flops=2 * rows * din * width, bytes_accessed=2 * din * (rows + width), transcendentals=rows
        ),
        name="project",
    )(*(pltpu.with_memory_space_constraint(each, pltpu.HBM) for each in (feats, tower_w, partners, buckets)))


def folded(terms):
    total = terms[:, 0:128]
    for at in range(128, terms.shape[1], 128):
        total = total + terms[:, at:at + 128]
    return total


def rows_to_lanes(sums):
    return jnp.sum(jnp.transpose(sums), axis=0, keepdims=True)


def weight_of(msg_ref, counts_ref, flip):
    rows = msg_ref.shape[0] - META
    meta = msg_ref[pl.ds(rows, META), :].astype(jnp.float32)
    lanes = lax.broadcasted_iota(jnp.int32, (1, rows), 1)
    valid = lanes < counts_ref[lax.axis_index("dp"), lax.axis_index("pool") ^ flip]
    return jnp.where(valid, jnp.exp2(meta[0:1] * -LOG2E), 0.0)


def pair_sums(seen, fresh, counts_ref, msgs, sums_ref, own_ref, sums_out, kept_at):
    rows = own_ref.shape[0] if own_ref is not None else msgs[0].shape[0] - META
    emb = {k: msgs[k][pl.ds(0, rows), :] for k in seen + fresh}
    weight = {k: weight_of(msgs[k], counts_ref, k) for k in seen + fresh}
    sums = {k: sums_ref[k] for k in seen if k}
    own_sums = own_ref[...] if own_ref is not None else jnp.zeros((rows, 128), jnp.float32)
    off_diagonal = lax.broadcasted_iota(jnp.int32, (rows, rows), 0) != lax.broadcasted_iota(
        jnp.int32, (rows, rows), 1
    )

    def powers_of(left, right):
        return jnp.exp2(f32_dot(emb[left], emb[right], ((1,), (1,))) * EXP2_SCALE)

    def down(powers, column):
        return jnp.sum(powers * column, axis=0, keepdims=True)

    own_column = column_of(weight[0])[:, 0:1]
    for k in fresh:
        powers = powers_of(0, k)
        if k == 0:
            powers = jnp.where(off_diagonal, powers, 0.0)
        else:
            sums[k] = down(powers, own_column)
        kept_at(k)[...] = powers
        own_sums = own_sums + folded(powers * weight[k])
    others = [k for k in seen if k]
    for k in fresh:
        if k == 0:
            continue
        column = column_of(weight[k])[:, 0:1]
        mine = folded(jnp.where(off_diagonal, powers_of(k, k), 0.0) * weight[k])
        for other in others:
            powers = powers_of(k, other)
            mine = mine + folded(powers * weight[other])
            sums[other] = sums[other] + down(powers, column)
        sums[k] = sums[k] + rows_to_lanes(mine)
        others.append(k)
    return sums, own_sums, weight, own_column


def pairs_kernel(seen, fresh, *refs):
    known = seen + fresh
    counts_ref, refs = refs[0], refs[1:]
    msgs, refs = dict(zip(known, refs)), refs[len(known):]
    before = {}
    own_ref = None
    if seen:
        sums_ref, own_ref, refs = refs[0], refs[1], refs[2:]
        before = {k: sums_ref[at:at + 1, :] for at, k in enumerate(seen)}
    sums_out, own_out, kept_out = refs
    sums, own_sums, _, _ = pair_sums(
        seen, fresh, counts_ref, msgs, before, own_ref, sums_out, lambda k: kept_out.at[fresh.index(k)]
    )
    own_out[...] = own_sums
    for at, k in enumerate(known):
        sums_out[at:at + 1, :] = sums[k] if k else jnp.zeros_like(sums_out[0:1, :])


def pairs_cost(seen, fresh, rows, width):
    pairs = len(fresh) * len(seen) + len(fresh) * (len(fresh) + 1) // 2
    return pl.CostEstimate(
        flops=2 * pairs * rows * rows * width,
        bytes_accessed=2 * (len(seen) + len(fresh)) * rows * width + 4 * len(fresh) * rows * rows,
        transcendentals=pairs * rows * rows,
    )


def add_pairs(seen, fresh, counts, msgs, state):
    known = seen + fresh
    rows, width = msgs[0].shape[0] - META, msgs[0].shape[1]
    return pl.pallas_call(
        functools.partial(pairs_kernel, seen, fresh),
        out_shape=(
            jax.ShapeDtypeStruct((len(known), rows), jnp.float32),
            jax.ShapeDtypeStruct((rows, 128), jnp.float32),
            jax.ShapeDtypeStruct((len(fresh), rows, rows), jnp.float32),
        ),
        in_specs=[SMEM] + [VMEM] * (len(known) + len(state)),
        out_specs=(VMEM,) * 3,
        compiler_params=pltpu.CompilerParams(vmem_limit_bytes=VMEM_LIMIT),
        cost_estimate=pairs_cost(seen, fresh, rows, width),
        name="add_pairs",
    )(counts, *(msgs[k] for k in known), *state)


def grad_kernel(stages, fresh, *refs):
    seen = [k for stage in stages for k in stage]
    known = seen + fresh
    counts_ref, refs = refs[0], refs[1:]
    msgs, refs = dict(zip(known, refs)), refs[len(known):]
    sums_ref, own_ref, refs = refs[0], refs[1], refs[2:]
    stage_refs, refs = refs[:len(stages)], refs[len(stages):]
    normed_ref, inv_ref, out_ref, kept = refs
    rows, width = normed_ref.shape
    before = {k: sums_ref[at:at + 1, :] for at, k in enumerate(seen)}
    sums, own_sums, weight, own_weight = pair_sums(
        seen, fresh, counts_ref, msgs, before, own_ref, None, lambda k: kept.at[fresh.index(k)]
    )
    sums[0] = rows_to_lanes(own_sums)
    places = {k: kept.at[at] for at, k in enumerate(fresh)}
    for stage, ref in zip(stages, stage_refs):
        for at, k in enumerate(stage):
            places[k] = ref.at[at]

    me = lax.axis_index("pool")
    lanes = lax.broadcasted_iota(jnp.int32, (1, rows), 1)
    own_rows = me * rows + lax.broadcasted_iota(jnp.int32, (rows, 1), 0)

    def partner_of(k):
        meta = msgs[k][pl.ds(rows, META), :].astype(jnp.float32)
        return jnp.where(weight[k] > 0.0, meta[1:2] * DIGIT + meta[2:3], -1.0)

    recip = {k: jnp.where(weight[k] > 0.0, 1.0 / sums[k], 0.0) for k in known}
    own_recip = column_of(recip[0])[:, 0:1]
    own_partner = column_of(partner_of(0))[:, 0:1].astype(jnp.int32)
    both = jnp.zeros((2 * rows, width), jnp.float32)
    for k in known:
        columns = (me ^ k) * rows + lanes
        powers = places[k][...]
        along = powers * weight[k] * own_recip - jnp.where(own_partner == columns, 1.0, 0.0)
        across = powers * own_weight * recip[k] - jnp.where(
            partner_of(k).astype(jnp.int32) == own_rows, 1.0, 0.0
        )
        coefficients = jnp.concatenate([along.astype(jnp.bfloat16), across.astype(jnp.bfloat16)], axis=0)
        both = both + f32_dot(coefficients, msgs[k][pl.ds(0, rows), :], ((1,), (0,)))
    grad = both[:rows] + both[rows:]
    normed = normed_ref[...]
    inward = jnp.sum(normed * grad, axis=1, keepdims=True)
    out_ref[...] = ((grad - normed * inward) * inv_ref[:, 0:1]).astype(jnp.bfloat16)


def group_grad(stages, fresh, counts, msgs, state, kept, normed, inv):
    seen = [k for stage in stages for k in stage]
    known = seen + fresh
    rows, width = normed.shape
    return pl.pallas_call(
        functools.partial(grad_kernel, stages, fresh),
        out_shape=jax.ShapeDtypeStruct((rows, width), jnp.bfloat16),
        in_specs=[SMEM] + [VMEM] * (len(known) + len(state) + len(kept) + 2),
        out_specs=VMEM,
        scratch_shapes=[pltpu.VMEM((len(fresh), rows, rows), jnp.float32)],
        compiler_params=pltpu.CompilerParams(vmem_limit_bytes=VMEM_LIMIT),
        cost_estimate=pairs_cost(seen, fresh, rows, width),
        name="group_grad",
    )(counts, *(msgs[k] for k in known), *state, *kept, normed, inv)


def weight_kernel(parts, *refs):
    feats, grads, out_ref = refs[:parts], refs[parts:2 * parts], refs[2 * parts]
    result = f32_dot(feats[0][...], grads[0][...], ((0,), (0,)))
    for k in range(1, parts):
        result = result + f32_dot(feats[k][...], grads[k][...], ((0,), (0,)))
    out_ref[...] = result.astype(out_ref.dtype)


def weight_grad(feats, grads):
    parts = len(feats)
    rows, cols = feats[0].shape
    width = grads[0].shape[1]
    return pl.pallas_call(
        functools.partial(weight_kernel, parts),
        out_shape=jax.ShapeDtypeStruct((cols, width), jnp.bfloat16),
        in_specs=[VMEM] * (2 * parts),
        out_specs=VMEM,
        compiler_params=pltpu.CompilerParams(vmem_limit_bytes=VMEM_LIMIT),
        cost_estimate=pl.CostEstimate(
            flops=2 * parts * rows * cols * width, bytes_accessed=2 * parts * rows * cols, transcendentals=0
        ),
        name="weight_grad",
    )(*feats, *grads)


def swap(value, axis, flip):
    size = lax.axis_size(axis)
    return lax.ppermute(value, axis, [(at, at ^ flip) for at in range(size)])


def per_device(feats, tower_w, partners, popularity_buckets, row_counts):
    members = lax.axis_size("pool")
    parts = lax.axis_size("dp")
    minor = 1 << ((members.bit_length() - 1) // 2)
    msg, normed, inv, *cuts = project(feats, tower_w, partners[None, :], popularity_buckets[None, :], parts)

    msgs = {0: msg}
    bit = members // 2
    while bit >= minor:
        for k in list(msgs):
            msgs[k ^ bit] = swap(msgs[k], "pool", bit)
        bit //= 2
    majors = sorted(msgs)
    for near in range(1, minor):
        for far in majors:
            msgs[far + near] = swap(msgs[far], "pool", near)
    cuts = [cuts[0]] + [swap(cuts[k], "dp", k) for k in range(1, parts)]

    columns = [[far + near for near in range(minor)] for far in majors]
    stages = [sum(columns[:-2], []), columns[-2]]
    seen, state, kept = [], (), []
    for fresh in stages:
        *state, powers = add_pairs(seen, fresh, row_counts, msgs, state)
        kept.append(powers)
        seen = seen + fresh
    grad_proj = group_grad(stages, columns[-1], row_counts, msgs, state, kept, normed, inv)

    grads = {0: grad_proj}
    bit = parts // 2
    while bit:
        for k in list(grads):
            grads[k ^ bit] = swap(grads[k], "dp", bit)
        bit //= 2
    partial = weight_grad(cuts, [grads[k] for k in range(parts)])
    pieces = partial.reshape(members, partial.shape[0] // members, partial.shape[1])
    pieces = lax.all_to_all(pieces, "pool", split_axis=0, concat_axis=0)
    return jnp.sum(pieces.astype(jnp.float32), axis=0)


def solution(mesh):
    return jax.shard_map(
        per_device,
        mesh=mesh,
        in_specs=(P(("dp", "pool"), None), P(), P(("dp", "pool")), P(("dp", "pool")), P()),
        out_specs=P(("dp", "pool"), None),
        check_vma=False,
    )
```

time: 58.9 us -> 54 us (0.917)
  local copies, waits for them, and re-layouts: 3.15 us -> 0.01 us
  waiting for transfers between devices: 18.3 us -> 15.8 us
  blocking collectives: 13.4 us -> 14.2 us
    unnamed x10 -> x2, local copies, waits for them, and re-layouts: 3.15 us -> 0.01 us
    ppermute x13, waiting for transfers between devices: 18.3 us -> 15.8 us  [swap(): return lax.ppermute(value, axis, [(at, at ^ flip) for at in range(size)])]
    pallas_call x1, Pallas kernels: 1.23 us -> 2.42 us  [project(): pl.pallas_call(functools.partial(project_kernel, parts), out_shape=(jax.S...]
    all_to_all x1, blocking collectives: 13.4 us -> 14.2 us  [per_device(): pieces = lax.all_to_all(pieces, 'pool', split_axis=0, concat_axis=0)]
    pallas_call x1 -> x3, Pallas kernels: 6.4 us -> 5.62 us  [the longest x2 2.86 us: add_pairs(): pl.pallas_call(functools.partial(pairs_kernel, seen, fresh), out_shape=(j...]
  transfers between devices with their start and end apart: 13 -> 13, of which waited for: 6 -> 8; matrix products, arithmetic and copies ran while one was open for 0% -> 0% of each run, Pallas kernels for 11% -> 10%
where the time goes in v3:
time: 54 us; the launch traced here: 53.8 us
  waiting for transfers between devices  15.8 us (29%)
  starting transfers between devices  14.5 us (27%)
  blocking collectives  14.2 us (26%)
  Pallas kernels  8.53 us (16%)
  other arithmetic  0.67 us (1%)
    ppermute x13, waiting for transfers between devices, swap(): return lax.ppermute(value, axis, [(at, at ^ flip) for at in range(size)])  15.8 us
    ppermute x13, starting transfers between devices, swap(): return lax.ppermute(value, axis, [(at, at ^ flip) for at in range(size)])  14.5 us
    all_to_all x1, blocking collectives, per_device(): pieces = lax.all_to_all(pieces, 'pool', split_axis=0, concat_axis=0)  14.2 us
    pallas_call x2, Pallas kernels, add_pairs(): pl.pallas_call(functools.partial(pairs_kernel, seen, fresh), out_shape=(j...  2.86 us
    pallas_call x1, Pallas kernels, group_grad(): pl.pallas_call(functools.partial(grad_kernel, stages, fresh), out_shape=j...  2.76 us
    pallas_call x1, Pallas kernels, project(): pl.pallas_call(functools.partial(project_kernel, parts), out_shape=(jax.S...  2.42 us
  transfers between devices with their start and end apart: 13, of which 8 were waited for; matrix products, arithmetic and copies ran while one was open for 0% of the time, Pallas kernels for 10%

profile of v3, /device:TPU:0, one launch (start us, length us, event | category | flops | bytes accessed | tf_op | source)
XLA Modules:
  0.0 53.8 jit_solution(10655938177643289800)
XLA Ops:
  0.0 2.4 %project.1 = (bf16[272,256]{1,0:T(8,128)(2,1)S(1)}, f32[256,256]{1,0:T(8,128)S(1)}, f32[256,128]{1,0:T(8,128)S(1)}, bf16[256,512]{1,0:T(8,128)(2,1)S(1)}, bf16[2...) custom-call(bf16[256,2048]{1,0:T(8,128)(2,1)} %feats_hbm.1, ...), custom_call_target="tpu_custom_call" | custom-call | flops 268435456 | bytes 2097152 | tf_op jit(solution)/shard_map/project/pallas_call | solution.py:80
  2.4 4.1 %collective-permute-start.6 = (bf16[272,256]{1,0:T(8,128)(2,1)S(1)}, bf16[272,256]{1,0:T(8,128)(2,1)S(1)}, u32[]{:S(2)}, u32[]{:S(2)}) collective-permute-start(bf16[272,256]{1,0:T(8,128)(2,1)S(1)} %get-tuple-element.22.refs_1_), channel_id=1, source_target_pairs={{0,4},{1,5},{2,6},{3,7},{4,0},{5,1},{6,2},{7,3},{8,12},{9,13},{10,... | collective-permute-start | bytes 417800 | tf_op jit(solution)/shard_map/ppermute | solution.py:298
  6.5 1.6 %collective-permute-start.4 = (bf16[272,256]{1,0:T(8,128)(2,1)S(1)}, bf16[272,256]{1,0:T(8,128)(2,1)S(1)}, u32[]{:S(2)}, u32[]{:S(2)}) collective-permute-start(bf16[272,256]{1,0:T(8,128)(2,1)S(1)} %get-tuple-element.22.refs_1_), channel_id=1, source_target_pairs={{0,2},{1,3},{2,0},{3,1},{4,6},{5,7},{6,4},{7,5},{8,10},{9,11},{10,... | collective-permute-start | bytes 417800 | tf_op jit(solution)/shard_map/ppermute | solution.py:298
  8.1 5.2 %collective-permute-done.6.refs_5_ = bf16[272,256]{1,0:T(8,128)(2,1)S(1)} collective-permute-done((bf16[272,256]{1,0:T(8,128)(2,1)S(1)}, bf16[272,256]{1,0:T(8,128)(2,1)S(1)}, u32[]{:S(2)}, u32[]{:S(2)}) %collective-permute-start.6) | collective-permute-done | bytes 139296 | tf_op jit(solution)/shard_map/ppermute | solution.py:298
  13.3 0.6 %collective-permute-start.8 = (bf16[272,256]{1,0:T(8,128)(2,1)S(1)}, bf16[272,256]{1,0:T(8,128)(2,1)S(1)}, u32[]{:S(2)}, u32[]{:S(2)}) collective-permute-start(bf16[272,256]{1,0:T(8,128)(2,1)S(1)} %collective-permute-done.6.refs_5_), channel_id=1, source_target_pairs={{0,2},{1,3},{2,0},{3,1},{4,6},{5,7},{6,4},{7,5},{8,10},{9,11},{10,... | collective-permute-start | bytes 417800 | tf_op jit(solution)/shard_map/ppermute | solution.py:298
  13.9 1.5 %collective-permute-start.3 = (bf16[272,256]{1,0:T(8,128)(2,1)S(1)}, bf16[272,256]{1,0:T(8,128)(2,1)S(1)}, u32[]{:S(2)}, u32[]{:S(2)}) collective-permute-start(bf16[272,256]{1,0:T(8,128)(2,1)S(1)} %get-tuple-element.22.refs_1_), channel_id=1, source_target_pairs={{0,1},{1,0},{2,3},{3,2},{4,5},{5,4},{6,7},{7,6},{8,9},{9,8},{10,11... | collective-permute-start | bytes 417800 | tf_op jit(solution)/shard_map/ppermute | solution.py:298
  15.4 0.0 collective-permute-done.4.refs_3_
  15.4 0.5 collective-permute-start.5
  15.9 1.5 %collective-permute-start.7 = (bf16[272,256]{1,0:T(8,128)(2,1)S(1)}, bf16[272,256]{1,0:T(8,128)(2,1)S(1)}, u32[]{:S(2)}, u32[]{:S(2)}) collective-permute-start(bf16[272,256]{1,0:T(8,128)(2,1)S(1)} %collective-permute-done.6.refs_5_), channel_id=1, source_target_pairs={{0,1},{1,0},{2,3},{3,2},{4,5},{5,4},{6,7},{7,6},{8,9},{9,8},{10,11... | collective-permute-start | bytes 417800 | tf_op jit(solution)/shard_map/ppermute | solution.py:298
  17.4 0.9 %collective-permute-done.8.refs_7_ = bf16[272,256]{1,0:T(8,128)(2,1)S(1)} collective-permute-done((bf16[272,256]{1,0:T(8,128)(2,1)S(1)}, bf16[272,256]{1,0:T(8,128)(2,1)S(1)}, u32[]{:S(2)}, u32[]{:S(2)}) %collective-permute-start.8) | collective-permute-done | bytes 139296 | tf_op jit(solution)/shard_map/ppermute | solution.py:298
  18.4 1.5 %collective-permute-start.9 = (bf16[272,256]{1,0:T(8,128)(2,1)S(1)}, bf16[272,256]{1,0:T(8,128)(2,1)S(1)}, u32[]{:S(2)}, u32[]{:S(2)}) collective-permute-start(bf16[272,256]{1,0:T(8,128)(2,1)S(1)} %collective-permute-done.8.refs_7_), channel_id=1, source_target_pairs={{0,1},{1,0},{2,3},{3,2},{4,5},{5,4},{6,7},{7,6},{8,9},{9,8},{10,11... | collective-permute-start | bytes 417800 | tf_op jit(solution)/shard_map/ppermute | solution.py:298
  19.9 0.0 collective-permute-start
  19.9 0.6 %collective-permute-done.3.refs_2_ = bf16[272,256]{1,0:T(8,128)(2,1)S(1)} collective-permute-done((bf16[272,256]{1,0:T(8,128)(2,1)S(1)}, bf16[272,256]{1,0:T(8,128)(2,1)S(1)}, u32[]{:S(2)}, u32[]{:S(2)}) %collective-permute-start.3) | collective-permute-done | bytes 139296 | tf_op jit(solution)/shard_map/ppermute | solution.py:298
  20.5 1.5 %collective-permute-start.1 = (bf16[256,512]{1,0:T(8,128)(2,1)S(1)}, bf16[256,512]{1,0:T(8,128)(2,1)S(1)}, u32[]{:S(2)}, u32[]{:S(2)}) collective-permute-start(bf16[256,512]{1,0:T(8,128)(2,1)S(1)} %get-tuple-element.20), channel_id=1, source_target_pairs={{0,16},{8,24},{16,0},{24,8},{1,17},{9,25},{17,1},{25,9},{2,18},{10... | collective-permute-start | bytes 786440 | tf_op jit(solution)/shard_map/ppermute | solution.py:298
  22.0 1.5 %collective-permute-done.5.refs_4_ = bf16[272,256]{1,0:T(8,128)(2,1)S(1)} collective-permute-done((bf16[272,256]{1,0:T(8,128)(2,1)S(1)}, bf16[272,256]{1,0:T(8,128)(2,1)S(1)}, u32[]{:S(2)}, u32[]{:S(2)}) %collective-permute-start.5) | collective-permute-done | bytes 139296 | tf_op jit(solution)/shard_map/ppermute | solution.py:298
  23.5 0.0 collective-permute-start.2
  23.5 1.4 %add_pairs.2 = (f32[4,256]{1,0:T(4,128)S(1)}, f32[256,128]{1,0:T(8,128)S(1)}, f32[4,256,256]{2,1,0:T(8,128)S(1)}) custom-call(s32[4,8]{1,0:T(4,128)S(1)} %copy-done, bf16[272,256]{1,0:T(8,128)(2,1)S(1)} %get-tuple-element.22.refs_1_, bf16[272,256]{1,0:T(8,128)(2,1)S(1)} %collective-permute-done.3.refs_2_, ...), custom_call_target="tpu_custom_call" | custom-call | flops 335544320 | bytes 1572864 | tf_op jit(solution)/shard_map/add_pairs/pallas_call | solution.py:194
  24.9 1.6 %collective-permute-done.7.refs_6_ = bf16[272,256]{1,0:T(8,128)(2,1)S(1)} collective-permute-done((bf16[272,256]{1,0:T(8,128)(2,1)S(1)}, bf16[272,256]{1,0:T(8,128)(2,1)S(1)}, u32[]{:S(2)}, u32[]{:S(2)}) %collective-permute-start.7) | collective-permute-done | bytes 139296 | tf_op jit(solution)/shard_map/ppermute | solution.py:298
  26.5 1.5 %add_pairs.3 = (f32[6,256]{1,0:T(8,128)S(1)}, f32[256,128]{1,0:T(8,128)S(1)}, f32[2,256,256]{2,1,0:T(8,128)S(1)}) custom-call(s32[4,8]{1,0:T(4,128)S(1)} %copy-done, bf16[272,256]{1,0:T(8,128)(2,1)S(1)} %get-tuple-element.22.refs_1_, bf16[272,256]{1,0:T(8,128)(2,1)S(1)} %collective-permute-done.3.refs_2_, ...), custom_call_target="tpu_custom_call" | custom-call | flops 369098752 | bytes 1310720 | tf_op jit(solution)/shard_map/add_pairs/pallas_call | solution.py:194
  27.9 0.3 collective-permute-done.9.refs_8_
  28.2 2.8 %group_grad.1.refs_4_ = bf16[256,256]{1,0:T(8,128)(2,1)S(1)} custom-call(s32[4,8]{1,0:T(4,128)S(1)} %copy-done, bf16[272,256]{1,0:T(8,128)(2,1)S(1)} %get-tuple-element.22.refs_1_, bf16[272,256]{1,0:T(8,128)(2,1)S(1)} %collective-permute-done.3.refs_2_, bf16[272,256]{1,0:T(8,128)(2,1)S(1)} %collective-permute-done.4.refs_3_, ...), custom_call_target="tpu_custom_call" | custom-call | flops 503316480 | bytes 1572864 | tf_op jit(solution)/shard_map/group_grad/pallas_call | solution.py:259
  31.0 1.6 %collective-permute-start.11 = (bf16[256,256]{1,0:T(8,128)(2,1)S(1)}, bf16[256,256]{1,0:T(8,128)(2,1)S(1)}, u32[]{:S(2)}, u32[]{:S(2)}) collective-permute-start(bf16[256,256]{1,0:T(8,128)(2,1)S(1)} %group_grad.1.refs_4_), channel_id=1, source_target_pairs={{0,16},{8,24},{16,0},{24,8},{1,17},{9,25},{17,1},{25,9},{2,18},{10... | collective-permute-start | bytes 393224 | tf_op jit(solution)/shard_map/ppermute | solution.py:298
  32.5 0.0 collective-permute-start.10
  32.5 4.5 %collective-permute-done.11.refs_6_ = bf16[256,256]{1,0:T(8,128)(2,1)S(1)} collective-permute-done((bf16[256,256]{1,0:T(8,128)(2,1)S(1)}, bf16[256,256]{1,0:T(8,128)(2,1)S(1)}, u32[]{:S(2)}, u32[]{:S(2)}) %collective-permute-start.11) | collective-permute-done | bytes 131104 | tf_op jit(solution)/shard_map/ppermute | solution.py:298
  37.1 0.0 collective-permute-start.12
  37.1 0.0 collective-permute-done.refs_1_
  37.1 0.0 collective-permute-done.1.refs_2_
  37.1 0.0 collective-permute-done.10.refs_5_
  37.1 1.3 %collective-permute-done.12.refs_7_ = bf16[256,256]{1,0:T(8,128)(2,1)S(1)} collective-permute-done((bf16[256,256]{1,0:T(8,128)(2,1)S(1)}, bf16[256,256]{1,0:T(8,128)(2,1)S(1)}, u32[]{:S(2)}, u32[]{:S(2)}) %collective-permute-start.12) | collective-permute-done | bytes 131104 | tf_op jit(solution)/shard_map/ppermute | solution.py:298
  38.4 0.5 weight_grad.1
  38.9 14.2 %all_to_all.5 = bf16[8,64,256]{2,1,0:T(8,128)(2,1)S(1)} all-to-all(bf16[8,64,256]{2,1,0:T(8,128)(2,1)S(1)} %bitcast.3), channel_id=1, replica_groups=mesh['dp'=4,'pool'=8] {'pool'}, dimensions={0} | all-to-all | bytes 524288 | tf_op jit(solution)/shard_map/all_to_all | solution.py:336
  53.1 0.7 %convert_reduce_fusion = f32[64,256]{1,0:T(8,128)} fusion(bf16[8,64,256]{2,1,0:T(8,128)(2,1)S(1)} %all_to_all.5), kind=kLoop, calls=%fused_computation | loop fusion | flops 245760 | bytes 327680 | tf_op jit(solution)/shard_map/reduce_sum | solution.py:337
  (3 shorter events, 0.0 us)
Async XLA Ops:
  2.4 10.9 %collective-permute-start.6 = (bf16[272,256]{1,0:T(8,128)(2,1)S(1)}, bf16[272,256]{1,0:T(8,128)(2,1)S(1)}, u32[]{:S(2)}, u32[]{:S(2)}) collective-permute-start(bf16[272,256]{1,0:T(8,128)(2,1)S(1)} %get-tuple-element.22.refs_1_), channel_id=1, source_target_pairs={{0,4},{1,5},{2,6},{3,7},{4,0},{5,1},{6,2},{7,3},{8,12},{9,13},{10,... | collective-permute-start | bytes 417800 | tf_op jit(solution)/shard_map/ppermute | solution.py:298
  6.5 8.9 %collective-permute-start.4 = (bf16[272,256]{1,0:T(8,128)(2,1)S(1)}, bf16[272,256]{1,0:T(8,128)(2,1)S(1)}, u32[]{:S(2)}, u32[]{:S(2)}) collective-permute-start(bf16[272,256]{1,0:T(8,128)(2,1)S(1)} %get-tuple-element.22.refs_1_), channel_id=1, source_target_pairs={{0,2},{1,3},{2,0},{3,1},{4,6},{5,7},{6,4},{7,5},{8,10},{9,11},{10,... | collective-permute-start | bytes 417800 | tf_op jit(solution)/shard_map/ppermute | solution.py:298
  13.3 5.1 %collective-permute-start.8 = (bf16[272,256]{1,0:T(8,128)(2,1)S(1)}, bf16[272,256]{1,0:T(8,128)(2,1)S(1)}, u32[]{:S(2)}, u32[]{:S(2)}) collective-permute-start(bf16[272,256]{1,0:T(8,128)(2,1)S(1)} %collective-permute-done.6.refs_5_), channel_id=1, source_target_pairs={{0,2},{1,3},{2,0},{3,1},{4,6},{5,7},{6,4},{7,5},{8,10},{9,11},{10,... | collective-permute-start | bytes 417800 | tf_op jit(solution)/shard_map/ppermute | solution.py:298
  13.9 6.6 %collective-permute-start.3 = (bf16[272,256]{1,0:T(8,128)(2,1)S(1)}, bf16[272,256]{1,0:T(8,128)(2,1)S(1)}, u32[]{:S(2)}, u32[]{:S(2)}) collective-permute-start(bf16[272,256]{1,0:T(8,128)(2,1)S(1)} %get-tuple-element.22.refs_1_), channel_id=1, source_target_pairs={{0,1},{1,0},{2,3},{3,2},{4,5},{5,4},{6,7},{7,6},{8,9},{9,8},{10,11... | collective-permute-start | bytes 417800 | tf_op jit(solution)/shard_map/ppermute | solution.py:298
  15.4 8.1 %collective-permute-start.5 = (bf16[272,256]{1,0:T(8,128)(2,1)S(1)}, bf16[272,256]{1,0:T(8,128)(2,1)S(1)}, u32[]{:S(2)}, u32[]{:S(2)}) collective-permute-start(bf16[272,256]{1,0:T(8,128)(2,1)S(1)} %collective-permute-done.4.refs_3_), channel_id=1, source_target_pairs={{0,1},{1,0},{2,3},{3,2},{4,5},{5,4},{6,7},{7,6},{8,9},{9,8},{10,11... | collective-permute-start | bytes 417800 | tf_op jit(solution)/shard_map/ppermute | solution.py:298
  15.9 10.5 %collective-permute-start.7 = (bf16[272,256]{1,0:T(8,128)(2,1)S(1)}, bf16[272,256]{1,0:T(8,128)(2,1)S(1)}, u32[]{:S(2)}, u32[]{:S(2)}) collective-permute-start(bf16[272,256]{1,0:T(8,128)(2,1)S(1)} %collective-permute-done.6.refs_5_), channel_id=1, source_target_pairs={{0,1},{1,0},{2,3},{3,2},{4,5},{5,4},{6,7},{7,6},{8,9},{9,8},{10,11... | collective-permute-start | bytes 417800 | tf_op jit(solution)/shard_map/ppermute | solution.py:298
  18.4 9.8 %collective-permute-start.9 = (bf16[272,256]{1,0:T(8,128)(2,1)S(1)}, bf16[272,256]{1,0:T(8,128)(2,1)S(1)}, u32[]{:S(2)}, u32[]{:S(2)}) collective-permute-start(bf16[272,256]{1,0:T(8,128)(2,1)S(1)} %collective-permute-done.8.refs_7_), channel_id=1, source_target_pairs={{0,1},{1,0},{2,3},{3,2},{4,5},{5,4},{6,7},{7,6},{8,9},{9,8},{10,11... | collective-permute-start | bytes 417800 | tf_op jit(solution)/shard_map/ppermute | solution.py:298
  19.9 3.6 %copy-start = (s32[4,8]{1,0:T(4,128)S(1)}, s32[4,8]{1,0:T(4,128)}, u32[]{:S(2)}) copy-start(s32[4,8]{1,0:T(4,128)} %refs_0_.5) | copy-start | bytes 388
  19.9 17.2 %collective-permute-start = (bf16[256,512]{1,0:T(8,128)(2,1)S(1)}, bf16[256,512]{1,0:T(8,128)(2,1)S(1)}, u32[]{:S(2)}, u32[]{:S(2)}) collective-permute-start(bf16[256,512]{1,0:T(8,128)(2,1)S(1)} %get-tuple-element.19), channel_id=1, source_target_pairs={{0,8},{8,0},{16,24},{24,16},{1,9},{9,1},{17,25},{25,17},{2,10},{10... | collective-permute-start | bytes 786440 | tf_op jit(solution)/shard_map/ppermute | solution.py:298
  20.5 16.6 %collective-permute-start.1 = (bf16[256,512]{1,0:T(8,128)(2,1)S(1)}, bf16[256,512]{1,0:T(8,128)(2,1)S(1)}, u32[]{:S(2)}, u32[]{:S(2)}) collective-permute-start(bf16[256,512]{1,0:T(8,128)(2,1)S(1)} %get-tuple-element.20), channel_id=1, source_target_pairs={{0,16},{8,24},{16,0},{24,8},{1,17},{9,25},{17,1},{25,9},{2,18},{10... | collective-permute-start | bytes 786440 | tf_op jit(solution)/shard_map/ppermute | solution.py:298
  23.5 13.6 %collective-permute-start.2 = (bf16[256,512]{1,0:T(8,128)(2,1)S(1)}, bf16[256,512]{1,0:T(8,128)(2,1)S(1)}, u32[]{:S(2)}, u32[]{:S(2)}) collective-permute-start(bf16[256,512]{1,0:T(8,128)(2,1)S(1)} %get-tuple-element.21), channel_id=1, source_target_pairs={{0,24},{8,16},{16,8},{24,0},{1,25},{9,17},{17,9},{25,1},{2,26},{10... | collective-permute-start | bytes 786440 | tf_op jit(solution)/shard_map/ppermute | solution.py:298
  31.0 6.1 %collective-permute-start.11 = (bf16[256,256]{1,0:T(8,128)(2,1)S(1)}, bf16[256,256]{1,0:T(8,128)(2,1)S(1)}, u32[]{:S(2)}, u32[]{:S(2)}) collective-permute-start(bf16[256,256]{1,0:T(8,128)(2,1)S(1)} %group_grad.1.refs_4_), channel_id=1, source_target_pairs={{0,16},{8,24},{16,0},{24,8},{1,17},{9,25},{17,1},{25,9},{2,18},{10... | collective-permute-start | bytes 393224 | tf_op jit(solution)/shard_map/ppermute | solution.py:298
  32.5 4.5 %collective-permute-start.10 = (bf16[256,256]{1,0:T(8,128)(2,1)S(1)}, bf16[256,256]{1,0:T(8,128)(2,1)S(1)}, u32[]{:S(2)}, u32[]{:S(2)}) collective-permute-start(bf16[256,256]{1,0:T(8,128)(2,1)S(1)} %group_grad.1.refs_4_), channel_id=1, source_target_pairs={{0,8},{8,0},{16,24},{24,16},{1,9},{9,1},{17,25},{25,17},{2,10},{10... | collective-permute-start | bytes 393224 | tf_op jit(solution)/shard_map/ppermute | solution.py:298
  37.1 1.3 %collective-permute-start.12 = (bf16[256,256]{1,0:T(8,128)(2,1)S(1)}, bf16[256,256]{1,0:T(8,128)(2,1)S(1)}, u32[]{:S(2)}, u32[]{:S(2)}) collective-permute-start(bf16[256,256]{1,0:T(8,128)(2,1)S(1)} %collective-permute-done.11.refs_6_), channel_id=1, source_target_pairs={{0,8},{8,0},{16,24},{24,16},{1,9},{9,1},{17,25},{25,17},{2,10},{10... | collective-permute-start | bytes 393224 | tf_op jit(solution)/shard_map/ppermute | solution.py:298

commit v4 on v3

--- a/solution.py
+++ b/solution.py
@@ -19,6 +19,7 @@
 
 VMEM = pl.BlockSpec(memory_space=pltpu.VMEM)
 SMEM = pl.BlockSpec(memory_space=pltpu.SMEM)
+ANY = pl.BlockSpec(memory_space=pl.ANY)
 HBM = pl.BlockSpec(memory_space=pltpu.HBM)
 
 
@@ -298,6 +299,21 @@
     return lax.ppermute(value, axis, [(at, at ^ flip) for at in range(size)])
 
 
+def order_kernel(*refs):
+    pass
+
+
+def after(value, *earlier):
+    return pl.pallas_call(
+        order_kernel,
+        out_shape=jax.ShapeDtypeStruct(value.shape, value.dtype),
+        in_specs=[ANY] * (1 + len(earlier)),
+        out_specs=ANY,
+        input_output_aliases={0: 0},
+        name="after",
+    )(value, *earlier)
+
+
 def per_device(feats, tower_w, partners, popularity_buckets, row_counts):
     members = lax.axis_size("pool")
     parts = lax.axis_size("dp")
@@ -305,14 +321,24 @@
     msg, normed, inv, *cuts = project(feats, tower_w, partners[None, :], popularity_buckets[None, :], parts)
 
     msgs = {0: msg}
-    bit = members // 2
-    while bit >= minor:
-        for k in list(msgs):
-            msgs[k ^ bit] = swap(msgs[k], "pool", bit)
-        bit //= 2
-    majors = sorted(msgs)
     for near in range(1, minor):
-        for far in majors:
+        msgs[near] = swap(msg, "pool", near)
+    bits = []
+    bit = minor
+    while bit < members:
+        bits.append(bit)
+        msgs[bit] = swap(msg, "pool", bit)
+        bit *= 2
+    first = bits[0]
+    for near in range(1, minor):
+        msgs[first + near] = swap(msgs[first], "pool", near)
+    msgs[bits[-1]] = after(msgs[bits[-1]], *(msgs[base + near] for base in (0, first) for near in range(1, minor)))
+    for at, bit in enumerate(bits):
+        for k in range(bit + minor, 2 * bit, minor):
+            msgs[k] = swap(msgs[bit], "pool", k ^ bit) if k ^ bit in bits else swap(msgs[k ^ bit], "pool", bit)
+    majors = sorted(k for k in msgs if k % minor == 0)
+    for far in majors[2:]:
+        for near in range(1, minor):
             msgs[far + near] = swap(msgs[far], "pool", near)
     cuts = [cuts[0]] + [swap(cuts[k], "dp", k) for k in range(1, parts)]
 

time: 54 us -> 57.1 us (1.057)
  local copies, waits for them, and re-layouts: 0.01 us -> 3.13 us
  starting transfers between devices: 14.5 us -> 16.5 us
  waiting for transfers between devices: 15.8 us -> 14.4 us
  blocking collectives: 14.2 us -> 13.6 us
    unnamed x2 -> x18, local copies, waits for them, and re-layouts: 0.01 us -> 3.13 us
    ppermute x13, starting transfers between devices: 14.5 us -> 16.5 us  [swap(): return lax.ppermute(value, axis, [(at, at ^ flip) for at in range(size)])]
    ppermute x13, waiting for transfers between devices: 15.8 us -> 14.4 us  [swap(): return lax.ppermute(value, axis, [(at, at ^ flip) for at in range(size)])]
    all_to_all x1, blocking collectives: 14.2 us -> 13.6 us  [per_device(): pieces = lax.all_to_all(pieces, 'pool', split_axis=0, concat_axis=0)]
  transfers between devices with their start and end apart: 13 -> 13, of which waited for: 8 -> 4; matrix products, arithmetic and copies ran while one was open for 0% -> 0% of each run, Pallas kernels for 10% -> 10%
where the time goes in v4:
time: 57.1 us; the launch traced here: 56.9 us
  starting transfers between devices  16.5 us (29%)
  waiting for transfers between devices  14.4 us (25%)
  blocking collectives  13.6 us (24%)
  Pallas kernels  8.53 us (15%)
  local copies, waits for them, and re-layouts  3.13 us (5%)
  other arithmetic  0.67 us (1%)
    ppermute x13, starting transfers between devices, swap(): return lax.ppermute(value, axis, [(at, at ^ flip) for at in range(size)])  16.5 us
    ppermute x13, waiting for transfers between devices, swap(): return lax.ppermute(value, axis, [(at, at ^ flip) for at in range(size)])  14.4 us
    all_to_all x1, blocking collectives, per_device(): pieces = lax.all_to_all(pieces, 'pool', split_axis=0, concat_axis=0)  13.6 us
    unnamed x18, local copies, waits for them, and re-layouts  3.13 us
    pallas_call x2, Pallas kernels, add_pairs(): pl.pallas_call(functools.partial(pairs_kernel, seen, fresh), out_shape=(j...  2.83 us
    pallas_call x1, Pallas kernels, group_grad(): pl.pallas_call(functools.partial(grad_kernel, stages, fresh), out_shape=j...  2.79 us
    pallas_call x1, Pallas kernels, project(): pl.pallas_call(functools.partial(project_kernel, parts), out_shape=(jax.S...  2.42 us
  transfers between devices with their start and end apart: 13, of which 4 were waited for; matrix products, arithmetic and copies ran while one was open for 0% of the time, Pallas kernels for 10%

profile of v4, /device:TPU:0, one launch (start us, length us, event | category | flops | bytes accessed | tf_op | source)
XLA Modules:
  0.0 56.9 jit_solution(3352693426146219243)
XLA Ops:
  0.0 2.4 %project.1 = (bf16[272,256]{1,0:T(8,128)(2,1)S(1)}, f32[256,256]{1,0:T(8,128)S(1)}, f32[256,128]{1,0:T(8,128)S(1)}, bf16[256,512]{1,0:T(8,128)(2,1)S(1)}, bf16[2...) custom-call(bf16[256,2048]{1,0:T(8,128)(2,1)} %feats_hbm.1, ...), custom_call_target="tpu_custom_call" | custom-call | flops 268435456 | bytes 2097152 | tf_op jit(solution)/shard_map/project/pallas_call | solution.py:81
  2.4 3.1 %collective-permute-start.4 = (bf16[272,256]{1,0:T(8,128)(2,1)S(1)}, bf16[272,256]{1,0:T(8,128)(2,1)S(1)}, u32[]{:S(2)}, u32[]{:S(2)}) collective-permute-start(bf16[272,256]{1,0:T(8,128)(2,1)S(1)} %get-tuple-element.22.refs_1_), channel_id=1, source_target_pairs={{0,2},{1,3},{2,0},{3,1},{4,6},{5,7},{6,4},{7,5},{8,10},{9,11},{10,... | collective-permute-start | bytes 417800 | tf_op jit(solution)/shard_map/ppermute | solution.py:299
  5.5 1.5 %collective-permute-start.3 = (bf16[272,256]{1,0:T(8,128)(2,1)S(1)}, bf16[272,256]{1,0:T(8,128)(2,1)S(1)}, u32[]{:S(2)}, u32[]{:S(2)}) collective-permute-start(bf16[272,256]{1,0:T(8,128)(2,1)S(1)} %get-tuple-element.22.refs_1_), channel_id=1, source_target_pairs={{0,1},{1,0},{2,3},{3,2},{4,5},{5,4},{6,7},{7,6},{8,9},{9,8},{10,11... | collective-permute-start | bytes 417800 | tf_op jit(solution)/shard_map/ppermute | solution.py:299
  7.0 2.6 %collective-permute-start.6 = (bf16[272,256]{1,0:T(8,128)(2,1)S(1)}, bf16[272,256]{1,0:T(8,128)(2,1)S(1)}, u32[]{:S(2)}, u32[]{:S(2)}) collective-permute-start(bf16[272,256]{1,0:T(8,128)(2,1)S(1)} %get-tuple-element.22.refs_1_), channel_id=1, source_target_pairs={{0,4},{1,5},{2,6},{3,7},{4,0},{5,1},{6,2},{7,3},{8,12},{9,13},{10,... | collective-permute-start | bytes 417800 | tf_op jit(solution)/shard_map/ppermute | solution.py:299
  9.6 3.1 %collective-permute-start.5 = (bf16[272,256]{1,0:T(8,128)(2,1)S(1)}, bf16[272,256]{1,0:T(8,128)(2,1)S(1)}, u32[]{:S(2)}, u32[]{:S(2)}) collective-permute-start(bf16[272,256]{1,0:T(8,128)(2,1)S(1)} %collective-permute-done.4.refs_3_), channel_id=1, source_target_pairs={{0,1},{1,0},{2,3},{3,2},{4,5},{5,4},{6,7},{7,6},{8,9},{9,8},{10,11... | collective-permute-start | bytes 417800 | tf_op jit(solution)/shard_map/ppermute | solution.py:299
  12.7 0.0 collective-permute-done.3.refs_1_.refs_2_
  12.7 3.1 %collective-permute-done.6.refs_0_ = bf16[272,256]{1,0:T(8,128)(2,1)S(1)} collective-permute-done((bf16[272,256]{1,0:T(8,128)(2,1)S(1)}, bf16[272,256]{1,0:T(8,128)(2,1)S(1)}, u32[]{:S(2)}, u32[]{:S(2)}) %collective-permute-start.6) | collective-permute-done | bytes 139296 | tf_op jit(solution)/shard_map/ppermute | solution.py:299
  15.8 0.0 collective-permute-done.5.refs_2_.refs_4_
  15.8 0.6 %copy-done.6 = bf16[272,256]{1,0:T(8,128)(2,1)} copy-done((bf16[272,256]{1,0:T(8,128)(2,1)}, bf16[272,256]{1,0:T(8,128)(2,1)S(1)}, u32[]{:S(2)}) %copy-start.6) | copy-done | bytes 139288
  16.4 0.6 %copy-done.3 = bf16[272,256]{1,0:T(8,128)(2,1)} copy-done((bf16[272,256]{1,0:T(8,128)(2,1)}, bf16[272,256]{1,0:T(8,128)(2,1)S(1)}, u32[]{:S(2)}) %copy-start.3) | copy-done | bytes 139288
  17.1 0.0 collective-permute-start.8
  17.1 1.4 %collective-permute-start.7 = (bf16[272,256]{1,0:T(8,128)(2,1)}, bf16[272,256]{1,0:T(8,128)(2,1)S(1)}, u32[]{:S(2)}, u32[]{:S(2)}) collective-permute-start(bf16[272,256]{1,0:T(8,128)(2,1)} %after.1.refs_5_), channel_id=1, source_target_pairs={{0,1},{1,0},{2,3},{3,2},{4,5},{5,4},{6,7},{7,6},{8,9},{9,8},{10,11... | collective-permute-start | bytes 417800 | tf_op jit(solution)/shard_map/ppermute | solution.py:299
  18.5 3.8 %collective-permute-done.8.refs_7_ = bf16[272,256]{1,0:T(8,128)(2,1)S(1)} collective-permute-done((bf16[272,256]{1,0:T(8,128)(2,1)}, bf16[272,256]{1,0:T(8,128)(2,1)S(1)}, u32[]{:S(2)}, u32[]{:S(2)}) %collective-permute-start.8) | collective-permute-done | bytes 139296 | tf_op jit(solution)/shard_map/ppermute | solution.py:299
  22.3 1.3 %collective-permute-start.9 = (bf16[272,256]{1,0:T(8,128)(2,1)S(1)}, bf16[272,256]{1,0:T(8,128)(2,1)S(1)}, u32[]{:S(2)}, u32[]{:S(2)}) collective-permute-start(bf16[272,256]{1,0:T(8,128)(2,1)S(1)} %collective-permute-done.8.refs_7_), channel_id=1, source_target_pairs={{0,1},{1,0},{2,3},{3,2},{4,5},{5,4},{6,7},{7,6},{8,9},{9,8},{10,11... | collective-permute-start | bytes 417800 | tf_op jit(solution)/shard_map/ppermute | solution.py:299
  23.7 0.0 collective-permute-start
  23.7 1.5 %collective-permute-start.1 = (bf16[256,512]{1,0:T(8,128)(2,1)S(1)}, bf16[256,512]{1,0:T(8,128)(2,1)S(1)}, u32[]{:S(2)}, u32[]{:S(2)}) collective-permute-start(bf16[256,512]{1,0:T(8,128)(2,1)S(1)} %get-tuple-element.20), channel_id=1, source_target_pairs={{0,16},{8,24},{16,0},{24,8},{1,17},{9,25},{17,1},{25,9},{2,18},{10... | collective-permute-start | bytes 786440 | tf_op jit(solution)/shard_map/ppermute | solution.py:299
  25.2 0.3 collective-permute-start.2
  25.5 0.9 %copy-done.1 = bf16[272,256]{1,0:T(8,128)(2,1)S(1)} copy-done((bf16[272,256]{1,0:T(8,128)(2,1)S(1)}, bf16[272,256]{1,0:T(8,128)(2,1)}, u32[]{:S(2)}) %copy-start.1) | copy-done | bytes 139288
  26.4 0.9 %copy-done.4 = bf16[272,256]{1,0:T(8,128)(2,1)S(1)} copy-done((bf16[272,256]{1,0:T(8,128)(2,1)S(1)}, bf16[272,256]{1,0:T(8,128)(2,1)}, u32[]{:S(2)}) %copy-start.4) | copy-done | bytes 139288
  27.3 1.4 %add_pairs.2 = (f32[4,256]{1,0:T(4,128)S(1)}, f32[256,128]{1,0:T(8,128)S(1)}, f32[4,256,256]{2,1,0:T(8,128)S(1)}) custom-call(s32[4,8]{1,0:T(4,128)S(1)} %copy-done.8, bf16[272,256]{1,0:T(8,128)(2,1)S(1)} %get-tuple-element.22.refs_1_, bf16[272,256]{1,0:T(8,128)(2,1)S(1)} %copy-done.1, bf16[272,256]{1,0:T(8,128)(2,1)S(1)} %collective-permute-done.4.refs_3_, ...), custom_call_target="tpu_custom_call" | custom-call | flops 335544320 | bytes 1572864 | tf_op jit(solution)/shard_map/add_pairs/pallas_call | solution.py:195
  28.8 1.4 %add_pairs.3 = (f32[6,256]{1,0:T(8,128)S(1)}, f32[256,128]{1,0:T(8,128)S(1)}, f32[2,256,256]{2,1,0:T(8,128)S(1)}) custom-call(s32[4,8]{1,0:T(4,128)S(1)} %copy-done.8, bf16[272,256]{1,0:T(8,128)(2,1)S(1)} %get-tuple-element.22.refs_1_, bf16[272,256]{1,0:T(8,128)(2,1)S(1)} %copy-done.2, bf16[272,256]{1,0:T(8,128)(2,1)S(1)} %collective-permute-done.4.refs_3_, ...), custom_call_target="tpu_custom_call" | custom-call | flops 369098752 | bytes 1310720 | tf_op jit(solution)/shard_map/add_pairs/pallas_call | solution.py:195
  30.2 2.8 %group_grad.1.refs_4_ = bf16[256,256]{1,0:T(8,128)(2,1)S(1)} custom-call(s32[4,8]{1,0:T(4,128)S(1)} %copy-done.8, bf16[272,256]{1,0:T(8,128)(2,1)S(1)} %get-tuple-element.22.refs_1_, bf16[272,256]{1,0:T(8,128)(2,1)S(1)} %copy-done.2, bf16[272,256]{1,0:T(8,128)(2,1)S(1)} %collective-permute-done.4.refs_3_, bf16[272,256]{1,0:T(8,128)(2,1)S(1)} %copy-done.5, ...), custom_call_target="tpu_custom_call" | custom-call | flops 503316480 | bytes 1572864 | tf_op jit(solution)/shard_map/group_grad/pallas_call | solution.py:260
  33.0 1.6 %collective-permute-start.11 = (bf16[256,256]{1,0:T(8,128)(2,1)S(1)}, bf16[256,256]{1,0:T(8,128)(2,1)S(1)}, u32[]{:S(2)}, u32[]{:S(2)}) collective-permute-start(bf16[256,256]{1,0:T(8,128)(2,1)S(1)} %group_grad.1.refs_4_), channel_id=1, source_target_pairs={{0,16},{8,24},{16,0},{24,8},{1,17},{9,25},{17,1},{25,9},{2,18},{10... | collective-permute-start | bytes 393224 | tf_op jit(solution)/shard_map/ppermute | solution.py:299
  34.6 6.2 %collective-permute-done.11.refs_6_ = bf16[256,256]{1,0:T(8,128)(2,1)S(1)} collective-permute-done((bf16[256,256]{1,0:T(8,128)(2,1)S(1)}, bf16[256,256]{1,0:T(8,128)(2,1)S(1)}, u32[]{:S(2)}, u32[]{:S(2)}) %collective-permute-start.11) | collective-permute-done | bytes 131104 | tf_op jit(solution)/shard_map/ppermute | solution.py:299
  40.8 0.0 collective-permute-start.12
  40.8 0.0 collective-permute-done.refs_1_
  40.8 0.0 collective-permute-done.1.refs_2_
  40.8 0.0 collective-permute-done.2.refs_3_
  40.8 1.3 %collective-permute-done.12.refs_7_ = bf16[256,256]{1,0:T(8,128)(2,1)S(1)} collective-permute-done((bf16[256,256]{1,0:T(8,128)(2,1)S(1)}, bf16[256,256]{1,0:T(8,128)(2,1)S(1)}, u32[]{:S(2)}, u32[]{:S(2)}) %collective-permute-start.12) | collective-permute-done | bytes 131104 | tf_op jit(solution)/shard_map/ppermute | solution.py:299
  42.2 0.5 weight_grad.1
  42.6 13.6 %all_to_all.5 = bf16[8,64,256]{2,1,0:T(8,128)(2,1)S(1)} all-to-all(bf16[8,64,256]{2,1,0:T(8,128)(2,1)S(1)} %bitcast.3), channel_id=1, replica_groups=mesh['dp'=4,'pool'=8] {'pool'}, dimensions={0} | all-to-all | bytes 524288 | tf_op jit(solution)/shard_map/all_to_all | solution.py:362
  56.2 0.7 %convert_reduce_fusion = f32[64,256]{1,0:T(8,128)} fusion(bf16[8,64,256]{2,1,0:T(8,128)(2,1)S(1)} %all_to_all.5), kind=kLoop, calls=%fused_computation | loop fusion | flops 245760 | bytes 327680 | tf_op jit(solution)/shard_map/reduce_sum | solution.py:363
  (20 shorter events, 0.0 us)
Async XLA Ops:
  2.4 7.2 %collective-permute-start.4 = (bf16[272,256]{1,0:T(8,128)(2,1)S(1)}, bf16[272,256]{1,0:T(8,128)(2,1)S(1)}, u32[]{:S(2)}, u32[]{:S(2)}) collective-permute-start(bf16[272,256]{1,0:T(8,128)(2,1)S(1)} %get-tuple-element.22.refs_1_), channel_id=1, source_target_pairs={{0,2},{1,3},{2,0},{3,1},{4,6},{5,7},{6,4},{7,5},{8,10},{9,11},{10,... | collective-permute-start | bytes 417800 | tf_op jit(solution)/shard_map/ppermute | solution.py:299
  5.5 7.2 %collective-permute-start.3 = (bf16[272,256]{1,0:T(8,128)(2,1)S(1)}, bf16[272,256]{1,0:T(8,128)(2,1)S(1)}, u32[]{:S(2)}, u32[]{:S(2)}) collective-permute-start(bf16[272,256]{1,0:T(8,128)(2,1)S(1)} %get-tuple-element.22.refs_1_), channel_id=1, source_target_pairs={{0,1},{1,0},{2,3},{3,2},{4,5},{5,4},{6,7},{7,6},{8,9},{9,8},{10,11... | collective-permute-start | bytes 417800 | tf_op jit(solution)/shard_map/ppermute | solution.py:299
  7.0 8.7 %collective-permute-start.6 = (bf16[272,256]{1,0:T(8,128)(2,1)S(1)}, bf16[272,256]{1,0:T(8,128)(2,1)S(1)}, u32[]{:S(2)}, u32[]{:S(2)}) collective-permute-start(bf16[272,256]{1,0:T(8,128)(2,1)S(1)} %get-tuple-element.22.refs_1_), channel_id=1, source_target_pairs={{0,4},{1,5},{2,6},{3,7},{4,0},{5,1},{6,2},{7,3},{8,12},{9,13},{10,... | collective-permute-start | bytes 417800 | tf_op jit(solution)/shard_map/ppermute | solution.py:299
  9.6 6.1 %collective-permute-start.5 = (bf16[272,256]{1,0:T(8,128)(2,1)S(1)}, bf16[272,256]{1,0:T(8,128)(2,1)S(1)}, u32[]{:S(2)}, u32[]{:S(2)}) collective-permute-start(bf16[272,256]{1,0:T(8,128)(2,1)S(1)} %collective-permute-done.4.refs_3_), channel_id=1, source_target_pairs={{0,1},{1,0},{2,3},{3,2},{4,5},{5,4},{6,7},{7,6},{8,9},{9,8},{10,11... | collective-permute-start | bytes 417800 | tf_op jit(solution)/shard_map/ppermute | solution.py:299
  12.7 3.1 %copy-start = (bf16[272,256]{1,0:T(8,128)(2,1)}, bf16[272,256]{1,0:T(8,128)(2,1)S(1)}, u32[]{:S(2)}) copy-start(bf16[272,256]{1,0:T(8,128)(2,1)S(1)} %collective-permute-done.3.refs_1_.refs_2_) | copy-start | bytes 417796
  15.7 0.7 %copy-start.6 = (bf16[272,256]{1,0:T(8,128)(2,1)}, bf16[272,256]{1,0:T(8,128)(2,1)S(1)}, u32[]{:S(2)}) copy-start(bf16[272,256]{1,0:T(8,128)(2,1)S(1)} %collective-permute-done.6.refs_0_) | copy-start | bytes 417796
  16.4 0.7 %copy-start.3 = (bf16[272,256]{1,0:T(8,128)(2,1)}, bf16[272,256]{1,0:T(8,128)(2,1)S(1)}, u32[]{:S(2)}) copy-start(bf16[272,256]{1,0:T(8,128)(2,1)S(1)} %collective-permute-done.5.refs_2_.refs_4_) | copy-start | bytes 417796
  17.1 5.3 %collective-permute-start.8 = (bf16[272,256]{1,0:T(8,128)(2,1)}, bf16[272,256]{1,0:T(8,128)(2,1)S(1)}, u32[]{:S(2)}, u32[]{:S(2)}) collective-permute-start(bf16[272,256]{1,0:T(8,128)(2,1)} %after.1.refs_5_), channel_id=1, source_target_pairs={{0,2},{1,3},{2,0},{3,1},{4,6},{5,7},{6,4},{7,5},{8,10},{9,11},{10,... | collective-permute-start | bytes 417800 | tf_op jit(solution)/shard_map/ppermute | solution.py:299
  17.1 11.7 %collective-permute-start.7 = (bf16[272,256]{1,0:T(8,128)(2,1)}, bf16[272,256]{1,0:T(8,128)(2,1)S(1)}, u32[]{:S(2)}, u32[]{:S(2)}) collective-permute-start(bf16[272,256]{1,0:T(8,128)(2,1)} %after.1.refs_5_), channel_id=1, source_target_pairs={{0,1},{1,0},{2,3},{3,2},{4,5},{5,4},{6,7},{7,6},{8,9},{9,8},{10,11... | collective-permute-start | bytes 417800 | tf_op jit(solution)/shard_map/ppermute | solution.py:299
  22.3 7.9 %collective-permute-start.9 = (bf16[272,256]{1,0:T(8,128)(2,1)S(1)}, bf16[272,256]{1,0:T(8,128)(2,1)S(1)}, u32[]{:S(2)}, u32[]{:S(2)}) collective-permute-start(bf16[272,256]{1,0:T(8,128)(2,1)S(1)} %collective-permute-done.8.refs_7_), channel_id=1, source_target_pairs={{0,1},{1,0},{2,3},{3,2},{4,5},{5,4},{6,7},{7,6},{8,9},{9,8},{10,11... | collective-permute-start | bytes 417800 | tf_op jit(solution)/shard_map/ppermute | solution.py:299
  23.7 1.9 %copy-start.8 = (s32[4,8]{1,0:T(4,128)S(1)}, s32[4,8]{1,0:T(4,128)}, u32[]{:S(2)}) copy-start(s32[4,8]{1,0:T(4,128)} %refs_0_.5) | copy-start | bytes 388
  23.7 17.2 %collective-permute-start = (bf16[256,512]{1,0:T(8,128)(2,1)S(1)}, bf16[256,512]{1,0:T(8,128)(2,1)S(1)}, u32[]{:S(2)}, u32[]{:S(2)}) collective-permute-start(bf16[256,512]{1,0:T(8,128)(2,1)S(1)} %get-tuple-element.19), channel_id=1, source_target_pairs={{0,8},{8,0},{16,24},{24,16},{1,9},{9,1},{17,25},{25,17},{2,10},{10... | collective-permute-start | bytes 786440 | tf_op jit(solution)/shard_map/ppermute | solution.py:299
  23.7 17.2 %collective-permute-start.1 = (bf16[256,512]{1,0:T(8,128)(2,1)S(1)}, bf16[256,512]{1,0:T(8,128)(2,1)S(1)}, u32[]{:S(2)}, u32[]{:S(2)}) collective-permute-start(bf16[256,512]{1,0:T(8,128)(2,1)S(1)} %get-tuple-element.20), channel_id=1, source_target_pairs={{0,16},{8,24},{16,0},{24,8},{1,17},{9,25},{17,1},{25,9},{2,18},{10... | collective-permute-start | bytes 786440 | tf_op jit(solution)/shard_map/ppermute | solution.py:299
  25.2 15.6 %collective-permute-start.2 = (bf16[256,512]{1,0:T(8,128)(2,1)S(1)}, bf16[256,512]{1,0:T(8,128)(2,1)S(1)}, u32[]{:S(2)}, u32[]{:S(2)}) collective-permute-start(bf16[256,512]{1,0:T(8,128)(2,1)S(1)} %get-tuple-element.21), channel_id=1, source_target_pairs={{0,24},{8,16},{16,8},{24,0},{1,25},{9,17},{17,9},{25,1},{2,26},{10... | collective-permute-start | bytes 786440 | tf_op jit(solution)/shard_map/ppermute | solution.py:299
  25.5 0.9 %copy-start.1 = (bf16[272,256]{1,0:T(8,128)(2,1)S(1)}, bf16[272,256]{1,0:T(8,128)(2,1)}, u32[]{:S(2)}) copy-start(bf16[272,256]{1,0:T(8,128)(2,1)} %copy-done) | copy-start | bytes 417796
  26.4 0.9 %copy-start.4 = (bf16[272,256]{1,0:T(8,128)(2,1)S(1)}, bf16[272,256]{1,0:T(8,128)(2,1)}, u32[]{:S(2)}) copy-start(bf16[272,256]{1,0:T(8,128)(2,1)} %copy-done.3) | copy-start | bytes 417796
  27.3 1.4 %copy-start.2 = (bf16[272,256]{1,0:T(8,128)(2,1)S(1)}, bf16[272,256]{1,0:T(8,128)(2,1)}, u32[]{:S(2)}) copy-start(bf16[272,256]{1,0:T(8,128)(2,1)} %copy-done) | copy-start | bytes 417796
  27.3 1.4 %copy-start.7 = (bf16[272,256]{1,0:T(8,128)(2,1)S(1)}, bf16[272,256]{1,0:T(8,128)(2,1)}, u32[]{:S(2)}) copy-start(bf16[272,256]{1,0:T(8,128)(2,1)} %after.1.refs_5_) | copy-start | bytes 417796
  28.8 1.5 %copy-start.5 = (bf16[272,256]{1,0:T(8,128)(2,1)S(1)}, bf16[272,256]{1,0:T(8,128)(2,1)}, u32[]{:S(2)}) copy-start(bf16[272,256]{1,0:T(8,128)(2,1)} %copy-done.3) | copy-start | bytes 417796
  33.0 7.8 %collective-permute-start.11 = (bf16[256,256]{1,0:T(8,128)(2,1)S(1)}, bf16[256,256]{1,0:T(8,128)(2,1)S(1)}, u32[]{:S(2)}, u32[]{:S(2)}) collective-permute-start(bf16[256,256]{1,0:T(8,128)(2,1)S(1)} %group_grad.1.refs_4_), channel_id=1, source_target_pairs={{0,16},{8,24},{16,0},{24,8},{1,17},{9,25},{17,1},{25,9},{2,18},{10... | collective-permute-start | bytes 393224 | tf_op jit(solution)/shard_map/ppermute | solution.py:299
  34.6 6.2 %collective-permute-start.10 = (bf16[256,256]{1,0:T(8,128)(2,1)S(1)}, bf16[256,256]{1,0:T(8,128)(2,1)S(1)}, u32[]{:S(2)}, u32[]{:S(2)}) collective-permute-start(bf16[256,256]{1,0:T(8,128)(2,1)S(1)} %group_grad.1.refs_4_), channel_id=1, source_target_pairs={{0,8},{8,0},{16,24},{24,16},{1,9},{9,1},{17,25},{25,17},{2,10},{10... | collective-permute-start | bytes 393224 | tf_op jit(solution)/shard_map/ppermute | solution.py:299
  40.8 1.3 %collective-permute-start.12 = (bf16[256,256]{1,0:T(8,128)(2,1)S(1)}, bf16[256,256]{1,0:T(8,128)(2,1)S(1)}, u32[]{:S(2)}, u32[]{:S(2)}) collective-permute-start(bf16[256,256]{1,0:T(8,128)(2,1)S(1)} %collective-permute-done.11.refs_6_), channel_id=1, source_target_pairs={{0,8},{8,0},{16,24},{24,16},{1,9},{9,1},{17,25},{25,17},{2,10},{10... | collective-permute-start | bytes 393224 | tf_op jit(solution)/shard_map/ppermute | solution.py:299

commit v5 on v4

--- a/solution.py
+++ b/solution.py
@@ -19,7 +19,6 @@
 
 VMEM = pl.BlockSpec(memory_space=pltpu.VMEM)
 SMEM = pl.BlockSpec(memory_space=pltpu.SMEM)
-ANY = pl.BlockSpec(memory_space=pl.ANY)
 HBM = pl.BlockSpec(memory_space=pltpu.HBM)
 
 
@@ -31,11 +30,11 @@
     return jnp.transpose(jnp.broadcast_to(row, (128, row.shape[1])))
 
 
-def project_kernel(parts, feats_hbm, w_hbm, partners_hbm, buckets_hbm, msg_ref, normed_ref, inv_ref, *rest):
-    cuts = rest[:parts]
-    w_v, partners_ref, buckets_ref, sems, small_sems = rest[parts:]
+def project_kernel(parts, feats_hbm, w_hbm, partners_hbm, buckets_hbm, msg_ref, normed_ref, inv_ref,
+                   near_ref, far_ref, w_v, partners_ref, buckets_ref, sems, small_sems):
+    half, rows, step = near_ref.shape
+    cuts = [near_ref.at[k] for k in range(half)] + [far_ref.at[k] for k in range(half)]
     width = w_v.shape[1]
-    rows, step = cuts[0].shape
     me = lax.axis_index("dp")
     copies = []
     for k in range(parts):
@@ -85,9 +84,9 @@
             jax.ShapeDtypeStruct((rows, width), jnp.float32),
             jax.ShapeDtypeStruct((rows, 128), jnp.float32),
         )
-        + tuple(jax.ShapeDtypeStruct((rows, din // parts), feats.dtype) for _ in range(parts)),
+        + (jax.ShapeDtypeStruct((parts // 2, rows, din // parts), feats.dtype),) * 2,
         in_specs=[HBM, HBM, HBM, HBM],
-        out_specs=(VMEM,) * (3 + parts),
+        out_specs=(VMEM,) * 5,
         scratch_shapes=[
             pltpu.VMEM((din, width), jnp.bfloat16),
             pltpu.VMEM((1, rows), jnp.int32),
@@ -214,7 +213,7 @@
     msgs, refs = dict(zip(known, refs)), refs[len(known):]
     sums_ref, own_ref, refs = refs[0], refs[1], refs[2:]
     stage_refs, refs = refs[:len(stages)], refs[len(stages):]
-    normed_ref, inv_ref, out_ref, kept = refs
+    normed_ref, inv_ref, out_ref, kept = refs[-4:]
     rows, width = normed_ref.shape
     before = {k: sums_ref[at:at + 1, :] for at, k in enumerate(seen)}
     sums, own_sums, weight, own_weight = pair_sums(
@@ -253,45 +252,83 @@
     out_ref[...] = ((grad - normed * inward) * inv_ref[:, 0:1]).astype(jnp.bfloat16)
 
 
-def group_grad(stages, fresh, counts, msgs, state, kept, normed, inv):
+def group_grad(stages, fresh, counts, msgs, state, kept, earlier, normed, inv):
     seen = [k for stage in stages for k in stage]
     known = seen + fresh
     rows, width = normed.shape
     return pl.pallas_call(
         functools.partial(grad_kernel, stages, fresh),
         out_shape=jax.ShapeDtypeStruct((rows, width), jnp.bfloat16),
-        in_specs=[SMEM] + [VMEM] * (len(known) + len(state) + len(kept) + 2),
+        in_specs=[SMEM] + [VMEM] * (len(known) + len(state) + len(kept) + len(earlier) + 2),
         out_specs=VMEM,
         scratch_shapes=[pltpu.VMEM((len(fresh), rows, rows), jnp.float32)],
         compiler_params=pltpu.CompilerParams(vmem_limit_bytes=VMEM_LIMIT),
         cost_estimate=pairs_cost(seen, fresh, rows, width),
         name="group_grad",
-    )(counts, *(msgs[k] for k in known), *state, *kept, normed, inv)
-
-
-def weight_kernel(parts, *refs):
-    feats, grads, out_ref = refs[:parts], refs[parts:2 * parts], refs[2 * parts]
-    result = f32_dot(feats[0][...], grads[0][...], ((0,), (0,)))
-    for k in range(1, parts):
-        result = result + f32_dot(feats[k][...], grads[k][...], ((0,), (0,)))
-    out_ref[...] = result.astype(out_ref.dtype)
-
-
-def weight_grad(feats, grads):
-    parts = len(feats)
-    rows, cols = feats[0].shape
+    )(counts, *(msgs[k] for k in known), *state, *kept, *earlier, normed, inv)
+
+
+def distinct(arrays):
+    found = []
+    for array in arrays:
+        if all(array is not other for other in found):
+            found.append(array)
+    return found, [next(at for at, other in enumerate(found) if array is other) for array in arrays]
+
+
+def pack_kernel(places, *refs):
+    for at, (array, row) in enumerate(places):
+        refs[-1][at] = refs[array][row]
+
+
+def pack(pieces, earlier):
+    arrays, which = distinct([array for array, _ in pieces])
+    shape = (len(pieces),) + arrays[0].shape[1:]
+    return pl.pallas_call(
+        functools.partial(pack_kernel, [(at, piece[1]) for at, piece in zip(which, pieces)]),
+        out_shape=jax.ShapeDtypeStruct(shape, arrays[0].dtype),
+        in_specs=[VMEM] * len(arrays) + [VMEM],
+        out_specs=VMEM,
+        compiler_params=pltpu.CompilerParams(vmem_limit_bytes=VMEM_LIMIT),
+        cost_estimate=pl.CostEstimate(flops=0, bytes_accessed=4 * math.prod(shape), transcendentals=0),
+        name="pack",
+    )(*arrays, earlier)
+
+
+def weight_kernel(places, order, *refs):
+    own_ref, outs, total = refs[-2 - len(order)], refs[-1 - len(order):-1], refs[-1]
+    piece = own_ref.shape[0]
+    me = lax.axis_index("pool")
+    result = None
+    for array, row, grad in places:
+        term = f32_dot(refs[array][row], refs[grad][...], ((0,), (0,)))
+        result = term if result is None else result + term
+    total[...] = result
+    for k, out in zip([0] + order, (own_ref,) + outs):
+        first = pl.multiple_of((me ^ k) * piece, piece)
+        out[...] = total[pl.ds(first, piece), :].astype(out.dtype)
+
+
+def weight_grad(blocks, grads, order):
+    arrays, which = distinct([array for _, array, _ in blocks])
+    places = [(at, row, len(arrays) + source) for at, (source, _, row) in zip(which, blocks)]
+    parts = len(grads)
+    _, rows, cols = arrays[0].shape
     width = grads[0].shape[1]
-    return pl.pallas_call(
-        functools.partial(weight_kernel, parts),
-        out_shape=jax.ShapeDtypeStruct((cols, width), jnp.bfloat16),
-        in_specs=[VMEM] * (2 * parts),
-        out_specs=VMEM,
+    piece = (cols // (1 + len(order)), width)
+    return pl.pallas_call(
+        functools.partial(weight_kernel, places, order),
+        out_shape=(jax.ShapeDtypeStruct(piece, jnp.float32),)
+        + tuple(jax.ShapeDtypeStruct(piece, jnp.bfloat16) for _ in order),
+        in_specs=[VMEM] * (len(arrays) + parts),
+        out_specs=(VMEM,) * (1 + len(order)),
+        scratch_shapes=[pltpu.VMEM((cols, width), jnp.float32)],
         compiler_params=pltpu.CompilerParams(vmem_limit_bytes=VMEM_LIMIT),
         cost_estimate=pl.CostEstimate(
             flops=2 * parts * rows * cols * width, bytes_accessed=2 * parts * rows * cols, transcendentals=0
         ),
         name="weight_grad",
-    )(*feats, *grads)
+    )(*arrays, *grads)
 
 
 def swap(value, axis, flip):
@@ -299,17 +336,16 @@
     return lax.ppermute(value, axis, [(at, at ^ flip) for at in range(size)])
 
 
-def order_kernel(*refs):
-    pass
+def order_kernel(value_ref, *refs):
+    refs[-1][...] = value_ref[...]
 
 
 def after(value, *earlier):
     return pl.pallas_call(
         order_kernel,
         out_shape=jax.ShapeDtypeStruct(value.shape, value.dtype),
-        in_specs=[ANY] * (1 + len(earlier)),
-        out_specs=ANY,
-        input_output_aliases={0: 0},
+        in_specs=[VMEM] * (1 + len(earlier)),
+        out_specs=VMEM,
         name="after",
     )(value, *earlier)
 
@@ -318,7 +354,9 @@
     members = lax.axis_size("pool")
     parts = lax.axis_size("dp")
     minor = 1 << ((members.bit_length() - 1) // 2)
-    msg, normed, inv, *cuts = project(feats, tower_w, partners[None, :], popularity_buckets[None, :], parts)
+    msg, normed, inv, near_cuts, far_cuts = project(feats, tower_w, partners[None, :], popularity_buckets[None, :], parts)
+
+    came = swap(far_cuts, "dp", parts // 2)
 
     msgs = {0: msg}
     for near in range(1, minor):
@@ -332,24 +370,22 @@
     first = bits[0]
     for near in range(1, minor):
         msgs[first + near] = swap(msgs[first], "pool", near)
-    msgs[bits[-1]] = after(msgs[bits[-1]], *(msgs[base + near] for base in (0, first) for near in range(1, minor)))
+    relayed = after(msgs[bits[-1]], *(msgs[base + near] for base in (0, first) for near in range(1, minor)))
     for at, bit in enumerate(bits):
         for k in range(bit + minor, 2 * bit, minor):
-            msgs[k] = swap(msgs[bit], "pool", k ^ bit) if k ^ bit in bits else swap(msgs[k ^ bit], "pool", bit)
+            msgs[k] = swap(relayed if bit == bits[-1] else msgs[bit], "pool", k ^ bit)
     majors = sorted(k for k in msgs if k % minor == 0)
     for far in majors[2:]:
         for near in range(1, minor):
             msgs[far + near] = swap(msgs[far], "pool", near)
-    cuts = [cuts[0]] + [swap(cuts[k], "dp", k) for k in range(1, parts)]
-
     columns = [[far + near for near in range(minor)] for far in majors]
-    stages = [sum(columns[:-2], []), columns[-2]]
+    stages = [sum(columns[:-2], []), majors[-2:], columns[-2][1:]]
     seen, state, kept = [], (), []
     for fresh in stages:
         *state, powers = add_pairs(seen, fresh, row_counts, msgs, state)
         kept.append(powers)
         seen = seen + fresh
-    grad_proj = group_grad(stages, columns[-1], row_counts, msgs, state, kept, normed, inv)
+    grad_proj = group_grad(stages, columns[-1][1:], row_counts, msgs, state, kept, [], normed, inv)
 
     grads = {0: grad_proj}
     bit = parts // 2
@@ -357,10 +393,21 @@
         for k in list(grads):
             grads[k ^ bit] = swap(grads[k], "dp", bit)
         bit //= 2
-    partial = weight_grad(cuts, [grads[k] for k in range(parts)])
-    pieces = partial.reshape(members, partial.shape[0] // members, partial.shape[1])
-    pieces = lax.all_to_all(pieces, "pool", split_axis=0, concat_axis=0)
-    return jnp.sum(pieces.astype(jnp.float32), axis=0)
+    blocks = {k: [(0, near_cuts, k), (parts // 2, came, k)] for k in range(parts // 2)}
+    bit = parts // 4
+    while bit:
+        moving = [(k ^ bit, source ^ bit, array, at) for k in blocks if k & bit for source, array, at in blocks[k]]
+        passed = swap(pack([each[2:] for each in moving], grads[parts // 2]), "dp", bit)
+        blocks = {k: blocks[k] for k in blocks if not k & bit}
+        for at, (k, source, _, _) in enumerate(moving):
+            blocks[k].append((source, passed, at))
+        bit //= 2
+
+    order = sorted(range(1, members), key=lambda k: (k < members // 2, k))
+    total, *pieces = weight_grad(blocks[0], [grads[k] for k in range(parts)], order)
+    for k, piece in zip(order, pieces):
+        total = total + swap(piece, "pool", k).astype(jnp.float32)
+    return total
 
 
 def solution(mesh):

time: 57.1 us -> 56.1 us (0.982)
  blocking collectives: 13.6 us -> 0 us
  starting transfers between devices: 16.5 us -> 27.9 us
  Pallas kernels: 8.53 us -> 11.2 us
  waiting for transfers between devices: 14.4 us -> 12.8 us
    all_to_all x1 -> x0, blocking collectives: 13.6 us -> none  [per_device(): pieces = lax.all_to_all(pieces, 'pool', split_axis=0, concat_axis=0)]
    ppermute x13 -> x19, starting transfers between devices: 16.5 us -> 27.9 us  [swap(): return lax.ppermute(value, axis, [(at, at ^ flip) for at in range(size)])]
    pallas_call x1, Pallas kernels: 0.01 us -> 1.71 us  [after(): pl.pallas_call(order_kernel, out_shape=jax.ShapeDtypeStruct(value.shape,...]
    ppermute x13 -> x19, waiting for transfers between devices: 14.4 us -> 12.8 us  [swap(): return lax.ppermute(value, axis, [(at, at ^ flip) for at in range(size)])]
    pallas_call x2 -> x3, Pallas kernels: 2.83 us -> 4.09 us  [add_pairs(): pl.pallas_call(functools.partial(pairs_kernel, seen, fresh), out_shape=(j...]
    add x0 -> x1, other arithmetic: none -> 0.67 us  [per_device(): total = total + swap(piece, 'pool', k).astype(jnp.float32)]
    reduce_sum x1 -> x0, other arithmetic: 0.67 us -> none  [per_device(): return jnp.sum(pieces.astype(jnp.float32), axis=0)]
  transfers between devices with their start and end apart: 13 -> 19, of which waited for: 4 -> 7; matrix products, arithmetic and copies ran while one was open for 0% -> 0% of each run, Pallas kernels for 10% -> 15%
where the time goes in v5:
time: 56.1 us; the launch traced here: 55.9 us
  starting transfers between devices  27.9 us (50%)
  waiting for transfers between devices  12.8 us (23%)
  Pallas kernels  11.2 us (20%)
  local copies, waits for them, and re-layouts  3.13 us (6%)
  other arithmetic  0.67 us (1%)
    ppermute x19, starting transfers between devices, swap(): return lax.ppermute(value, axis, [(at, at ^ flip) for at in range(size)])  27.9 us
    ppermute x19, waiting for transfers between devices, swap(): return lax.ppermute(value, axis, [(at, at ^ flip) for at in range(size)])  12.8 us
    pallas_call x3, Pallas kernels, add_pairs(): pl.pallas_call(functools.partial(pairs_kernel, seen, fresh), out_shape=(j...  4.09 us
    unnamed x18, local copies, waits for them, and re-layouts  3.13 us
    pallas_call x1, Pallas kernels, group_grad(): pl.pallas_call(functools.partial(grad_kernel, stages, fresh), out_shape=j...  2.47 us
    pallas_call x1, Pallas kernels, project(): pl.pallas_call(functools.partial(project_kernel, parts), out_shape=(jax.S...  2.42 us
    pallas_call x1, Pallas kernels, after(): pl.pallas_call(order_kernel, out_shape=jax.ShapeDtypeStruct(value.shape,...  1.71 us
  transfers between devices with their start and end apart: 19, of which 7 were waited for; matrix products, arithmetic and copies ran while one was open for 0% of the time, Pallas kernels for 15%

profile of v5, /device:TPU:0, one launch (start us, length us, event | category | flops | bytes accessed | tf_op | source)
XLA Modules:
  0.0 55.9 jit_solution(3660316008805124470)
XLA Ops:
  0.0 2.4 %project.1 = (bf16[272,256]{1,0:T(8,128)(2,1)S(1)}, f32[256,256]{1,0:T(8,128)S(1)}, f32[256,128]{1,0:T(8,128)S(1)}, bf16[2,256,512]{2,1,0:T(8,128)(2,1)S(1)}, bf16[2,256,512]{2,1,0:T(8,128)(2,1)S(1)}) custom-call(bf16[256,2048]{1,0:T(8,128)(2,1)} %feats_hbm.1, bf16[2048,256]{1,0:T(8,128)(2,1)} %w_hbm.1, s32[1,256]{1,0:T(1,128)} %bitcast.2, s32[1,256]{1,0:T(1,128)} %bitcast.3), custom_call_target="tpu_custom_call" | custom-call | flops 268435456 | bytes 2097152 | tf_op jit(solution)/shard_map/project/pallas_call | solution.py:80
  2.4 3.1 %collective-permute-start.2 = (bf16[272,256]{1,0:T(8,128)(2,1)S(1)}, bf16[272,256]{1,0:T(8,128)(2,1)S(1)}, u32[]{:S(2)}, u32[]{:S(2)}) collective-permute-start(bf16[272,256]{1,0:T(8,128)(2,1)S(1)} %get-tuple-element.29.refs_1_), channel_id=1, source_target_pairs={{0,2},{1,3},{2,0},{3,1},{4,6},{5,7},{6,4},{7,5},{8,10},{9,11},{10,... | collective-permute-start | bytes 417800 | tf_op jit(solution)/shard_map/ppermute | solution.py:336
  5.5 1.5 %collective-permute-start.1 = (bf16[272,256]{1,0:T(8,128)(2,1)S(1)}, bf16[272,256]{1,0:T(8,128)(2,1)S(1)}, u32[]{:S(2)}, u32[]{:S(2)}) collective-permute-start(bf16[272,256]{1,0:T(8,128)(2,1)S(1)} %get-tuple-element.29.refs_1_), channel_id=1, source_target_pairs={{0,1},{1,0},{2,3},{3,2},{4,5},{5,4},{6,7},{7,6},{8,9},{9,8},{10,11... | collective-permute-start | bytes 417800 | tf_op jit(solution)/shard_map/ppermute | solution.py:336
  7.0 2.6 %collective-permute-start.4 = (bf16[272,256]{1,0:T(8,128)(2,1)S(1)}, bf16[272,256]{1,0:T(8,128)(2,1)S(1)}, u32[]{:S(2)}, u32[]{:S(2)}) collective-permute-start(bf16[272,256]{1,0:T(8,128)(2,1)S(1)} %get-tuple-element.29.refs_1_), channel_id=1, source_target_pairs={{0,4},{1,5},{2,6},{3,7},{4,0},{5,1},{6,2},{7,3},{8,12},{9,13},{10,... | collective-permute-start | bytes 417800 | tf_op jit(solution)/shard_map/ppermute | solution.py:336
  9.6 3.1 %collective-permute-start.3 = (bf16[272,256]{1,0:T(8,128)(2,1)S(1)}, bf16[272,256]{1,0:T(8,128)(2,1)S(1)}, u32[]{:S(2)}, u32[]{:S(2)}) collective-permute-start(bf16[272,256]{1,0:T(8,128)(2,1)S(1)} %collective-permute-done.2.refs_3_), channel_id=1, source_target_pairs={{0,1},{1,0},{2,3},{3,2},{4,5},{5,4},{6,7},{7,6},{8,9},{9,8},{10,11... | collective-permute-start | bytes 417800 | tf_op jit(solution)/shard_map/ppermute | solution.py:336
  12.7 1.5 %collective-permute-start = (bf16[2,256,512]{2,1,0:T(8,128)(2,1)S(1)}, bf16[2,256,512]{2,1,0:T(8,128)(2,1)S(1)}, u32[]{:S(2)}, u32[]{:S(2)}) collective-permute-start(bf16[2,256,512]{2,1,0:T(8,128)(2,1)S(1)} %get-tuple-element.28), channel_id=1, source_target_pairs={{0,16},{8,24},{16,0},{24,8},{1,17},{9,25},{17,1},{25,9},{2,18},{10... | collective-permute-start | bytes 1572872 | tf_op jit(solution)/shard_map/ppermute | solution.py:336
  14.2 1.6 %collective-permute-done.4.value_ref.refs_5_ = bf16[272,256]{1,0:T(8,128)(2,1)S(1)} collective-permute-done((bf16[272,256]{1,0:T(8,128)(2,1)S(1)}, bf16[272,256]{1,0:T(8,128)(2,1)S(1)}, u32[]{:S(2)}, u32[]{:S(2)}) %collective-permute-start.4) | collective-permute-done | bytes 139296 | tf_op jit(solution)/shard_map/ppermute | solution.py:336
  15.8 0.7 %copy-done.3 = bf16[272,256]{1,0:T(8,128)(2,1)} copy-done((bf16[272,256]{1,0:T(8,128)(2,1)}, bf16[272,256]{1,0:T(8,128)(2,1)S(1)}, u32[]{:S(2)}) %copy-start.3) | copy-done | bytes 139288
  16.4 0.6 %copy-done.5 = bf16[272,256]{1,0:T(8,128)(2,1)} copy-done((bf16[272,256]{1,0:T(8,128)(2,1)}, bf16[272,256]{1,0:T(8,128)(2,1)S(1)}, u32[]{:S(2)}) %copy-start.5) | copy-done | bytes 139288
  17.1 1.7 %after.1 = bf16[272,256]{1,0:T(8,128)(2,1)} custom-call(bf16[272,256]{1,0:T(8,128)(2,1)} %copy-done.3, bf16[272,256]{1,0:T(8,128)(2,1)} %copy-done, bf16[272,256]{1,0:T(8,128)(2,1)} %copy-done.5), custom_call_target="tpu_custom_call" | custom-call | tf_op jit(solution)/shard_map/after/pallas_call | solution.py:344
  18.8 1.4 %collective-permute-start.6 = (bf16[272,256]{1,0:T(8,128)(2,1)}, bf16[272,256]{1,0:T(8,128)(2,1)S(1)}, u32[]{:S(2)}, u32[]{:S(2)}) collective-permute-start(bf16[272,256]{1,0:T(8,128)(2,1)} %copy-done.3), channel_id=1, source_target_pairs={{0,1},{1,0},{2,3},{3,2},{4,5},{5,4},{6,7},{7,6},{8,9},{9,8},{10,11... | collective-permute-start | bytes 417800 | tf_op jit(solution)/shard_map/ppermute | solution.py:336
  20.2 3.8 %collective-permute-done.5.refs_6_ = bf16[272,256]{1,0:T(8,128)(2,1)S(1)} collective-permute-done((bf16[272,256]{1,0:T(8,128)(2,1)}, bf16[272,256]{1,0:T(8,128)(2,1)S(1)}, u32[]{:S(2)}, u32[]{:S(2)}) %collective-permute-start.5) | collective-permute-done | bytes 139296 | tf_op jit(solution)/shard_map/ppermute | solution.py:336
  24.0 1.3 %collective-permute-start.7 = (bf16[272,256]{1,0:T(8,128)(2,1)S(1)}, bf16[272,256]{1,0:T(8,128)(2,1)S(1)}, u32[]{:S(2)}, u32[]{:S(2)}) collective-permute-start(bf16[272,256]{1,0:T(8,128)(2,1)S(1)} %collective-permute-done.5.refs_6_), channel_id=1, source_target_pairs={{0,1},{1,0},{2,3},{3,2},{4,5},{5,4},{6,7},{7,6},{8,9},{9,8},{10,11... | collective-permute-start | bytes 417800 | tf_op jit(solution)/shard_map/ppermute | solution.py:336
  25.4 0.9 %copy-done.1 = bf16[272,256]{1,0:T(8,128)(2,1)S(1)} copy-done((bf16[272,256]{1,0:T(8,128)(2,1)S(1)}, bf16[272,256]{1,0:T(8,128)(2,1)}, u32[]{:S(2)}) %copy-start.1) | copy-done | bytes 139288
  26.3 0.9 %copy-done.6 = bf16[272,256]{1,0:T(8,128)(2,1)S(1)} copy-done((bf16[272,256]{1,0:T(8,128)(2,1)S(1)}, bf16[272,256]{1,0:T(8,128)(2,1)}, u32[]{:S(2)}) %copy-start.6) | copy-done | bytes 139288
  27.2 1.4 %add_pairs.3 = (f32[4,256]{1,0:T(4,128)S(1)}, f32[256,128]{1,0:T(8,128)S(1)}, f32[4,256,256]{2,1,0:T(8,128)S(1)}) custom-call(s32[4,8]{1,0:T(4,128)S(1)} %copy-done.8, bf16[272,256]{1,0:T(8,128)(2,1)S(1)} %get-tuple-element.29.refs_1_, bf16[272,256]{1,0:T(8,128)(2,1)S(1)} %copy-done.1, bf16[272,256]{1,0:T(8,128)(2,1)S(1)} %collective-permute-done.2.refs_3_, ...), custom_call_target="tpu_custom_call" | custom-call | flops 335544320 | bytes 1572864 | tf_op jit(solution)/shard_map/add_pairs/pallas_call | solution.py:194
  28.6 1.5 %add_pairs.4 = (f32[6,256]{1,0:T(8,128)S(1)}, f32[256,128]{1,0:T(8,128)S(1)}, f32[2,256,256]{2,1,0:T(8,128)S(1)}) custom-call(s32[4,8]{1,0:T(4,128)S(1)} %copy-done.8, bf16[272,256]{1,0:T(8,128)(2,1)S(1)} %get-tuple-element.29.refs_1_, bf16[272,256]{1,0:T(8,128)(2,1)S(1)} %copy-done.2, bf16[272,256]{1,0:T(8,128)(2,1)S(1)} %collective-permute-done.2.refs_3_, ...), custom_call_target="tpu_custom_call" | custom-call | flops 369098752 | bytes 1310720 | tf_op jit(solution)/shard_map/add_pairs/pallas_call | solution.py:194
  30.1 1.2 %add_pairs.5 = (f32[7,256]{1,0:T(8,128)S(1)}, f32[256,128]{1,0:T(8,128)S(1)}, f32[1,256,256]{2,1,0:T(8,128)S(1)}) custom-call(s32[4,8]{1,0:T(4,128)S(1)} %copy-done.8, bf16[272,256]{1,0:T(8,128)(2,1)S(1)} %get-tuple-element.29.refs_1_, bf16[272,256]{1,0:T(8,128)(2,1)S(1)} %copy-done.2, bf16[272,256]{1,0:T(8,128)(2,1)S(1)} %collective-permute-done.2.refs_3_, ...), custom_call_target="tpu_custom_call" | custom-call | flops 234881024 | bytes 1179648 | tf_op jit(solution)/shard_map/add_pairs/pallas_call | solution.py:194
  31.3 2.5 %group_grad.1.refs_3_ = bf16[256,256]{1,0:T(8,128)(2,1)S(1)} custom-call(s32[4,8]{1,0:T(4,128)S(1)} %copy-done.8, bf16[272,256]{1,0:T(8,128)(2,1)S(1)} %get-tuple-element.29.refs_1_, bf16[272,256]{1,0:T(8,128)(2,1)S(1)} %copy-done.2, bf16[272,256]{1,0:T(8,128)(2,1)S(1)} %collective-permute-done.2.refs_3_, bf16[272,256]{1,0:T(8,128)(2,1)S(1)} %copy-done.7, ...), custom_call_target="tpu_custom_call" | custom-call | flops 268435456 | bytes 1310720 | tf_op jit(solution)/shard_map/group_grad/pallas_call | solution.py:259
  33.8 1.6 %collective-permute-start.8 = (bf16[256,256]{1,0:T(8,128)(2,1)S(1)}, bf16[256,256]{1,0:T(8,128)(2,1)S(1)}, u32[]{:S(2)}, u32[]{:S(2)}) collective-permute-start(bf16[256,256]{1,0:T(8,128)(2,1)S(1)} %group_grad.1.refs_3_), channel_id=1, source_target_pairs={{0,16},{8,24},{16,0},{24,8},{1,17},{9,25},{17,1},{25,9},{2,18},{10... | collective-permute-start | bytes 393224 | tf_op jit(solution)/shard_map/ppermute | solution.py:336
  35.4 3.4 %collective-permute-done.8.refs_2_.refs_5_ = bf16[256,256]{1,0:T(8,128)(2,1)S(1)} collective-permute-done((bf16[256,256]{1,0:T(8,128)(2,1)S(1)}, bf16[256,256]{1,0:T(8,128)(2,1)S(1)}, u32[]{:S(2)}, u32[]{:S(2)}) %collective-permute-start.8) | collective-permute-done | bytes 131104 | tf_op jit(solution)/shard_map/ppermute | solution.py:336
  39.5 1.5 %collective-permute-done.10.refs_4_ = bf16[256,256]{1,0:T(8,128)(2,1)S(1)} collective-permute-done((bf16[256,256]{1,0:T(8,128)(2,1)S(1)}, bf16[256,256]{1,0:T(8,128)(2,1)S(1)}, u32[]{:S(2)}, u32[]{:S(2)}) %collective-permute-start.10) | collective-permute-done | bytes 131104 | tf_op jit(solution)/shard_map/ppermute | solution.py:336
  41.2 0.5 weight_grad.1
  41.8 2.0 %collective-permute-start.12 = (bf16[64,256]{1,0:T(8,128)(2,1)S(1)}, bf16[64,256]{1,0:T(8,128)(2,1)S(1)}, u32[]{:S(2)}, u32[]{:S(2)}) collective-permute-start(bf16[64,256]{1,0:T(8,128)(2,1)S(1)} %get-tuple-element.42), channel_id=1, source_target_pairs={{0,4},{1,5},{2,6},{3,7},{4,0},{5,1},{6,2},{7,3},{8,12},{9,13},{10,... | collective-permute-start | bytes 98312 | tf_op jit(solution)/shard_map/ppermute | solution.py:336
  43.7 1.1 %collective-permute-start.13 = (bf16[64,256]{1,0:T(8,128)(2,1)S(1)}, bf16[64,256]{1,0:T(8,128)(2,1)S(1)}, u32[]{:S(2)}, u32[]{:S(2)}) collective-permute-start(bf16[64,256]{1,0:T(8,128)(2,1)S(1)} %get-tuple-element.43), channel_id=1, source_target_pairs={{0,5},{1,4},{2,7},{3,6},{4,1},{5,0},{6,3},{7,2},{8,13},{9,12},{10,... | collective-permute-start | bytes 98312 | tf_op jit(solution)/shard_map/ppermute | solution.py:336
  44.9 2.7 %collective-permute-start.14 = (bf16[64,256]{1,0:T(8,128)(2,1)S(1)}, bf16[64,256]{1,0:T(8,128)(2,1)S(1)}, u32[]{:S(2)}, u32[]{:S(2)}) collective-permute-start(bf16[64,256]{1,0:T(8,128)(2,1)S(1)} %get-tuple-element.44), channel_id=1, source_target_pairs={{0,6},{1,7},{2,4},{3,5},{4,2},{5,3},{6,0},{7,1},{8,14},{9,15},{10,... | collective-permute-start | bytes 98312 | tf_op jit(solution)/shard_map/ppermute | solution.py:336
  47.6 1.9 %collective-permute-start.15 = (bf16[64,256]{1,0:T(8,128)(2,1)S(1)}, bf16[64,256]{1,0:T(8,128)(2,1)S(1)}, u32[]{:S(2)}, u32[]{:S(2)}) collective-permute-start(bf16[64,256]{1,0:T(8,128)(2,1)S(1)} %get-tuple-element.45), channel_id=1, source_target_pairs={{0,7},{1,6},{2,5},{3,4},{4,3},{5,2},{6,1},{7,0},{8,15},{9,14},{10,... | collective-permute-start | bytes 98312 | tf_op jit(solution)/shard_map/ppermute | solution.py:336
  49.5 0.7 %collective-permute-start.16 = (bf16[64,256]{1,0:T(8,128)(2,1)S(1)}, bf16[64,256]{1,0:T(8,128)(2,1)S(1)}, u32[]{:S(2)}, u32[]{:S(2)}) collective-permute-start(bf16[64,256]{1,0:T(8,128)(2,1)S(1)} %get-tuple-element.46), channel_id=1, source_target_pairs={{0,1},{1,0},{2,3},{3,2},{4,5},{5,4},{6,7},{7,6},{8,9},{9,8},{10,11... | collective-permute-start | bytes 98312 | tf_op jit(solution)/shard_map/ppermute | solution.py:336
  50.2 2.8 %collective-permute-start.18 = (bf16[64,256]{1,0:T(8,128)(2,1)S(1)}, bf16[64,256]{1,0:T(8,128)(2,1)S(1)}, u32[]{:S(2)}, u32[]{:S(2)}) collective-permute-start(bf16[64,256]{1,0:T(8,128)(2,1)S(1)} %get-tuple-element.48), channel_id=1, source_target_pairs={{0,3},{1,2},{2,1},{3,0},{4,7},{5,6},{6,5},{7,4},{8,11},{9,10},{10,... | collective-permute-start | bytes 98312 | tf_op jit(solution)/shard_map/ppermute | solution.py:336
  53.0 1.5 %collective-permute-done.15 = bf16[64,256]{1,0:T(8,128)(2,1)S(1)} collective-permute-done((bf16[64,256]{1,0:T(8,128)(2,1)S(1)}, bf16[64,256]{1,0:T(8,128)(2,1)S(1)}, u32[]{:S(2)}, u32[]{:S(2)}) %collective-permute-start.15) | collective-permute-done | bytes 32800 | tf_op jit(solution)/shard_map/ppermute | solution.py:336
  54.5 0.7 %collective-permute-done.18 = bf16[64,256]{1,0:T(8,128)(2,1)S(1)} collective-permute-done((bf16[64,256]{1,0:T(8,128)(2,1)S(1)}, bf16[64,256]{1,0:T(8,128)(2,1)S(1)}, u32[]{:S(2)}, u32[]{:S(2)}) %collective-permute-start.18) | collective-permute-done | bytes 32800 | tf_op jit(solution)/shard_map/ppermute | solution.py:336
  55.2 0.7 %convert_add_fusion = f32[64,256]{1,0:T(8,128)} fusion(bf16[64,256]{1,0:T(8,128)(2,1)S(1)} %collective-permute-done.18, bf16[64,256]{1,0:T(8,128)(2,1)S(1)} %collective-permute-done.17, bf16[64,256]{1,0:T(8,128)(2,1)S(1)} %collective-permute-done.16, bf16[64,256]{1,0:T(8,128)(2,1)S(1)} %collective-permute-done.15, ...), kind=kLoop, calls=%fused_computation | loop fusion | flops 229376 | bytes 360448 | tf_op jit(solution)/shard_map/add | solution.py:409
  (33 shorter events, 0.9 us)
Async XLA Ops:
  2.4 7.2 %collective-permute-start.2 = (bf16[272,256]{1,0:T(8,128)(2,1)S(1)}, bf16[272,256]{1,0:T(8,128)(2,1)S(1)}, u32[]{:S(2)}, u32[]{:S(2)}) collective-permute-start(bf16[272,256]{1,0:T(8,128)(2,1)S(1)} %get-tuple-element.29.refs_1_), channel_id=1, source_target_pairs={{0,2},{1,3},{2,0},{3,1},{4,6},{5,7},{6,4},{7,5},{8,10},{9,11},{10,... | collective-permute-start | bytes 417800 | tf_op jit(solution)/shard_map/ppermute | solution.py:336
  5.5 8.7 %collective-permute-start.1 = (bf16[272,256]{1,0:T(8,128)(2,1)S(1)}, bf16[272,256]{1,0:T(8,128)(2,1)S(1)}, u32[]{:S(2)}, u32[]{:S(2)}) collective-permute-start(bf16[272,256]{1,0:T(8,128)(2,1)S(1)} %get-tuple-element.29.refs_1_), channel_id=1, source_target_pairs={{0,1},{1,0},{2,3},{3,2},{4,5},{5,4},{6,7},{7,6},{8,9},{9,8},{10,11... | collective-permute-start | bytes 417800 | tf_op jit(solution)/shard_map/ppermute | solution.py:336
  7.0 8.7 %collective-permute-start.4 = (bf16[272,256]{1,0:T(8,128)(2,1)S(1)}, bf16[272,256]{1,0:T(8,128)(2,1)S(1)}, u32[]{:S(2)}, u32[]{:S(2)}) collective-permute-start(bf16[272,256]{1,0:T(8,128)(2,1)S(1)} %get-tuple-element.29.refs_1_), channel_id=1, source_target_pairs={{0,4},{1,5},{2,6},{3,7},{4,0},{5,1},{6,2},{7,3},{8,12},{9,13},{10,... | collective-permute-start | bytes 417800 | tf_op jit(solution)/shard_map/ppermute | solution.py:336
  9.6 6.1 %collective-permute-start.3 = (bf16[272,256]{1,0:T(8,128)(2,1)S(1)}, bf16[272,256]{1,0:T(8,128)(2,1)S(1)}, u32[]{:S(2)}, u32[]{:S(2)}) collective-permute-start(bf16[272,256]{1,0:T(8,128)(2,1)S(1)} %collective-permute-done.2.refs_3_), channel_id=1, source_target_pairs={{0,1},{1,0},{2,3},{3,2},{4,5},{5,4},{6,7},{7,6},{8,9},{9,8},{10,11... | collective-permute-start | bytes 417800 | tf_op jit(solution)/shard_map/ppermute | solution.py:336
  12.7 12.7 %copy-start.8 = (s32[4,8]{1,0:T(4,128)S(1)}, s32[4,8]{1,0:T(4,128)}, u32[]{:S(2)}) copy-start(s32[4,8]{1,0:T(4,128)} %refs_0_.7) | copy-start | bytes 388
  12.7 22.7 %collective-permute-start = (bf16[2,256,512]{2,1,0:T(8,128)(2,1)S(1)}, bf16[2,256,512]{2,1,0:T(8,128)(2,1)S(1)}, u32[]{:S(2)}, u32[]{:S(2)}) collective-permute-start(bf16[2,256,512]{2,1,0:T(8,128)(2,1)S(1)} %get-tuple-element.28), channel_id=1, source_target_pairs={{0,16},{8,24},{16,0},{24,8},{1,17},{9,25},{17,1},{25,9},{2,18},{10... | collective-permute-start | bytes 1572872 | tf_op jit(solution)/shard_map/ppermute | solution.py:336
  14.2 1.6 %copy-start = (bf16[272,256]{1,0:T(8,128)(2,1)}, bf16[272,256]{1,0:T(8,128)(2,1)S(1)}, u32[]{:S(2)}) copy-start(bf16[272,256]{1,0:T(8,128)(2,1)S(1)} %collective-permute-done.1.refs_0_.refs_2_) | copy-start | bytes 417796
  15.7 0.7 %copy-start.3 = (bf16[272,256]{1,0:T(8,128)(2,1)}, bf16[272,256]{1,0:T(8,128)(2,1)S(1)}, u32[]{:S(2)}) copy-start(bf16[272,256]{1,0:T(8,128)(2,1)S(1)} %collective-permute-done.4.value_ref.refs_5_) | copy-start | bytes 417796
  16.4 0.6 %copy-start.5 = (bf16[272,256]{1,0:T(8,128)(2,1)}, bf16[272,256]{1,0:T(8,128)(2,1)S(1)}, u32[]{:S(2)}) copy-start(bf16[272,256]{1,0:T(8,128)(2,1)S(1)} %collective-permute-done.3.refs_1_.refs_4_) | copy-start | bytes 417796
  18.8 5.3 %collective-permute-start.5 = (bf16[272,256]{1,0:T(8,128)(2,1)}, bf16[272,256]{1,0:T(8,128)(2,1)S(1)}, u32[]{:S(2)}, u32[]{:S(2)}) collective-permute-start(bf16[272,256]{1,0:T(8,128)(2,1)} %after.1), channel_id=1, source_target_pairs={{0,2},{1,3},{2,0},{3,1},{4,6},{5,7},{6,4},{7,5},{8,10},{9,11},{10,... | collective-permute-start | bytes 417800 | tf_op jit(solution)/shard_map/ppermute | solution.py:336
  18.8 11.3 %collective-permute-start.6 = (bf16[272,256]{1,0:T(8,128)(2,1)}, bf16[272,256]{1,0:T(8,128)(2,1)S(1)}, u32[]{:S(2)}, u32[]{:S(2)}) collective-permute-start(bf16[272,256]{1,0:T(8,128)(2,1)} %copy-done.3), channel_id=1, source_target_pairs={{0,1},{1,0},{2,3},{3,2},{4,5},{5,4},{6,7},{7,6},{8,9},{9,8},{10,11... | collective-permute-start | bytes 417800 | tf_op jit(solution)/shard_map/ppermute | solution.py:336
  24.0 7.3 %collective-permute-start.7 = (bf16[272,256]{1,0:T(8,128)(2,1)S(1)}, bf16[272,256]{1,0:T(8,128)(2,1)S(1)}, u32[]{:S(2)}, u32[]{:S(2)}) collective-permute-start(bf16[272,256]{1,0:T(8,128)(2,1)S(1)} %collective-permute-done.5.refs_6_), channel_id=1, source_target_pairs={{0,1},{1,0},{2,3},{3,2},{4,5},{5,4},{6,7},{7,6},{8,9},{9,8},{10,11... | collective-permute-start | bytes 417800 | tf_op jit(solution)/shard_map/ppermute | solution.py:336
  25.4 0.9 %copy-start.1 = (bf16[272,256]{1,0:T(8,128)(2,1)S(1)}, bf16[272,256]{1,0:T(8,128)(2,1)}, u32[]{:S(2)}) copy-start(bf16[272,256]{1,0:T(8,128)(2,1)} %copy-done) | copy-start | bytes 417796
  26.3 0.9 %copy-start.6 = (bf16[272,256]{1,0:T(8,128)(2,1)S(1)}, bf16[272,256]{1,0:T(8,128)(2,1)}, u32[]{:S(2)}) copy-start(bf16[272,256]{1,0:T(8,128)(2,1)} %copy-done.5) | copy-start | bytes 417796
  27.2 1.4 %copy-start.2 = (bf16[272,256]{1,0:T(8,128)(2,1)S(1)}, bf16[272,256]{1,0:T(8,128)(2,1)}, u32[]{:S(2)}) copy-start(bf16[272,256]{1,0:T(8,128)(2,1)} %copy-done) | copy-start | bytes 417796
  27.2 1.4 %copy-start.4 = (bf16[272,256]{1,0:T(8,128)(2,1)S(1)}, bf16[272,256]{1,0:T(8,128)(2,1)}, u32[]{:S(2)}) copy-start(bf16[272,256]{1,0:T(8,128)(2,1)} %copy-done.3) | copy-start | bytes 417796
  30.1 1.3 %copy-start.7 = (bf16[272,256]{1,0:T(8,128)(2,1)S(1)}, bf16[272,256]{1,0:T(8,128)(2,1)}, u32[]{:S(2)}) copy-start(bf16[272,256]{1,0:T(8,128)(2,1)} %copy-done.5) | copy-start | bytes 417796
  33.8 5.0 %collective-permute-start.8 = (bf16[256,256]{1,0:T(8,128)(2,1)S(1)}, bf16[256,256]{1,0:T(8,128)(2,1)S(1)}, u32[]{:S(2)}, u32[]{:S(2)}) collective-permute-start(bf16[256,256]{1,0:T(8,128)(2,1)S(1)} %group_grad.1.refs_3_), channel_id=1, source_target_pairs={{0,16},{8,24},{16,0},{24,8},{1,17},{9,25},{17,1},{25,9},{2,18},{10... | collective-permute-start | bytes 393224 | tf_op jit(solution)/shard_map/ppermute | solution.py:336
  38.9 2.4 %collective-permute-start.9 = (bf16[2,256,512]{2,1,0:T(8,128)(2,1)S(1)}, bf16[2,256,512]{2,1,0:T(8,128)(2,1)S(1)}, u32[]{:S(2)}, u32[]{:S(2)}) collective-permute-start(bf16[2,256,512]{2,1,0:T(8,128)(2,1)S(1)} %pack.1), channel_id=1, source_target_pairs={{0,8},{8,0},{16,24},{24,16},{1,9},{9,1},{17,25},{25,17},{2,10},{10... | collective-permute-start | bytes 1572872 | tf_op jit(solution)/shard_map/ppermute | solution.py:336
  39.0 2.1 %collective-permute-start.10 = (bf16[256,256]{1,0:T(8,128)(2,1)S(1)}, bf16[256,256]{1,0:T(8,128)(2,1)S(1)}, u32[]{:S(2)}, u32[]{:S(2)}) collective-permute-start(bf16[256,256]{1,0:T(8,128)(2,1)S(1)} %group_grad.1.refs_3_), channel_id=1, source_target_pairs={{0,8},{8,0},{16,24},{24,16},{1,9},{9,1},{17,25},{25,17},{2,10},{10... | collective-permute-start | bytes 393224 | tf_op jit(solution)/shard_map/ppermute | solution.py:336
  39.5 1.8 %collective-permute-start.11 = (bf16[256,256]{1,0:T(8,128)(2,1)S(1)}, bf16[256,256]{1,0:T(8,128)(2,1)S(1)}, u32[]{:S(2)}, u32[]{:S(2)}) collective-permute-start(bf16[256,256]{1,0:T(8,128)(2,1)S(1)} %collective-permute-done.8.refs_2_.refs_5_), channel_id=1, source_target_pairs={{0,8},{8,0},{16,24},{24,16},{1,9},{9,1},{17,25},{25,17},{2,10},{10... | collective-permute-start | bytes 393224 | tf_op jit(solution)/shard_map/ppermute | solution.py:336
  41.8 8.4 %collective-permute-start.12 = (bf16[64,256]{1,0:T(8,128)(2,1)S(1)}, bf16[64,256]{1,0:T(8,128)(2,1)S(1)}, u32[]{:S(2)}, u32[]{:S(2)}) collective-permute-start(bf16[64,256]{1,0:T(8,128)(2,1)S(1)} %get-tuple-element.42), channel_id=1, source_target_pairs={{0,4},{1,5},{2,6},{3,7},{4,0},{5,1},{6,2},{7,3},{8,12},{9,13},{10,... | collective-permute-start | bytes 98312 | tf_op jit(solution)/shard_map/ppermute | solution.py:336
  43.7 6.5 %collective-permute-start.13 = (bf16[64,256]{1,0:T(8,128)(2,1)S(1)}, bf16[64,256]{1,0:T(8,128)(2,1)S(1)}, u32[]{:S(2)}, u32[]{:S(2)}) collective-permute-start(bf16[64,256]{1,0:T(8,128)(2,1)S(1)} %get-tuple-element.43), channel_id=1, source_target_pairs={{0,5},{1,4},{2,7},{3,6},{4,1},{5,0},{6,3},{7,2},{8,13},{9,12},{10,... | collective-permute-start | bytes 98312 | tf_op jit(solution)/shard_map/ppermute | solution.py:336
  44.9 8.1 %collective-permute-start.14 = (bf16[64,256]{1,0:T(8,128)(2,1)S(1)}, bf16[64,256]{1,0:T(8,128)(2,1)S(1)}, u32[]{:S(2)}, u32[]{:S(2)}) collective-permute-start(bf16[64,256]{1,0:T(8,128)(2,1)S(1)} %get-tuple-element.44), channel_id=1, source_target_pairs={{0,6},{1,7},{2,4},{3,5},{4,2},{5,3},{6,0},{7,1},{8,14},{9,15},{10,... | collective-permute-start | bytes 98312 | tf_op jit(solution)/shard_map/ppermute | solution.py:336
  47.6 6.9 %collective-permute-start.15 = (bf16[64,256]{1,0:T(8,128)(2,1)S(1)}, bf16[64,256]{1,0:T(8,128)(2,1)S(1)}, u32[]{:S(2)}, u32[]{:S(2)}) collective-permute-start(bf16[64,256]{1,0:T(8,128)(2,1)S(1)} %get-tuple-element.45), channel_id=1, source_target_pairs={{0,7},{1,6},{2,5},{3,4},{4,3},{5,2},{6,1},{7,0},{8,15},{9,14},{10,... | collective-permute-start | bytes 98312 | tf_op jit(solution)/shard_map/ppermute | solution.py:336
  49.5 5.0 %collective-permute-start.16 = (bf16[64,256]{1,0:T(8,128)(2,1)S(1)}, bf16[64,256]{1,0:T(8,128)(2,1)S(1)}, u32[]{:S(2)}, u32[]{:S(2)}) collective-permute-start(bf16[64,256]{1,0:T(8,128)(2,1)S(1)} %get-tuple-element.46), channel_id=1, source_target_pairs={{0,1},{1,0},{2,3},{3,2},{4,5},{5,4},{6,7},{7,6},{8,9},{9,8},{10,11... | collective-permute-start | bytes 98312 | tf_op jit(solution)/shard_map/ppermute | solution.py:336
  50.2 4.3 %collective-permute-start.17 = (bf16[64,256]{1,0:T(8,128)(2,1)S(1)}, bf16[64,256]{1,0:T(8,128)(2,1)S(1)}, u32[]{:S(2)}, u32[]{:S(2)}) collective-permute-start(bf16[64,256]{1,0:T(8,128)(2,1)S(1)} %get-tuple-element.47), channel_id=1, source_target_pairs={{0,2},{1,3},{2,0},{3,1},{4,6},{5,7},{6,4},{7,5},{8,10},{9,11},{10,... | collective-permute-start | bytes 98312 | tf_op jit(solution)/shard_map/ppermute | solution.py:336
  50.2 5.0 %collective-permute-start.18 = (bf16[64,256]{1,0:T(8,128)(2,1)S(1)}, bf16[64,256]{1,0:T(8,128)(2,1)S(1)}, u32[]{:S(2)}, u32[]{:S(2)}) collective-permute-start(bf16[64,256]{1,0:T(8,128)(2,1)S(1)} %get-tuple-element.48), channel_id=1, source_target_pairs={{0,3},{1,2},{2,1},{3,0},{4,7},{5,6},{6,5},{7,4},{8,11},{9,10},{10,... | collective-permute-start | bytes 98312 | tf_op jit(solution)/shard_map/ppermute | solution.py:336

commit v6 on v5

--- a/solution.py
+++ b/solution.py
@@ -15,7 +15,8 @@
 DIGIT = 1 << DIGIT_BITS
 EXP2_SCALE = math.log2(math.e) / sharpness_scaler
 LOG2E = math.log2(math.e)
-VMEM_LIMIT = 48 * 1024 * 1024
+VMEM_LIMIT = 40 * 1024 * 1024
+SMALL_VMEM_LIMIT = 8 * 1024 * 1024
 
 VMEM = pl.BlockSpec(memory_space=pltpu.VMEM)
 SMEM = pl.BlockSpec(memory_space=pltpu.SMEM)
@@ -249,7 +250,7 @@
     grad = both[:rows] + both[rows:]
     normed = normed_ref[...]
     inward = jnp.sum(normed * grad, axis=1, keepdims=True)
-    out_ref[...] = ((grad - normed * inward) * inv_ref[:, 0:1]).astype(jnp.bfloat16)
+    out_ref[0] = ((grad - normed * inward) * inv_ref[:, 0:1]).astype(jnp.bfloat16)
 
 
 def group_grad(stages, fresh, counts, msgs, state, kept, earlier, normed, inv):
@@ -258,7 +259,7 @@
     rows, width = normed.shape
     return pl.pallas_call(
         functools.partial(grad_kernel, stages, fresh),
-        out_shape=jax.ShapeDtypeStruct((rows, width), jnp.bfloat16),
+        out_shape=jax.ShapeDtypeStruct((1, rows, width), jnp.bfloat16),
         in_specs=[SMEM] + [VMEM] * (len(known) + len(state) + len(kept) + len(earlier) + 2),
         out_specs=VMEM,
         scratch_shapes=[pltpu.VMEM((len(fresh), rows, rows), jnp.float32)],
@@ -281,54 +282,48 @@
         refs[-1][at] = refs[array][row]
 
 
-def pack(pieces, earlier):
+def pack(pieces, earlier=()):
     arrays, which = distinct([array for array, _ in pieces])
     shape = (len(pieces),) + arrays[0].shape[1:]
     return pl.pallas_call(
         functools.partial(pack_kernel, [(at, piece[1]) for at, piece in zip(which, pieces)]),
         out_shape=jax.ShapeDtypeStruct(shape, arrays[0].dtype),
-        in_specs=[VMEM] * len(arrays) + [VMEM],
+        in_specs=[VMEM] * (len(arrays) + len(earlier)),
         out_specs=VMEM,
         compiler_params=pltpu.CompilerParams(vmem_limit_bytes=VMEM_LIMIT),
         cost_estimate=pl.CostEstimate(flops=0, bytes_accessed=4 * math.prod(shape), transcendentals=0),
         name="pack",
-    )(*arrays, earlier)
-
-
-def weight_kernel(places, order, *refs):
-    own_ref, outs, total = refs[-2 - len(order)], refs[-1 - len(order):-1], refs[-1]
-    piece = own_ref.shape[0]
-    me = lax.axis_index("pool")
+    )(*arrays, *earlier)
+
+
+def weight_kernel(places, *refs):
     result = None
-    for array, row, grad in places:
-        term = f32_dot(refs[array][row], refs[grad][...], ((0,), (0,)))
+    for array, row, grad_array, grad_row in places:
+        term = f32_dot(refs[array][row], refs[grad_array][grad_row], ((0,), (0,)))
         result = term if result is None else result + term
-    total[...] = result
-    for k, out in zip([0] + order, (own_ref,) + outs):
-        first = pl.multiple_of((me ^ k) * piece, piece)
-        out[...] = total[pl.ds(first, piece), :].astype(out.dtype)
-
-
-def weight_grad(blocks, grads, order):
-    arrays, which = distinct([array for _, array, _ in blocks])
-    places = [(at, row, len(arrays) + source) for at, (source, _, row) in zip(which, blocks)]
-    parts = len(grads)
-    _, rows, cols = arrays[0].shape
-    width = grads[0].shape[1]
-    piece = (cols // (1 + len(order)), width)
-    return pl.pallas_call(
-        functools.partial(weight_kernel, places, order),
-        out_shape=(jax.ShapeDtypeStruct(piece, jnp.float32),)
-        + tuple(jax.ShapeDtypeStruct(piece, jnp.bfloat16) for _ in order),
-        in_specs=[VMEM] * (len(arrays) + parts),
-        out_specs=(VMEM,) * (1 + len(order)),
-        scratch_shapes=[pltpu.VMEM((cols, width), jnp.float32)],
+    refs[-1][...] = result.astype(jnp.bfloat16)
+
+
+def weight_grad(blocks, grads):
+    blocks, grads = sorted(blocks, key=lambda each: each[0]), sorted(grads, key=lambda each: each[0])
+    arrays, which = distinct([array for _, array, _ in blocks + grads])
+    parts = len(blocks)
+    places = [
+        (which[at], blocks[at][2], which[parts + at], grads[at][2]) for at in range(parts)
+    ]
+    _, rows, cols = blocks[0][1].shape
+    width = grads[0][1].shape[2]
+    return pl.pallas_call(
+        functools.partial(weight_kernel, places),
+        out_shape=jax.ShapeDtypeStruct((cols, width), jnp.bfloat16),
+        in_specs=[VMEM] * len(arrays),
+        out_specs=VMEM,
         compiler_params=pltpu.CompilerParams(vmem_limit_bytes=VMEM_LIMIT),
         cost_estimate=pl.CostEstimate(
             flops=2 * parts * rows * cols * width, bytes_accessed=2 * parts * rows * cols, transcendentals=0
         ),
         name="weight_grad",
-    )(*arrays, *grads)
+    )(*arrays)
 
 
 def swap(value, axis, flip):
@@ -346,6 +341,7 @@
         out_shape=jax.ShapeDtypeStruct(value.shape, value.dtype),
         in_specs=[VMEM] * (1 + len(earlier)),
         out_specs=VMEM,
+        compiler_params=pltpu.CompilerParams(vmem_limit_bytes=SMALL_VMEM_LIMIT),
         name="after",
     )(value, *earlier)
 
@@ -370,44 +366,56 @@
     first = bits[0]
     for near in range(1, minor):
         msgs[first + near] = swap(msgs[first], "pool", near)
-    relayed = after(msgs[bits[-1]], *(msgs[base + near] for base in (0, first) for near in range(1, minor)))
-    for at, bit in enumerate(bits):
-        for k in range(bit + minor, 2 * bit, minor):
-            msgs[k] = swap(relayed if bit == bits[-1] else msgs[bit], "pool", k ^ bit)
-    majors = sorted(k for k in msgs if k % minor == 0)
-    for far in majors[2:]:
+    majors = list(range(0, members, minor))
+    early = [far + near for far in majors[:-2] for near in range(minor)]
+    held = early[1 - minor:]
+    early = early[:1 - minor]
+    state, kept, stages = (), [], []
+
+    def add(fresh):
+        nonlocal state
+        *state, powers = add_pairs(sum(stages, []), fresh, row_counts, msgs, state)
+        kept.append(powers)
+        stages.append(fresh)
+
+    add(early)
+    last = bits[-1]
+    for k in range(first + minor, last, minor):
+        msgs[k] = swap(msgs[first], "pool", k ^ first)
+    relayed = after(msgs[last], state[1], *(msgs[k] for k in held))
+    for k in range(last + minor, members, minor):
+        msgs[k] = swap(relayed, "pool", k ^ last)
+    for far in majors[2:-1]:
         for near in range(1, minor):
             msgs[far + near] = swap(msgs[far], "pool", near)
-    columns = [[far + near for near in range(minor)] for far in majors]
-    stages = [sum(columns[:-2], []), majors[-2:], columns[-2][1:]]
-    seen, state, kept = [], (), []
-    for fresh in stages:
-        *state, powers = add_pairs(seen, fresh, row_counts, msgs, state)
-        kept.append(powers)
-        seen = seen + fresh
-    grad_proj = group_grad(stages, columns[-1][1:], row_counts, msgs, state, kept, [], normed, inv)
-
-    grads = {0: grad_proj}
+    add(held + majors[2:-1])
+    relayed = after(msgs[majors[-1]], state[1])
+    for near in range(1, minor):
+        msgs[majors[-1] + near] = swap(relayed, "pool", near)
+    add([majors[-1]])
+    add([far + near for far in majors[2:-1] for near in range(1, minor)])
+    grad_proj = group_grad(
+        stages, [majors[-1] + near for near in range(1, minor)], row_counts, msgs, state, kept, [], normed, inv
+    )
+
     bit = parts // 2
-    while bit:
-        for k in list(grads):
-            grads[k ^ bit] = swap(grads[k], "dp", bit)
-        bit //= 2
-    blocks = {k: [(0, near_cuts, k), (parts // 2, came, k)] for k in range(parts // 2)}
-    bit = parts // 4
+    grads = [(0, grad_proj, 0), (bit, swap(grad_proj, "dp", bit), 0)]
+    blocks = {k: [(0, near_cuts, k), (bit, came, k)] for k in range(bit)}
+    bit //= 2
     while bit:
         moving = [(k ^ bit, source ^ bit, array, at) for k in blocks if k & bit for source, array, at in blocks[k]]
-        passed = swap(pack([each[2:] for each in moving], grads[parts // 2]), "dp", bit)
         blocks = {k: blocks[k] for k in blocks if not k & bit}
+        passed = swap(pack([each[2:] for each in moving], [grads[-1][1]]), "dp", bit)
         for at, (k, source, _, _) in enumerate(moving):
             blocks[k].append((source, passed, at))
+        sent = swap(pack([each[1:] for each in grads]), "dp", bit)
+        grads += [(each[0] ^ bit, sent, at) for at, each in enumerate(grads)]
         bit //= 2
 
-    order = sorted(range(1, members), key=lambda k: (k < members // 2, k))
-    total, *pieces = weight_grad(blocks[0], [grads[k] for k in range(parts)], order)
-    for k, piece in zip(order, pieces):
-        total = total + swap(piece, "pool", k).astype(jnp.float32)
-    return total
+    partial = weight_grad(blocks[0], grads)
+    pieces = partial.reshape(members, partial.shape[0] // members, partial.shape[1])
+    pieces = lax.all_to_all(pieces, "pool", split_axis=0, concat_axis=0)
+    return jnp.sum(pieces.astype(jnp.float32), axis=0)
 
 
 def solution(mesh):

time: 56.1 us -> 52.3 us (0.932)
  blocking collectives: 0 us -> 15 us
  starting transfers between devices: 27.9 us -> 18.1 us
  waiting for transfers between devices: 12.8 us -> 7.88 us
  local copies, waits for them, and re-layouts: 3.13 us -> 0.01 us
  Pallas kernels: 11.2 us -> 10.3 us
    all_to_all x0 -> x1, blocking collectives: none -> 15 us  [per_device(): pieces = lax.all_to_all(pieces, 'pool', split_axis=0, concat_axis=0)]
    ppermute x19 -> x11, starting transfers between devices: 27.9 us -> 18.1 us  [swap(): return lax.ppermute(value, axis, [(at, at ^ flip) for at in range(size)])]
    ppermute x19 -> x11, waiting for transfers between devices: 12.8 us -> 7.88 us  [swap(): return lax.ppermute(value, axis, [(at, at ^ flip) for at in range(size)])]
    unnamed x18 -> x2, local copies, waits for them, and re-layouts: 3.13 us -> 0.01 us
    pallas_call x1 -> x2, Pallas kernels: 1.71 us -> 0.02 us  [after(): pl.pallas_call(order_kernel, out_shape=jax.ShapeDtypeStruct(value.shape,...]
    pallas_call x3 -> x4, Pallas kernels: 4.09 us -> 4.86 us  [add_pairs(): pl.pallas_call(functools.partial(pairs_kernel, seen, fresh), out_shape=(j...]
    add x1 -> x0, other arithmetic: 0.67 us -> none  [per_device(): total = total + swap(piece, 'pool', k).astype(jnp.float32)]
    reduce_sum x0 -> x1, other arithmetic: none -> 0.67 us  [per_device(): return jnp.sum(pieces.astype(jnp.float32), axis=0)]
  transfers between devices with their start and end apart: 19 -> 11, of which waited for: 7 -> 5; matrix products, arithmetic and copies ran while one was open for 0% -> 0% of each run, Pallas kernels for 15% -> 14%
where the time goes in v6:
time: 52.3 us; the launch traced here: 52.1 us
  starting transfers between devices  18.1 us (35%)
  blocking collectives  15 us (29%)
  Pallas kernels  10.3 us (20%)
  waiting for transfers between devices  7.88 us (15%)
  other arithmetic  0.67 us (1%)
    ppermute x11, starting transfers between devices, swap(): return lax.ppermute(value, axis, [(at, at ^ flip) for at in range(size)])  18.1 us
    all_to_all x1, blocking collectives, per_device(): pieces = lax.all_to_all(pieces, 'pool', split_axis=0, concat_axis=0)  15 us
    ppermute x11, waiting for transfers between devices, swap(): return lax.ppermute(value, axis, [(at, at ^ flip) for at in range(size)])  7.88 us
    pallas_call x4, Pallas kernels, add_pairs(): pl.pallas_call(functools.partial(pairs_kernel, seen, fresh), out_shape=(j...  4.86 us
    pallas_call x1, Pallas kernels, group_grad(): pl.pallas_call(functools.partial(grad_kernel, stages, fresh), out_shape=j...  2.48 us
    pallas_call x1, Pallas kernels, project(): pl.pallas_call(functools.partial(project_kernel, parts), out_shape=(jax.S...  2.42 us
  transfers between devices with their start and end apart: 11, of which 5 were waited for; matrix products, arithmetic and copies ran while one was open for 0% of the time, Pallas kernels for 14%

profile of v6, /device:TPU:0, one launch (start us, length us, event | category | flops | bytes accessed | tf_op | source)
XLA Modules:
  0.0 52.1 jit_solution(1156808997123407612)
XLA Ops:
  0.0 2.4 %project.1 = (bf16[272,256]{1,0:T(8,128)(2,1)S(1)}, f32[256,256]{1,0:T(8,128)S(1)}, f32[256,128]{1,0:T(8,128)S(1)}, bf16[2,256,512]{2,1,0:T(8,128)(2,1)S(1)}, bf16[2,256,512]{2,1,0:T(8,128)(2,1)S(1)}) custom-call(bf16[256,2048]{1,0:T(8,128)(2,1)} %feats_hbm.1, bf16[2048,256]{1,0:T(8,128)(2,1)} %w_hbm.1, s32[1,256]{1,0:T(1,128)} %bitcast.4, s32[1,256]{1,0:T(1,128)} %bitcast.5), custom_call_target="tpu_custom_call" | custom-call | flops 268435456 | bytes 2097152 | tf_op jit(solution)/shard_map/project/pallas_call | solution.py:81
  2.4 0.0 copy-start
  2.4 3.1 %collective-permute-start.2 = (bf16[272,256]{1,0:T(8,128)(2,1)S(1)}, bf16[272,256]{1,0:T(8,128)(2,1)S(1)}, u32[]{:S(2)}, u32[]{:S(2)}) collective-permute-start(bf16[272,256]{1,0:T(8,128)(2,1)S(1)} %get-tuple-element.24.refs_1_), channel_id=1, source_target_pairs={{0,2},{1,3},{2,0},{3,1},{4,6},{5,7},{6,4},{7,5},{8,10},{9,11},{10,... | collective-permute-start | bytes 417800 | tf_op jit(solution)/shard_map/ppermute | solution.py:331
  5.5 1.5 %collective-permute-start.1 = (bf16[272,256]{1,0:T(8,128)(2,1)S(1)}, bf16[272,256]{1,0:T(8,128)(2,1)S(1)}, u32[]{:S(2)}, u32[]{:S(2)}) collective-permute-start(bf16[272,256]{1,0:T(8,128)(2,1)S(1)} %get-tuple-element.24.refs_1_), channel_id=1, source_target_pairs={{0,1},{1,0},{2,3},{3,2},{4,5},{5,4},{6,7},{7,6},{8,9},{9,8},{10,11... | collective-permute-start | bytes 417800 | tf_op jit(solution)/shard_map/ppermute | solution.py:331
  7.0 2.6 %collective-permute-start.4 = (bf16[272,256]{1,0:T(8,128)(2,1)S(1)}, bf16[272,256]{1,0:T(8,128)(2,1)S(1)}, u32[]{:S(2)}, u32[]{:S(2)}) collective-permute-start(bf16[272,256]{1,0:T(8,128)(2,1)S(1)} %get-tuple-element.24.refs_1_), channel_id=1, source_target_pairs={{0,4},{1,5},{2,6},{3,7},{4,0},{5,1},{6,2},{7,3},{8,12},{9,13},{10,... | collective-permute-start | bytes 417800 | tf_op jit(solution)/shard_map/ppermute | solution.py:331
  9.6 0.0 collective-permute-done.2.refs_3_
  9.6 3.1 %collective-permute-start.3 = (bf16[272,256]{1,0:T(8,128)(2,1)S(1)}, bf16[272,256]{1,0:T(8,128)(2,1)S(1)}, u32[]{:S(2)}, u32[]{:S(2)}) collective-permute-start(bf16[272,256]{1,0:T(8,128)(2,1)S(1)} %collective-permute-done.2.refs_3_), channel_id=1, source_target_pairs={{0,1},{1,0},{2,3},{3,2},{4,5},{5,4},{6,7},{7,6},{8,9},{9,8},{10,11... | collective-permute-start | bytes 417800 | tf_op jit(solution)/shard_map/ppermute | solution.py:331
  12.7 1.5 %collective-permute-start = (bf16[2,256,512]{2,1,0:T(8,128)(2,1)S(1)}, bf16[2,256,512]{2,1,0:T(8,128)(2,1)S(1)}, u32[]{:S(2)}, u32[]{:S(2)}) collective-permute-start(bf16[2,256,512]{2,1,0:T(8,128)(2,1)S(1)} %get-tuple-element.23), channel_id=1, source_target_pairs={{0,16},{8,24},{16,0},{24,8},{1,17},{9,25},{17,1},{25,9},{2,18},{10... | collective-permute-start | bytes 1572872 | tf_op jit(solution)/shard_map/ppermute | solution.py:331
  14.2 0.0 collective-permute-done.1.refs_2_
  14.2 1.1 %add_pairs.4 = (f32[3,256]{1,0:T(4,128)S(1)}, f32[256,128]{1,0:T(8,128)S(1)}, f32[3,256,256]{2,1,0:T(8,128)S(1)}) custom-call(s32[4,8]{1,0:T(4,128)S(1)} %copy-done, bf16[272,256]{1,0:T(8,128)(2,1)S(1)} %get-tuple-element.24.refs_1_, bf16[272,256]{1,0:T(8,128)(2,1)S(1)} %collective-permute-done.1.refs_2_, bf16[272,256]{1,0:T(8,128)(2,1)S(1)} %collective-permute-done.2.refs_3_), custom_call_target="tpu_custom_call" | custom-call | flops 201326592 | bytes 1179648 | tf_op jit(solution)/shard_map/add_pairs/pallas_call | solution.py:195
  15.3 0.4 collective-permute-done.4.value_ref.refs_5_
  15.8 0.0 collective-permute-done.3.refs_1_.refs_4_
  15.8 0.3 collective-permute-start.5
  16.1 1.8 %collective-permute-start.6 = (bf16[272,256]{1,0:T(8,128)(2,1)S(1)}, bf16[272,256]{1,0:T(8,128)(2,1)S(1)}, u32[]{:S(2)}, u32[]{:S(2)}) collective-permute-start(bf16[272,256]{1,0:T(8,128)(2,1)S(1)} %collective-permute-done.4.value_ref.refs_5_), channel_id=1, source_target_pairs={{0,1},{1,0},{2,3},{3,2},{4,5},{5,4},{6,7},{7,6},{8,9},{9,8},{10,11... | collective-permute-start | bytes 417800 | tf_op jit(solution)/shard_map/ppermute | solution.py:331
  17.9 1.3 %add_pairs.5 = (f32[5,256]{1,0:T(8,128)S(1)}, f32[256,128]{1,0:T(8,128)S(1)}, f32[2,256,256]{2,1,0:T(8,128)S(1)}) custom-call(s32[4,8]{1,0:T(4,128)S(1)} %copy-done, bf16[272,256]{1,0:T(8,128)(2,1)S(1)} %get-tuple-element.24.refs_1_, bf16[272,256]{1,0:T(8,128)(2,1)S(1)} %collective-permute-done.1.refs_2_, ...), custom_call_target="tpu_custom_call" | custom-call | flops 301989888 | bytes 1179648 | tf_op jit(solution)/shard_map/add_pairs/pallas_call | solution.py:195
  19.3 1.6 %collective-permute-done.5.value_ref.refs_6_ = bf16[272,256]{1,0:T(8,128)(2,1)S(1)} collective-permute-done((bf16[272,256]{1,0:T(8,128)(2,1)S(1)}, bf16[272,256]{1,0:T(8,128)(2,1)S(1)}, u32[]{:S(2)}, u32[]{:S(2)}) %collective-permute-start.5) | collective-permute-done | bytes 139296 | tf_op jit(solution)/shard_map/ppermute | solution.py:331
  20.9 2.0 %collective-permute-start.7 = (bf16[272,256]{1,0:T(8,128)(2,1)S(1)}, bf16[272,256]{1,0:T(8,128)(2,1)S(1)}, u32[]{:S(2)}, u32[]{:S(2)}) collective-permute-start(bf16[272,256]{1,0:T(8,128)(2,1)S(1)} %after.3), channel_id=1, source_target_pairs={{0,1},{1,0},{2,3},{3,2},{4,5},{5,4},{6,7},{7,6},{8,9},{9,8},{10,11... | collective-permute-start | bytes 417800 | tf_op jit(solution)/shard_map/ppermute | solution.py:331
  22.9 1.2 %add_pairs.6 = (f32[6,256]{1,0:T(8,128)S(1)}, f32[256,128]{1,0:T(8,128)S(1)}, f32[1,256,256]{2,1,0:T(8,128)S(1)}) custom-call(s32[4,8]{1,0:T(4,128)S(1)} %copy-done, bf16[272,256]{1,0:T(8,128)(2,1)S(1)} %get-tuple-element.24.refs_1_, bf16[272,256]{1,0:T(8,128)(2,1)S(1)} %collective-permute-done.1.refs_2_, ...), custom_call_target="tpu_custom_call" | custom-call | flops 201326592 | bytes 1048576 | tf_op jit(solution)/shard_map/add_pairs/pallas_call | solution.py:195
  24.1 0.0 collective-permute-done.6.refs_7_
  24.1 1.2 %add_pairs.7 = (f32[7,256]{1,0:T(8,128)S(1)}, f32[256,128]{1,0:T(8,128)S(1)}, f32[1,256,256]{2,1,0:T(8,128)S(1)}) custom-call(s32[4,8]{1,0:T(4,128)S(1)} %copy-done, bf16[272,256]{1,0:T(8,128)(2,1)S(1)} %get-tuple-element.24.refs_1_, bf16[272,256]{1,0:T(8,128)(2,1)S(1)} %collective-permute-done.1.refs_2_, ...), custom_call_target="tpu_custom_call" | custom-call | flops 234881024 | bytes 1179648 | tf_op jit(solution)/shard_map/add_pairs/pallas_call | solution.py:195
  25.3 0.7 %collective-permute-done.7.refs_8_ = bf16[272,256]{1,0:T(8,128)(2,1)S(1)} collective-permute-done((bf16[272,256]{1,0:T(8,128)(2,1)S(1)}, bf16[272,256]{1,0:T(8,128)(2,1)S(1)}, u32[]{:S(2)}, u32[]{:S(2)}) %collective-permute-start.7) | collective-permute-done | bytes 139296 | tf_op jit(solution)/shard_map/ppermute | solution.py:331
  26.0 2.5 %group_grad.1.refs_0_.refs_3_ = bf16[1,256,256]{2,1,0:T(8,128)(2,1)S(1)} custom-call(s32[4,8]{1,0:T(4,128)S(1)} %copy-done, bf16[272,256]{1,0:T(8,128)(2,1)S(1)} %get-tuple-element.24.refs_1_, bf16[272,256]{1,0:T(8,128)(2,1)S(1)} %collective-permute-done.1.refs_2_, bf16[272,256]{1,0:T(8,128)(2,1)S(1)} %collective-permute-done.2.refs_3_, ...), custom_call_target="tpu_custom_call" | custom-call | flops 268435456 | bytes 1310720 | tf_op jit(solution)/shard_map/group_grad/pallas_call | solution.py:260
  28.5 1.6 %collective-permute-start.8 = (bf16[1,256,256]{2,1,0:T(8,128)(2,1)S(1)}, bf16[1,256,256]{2,1,0:T(8,128)(2,1)S(1)}, u32[]{:S(2)}, u32[]{:S(2)}) collective-permute-start(bf16[1,256,256]{2,1,0:T(8,128)(2,1)S(1)} %group_grad.1.refs_0_.refs_3_), channel_id=1, source_target_pairs={{0,16},{8,24},{16,0},{24,8},{1,17},{9,25},{17,1},{25,9},{2,18},{10... | collective-permute-start | bytes 393224 | tf_op jit(solution)/shard_map/ppermute | solution.py:331
  30.1 0.0 collective-permute-done.refs_1_.refs_2_
  30.1 3.4 %collective-permute-done.8.refs_2_.refs_1_.refs_5_ = bf16[1,256,256]{2,1,0:T(8,128)(2,1)S(1)} collective-permute-done((bf16[1,256,256]{2,1,0:T(8,128)(2,1)S(1)}, bf16[1,256,256]{2,1,0:T(8,128)(2,1)S(1)}, u32[]{:S(2)}, u32[]{:S(2)}) %collective-permute-start.8) | collective-permute-done | bytes 131104 | tf_op jit(solution)/shard_map/ppermute | solution.py:331
  33.6 0.1 collective-permute-start.9
  33.7 0.6 %collective-permute-start.10 = (bf16[2,256,256]{2,1,0:T(8,128)(2,1)S(1)}, bf16[2,256,256]{2,1,0:T(8,128)(2,1)S(1)}, u32[]{:S(2)}, u32[]{:S(2)}) collective-permute-start(bf16[2,256,256]{2,1,0:T(8,128)(2,1)S(1)} %pack.3), channel_id=1, source_target_pairs={{0,8},{8,0},{16,24},{24,16},{1,9},{9,1},{17,25},{25,17},{2,10},{10... | collective-permute-start | bytes 786440 | tf_op jit(solution)/shard_map/ppermute | solution.py:331
  34.3 1.7 %collective-permute-done.10.refs_4_ = bf16[2,256,256]{2,1,0:T(8,128)(2,1)S(1)} collective-permute-done((bf16[2,256,256]{2,1,0:T(8,128)(2,1)S(1)}, bf16[2,256,256]{2,1,0:T(8,128)(2,1)S(1)}, u32[]{:S(2)}, u32[]{:S(2)}) %collective-permute-start.10) | collective-permute-done | bytes 262176 | tf_op jit(solution)/shard_map/ppermute | solution.py:331
  35.9 0.0 collective-permute-done.9.refs_1_
  36.0 0.5 weight_grad.1
  36.4 15.0 %all_to_all.5 = bf16[8,64,256]{2,1,0:T(8,128)(2,1)S(1)} all-to-all(bf16[8,64,256]{2,1,0:T(8,128)(2,1)S(1)} %bitcast.3), channel_id=1, replica_groups=mesh['dp'=4,'pool'=8] {'pool'}, dimensions={0} | all-to-all | bytes 524288 | tf_op jit(solution)/shard_map/all_to_all | solution.py:417
  51.4 0.7 %convert_reduce_fusion = f32[64,256]{1,0:T(8,128)} fusion(bf16[8,64,256]{2,1,0:T(8,128)(2,1)S(1)} %all_to_all.5), kind=kLoop, calls=%fused_computation | loop fusion | flops 245760 | bytes 327680 | tf_op jit(solution)/shard_map/reduce_sum | solution.py:418
  (5 shorter events, 0.1 us)
Async XLA Ops:
  2.4 11.8 %copy-start = (s32[4,8]{1,0:T(4,128)S(1)}, s32[4,8]{1,0:T(4,128)}, u32[]{:S(2)}) copy-start(s32[4,8]{1,0:T(4,128)} %refs_0_.9) | copy-start | bytes 388
  2.4 7.2 %collective-permute-start.2 = (bf16[272,256]{1,0:T(8,128)(2,1)S(1)}, bf16[272,256]{1,0:T(8,128)(2,1)S(1)}, u32[]{:S(2)}, u32[]{:S(2)}) collective-permute-start(bf16[272,256]{1,0:T(8,128)(2,1)S(1)} %get-tuple-element.24.refs_1_), channel_id=1, source_target_pairs={{0,2},{1,3},{2,0},{3,1},{4,6},{5,7},{6,4},{7,5},{8,10},{9,11},{10,... | collective-permute-start | bytes 417800 | tf_op jit(solution)/shard_map/ppermute | solution.py:331
  5.5 8.7 %collective-permute-start.1 = (bf16[272,256]{1,0:T(8,128)(2,1)S(1)}, bf16[272,256]{1,0:T(8,128)(2,1)S(1)}, u32[]{:S(2)}, u32[]{:S(2)}) collective-permute-start(bf16[272,256]{1,0:T(8,128)(2,1)S(1)} %get-tuple-element.24.refs_1_), channel_id=1, source_target_pairs={{0,1},{1,0},{2,3},{3,2},{4,5},{5,4},{6,7},{7,6},{8,9},{9,8},{10,11... | collective-permute-start | bytes 417800 | tf_op jit(solution)/shard_map/ppermute | solution.py:331
  7.0 8.7 %collective-permute-start.4 = (bf16[272,256]{1,0:T(8,128)(2,1)S(1)}, bf16[272,256]{1,0:T(8,128)(2,1)S(1)}, u32[]{:S(2)}, u32[]{:S(2)}) collective-permute-start(bf16[272,256]{1,0:T(8,128)(2,1)S(1)} %get-tuple-element.24.refs_1_), channel_id=1, source_target_pairs={{0,4},{1,5},{2,6},{3,7},{4,0},{5,1},{6,2},{7,3},{8,12},{9,13},{10,... | collective-permute-start | bytes 417800 | tf_op jit(solution)/shard_map/ppermute | solution.py:331
  9.6 6.1 %collective-permute-start.3 = (bf16[272,256]{1,0:T(8,128)(2,1)S(1)}, bf16[272,256]{1,0:T(8,128)(2,1)S(1)}, u32[]{:S(2)}, u32[]{:S(2)}) collective-permute-start(bf16[272,256]{1,0:T(8,128)(2,1)S(1)} %collective-permute-done.2.refs_3_), channel_id=1, source_target_pairs={{0,1},{1,0},{2,3},{3,2},{4,5},{5,4},{6,7},{7,6},{8,9},{9,8},{10,11... | collective-permute-start | bytes 417800 | tf_op jit(solution)/shard_map/ppermute | solution.py:331
  12.7 17.4 %collective-permute-start = (bf16[2,256,512]{2,1,0:T(8,128)(2,1)S(1)}, bf16[2,256,512]{2,1,0:T(8,128)(2,1)S(1)}, u32[]{:S(2)}, u32[]{:S(2)}) collective-permute-start(bf16[2,256,512]{2,1,0:T(8,128)(2,1)S(1)} %get-tuple-element.23), channel_id=1, source_target_pairs={{0,16},{8,24},{16,0},{24,8},{1,17},{9,25},{17,1},{25,9},{2,18},{10... | collective-permute-start | bytes 1572872 | tf_op jit(solution)/shard_map/ppermute | solution.py:331
  15.8 5.1 %collective-permute-start.5 = (bf16[272,256]{1,0:T(8,128)(2,1)S(1)}, bf16[272,256]{1,0:T(8,128)(2,1)S(1)}, u32[]{:S(2)}, u32[]{:S(2)}) collective-permute-start(bf16[272,256]{1,0:T(8,128)(2,1)S(1)} %after.2), channel_id=1, source_target_pairs={{0,2},{1,3},{2,0},{3,1},{4,6},{5,7},{6,4},{7,5},{8,10},{9,11},{10,... | collective-permute-start | bytes 417800 | tf_op jit(solution)/shard_map/ppermute | solution.py:331
  16.1 8.0 %collective-permute-start.6 = (bf16[272,256]{1,0:T(8,128)(2,1)S(1)}, bf16[272,256]{1,0:T(8,128)(2,1)S(1)}, u32[]{:S(2)}, u32[]{:S(2)}) collective-permute-start(bf16[272,256]{1,0:T(8,128)(2,1)S(1)} %collective-permute-done.4.value_ref.refs_5_), channel_id=1, source_target_pairs={{0,1},{1,0},{2,3},{3,2},{4,5},{5,4},{6,7},{7,6},{8,9},{9,8},{10,11... | collective-permute-start | bytes 417800 | tf_op jit(solution)/shard_map/ppermute | solution.py:331
  20.9 5.1 %collective-permute-start.7 = (bf16[272,256]{1,0:T(8,128)(2,1)S(1)}, bf16[272,256]{1,0:T(8,128)(2,1)S(1)}, u32[]{:S(2)}, u32[]{:S(2)}) collective-permute-start(bf16[272,256]{1,0:T(8,128)(2,1)S(1)} %after.3), channel_id=1, source_target_pairs={{0,1},{1,0},{2,3},{3,2},{4,5},{5,4},{6,7},{7,6},{8,9},{9,8},{10,11... | collective-permute-start | bytes 417800 | tf_op jit(solution)/shard_map/ppermute | solution.py:331
  28.5 5.0 %collective-permute-start.8 = (bf16[1,256,256]{2,1,0:T(8,128)(2,1)S(1)}, bf16[1,256,256]{2,1,0:T(8,128)(2,1)S(1)}, u32[]{:S(2)}, u32[]{:S(2)}) collective-permute-start(bf16[1,256,256]{2,1,0:T(8,128)(2,1)S(1)} %group_grad.1.refs_0_.refs_3_), channel_id=1, source_target_pairs={{0,16},{8,24},{16,0},{24,8},{1,17},{9,25},{17,1},{25,9},{2,18},{10... | collective-permute-start | bytes 393224 | tf_op jit(solution)/shard_map/ppermute | solution.py:331
  33.6 2.4 %collective-permute-start.9 = (bf16[2,256,512]{2,1,0:T(8,128)(2,1)S(1)}, bf16[2,256,512]{2,1,0:T(8,128)(2,1)S(1)}, u32[]{:S(2)}, u32[]{:S(2)}) collective-permute-start(bf16[2,256,512]{2,1,0:T(8,128)(2,1)S(1)} %pack.2), channel_id=1, source_target_pairs={{0,8},{8,0},{16,24},{24,16},{1,9},{9,1},{17,25},{25,17},{2,10},{10... | collective-permute-start | bytes 1572872 | tf_op jit(solution)/shard_map/ppermute | solution.py:331
  33.7 2.2 %collective-permute-start.10 = (bf16[2,256,256]{2,1,0:T(8,128)(2,1)S(1)}, bf16[2,256,256]{2,1,0:T(8,128)(2,1)S(1)}, u32[]{:S(2)}, u32[]{:S(2)}) collective-permute-start(bf16[2,256,256]{2,1,0:T(8,128)(2,1)S(1)} %pack.3), channel_id=1, source_target_pairs={{0,8},{8,0},{16,24},{24,16},{1,9},{9,1},{17,25},{25,17},{2,10},{10... | collective-permute-start | bytes 786440 | tf_op jit(solution)/shard_map/ppermute | solution.py:331

commit v7 on v6

--- a/solution.py
+++ b/solution.py
@@ -37,6 +37,12 @@
     cuts = [near_ref.at[k] for k in range(half)] + [far_ref.at[k] for k in range(half)]
     width = w_v.shape[1]
     me = lax.axis_index("dp")
+    small = (
+        pltpu.make_async_copy(partners_hbm, partners_ref, small_sems.at[0]),
+        pltpu.make_async_copy(buckets_hbm, buckets_ref, small_sems.at[1]),
+    )
+    for copy in small:
+        copy.start()
     copies = []
     for k in range(parts):
         first = pl.multiple_of((me ^ k) * step, step)
@@ -48,12 +54,11 @@
         pair[0].start()
         pair[1].start()
         copies.append(pair)
-    small = (
-        pltpu.make_async_copy(partners_hbm, partners_ref, small_sems.at[0]),
-        pltpu.make_async_copy(buckets_hbm, buckets_ref, small_sems.at[1]),
-    )
-    for copy in small:
-        copy.start()
+    projected = jnp.zeros((rows, width), jnp.float32)
+    for k in range(parts):
+        copies[k][0].wait()
+        copies[k][1].wait()
+        projected = projected + f32_dot(cuts[k][...], w_v[pl.ds(k * step, step), :], ((1,), (0,)))
     for copy in small:
         copy.wait()
     partners = partners_ref[...]
@@ -63,11 +68,6 @@
     kinds = lax.broadcasted_iota(jnp.int32, (META, rows), 0)
     meta = jnp.where(kinds == 0, logq, jnp.where(kinds == 1, high, jnp.where(kinds == 2, low, 0.0)))
     msg_ref[pl.ds(rows, META), :] = meta.astype(jnp.bfloat16)
-    projected = jnp.zeros((rows, width), jnp.float32)
-    for k in range(parts):
-        copies[k][0].wait()
-        copies[k][1].wait()
-        projected = projected + f32_dot(cuts[k][...], w_v[pl.ds(k * step, step), :], ((1,), (0,)))
     inv_norm = lax.rsqrt(jnp.sum(projected * projected, axis=1, keepdims=True) + epsilon)
     normed = projected * inv_norm
     normed_ref[...] = normed
@@ -296,34 +296,64 @@
     )(*arrays, *earlier)
 
 
-def weight_kernel(places, *refs):
+def weight_kernel(places, minor, inputs, *refs):
+    arrays, outs, total = refs[:inputs], refs[inputs:-1], refs[-1]
+    majors, piece, _ = outs[0].shape
+    me = lax.axis_index("pool")
     result = None
     for array, row, grad_array, grad_row in places:
-        term = f32_dot(refs[array][row], refs[grad_array][grad_row], ((0,), (0,)))
+        term = f32_dot(arrays[array][row], arrays[grad_array][grad_row], ((0,), (0,)))
         result = term if result is None else result + term
-    refs[-1][...] = result.astype(jnp.bfloat16)
-
-
-def weight_grad(blocks, grads):
+    total[...] = result
+    for near, out in enumerate(outs):
+        for far in range(majors):
+            first = pl.multiple_of((me ^ (far * minor + near)) * piece, piece)
+            out[far] = total[pl.ds(first, piece), :].astype(out.dtype)
+
+
+def weight_grad(blocks, grads, members, minor):
     blocks, grads = sorted(blocks, key=lambda each: each[0]), sorted(grads, key=lambda each: each[0])
     arrays, which = distinct([array for _, array, _ in blocks + grads])
     parts = len(blocks)
-    places = [
-        (which[at], blocks[at][2], which[parts + at], grads[at][2]) for at in range(parts)
-    ]
+    places = [(which[at], blocks[at][2], which[parts + at], grads[at][2]) for at in range(parts)]
     _, rows, cols = blocks[0][1].shape
     width = grads[0][1].shape[2]
-    return pl.pallas_call(
-        functools.partial(weight_kernel, places),
-        out_shape=jax.ShapeDtypeStruct((cols, width), jnp.bfloat16),
+    pieces = (members // minor, cols // members, width)
+    return pl.pallas_call(
+        functools.partial(weight_kernel, places, minor, len(arrays)),
+        out_shape=(jax.ShapeDtypeStruct(pieces, jnp.float32),)
+        + (jax.ShapeDtypeStruct(pieces, jnp.bfloat16),) * (minor - 1),
         in_specs=[VMEM] * len(arrays),
-        out_specs=VMEM,
+        out_specs=(VMEM,) * minor,
+        scratch_shapes=[pltpu.VMEM((cols, width), jnp.float32)],
         compiler_params=pltpu.CompilerParams(vmem_limit_bytes=VMEM_LIMIT),
         cost_estimate=pl.CostEstimate(
             flops=2 * parts * rows * cols * width, bytes_accessed=2 * parts * rows * cols, transcendentals=0
         ),
         name="weight_grad",
     )(*arrays)
+
+
+def add_pieces_kernel(came, own_ref, *refs):
+    for far, out in enumerate(refs[came:]):
+        total = own_ref[far]
+        for ref in refs[:came]:
+            total = total + ref[far].astype(jnp.float32)
+        out[...] = total.astype(out.dtype)
+
+
+def add_pieces(own, came):
+    majors, *piece = own.shape
+    return pl.pallas_call(
+        functools.partial(add_pieces_kernel, len(came)),
+        out_shape=(jax.ShapeDtypeStruct(piece, jnp.float32),)
+        + (jax.ShapeDtypeStruct(piece, jnp.bfloat16),) * (majors - 1),
+        in_specs=[VMEM] * (1 + len(came)),
+        out_specs=(VMEM,) * majors,
+        compiler_params=pltpu.CompilerParams(vmem_limit_bytes=SMALL_VMEM_LIMIT),
+        cost_estimate=pl.CostEstimate(flops=own.size, bytes_accessed=8 * own.size, transcendentals=0),
+        name="add_pieces",
+    )(own, *came)
 
 
 def swap(value, axis, flip):
@@ -382,7 +412,7 @@
     last = bits[-1]
     for k in range(first + minor, last, minor):
         msgs[k] = swap(msgs[first], "pool", k ^ first)
-    relayed = after(msgs[last], state[1], *(msgs[k] for k in held))
+    relayed = after(msgs[last], state[1])
     for k in range(last + minor, members, minor):
         msgs[k] = swap(relayed, "pool", k ^ last)
     for far in majors[2:-1]:
@@ -394,28 +424,33 @@
         msgs[majors[-1] + near] = swap(relayed, "pool", near)
     add([majors[-1]])
     add([far + near for far in majors[2:-1] for near in range(1, minor)])
-    grad_proj = group_grad(
-        stages, [majors[-1] + near for near in range(1, minor)], row_counts, msgs, state, kept, [], normed, inv
-    )
-
     bit = parts // 2
-    grads = [(0, grad_proj, 0), (bit, swap(grad_proj, "dp", bit), 0)]
     blocks = {k: [(0, near_cuts, k), (bit, came, k)] for k in range(bit)}
     bit //= 2
     while bit:
         moving = [(k ^ bit, source ^ bit, array, at) for k in blocks if k & bit for source, array, at in blocks[k]]
         blocks = {k: blocks[k] for k in blocks if not k & bit}
-        passed = swap(pack([each[2:] for each in moving], [grads[-1][1]]), "dp", bit)
+        passed = swap(pack([each[2:] for each in moving], [state[1]]), "dp", bit)
         for at, (k, source, _, _) in enumerate(moving):
             blocks[k].append((source, passed, at))
-        sent = swap(pack([each[1:] for each in grads]), "dp", bit)
+        bit //= 2
+    grad_proj = group_grad(
+        stages, [majors[-1] + near for near in range(1, minor)], row_counts, msgs, state, kept, [], normed, inv
+    )
+
+    bit = parts // 2
+    grads = [(0, grad_proj, 0)]
+    while bit:
+        sent = swap(grad_proj if len(grads) == 1 else pack([each[1:] for each in grads]), "dp", bit)
         grads += [(each[0] ^ bit, sent, at) for at, each in enumerate(grads)]
         bit //= 2
 
-    partial = weight_grad(blocks[0], grads)
-    pieces = partial.reshape(members, partial.shape[0] // members, partial.shape[1])
-    pieces = lax.all_to_all(pieces, "pool", split_axis=0, concat_axis=0)
-    return jnp.sum(pieces.astype(jnp.float32), axis=0)
+    own, *pieces = weight_grad(blocks[0], grads, members, minor)
+    pieces = [swap(each, "pool", near + 1) for near, each in enumerate(pieces)]
+    total, *pieces = add_pieces(own, pieces)
+    for far in reversed(range(1, members // minor)):
+        total = total + swap(pieces[far - 1], "pool", far * minor).astype(jnp.float32)
+    return total
 
 
 def solution(mesh):

time: 52.3 us -> 50.6 us (0.967)
  blocking collectives: 15 us -> 0 us
  waiting for transfers between devices: 7.88 us -> 20.9 us
    all_to_all x1 -> x0, blocking collectives: 15 us -> none  [per_device(): pieces = lax.all_to_all(pieces, 'pool', split_axis=0, concat_axis=0)]
    ppermute x11 -> x15, waiting for transfers between devices: 7.88 us -> 20.9 us  [swap(): return lax.ppermute(value, axis, [(at, at ^ flip) for at in range(size)])]
    reduce_sum x1 -> x0, other arithmetic: 0.67 us -> none  [per_device(): return jnp.sum(pieces.astype(jnp.float32), axis=0)]
    add x0 -> x1, other arithmetic: none -> 0.65 us  [per_device(): total + swap(pieces[far - 1], 'pool', far * minor).astype(jnp.float32)]
    ppermute x11 -> x15, starting transfers between devices: 18.1 us -> 18.5 us  [swap(): return lax.ppermute(value, axis, [(at, at ^ flip) for at in range(size)])]
  transfers between devices with their start and end apart: 11 -> 15, of which waited for: 5 -> 8; matrix products, arithmetic and copies ran while one was open for 0% -> 0% of each run, Pallas kernels for 14% -> 15%
where the time goes in v7:
time: 50.6 us; the launch traced here: 50.5 us
  waiting for transfers between devices  20.9 us (41%)
  starting transfers between devices  18.5 us (37%)
  Pallas kernels  10.2 us (20%)
  other arithmetic  0.65 us (1%)
    ppermute x15, waiting for transfers between devices, swap(): return lax.ppermute(value, axis, [(at, at ^ flip) for at in range(size)])  20.9 us
    ppermute x15, starting transfers between devices, swap(): return lax.ppermute(value, axis, [(at, at ^ flip) for at in range(size)])  18.5 us
    pallas_call x4, Pallas kernels, add_pairs(): pl.pallas_call(functools.partial(pairs_kernel, seen, fresh), out_shape=(j...  4.87 us
    pallas_call x1, Pallas kernels, group_grad(): pl.pallas_call(functools.partial(grad_kernel, stages, fresh), out_shape=j...  2.49 us
    pallas_call x1, Pallas kernels, project(): pl.pallas_call(functools.partial(project_kernel, parts), out_shape=(jax.S...  2.27 us
  transfers between devices with their start and end apart: 15, of which 8 were waited for; matrix products, arithmetic and copies ran while one was open for 0% of the time, Pallas kernels for 15%

profile of v7, /device:TPU:0, one launch (start us, length us, event | category | flops | bytes accessed | tf_op | source)
XLA Modules:
  0.0 50.5 jit_solution(11921242726391752017)
XLA Ops:
  0.0 2.3 %project.1 = (bf16[272,256]{1,0:T(8,128)(2,1)S(1)}, f32[256,256]{1,0:T(8,128)S(1)}, f32[256,128]{1,0:T(8,128)S(1)}, bf16[2,256,512]{2,1,0:T(8,128)(2,1)S(1)}, bf16[2,256,512]{2,1,0:T(8,128)(2,1)S(1)}) custom-call(bf16[256,2048]{1,0:T(8,128)(2,1)} %feats_hbm.1, bf16[2048,256]{1,0:T(8,128)(2,1)} %w_hbm.1, s32[1,256]{1,0:T(1,128)} %bitcast.2, s32[1,256]{1,0:T(1,128)} %bitcast.3), custom_call_target="tpu_custom_call" | custom-call | flops 268435456 | bytes 2097152 | tf_op jit(solution)/shard_map/project/pallas_call | solution.py:81
  2.3 0.0 copy-start
  2.3 3.0 %collective-permute-start = (bf16[2,256,512]{2,1,0:T(8,128)(2,1)S(1)}, bf16[2,256,512]{2,1,0:T(8,128)(2,1)S(1)}, u32[]{:S(2)}, u32[]{:S(2)}) collective-permute-start(bf16[2,256,512]{2,1,0:T(8,128)(2,1)S(1)} %get-tuple-element.29), channel_id=1, source_target_pairs={{0,16},{8,24},{16,0},{24,8},{1,17},{9,25},{17,1},{25,9},{2,18},{10... | collective-permute-start | bytes 1572872 | tf_op jit(solution)/shard_map/ppermute | solution.py:361
  5.3 1.6 %collective-permute-start.2 = (bf16[272,256]{1,0:T(8,128)(2,1)S(1)}, bf16[272,256]{1,0:T(8,128)(2,1)S(1)}, u32[]{:S(2)}, u32[]{:S(2)}) collective-permute-start(bf16[272,256]{1,0:T(8,128)(2,1)S(1)} %get-tuple-element.30.refs_1_), channel_id=1, source_target_pairs={{0,2},{1,3},{2,0},{3,1},{4,6},{5,7},{6,4},{7,5},{8,10},{9,11},{10,... | collective-permute-start | bytes 417800 | tf_op jit(solution)/shard_map/ppermute | solution.py:361
  6.9 1.5 %collective-permute-start.1 = (bf16[272,256]{1,0:T(8,128)(2,1)S(1)}, bf16[272,256]{1,0:T(8,128)(2,1)S(1)}, u32[]{:S(2)}, u32[]{:S(2)}) collective-permute-start(bf16[272,256]{1,0:T(8,128)(2,1)S(1)} %get-tuple-element.30.refs_1_), channel_id=1, source_target_pairs={{0,1},{1,0},{2,3},{3,2},{4,5},{5,4},{6,7},{7,6},{8,9},{9,8},{10,11... | collective-permute-start | bytes 417800 | tf_op jit(solution)/shard_map/ppermute | solution.py:361
  8.4 2.6 %collective-permute-start.4 = (bf16[272,256]{1,0:T(8,128)(2,1)S(1)}, bf16[272,256]{1,0:T(8,128)(2,1)S(1)}, u32[]{:S(2)}, u32[]{:S(2)}) collective-permute-start(bf16[272,256]{1,0:T(8,128)(2,1)S(1)} %get-tuple-element.30.refs_1_), channel_id=1, source_target_pairs={{0,4},{1,5},{2,6},{3,7},{4,0},{5,1},{6,2},{7,3},{8,12},{9,13},{10,... | collective-permute-start | bytes 417800 | tf_op jit(solution)/shard_map/ppermute | solution.py:361
  11.0 0.0 collective-permute-done.2.refs_3_
  11.0 2.5 %collective-permute-start.3 = (bf16[272,256]{1,0:T(8,128)(2,1)S(1)}, bf16[272,256]{1,0:T(8,128)(2,1)S(1)}, u32[]{:S(2)}, u32[]{:S(2)}) collective-permute-start(bf16[272,256]{1,0:T(8,128)(2,1)S(1)} %collective-permute-done.2.refs_3_), channel_id=1, source_target_pairs={{0,1},{1,0},{2,3},{3,2},{4,5},{5,4},{6,7},{7,6},{8,9},{9,8},{10,11... | collective-permute-start | bytes 417800 | tf_op jit(solution)/shard_map/ppermute | solution.py:361
  13.5 1.1 %add_pairs.4 = (f32[3,256]{1,0:T(4,128)S(1)}, f32[256,128]{1,0:T(8,128)S(1)}, f32[3,256,256]{2,1,0:T(8,128)S(1)}) custom-call(s32[4,8]{1,0:T(4,128)S(1)} %copy-done, bf16[272,256]{1,0:T(8,128)(2,1)S(1)} %get-tuple-element.30.refs_1_, bf16[272,256]{1,0:T(8,128)(2,1)S(1)} %collective-permute-done.1.refs_2_, bf16[272,256]{1,0:T(8,128)(2,1)S(1)} %collective-permute-done.2.refs_3_), custom_call_target="tpu_custom_call" | custom-call | flops 201326592 | bytes 1179648 | tf_op jit(solution)/shard_map/add_pairs/pallas_call | solution.py:195
  14.6 2.2 %collective-permute-done.4.value_ref.refs_5_ = bf16[272,256]{1,0:T(8,128)(2,1)S(1)} collective-permute-done((bf16[272,256]{1,0:T(8,128)(2,1)S(1)}, bf16[272,256]{1,0:T(8,128)(2,1)S(1)}, u32[]{:S(2)}, u32[]{:S(2)}) %collective-permute-start.4) | collective-permute-done | bytes 139296 | tf_op jit(solution)/shard_map/ppermute | solution.py:361
  16.9 0.1 collective-permute-start.5
  16.9 0.8 %collective-permute-start.6 = (bf16[272,256]{1,0:T(8,128)(2,1)S(1)}, bf16[272,256]{1,0:T(8,128)(2,1)S(1)}, u32[]{:S(2)}, u32[]{:S(2)}) collective-permute-start(bf16[272,256]{1,0:T(8,128)(2,1)S(1)} %collective-permute-done.4.value_ref.refs_5_), channel_id=1, source_target_pairs={{0,1},{1,0},{2,3},{3,2},{4,5},{5,4},{6,7},{7,6},{8,9},{9,8},{10,11... | collective-permute-start | bytes 417800 | tf_op jit(solution)/shard_map/ppermute | solution.py:361
  17.7 1.3 %add_pairs.5 = (f32[5,256]{1,0:T(8,128)S(1)}, f32[256,128]{1,0:T(8,128)S(1)}, f32[2,256,256]{2,1,0:T(8,128)S(1)}) custom-call(s32[4,8]{1,0:T(4,128)S(1)} %copy-done, bf16[272,256]{1,0:T(8,128)(2,1)S(1)} %get-tuple-element.30.refs_1_, bf16[272,256]{1,0:T(8,128)(2,1)S(1)} %collective-permute-done.1.refs_2_, ...), custom_call_target="tpu_custom_call" | custom-call | flops 301989888 | bytes 1179648 | tf_op jit(solution)/shard_map/add_pairs/pallas_call | solution.py:195
  19.1 2.9 %collective-permute-done.5.refs_6_.value_ref = bf16[272,256]{1,0:T(8,128)(2,1)S(1)} collective-permute-done((bf16[272,256]{1,0:T(8,128)(2,1)S(1)}, bf16[272,256]{1,0:T(8,128)(2,1)S(1)}, u32[]{:S(2)}, u32[]{:S(2)}) %collective-permute-start.5) | collective-permute-done | bytes 139296 | tf_op jit(solution)/shard_map/ppermute | solution.py:361
  22.0 0.7 %collective-permute-start.8 = (bf16[272,256]{1,0:T(8,128)(2,1)S(1)}, bf16[272,256]{1,0:T(8,128)(2,1)S(1)}, u32[]{:S(2)}, u32[]{:S(2)}) collective-permute-start(bf16[272,256]{1,0:T(8,128)(2,1)S(1)} %after.3), channel_id=1, source_target_pairs={{0,1},{1,0},{2,3},{3,2},{4,5},{5,4},{6,7},{7,6},{8,9},{9,8},{10,11... | collective-permute-start | bytes 417800 | tf_op jit(solution)/shard_map/ppermute | solution.py:361
  22.7 1.2 %add_pairs.6 = (f32[6,256]{1,0:T(8,128)S(1)}, f32[256,128]{1,0:T(8,128)S(1)}, f32[1,256,256]{2,1,0:T(8,128)S(1)}) custom-call(s32[4,8]{1,0:T(4,128)S(1)} %copy-done, bf16[272,256]{1,0:T(8,128)(2,1)S(1)} %get-tuple-element.30.refs_1_, bf16[272,256]{1,0:T(8,128)(2,1)S(1)} %collective-permute-done.1.refs_2_, ...), custom_call_target="tpu_custom_call" | custom-call | flops 201326592 | bytes 1048576 | tf_op jit(solution)/shard_map/add_pairs/pallas_call | solution.py:195
  23.9 1.2 %add_pairs.7 = (f32[7,256]{1,0:T(8,128)S(1)}, f32[256,128]{1,0:T(8,128)S(1)}, f32[1,256,256]{2,1,0:T(8,128)S(1)}) custom-call(s32[4,8]{1,0:T(4,128)S(1)} %copy-done, bf16[272,256]{1,0:T(8,128)(2,1)S(1)} %get-tuple-element.30.refs_1_, bf16[272,256]{1,0:T(8,128)(2,1)S(1)} %collective-permute-done.1.refs_2_, ...), custom_call_target="tpu_custom_call" | custom-call | flops 234881024 | bytes 1179648 | tf_op jit(solution)/shard_map/add_pairs/pallas_call | solution.py:195
  25.1 0.1 collective-permute-start.7
  25.2 1.9 %collective-permute-done.8.refs_8_ = bf16[272,256]{1,0:T(8,128)(2,1)S(1)} collective-permute-done((bf16[272,256]{1,0:T(8,128)(2,1)S(1)}, bf16[272,256]{1,0:T(8,128)(2,1)S(1)}, u32[]{:S(2)}, u32[]{:S(2)}) %collective-permute-start.8) | collective-permute-done | bytes 139296 | tf_op jit(solution)/shard_map/ppermute | solution.py:361
  27.1 2.5 %group_grad.1.refs_0_.refs_3_ = bf16[1,256,256]{2,1,0:T(8,128)(2,1)S(1)} custom-call(s32[4,8]{1,0:T(4,128)S(1)} %copy-done, bf16[272,256]{1,0:T(8,128)(2,1)S(1)} %get-tuple-element.30.refs_1_, bf16[272,256]{1,0:T(8,128)(2,1)S(1)} %collective-permute-done.1.refs_2_, bf16[272,256]{1,0:T(8,128)(2,1)S(1)} %collective-permute-done.2.refs_3_, ...), custom_call_target="tpu_custom_call" | custom-call | flops 268435456 | bytes 1310720 | tf_op jit(solution)/shard_map/group_grad/pallas_call | solution.py:260
  29.6 0.6 %collective-permute-start.9 = (bf16[1,256,256]{2,1,0:T(8,128)(2,1)S(1)}, bf16[1,256,256]{2,1,0:T(8,128)(2,1)S(1)}, u32[]{:S(2)}, u32[]{:S(2)}) collective-permute-start(bf16[1,256,256]{2,1,0:T(8,128)(2,1)S(1)} %group_grad.1.refs_0_.refs_3_), channel_id=1, source_target_pairs={{0,16},{8,24},{16,0},{24,8},{1,17},{9,25},{17,1},{25,9},{2,18},{10... | collective-permute-start | bytes 393224 | tf_op jit(solution)/shard_map/ppermute | solution.py:361
  30.2 4.5 %collective-permute-done.9.refs_1_.refs_5_ = bf16[1,256,256]{2,1,0:T(8,128)(2,1)S(1)} collective-permute-done((bf16[1,256,256]{2,1,0:T(8,128)(2,1)S(1)}, bf16[1,256,256]{2,1,0:T(8,128)(2,1)S(1)}, u32[]{:S(2)}, u32[]{:S(2)}) %collective-permute-start.9) | collective-permute-done | bytes 131104 | tf_op jit(solution)/shard_map/ppermute | solution.py:361
  34.7 0.1 collective-permute-start.10
  34.7 1.5 %collective-permute-done.10.refs_4_ = bf16[2,256,256]{2,1,0:T(8,128)(2,1)S(1)} collective-permute-done((bf16[2,256,256]{2,1,0:T(8,128)(2,1)S(1)}, bf16[2,256,256]{2,1,0:T(8,128)(2,1)S(1)}, u32[]{:S(2)}, u32[]{:S(2)}) %collective-permute-start.10) | collective-permute-done | bytes 262176 | tf_op jit(solution)/shard_map/ppermute | solution.py:361
  36.3 0.5 %weight_grad.1 = (f32[4,64,256]{2,1,0:T(8,128)S(1)}, bf16[4,64,256]{2,1,0:T(8,128)(2,1)S(1)}) custom-call(bf16[2,256,512]{2,1,0:T(8,128)(2,1)S(1)} %get-tuple-element.28.refs_0_, bf16[2,256,512]{2,1,0:T(8,128)(2,1)S(1)} %collective-permute-done.7.refs_1_, bf16[2,256,512]{2,1,0:T(8,128)(2,1)S(1)} %collective-permute-done.refs_1_.refs_2_, ...), custom_call_target="tpu_custom_call" | custom-call | flops 268435456 | bytes 1048576 | tf_op jit(solution)/shard_map/weight_grad/pallas_call | solution.py:322
  36.8 0.7 %collective-permute-start.11 = (bf16[4,64,256]{2,1,0:T(8,128)(2,1)S(1)}, bf16[4,64,256]{2,1,0:T(8,128)(2,1)S(1)}, u32[]{:S(2)}, u32[]{:S(2)}) collective-permute-start(bf16[4,64,256]{2,1,0:T(8,128)(2,1)S(1)} %get-tuple-element.46), channel_id=1, source_target_pairs={{0,1},{1,0},{2,3},{3,2},{4,5},{5,4},{6,7},{7,6},{8,9},{9,8},{10,11... | collective-permute-start | bytes 393224 | tf_op jit(solution)/shard_map/ppermute | solution.py:361
  37.5 4.9 %collective-permute-done.11.refs_0_ = bf16[4,64,256]{2,1,0:T(8,128)(2,1)S(1)} collective-permute-done((bf16[4,64,256]{2,1,0:T(8,128)(2,1)S(1)}, bf16[4,64,256]{2,1,0:T(8,128)(2,1)S(1)}, u32[]{:S(2)}, u32[]{:S(2)}) %collective-permute-start.11) | collective-permute-done | bytes 131104 | tf_op jit(solution)/shard_map/ppermute | solution.py:361
  42.4 2.6 %collective-permute-start.12 = (bf16[64,256]{1,0:T(8,128)(2,1)S(1)}, bf16[64,256]{1,0:T(8,128)(2,1)S(1)}, u32[]{:S(2)}, u32[]{:S(2)}) collective-permute-start(bf16[64,256]{1,0:T(8,128)(2,1)S(1)} %get-tuple-element.48), channel_id=1, source_target_pairs={{0,6},{1,7},{2,4},{3,5},{4,2},{5,3},{6,0},{7,1},{8,14},{9,15},{10,... | collective-permute-start | bytes 98312 | tf_op jit(solution)/shard_map/ppermute | solution.py:361
  45.0 1.9 %collective-permute-start.14 = (bf16[64,256]{1,0:T(8,128)(2,1)S(1)}, bf16[64,256]{1,0:T(8,128)(2,1)S(1)}, u32[]{:S(2)}, u32[]{:S(2)}) collective-permute-start(bf16[64,256]{1,0:T(8,128)(2,1)S(1)} %get-tuple-element.50), channel_id=1, source_target_pairs={{0,2},{1,3},{2,0},{3,1},{4,6},{5,7},{6,4},{7,5},{8,10},{9,11},{10,... | collective-permute-start | bytes 98312 | tf_op jit(solution)/shard_map/ppermute | solution.py:361
  46.9 1.4 %collective-permute-done.12 = bf16[64,256]{1,0:T(8,128)(2,1)S(1)} collective-permute-done((bf16[64,256]{1,0:T(8,128)(2,1)S(1)}, bf16[64,256]{1,0:T(8,128)(2,1)S(1)}, u32[]{:S(2)}, u32[]{:S(2)}) %collective-permute-start.12) | collective-permute-done | bytes 32800 | tf_op jit(solution)/shard_map/ppermute | solution.py:361
  48.2 1.6 %collective-permute-done.13 = bf16[64,256]{1,0:T(8,128)(2,1)S(1)} collective-permute-done((bf16[64,256]{1,0:T(8,128)(2,1)S(1)}, bf16[64,256]{1,0:T(8,128)(2,1)S(1)}, u32[]{:S(2)}, u32[]{:S(2)}) %collective-permute-start.13) | collective-permute-done | bytes 32800 | tf_op jit(solution)/shard_map/ppermute | solution.py:361
  49.8 0.6 %convert_add_fusion = f32[64,256]{1,0:T(8,128)} fusion(bf16[64,256]{1,0:T(8,128)(2,1)S(1)} %collective-permute-done.14, bf16[64,256]{1,0:T(8,128)(2,1)S(1)} %collective-permute-done.13, f32[64,256]{1,0:T(8,128)S(1)} %get-tuple-element.47, bf16[64,256]{1,0:T(8,128)(2,1)S(1)} %collective-permute-done.12), kind=kLoop, calls=%fused_computation | loop fusion | flops 98304 | bytes 229376 | tf_op jit(solution)/shard_map/add | solution.py:452
  (13 shorter events, 0.1 us)
Async XLA Ops:
  2.3 11.2 %copy-start = (s32[4,8]{1,0:T(4,128)S(1)}, s32[4,8]{1,0:T(4,128)}, u32[]{:S(2)}) copy-start(s32[4,8]{1,0:T(4,128)} %refs_0_.9) | copy-start | bytes 388
  2.3 22.8 %collective-permute-start = (bf16[2,256,512]{2,1,0:T(8,128)(2,1)S(1)}, bf16[2,256,512]{2,1,0:T(8,128)(2,1)S(1)}, u32[]{:S(2)}, u32[]{:S(2)}) collective-permute-start(bf16[2,256,512]{2,1,0:T(8,128)(2,1)S(1)} %get-tuple-element.29), channel_id=1, source_target_pairs={{0,16},{8,24},{16,0},{24,8},{1,17},{9,25},{17,1},{25,9},{2,18},{10... | collective-permute-start | bytes 1572872 | tf_op jit(solution)/shard_map/ppermute | solution.py:361
  5.3 5.7 %collective-permute-start.2 = (bf16[272,256]{1,0:T(8,128)(2,1)S(1)}, bf16[272,256]{1,0:T(8,128)(2,1)S(1)}, u32[]{:S(2)}, u32[]{:S(2)}) collective-permute-start(bf16[272,256]{1,0:T(8,128)(2,1)S(1)} %get-tuple-element.30.refs_1_), channel_id=1, source_target_pairs={{0,2},{1,3},{2,0},{3,1},{4,6},{5,7},{6,4},{7,5},{8,10},{9,11},{10,... | collective-permute-start | bytes 417800 | tf_op jit(solution)/shard_map/ppermute | solution.py:361
  6.9 6.6 %collective-permute-start.1 = (bf16[272,256]{1,0:T(8,128)(2,1)S(1)}, bf16[272,256]{1,0:T(8,128)(2,1)S(1)}, u32[]{:S(2)}, u32[]{:S(2)}) collective-permute-start(bf16[272,256]{1,0:T(8,128)(2,1)S(1)} %get-tuple-element.30.refs_1_), channel_id=1, source_target_pairs={{0,1},{1,0},{2,3},{3,2},{4,5},{5,4},{6,7},{7,6},{8,9},{9,8},{10,11... | collective-permute-start | bytes 417800 | tf_op jit(solution)/shard_map/ppermute | solution.py:361
  8.4 8.5 %collective-permute-start.4 = (bf16[272,256]{1,0:T(8,128)(2,1)S(1)}, bf16[272,256]{1,0:T(8,128)(2,1)S(1)}, u32[]{:S(2)}, u32[]{:S(2)}) collective-permute-start(bf16[272,256]{1,0:T(8,128)(2,1)S(1)} %get-tuple-element.30.refs_1_), channel_id=1, source_target_pairs={{0,4},{1,5},{2,6},{3,7},{4,0},{5,1},{6,2},{7,3},{8,12},{9,13},{10,... | collective-permute-start | bytes 417800 | tf_op jit(solution)/shard_map/ppermute | solution.py:361
  11.0 6.7 %collective-permute-start.3 = (bf16[272,256]{1,0:T(8,128)(2,1)S(1)}, bf16[272,256]{1,0:T(8,128)(2,1)S(1)}, u32[]{:S(2)}, u32[]{:S(2)}) collective-permute-start(bf16[272,256]{1,0:T(8,128)(2,1)S(1)} %collective-permute-done.2.refs_3_), channel_id=1, source_target_pairs={{0,1},{1,0},{2,3},{3,2},{4,5},{5,4},{6,7},{7,6},{8,9},{9,8},{10,11... | collective-permute-start | bytes 417800 | tf_op jit(solution)/shard_map/ppermute | solution.py:361
  16.9 5.1 %collective-permute-start.5 = (bf16[272,256]{1,0:T(8,128)(2,1)S(1)}, bf16[272,256]{1,0:T(8,128)(2,1)S(1)}, u32[]{:S(2)}, u32[]{:S(2)}) collective-permute-start(bf16[272,256]{1,0:T(8,128)(2,1)S(1)} %after.2), channel_id=1, source_target_pairs={{0,2},{1,3},{2,0},{3,1},{4,6},{5,7},{6,4},{7,5},{8,10},{9,11},{10,... | collective-permute-start | bytes 417800 | tf_op jit(solution)/shard_map/ppermute | solution.py:361
  16.9 6.9 %collective-permute-start.6 = (bf16[272,256]{1,0:T(8,128)(2,1)S(1)}, bf16[272,256]{1,0:T(8,128)(2,1)S(1)}, u32[]{:S(2)}, u32[]{:S(2)}) collective-permute-start(bf16[272,256]{1,0:T(8,128)(2,1)S(1)} %collective-permute-done.4.value_ref.refs_5_), channel_id=1, source_target_pairs={{0,1},{1,0},{2,3},{3,2},{4,5},{5,4},{6,7},{7,6},{8,9},{9,8},{10,11... | collective-permute-start | bytes 417800 | tf_op jit(solution)/shard_map/ppermute | solution.py:361
  22.0 5.1 %collective-permute-start.8 = (bf16[272,256]{1,0:T(8,128)(2,1)S(1)}, bf16[272,256]{1,0:T(8,128)(2,1)S(1)}, u32[]{:S(2)}, u32[]{:S(2)}) collective-permute-start(bf16[272,256]{1,0:T(8,128)(2,1)S(1)} %after.3), channel_id=1, source_target_pairs={{0,1},{1,0},{2,3},{3,2},{4,5},{5,4},{6,7},{7,6},{8,9},{9,8},{10,11... | collective-permute-start | bytes 417800 | tf_op jit(solution)/shard_map/ppermute | solution.py:361
  25.1 11.1 %collective-permute-start.7 = (bf16[2,256,512]{2,1,0:T(8,128)(2,1)S(1)}, bf16[2,256,512]{2,1,0:T(8,128)(2,1)S(1)}, u32[]{:S(2)}, u32[]{:S(2)}) collective-permute-start(bf16[2,256,512]{2,1,0:T(8,128)(2,1)S(1)} %pack.2), channel_id=1, source_target_pairs={{0,8},{8,0},{16,24},{24,16},{1,9},{9,1},{17,25},{25,17},{2,10},{10... | collective-permute-start | bytes 1572872 | tf_op jit(solution)/shard_map/ppermute | solution.py:361
  29.6 5.0 %collective-permute-start.9 = (bf16[1,256,256]{2,1,0:T(8,128)(2,1)S(1)}, bf16[1,256,256]{2,1,0:T(8,128)(2,1)S(1)}, u32[]{:S(2)}, u32[]{:S(2)}) collective-permute-start(bf16[1,256,256]{2,1,0:T(8,128)(2,1)S(1)} %group_grad.1.refs_0_.refs_3_), channel_id=1, source_target_pairs={{0,16},{8,24},{16,0},{24,8},{1,17},{9,25},{17,1},{25,9},{2,18},{10... | collective-permute-start | bytes 393224 | tf_op jit(solution)/shard_map/ppermute | solution.py:361
  34.7 1.6 %collective-permute-start.10 = (bf16[2,256,256]{2,1,0:T(8,128)(2,1)S(1)}, bf16[2,256,256]{2,1,0:T(8,128)(2,1)S(1)}, u32[]{:S(2)}, u32[]{:S(2)}) collective-permute-start(bf16[2,256,256]{2,1,0:T(8,128)(2,1)S(1)} %pack.3), channel_id=1, source_target_pairs={{0,8},{8,0},{16,24},{24,16},{1,9},{9,1},{17,25},{25,17},{2,10},{10... | collective-permute-start | bytes 786440 | tf_op jit(solution)/shard_map/ppermute | solution.py:361
  36.8 5.6 %collective-permute-start.11 = (bf16[4,64,256]{2,1,0:T(8,128)(2,1)S(1)}, bf16[4,64,256]{2,1,0:T(8,128)(2,1)S(1)}, u32[]{:S(2)}, u32[]{:S(2)}) collective-permute-start(bf16[4,64,256]{2,1,0:T(8,128)(2,1)S(1)} %get-tuple-element.46), channel_id=1, source_target_pairs={{0,1},{1,0},{2,3},{3,2},{4,5},{5,4},{6,7},{7,6},{8,9},{9,8},{10,11... | collective-permute-start | bytes 393224 | tf_op jit(solution)/shard_map/ppermute | solution.py:361
  42.4 5.8 %collective-permute-start.12 = (bf16[64,256]{1,0:T(8,128)(2,1)S(1)}, bf16[64,256]{1,0:T(8,128)(2,1)S(1)}, u32[]{:S(2)}, u32[]{:S(2)}) collective-permute-start(bf16[64,256]{1,0:T(8,128)(2,1)S(1)} %get-tuple-element.48), channel_id=1, source_target_pairs={{0,6},{1,7},{2,4},{3,5},{4,2},{5,3},{6,0},{7,1},{8,14},{9,15},{10,... | collective-permute-start | bytes 98312 | tf_op jit(solution)/shard_map/ppermute | solution.py:361
  45.0 4.8 %collective-permute-start.13 = (bf16[64,256]{1,0:T(8,128)(2,1)S(1)}, bf16[64,256]{1,0:T(8,128)(2,1)S(1)}, u32[]{:S(2)}, u32[]{:S(2)}) collective-permute-start(bf16[64,256]{1,0:T(8,128)(2,1)S(1)} %get-tuple-element.49), channel_id=1, source_target_pairs={{0,4},{1,5},{2,6},{3,7},{4,0},{5,1},{6,2},{7,3},{8,12},{9,13},{10,... | collective-permute-start | bytes 98312 | tf_op jit(solution)/shard_map/ppermute | solution.py:361
  45.0 4.8 %collective-permute-start.14 = (bf16[64,256]{1,0:T(8,128)(2,1)S(1)}, bf16[64,256]{1,0:T(8,128)(2,1)S(1)}, u32[]{:S(2)}, u32[]{:S(2)}) collective-permute-start(bf16[64,256]{1,0:T(8,128)(2,1)S(1)} %get-tuple-element.50), channel_id=1, source_target_pairs={{0,2},{1,3},{2,0},{3,1},{4,6},{5,7},{6,4},{7,5},{8,10},{9,11},{10,... | collective-permute-start | bytes 98312 | tf_op jit(solution)/shard_map/ppermute | solution.py:361

commit v8 on v7

--- a/solution.py
+++ b/solution.py
@@ -382,24 +382,27 @@
     minor = 1 << ((members.bit_length() - 1) // 2)
     msg, normed, inv, near_cuts, far_cuts = project(feats, tower_w, partners[None, :], popularity_buckets[None, :], parts)
 
-    came = swap(far_cuts, "dp", parts // 2)
-
+    majors = list(range(0, members, minor))
+    last = members // 2
     msgs = {0: msg}
+    msgs[last] = swap(msg, "pool", last)
+    for k in majors[1:]:
+        if k < last:
+            msgs[k] = swap(msg, "pool", k)
     for near in range(1, minor):
         msgs[near] = swap(msg, "pool", near)
-    bits = []
-    bit = minor
-    while bit < members:
-        bits.append(bit)
-        msgs[bit] = swap(msg, "pool", bit)
-        bit *= 2
-    first = bits[0]
+    for far in majors[1:-2]:
+        for near in range(1, minor):
+            msgs[far + near] = swap(msgs[far], "pool", near)
+    relayed = msgs[last]
+    for k in majors:
+        if k > last:
+            msgs[k] = swap(relayed, "pool", k ^ last)
     for near in range(1, minor):
-        msgs[first + near] = swap(msgs[first], "pool", near)
-    majors = list(range(0, members, minor))
-    early = [far + near for far in majors[:-2] for near in range(minor)]
-    held = early[1 - minor:]
-    early = early[:1 - minor]
+        msgs[last + near] = swap(msgs[last], "pool", near)
+
+    came = swap(far_cuts, "dp", parts // 2)
+
     state, kept, stages = (), [], []
 
     def add(fresh):
@@ -408,22 +411,13 @@
         kept.append(powers)
         stages.append(fresh)
 
-    add(early)
-    last = bits[-1]
-    for k in range(first + minor, last, minor):
-        msgs[k] = swap(msgs[first], "pool", k ^ first)
-    relayed = after(msgs[last], state[1])
-    for k in range(last + minor, members, minor):
-        msgs[k] = swap(relayed, "pool", k ^ last)
-    for far in majors[2:-1]:
-        for near in range(1, minor):
-            msgs[far + near] = swap(msgs[far], "pool", near)
-    add(held + majors[2:-1])
-    relayed = after(msgs[majors[-1]], state[1])
+    add(majors[:-1] + list(range(1, minor)))
+    add([far + near for far in majors[1:-2] for near in range(1, minor)])
+    msgs3 = after(msgs[majors[-1]], state[1])
     for near in range(1, minor):
-        msgs[majors[-1] + near] = swap(relayed, "pool", near)
+        msgs[majors[-1] + near] = swap(msgs3, "pool", near)
     add([majors[-1]])
-    add([far + near for far in majors[2:-1] for near in range(1, minor)])
+    add([majors[-2] + near for near in range(1, minor)])
     bit = parts // 2
     blocks = {k: [(0, near_cuts, k), (bit, came, k)] for k in range(bit)}
     bit //= 2
@@ -434,9 +428,9 @@
         for at, (k, source, _, _) in enumerate(moving):
             blocks[k].append((source, passed, at))
         bit //= 2
-    grad_proj = group_grad(
-        stages, [majors[-1] + near for near in range(1, minor)], row_counts, msgs, state, kept, [], normed, inv
-    )
+
+    final = [majors[-1] + near for near in range(1, minor)]
+    grad_proj = group_grad(stages, final, row_counts, msgs, state, kept, [], normed, inv)
 
     bit = parts // 2
     grads = [(0, grad_proj, 0)]

time: 50.6 us -> 49.3 us (0.974)
  waiting for transfers between devices: 20.9 us -> 17.9 us
  starting transfers between devices: 18.5 us -> 20.3 us
    ppermute x15, waiting for transfers between devices: 20.9 us -> 17.9 us  [swap(): return lax.ppermute(value, axis, [(at, at ^ flip) for at in range(size)])]
    ppermute x15, starting transfers between devices: 18.5 us -> 20.3 us  [swap(): return lax.ppermute(value, axis, [(at, at ^ flip) for at in range(size)])]
  transfers between devices with their start and end apart: 15 -> 15, of which waited for: 8 -> 9; matrix products, arithmetic and copies ran while one was open for 0% -> 0% of each run, Pallas kernels for 15% -> 15%
where the time goes in v8:
time: 49.3 us; the launch traced here: 49.2 us
  starting transfers between devices  20.3 us (41%)
  waiting for transfers between devices  17.9 us (36%)
  Pallas kernels  10.2 us (21%)
  other arithmetic  0.65 us (1%)
    ppermute x15, starting transfers between devices, swap(): return lax.ppermute(value, axis, [(at, at ^ flip) for at in range(size)])  20.3 us
    ppermute x15, waiting for transfers between devices, swap(): return lax.ppermute(value, axis, [(at, at ^ flip) for at in range(size)])  17.9 us
    pallas_call x4, Pallas kernels, add_pairs(): pl.pallas_call(functools.partial(pairs_kernel, seen, fresh), out_shape=(j...  4.9 us
    pallas_call x1, Pallas kernels, group_grad(): pl.pallas_call(functools.partial(grad_kernel, stages, fresh), out_shape=j...  2.47 us
    pallas_call x1, Pallas kernels, project(): pl.pallas_call(functools.partial(project_kernel, parts), out_shape=(jax.S...  2.27 us
  transfers between devices with their start and end apart: 15, of which 9 were waited for; matrix products, arithmetic and copies ran while one was open for 0% of the time, Pallas kernels for 15%

profile of v8, /device:TPU:0, one launch (start us, length us, event | category | flops | bytes accessed | tf_op | source)
XLA Modules:
  0.0 49.2 jit_solution(5444455855366588146)
XLA Ops:
  0.0 2.3 %project.1 = (bf16[272,256]{1,0:T(8,128)(2,1)S(1)}, f32[256,256]{1,0:T(8,128)S(1)}, f32[256,128]{1,0:T(8,128)S(1)}, bf16[2,256,512]{2,1,0:T(8,128)(2,1)S(1)}, bf16[2,256,512]{2,1,0:T(8,128)(2,1)S(1)}) custom-call(bf16[256,2048]{1,0:T(8,128)(2,1)} %feats_hbm.1, bf16[2048,256]{1,0:T(8,128)(2,1)} %w_hbm.1, s32[1,256]{1,0:T(1,128)} %bitcast.2, s32[1,256]{1,0:T(1,128)} %bitcast.3), custom_call_target="tpu_custom_call" | custom-call | flops 268435456 | bytes 2097152 | tf_op jit(solution)/shard_map/project/pallas_call | solution.py:81
  2.3 3.0 %collective-permute-start = (bf16[2,256,512]{2,1,0:T(8,128)(2,1)S(1)}, bf16[2,256,512]{2,1,0:T(8,128)(2,1)S(1)}, u32[]{:S(2)}, u32[]{:S(2)}) collective-permute-start(bf16[2,256,512]{2,1,0:T(8,128)(2,1)S(1)} %get-tuple-element.29), channel_id=1, source_target_pairs={{0,16},{8,24},{16,0},{24,8},{1,17},{9,25},{17,1},{25,9},{2,18},{10... | collective-permute-start | bytes 1572872 | tf_op jit(solution)/shard_map/ppermute | solution.py:361
  5.3 1.6 %collective-permute-start.1 = (bf16[272,256]{1,0:T(8,128)(2,1)S(1)}, bf16[272,256]{1,0:T(8,128)(2,1)S(1)}, u32[]{:S(2)}, u32[]{:S(2)}) collective-permute-start(bf16[272,256]{1,0:T(8,128)(2,1)S(1)} %get-tuple-element.30.refs_1_), channel_id=1, source_target_pairs={{0,2},{1,3},{2,0},{3,1},{4,6},{5,7},{6,4},{7,5},{8,10},{9,11},{10,... | collective-permute-start | bytes 417800 | tf_op jit(solution)/shard_map/ppermute | solution.py:361
  6.9 2.6 %collective-permute-start.2 = (bf16[272,256]{1,0:T(8,128)(2,1)S(1)}, bf16[272,256]{1,0:T(8,128)(2,1)S(1)}, u32[]{:S(2)}, u32[]{:S(2)}) collective-permute-start(bf16[272,256]{1,0:T(8,128)(2,1)S(1)} %get-tuple-element.30.refs_1_), channel_id=1, source_target_pairs={{0,4},{1,5},{2,6},{3,7},{4,0},{5,1},{6,2},{7,3},{8,12},{9,13},{10,... | collective-permute-start | bytes 417800 | tf_op jit(solution)/shard_map/ppermute | solution.py:361
  9.5 1.5 %collective-permute-start.3 = (bf16[272,256]{1,0:T(8,128)(2,1)S(1)}, bf16[272,256]{1,0:T(8,128)(2,1)S(1)}, u32[]{:S(2)}, u32[]{:S(2)}) collective-permute-start(bf16[272,256]{1,0:T(8,128)(2,1)S(1)} %get-tuple-element.30.refs_1_), channel_id=1, source_target_pairs={{0,1},{1,0},{2,3},{3,2},{4,5},{5,4},{6,7},{7,6},{8,9},{9,8},{10,11... | collective-permute-start | bytes 417800 | tf_op jit(solution)/shard_map/ppermute | solution.py:361
  11.0 1.5 %collective-permute-done.1.refs_2_ = bf16[272,256]{1,0:T(8,128)(2,1)S(1)} collective-permute-done((bf16[272,256]{1,0:T(8,128)(2,1)S(1)}, bf16[272,256]{1,0:T(8,128)(2,1)S(1)}, u32[]{:S(2)}, u32[]{:S(2)}) %collective-permute-start.1) | collective-permute-done | bytes 139296 | tf_op jit(solution)/shard_map/ppermute | solution.py:361
  12.5 1.5 %collective-permute-start.4 = (bf16[272,256]{1,0:T(8,128)(2,1)S(1)}, bf16[272,256]{1,0:T(8,128)(2,1)S(1)}, u32[]{:S(2)}, u32[]{:S(2)}) collective-permute-start(bf16[272,256]{1,0:T(8,128)(2,1)S(1)} %collective-permute-done.1.refs_2_), channel_id=1, source_target_pairs={{0,1},{1,0},{2,3},{3,2},{4,5},{5,4},{6,7},{7,6},{8,9},{9,8},{10,11... | collective-permute-start | bytes 417800 | tf_op jit(solution)/shard_map/ppermute | solution.py:361
  14.0 1.8 %collective-permute-done.2.refs_3_ = bf16[272,256]{1,0:T(8,128)(2,1)S(1)} collective-permute-done((bf16[272,256]{1,0:T(8,128)(2,1)S(1)}, bf16[272,256]{1,0:T(8,128)(2,1)S(1)}, u32[]{:S(2)}, u32[]{:S(2)}) %collective-permute-start.2) | collective-permute-done | bytes 139296 | tf_op jit(solution)/shard_map/ppermute | solution.py:361
  15.8 0.3 collective-permute-start.5
  16.1 1.5 %collective-permute-start.6 = (bf16[272,256]{1,0:T(8,128)(2,1)S(1)}, bf16[272,256]{1,0:T(8,128)(2,1)S(1)}, u32[]{:S(2)}, u32[]{:S(2)}) collective-permute-start(bf16[272,256]{1,0:T(8,128)(2,1)S(1)} %collective-permute-done.2.refs_3_), channel_id=1, source_target_pairs={{0,1},{1,0},{2,3},{3,2},{4,5},{5,4},{6,7},{7,6},{8,9},{9,8},{10,11... | collective-permute-start | bytes 417800 | tf_op jit(solution)/shard_map/ppermute | solution.py:361
  17.6 1.4 %add_pairs.4 = (f32[4,256]{1,0:T(4,128)S(1)}, f32[256,128]{1,0:T(8,128)S(1)}, f32[4,256,256]{2,1,0:T(8,128)S(1)}) custom-call(s32[4,8]{1,0:T(4,128)S(1)} %copy-done, bf16[272,256]{1,0:T(8,128)(2,1)S(1)} %get-tuple-element.30.refs_1_, bf16[272,256]{1,0:T(8,128)(2,1)S(1)} %collective-permute-done.1.refs_2_, ...), custom_call_target="tpu_custom_call" | custom-call | flops 335544320 | bytes 1572864 | tf_op jit(solution)/shard_map/add_pairs/pallas_call | solution.py:195
  19.0 1.1 %add_pairs.5 = (f32[5,256]{1,0:T(8,128)S(1)}, f32[256,128]{1,0:T(8,128)S(1)}, f32[1,256,256]{2,1,0:T(8,128)S(1)}) custom-call(s32[4,8]{1,0:T(4,128)S(1)} %copy-done, bf16[272,256]{1,0:T(8,128)(2,1)S(1)} %get-tuple-element.30.refs_1_, bf16[272,256]{1,0:T(8,128)(2,1)S(1)} %collective-permute-done.1.refs_2_, ...), custom_call_target="tpu_custom_call" | custom-call | flops 167772160 | bytes 917504 | tf_op jit(solution)/shard_map/add_pairs/pallas_call | solution.py:195
  20.1 0.7 %collective-permute-done.5.refs_6_.value_ref = bf16[272,256]{1,0:T(8,128)(2,1)S(1)} collective-permute-done((bf16[272,256]{1,0:T(8,128)(2,1)S(1)}, bf16[272,256]{1,0:T(8,128)(2,1)S(1)}, u32[]{:S(2)}, u32[]{:S(2)}) %collective-permute-start.5) | collective-permute-done | bytes 139296 | tf_op jit(solution)/shard_map/ppermute | solution.py:361
  20.9 1.6 %collective-permute-start.8 = (bf16[272,256]{1,0:T(8,128)(2,1)S(1)}, bf16[272,256]{1,0:T(8,128)(2,1)S(1)}, u32[]{:S(2)}, u32[]{:S(2)}) collective-permute-start(bf16[272,256]{1,0:T(8,128)(2,1)S(1)} %after.1), channel_id=1, source_target_pairs={{0,1},{1,0},{2,3},{3,2},{4,5},{5,4},{6,7},{7,6},{8,9},{9,8},{10,11... | collective-permute-start | bytes 417800 | tf_op jit(solution)/shard_map/ppermute | solution.py:361
  22.4 1.2 %add_pairs.6 = (f32[6,256]{1,0:T(8,128)S(1)}, f32[256,128]{1,0:T(8,128)S(1)}, f32[1,256,256]{2,1,0:T(8,128)S(1)}) custom-call(s32[4,8]{1,0:T(4,128)S(1)} %copy-done, bf16[272,256]{1,0:T(8,128)(2,1)S(1)} %get-tuple-element.30.refs_1_, bf16[272,256]{1,0:T(8,128)(2,1)S(1)} %collective-permute-done.1.refs_2_, ...), custom_call_target="tpu_custom_call" | custom-call | flops 201326592 | bytes 1048576 | tf_op jit(solution)/shard_map/add_pairs/pallas_call | solution.py:195
  23.6 1.2 %add_pairs.7 = (f32[7,256]{1,0:T(8,128)S(1)}, f32[256,128]{1,0:T(8,128)S(1)}, f32[1,256,256]{2,1,0:T(8,128)S(1)}) custom-call(s32[4,8]{1,0:T(4,128)S(1)} %copy-done, bf16[272,256]{1,0:T(8,128)(2,1)S(1)} %get-tuple-element.30.refs_1_, bf16[272,256]{1,0:T(8,128)(2,1)S(1)} %collective-permute-done.1.refs_2_, ...), custom_call_target="tpu_custom_call" | custom-call | flops 234881024 | bytes 1179648 | tf_op jit(solution)/shard_map/add_pairs/pallas_call | solution.py:195
  24.9 0.1 collective-permute-start.7
  25.0 1.0 %collective-permute-done.8.refs_8_ = bf16[272,256]{1,0:T(8,128)(2,1)S(1)} collective-permute-done((bf16[272,256]{1,0:T(8,128)(2,1)S(1)}, bf16[272,256]{1,0:T(8,128)(2,1)S(1)}, u32[]{:S(2)}, u32[]{:S(2)}) %collective-permute-start.8) | collective-permute-done | bytes 139296 | tf_op jit(solution)/shard_map/ppermute | solution.py:361
  26.0 2.5 %group_grad.1.refs_0_.refs_3_ = bf16[1,256,256]{2,1,0:T(8,128)(2,1)S(1)} custom-call(s32[4,8]{1,0:T(4,128)S(1)} %copy-done, bf16[272,256]{1,0:T(8,128)(2,1)S(1)} %get-tuple-element.30.refs_1_, bf16[272,256]{1,0:T(8,128)(2,1)S(1)} %collective-permute-done.1.refs_2_, bf16[272,256]{1,0:T(8,128)(2,1)S(1)} %collective-permute-done.2.refs_3_, ...), custom_call_target="tpu_custom_call" | custom-call | flops 268435456 | bytes 1310720 | tf_op jit(solution)/shard_map/group_grad/pallas_call | solution.py:260
  28.5 0.6 %collective-permute-start.9 = (bf16[1,256,256]{2,1,0:T(8,128)(2,1)S(1)}, bf16[1,256,256]{2,1,0:T(8,128)(2,1)S(1)}, u32[]{:S(2)}, u32[]{:S(2)}) collective-permute-start(bf16[1,256,256]{2,1,0:T(8,128)(2,1)S(1)} %group_grad.1.refs_0_.refs_3_), channel_id=1, source_target_pairs={{0,16},{8,24},{16,0},{24,8},{1,17},{9,25},{17,1},{25,9},{2,18},{10... | collective-permute-start | bytes 393224 | tf_op jit(solution)/shard_map/ppermute | solution.py:361
  29.0 4.5 %collective-permute-done.9.refs_1_.refs_5_ = bf16[1,256,256]{2,1,0:T(8,128)(2,1)S(1)} collective-permute-done((bf16[1,256,256]{2,1,0:T(8,128)(2,1)S(1)}, bf16[1,256,256]{2,1,0:T(8,128)(2,1)S(1)}, u32[]{:S(2)}, u32[]{:S(2)}) %collective-permute-start.9) | collective-permute-done | bytes 131104 | tf_op jit(solution)/shard_map/ppermute | solution.py:361
  33.5 0.1 collective-permute-start.10
  33.6 1.5 %collective-permute-done.10.refs_4_ = bf16[2,256,256]{2,1,0:T(8,128)(2,1)S(1)} collective-permute-done((bf16[2,256,256]{2,1,0:T(8,128)(2,1)S(1)}, bf16[2,256,256]{2,1,0:T(8,128)(2,1)S(1)}, u32[]{:S(2)}, u32[]{:S(2)}) %collective-permute-start.10) | collective-permute-done | bytes 262176 | tf_op jit(solution)/shard_map/ppermute | solution.py:361
  35.1 0.5 %weight_grad.1 = (f32[4,64,256]{2,1,0:T(8,128)S(1)}, bf16[4,64,256]{2,1,0:T(8,128)(2,1)S(1)}) custom-call(bf16[2,256,512]{2,1,0:T(8,128)(2,1)S(1)} %get-tuple-element.28.refs_0_, bf16[2,256,512]{2,1,0:T(8,128)(2,1)S(1)} %collective-permute-done.7.refs_1_, bf16[2,256,512]{2,1,0:T(8,128)(2,1)S(1)} %collective-permute-done.refs_1_.refs_2_, ...), custom_call_target="tpu_custom_call" | custom-call | flops 268435456 | bytes 1048576 | tf_op jit(solution)/shard_map/weight_grad/pallas_call | solution.py:322
  35.6 1.6 %collective-permute-start.11 = (bf16[4,64,256]{2,1,0:T(8,128)(2,1)S(1)}, bf16[4,64,256]{2,1,0:T(8,128)(2,1)S(1)}, u32[]{:S(2)}, u32[]{:S(2)}) collective-permute-start(bf16[4,64,256]{2,1,0:T(8,128)(2,1)S(1)} %get-tuple-element.46), channel_id=1, source_target_pairs={{0,1},{1,0},{2,3},{3,2},{4,5},{5,4},{6,7},{7,6},{8,9},{9,8},{10,11... | collective-permute-start | bytes 393224 | tf_op jit(solution)/shard_map/ppermute | solution.py:361
  37.2 4.0 %collective-permute-done.11.refs_0_ = bf16[4,64,256]{2,1,0:T(8,128)(2,1)S(1)} collective-permute-done((bf16[4,64,256]{2,1,0:T(8,128)(2,1)S(1)}, bf16[4,64,256]{2,1,0:T(8,128)(2,1)S(1)}, u32[]{:S(2)}, u32[]{:S(2)}) %collective-permute-start.11) | collective-permute-done | bytes 131104 | tf_op jit(solution)/shard_map/ppermute | solution.py:361
  41.3 2.4 %collective-permute-start.12 = (bf16[64,256]{1,0:T(8,128)(2,1)S(1)}, bf16[64,256]{1,0:T(8,128)(2,1)S(1)}, u32[]{:S(2)}, u32[]{:S(2)}) collective-permute-start(bf16[64,256]{1,0:T(8,128)(2,1)S(1)} %get-tuple-element.48), channel_id=1, source_target_pairs={{0,6},{1,7},{2,4},{3,5},{4,2},{5,3},{6,0},{7,1},{8,14},{9,15},{10,... | collective-permute-start | bytes 98312 | tf_op jit(solution)/shard_map/ppermute | solution.py:361
  43.7 0.1 collective-permute-start.13
  43.8 1.9 %collective-permute-start.14 = (bf16[64,256]{1,0:T(8,128)(2,1)S(1)}, bf16[64,256]{1,0:T(8,128)(2,1)S(1)}, u32[]{:S(2)}, u32[]{:S(2)}) collective-permute-start(bf16[64,256]{1,0:T(8,128)(2,1)S(1)} %get-tuple-element.50), channel_id=1, source_target_pairs={{0,2},{1,3},{2,0},{3,1},{4,6},{5,7},{6,4},{7,5},{8,10},{9,11},{10,... | collective-permute-start | bytes 98312 | tf_op jit(solution)/shard_map/ppermute | solution.py:361
  45.7 1.3 %collective-permute-done.12 = bf16[64,256]{1,0:T(8,128)(2,1)S(1)} collective-permute-done((bf16[64,256]{1,0:T(8,128)(2,1)S(1)}, bf16[64,256]{1,0:T(8,128)(2,1)S(1)}, u32[]{:S(2)}, u32[]{:S(2)}) %collective-permute-start.12) | collective-permute-done | bytes 32800 | tf_op jit(solution)/shard_map/ppermute | solution.py:361
  47.1 1.5 %collective-permute-done.13 = bf16[64,256]{1,0:T(8,128)(2,1)S(1)} collective-permute-done((bf16[64,256]{1,0:T(8,128)(2,1)S(1)}, bf16[64,256]{1,0:T(8,128)(2,1)S(1)}, u32[]{:S(2)}, u32[]{:S(2)}) %collective-permute-start.13) | collective-permute-done | bytes 32800 | tf_op jit(solution)/shard_map/ppermute | solution.py:361
  48.5 0.6 %convert_add_fusion = f32[64,256]{1,0:T(8,128)} fusion(bf16[64,256]{1,0:T(8,128)(2,1)S(1)} %collective-permute-done.14, bf16[64,256]{1,0:T(8,128)(2,1)S(1)} %collective-permute-done.13, f32[64,256]{1,0:T(8,128)S(1)} %get-tuple-element.47, bf16[64,256]{1,0:T(8,128)(2,1)S(1)} %collective-permute-done.12), kind=kLoop, calls=%fused_computation | loop fusion | flops 98304 | bytes 229376 | tf_op jit(solution)/shard_map/add | solution.py:446
  (12 shorter events, 0.1 us)
Async XLA Ops:
  2.3 15.4 %copy-start = (s32[4,8]{1,0:T(4,128)S(1)}, s32[4,8]{1,0:T(4,128)}, u32[]{:S(2)}) copy-start(s32[4,8]{1,0:T(4,128)} %refs_0_.9) | copy-start | bytes 388
  2.3 22.5 %collective-permute-start = (bf16[2,256,512]{2,1,0:T(8,128)(2,1)S(1)}, bf16[2,256,512]{2,1,0:T(8,128)(2,1)S(1)}, u32[]{:S(2)}, u32[]{:S(2)}) collective-permute-start(bf16[2,256,512]{2,1,0:T(8,128)(2,1)S(1)} %get-tuple-element.29), channel_id=1, source_target_pairs={{0,16},{8,24},{16,0},{24,8},{1,17},{9,25},{17,1},{25,9},{2,18},{10... | collective-permute-start | bytes 1572872 | tf_op jit(solution)/shard_map/ppermute | solution.py:361
  5.3 7.2 %collective-permute-start.1 = (bf16[272,256]{1,0:T(8,128)(2,1)S(1)}, bf16[272,256]{1,0:T(8,128)(2,1)S(1)}, u32[]{:S(2)}, u32[]{:S(2)}) collective-permute-start(bf16[272,256]{1,0:T(8,128)(2,1)S(1)} %get-tuple-element.30.refs_1_), channel_id=1, source_target_pairs={{0,2},{1,3},{2,0},{3,1},{4,6},{5,7},{6,4},{7,5},{8,10},{9,11},{10,... | collective-permute-start | bytes 417800 | tf_op jit(solution)/shard_map/ppermute | solution.py:361
  6.9 8.9 %collective-permute-start.2 = (bf16[272,256]{1,0:T(8,128)(2,1)S(1)}, bf16[272,256]{1,0:T(8,128)(2,1)S(1)}, u32[]{:S(2)}, u32[]{:S(2)}) collective-permute-start(bf16[272,256]{1,0:T(8,128)(2,1)S(1)} %get-tuple-element.30.refs_1_), channel_id=1, source_target_pairs={{0,4},{1,5},{2,6},{3,7},{4,0},{5,1},{6,2},{7,3},{8,12},{9,13},{10,... | collective-permute-start | bytes 417800 | tf_op jit(solution)/shard_map/ppermute | solution.py:361
  9.5 8.1 %collective-permute-start.3 = (bf16[272,256]{1,0:T(8,128)(2,1)S(1)}, bf16[272,256]{1,0:T(8,128)(2,1)S(1)}, u32[]{:S(2)}, u32[]{:S(2)}) collective-permute-start(bf16[272,256]{1,0:T(8,128)(2,1)S(1)} %get-tuple-element.30.refs_1_), channel_id=1, source_target_pairs={{0,1},{1,0},{2,3},{3,2},{4,5},{5,4},{6,7},{7,6},{8,9},{9,8},{10,11... | collective-permute-start | bytes 417800 | tf_op jit(solution)/shard_map/ppermute | solution.py:361
  12.5 6.5 %collective-permute-start.4 = (bf16[272,256]{1,0:T(8,128)(2,1)S(1)}, bf16[272,256]{1,0:T(8,128)(2,1)S(1)}, u32[]{:S(2)}, u32[]{:S(2)}) collective-permute-start(bf16[272,256]{1,0:T(8,128)(2,1)S(1)} %collective-permute-done.1.refs_2_), channel_id=1, source_target_pairs={{0,1},{1,0},{2,3},{3,2},{4,5},{5,4},{6,7},{7,6},{8,9},{9,8},{10,11... | collective-permute-start | bytes 417800 | tf_op jit(solution)/shard_map/ppermute | solution.py:361
  15.8 5.1 %collective-permute-start.5 = (bf16[272,256]{1,0:T(8,128)(2,1)S(1)}, bf16[272,256]{1,0:T(8,128)(2,1)S(1)}, u32[]{:S(2)}, u32[]{:S(2)}) collective-permute-start(bf16[272,256]{1,0:T(8,128)(2,1)S(1)} %collective-permute-done.2.refs_3_), channel_id=1, source_target_pairs={{0,2},{1,3},{2,0},{3,1},{4,6},{5,7},{6,4},{7,5},{8,10},{9,11},{10,... | collective-permute-start | bytes 417800 | tf_op jit(solution)/shard_map/ppermute | solution.py:361
  16.1 7.5 %collective-permute-start.6 = (bf16[272,256]{1,0:T(8,128)(2,1)S(1)}, bf16[272,256]{1,0:T(8,128)(2,1)S(1)}, u32[]{:S(2)}, u32[]{:S(2)}) collective-permute-start(bf16[272,256]{1,0:T(8,128)(2,1)S(1)} %collective-permute-done.2.refs_3_), channel_id=1, source_target_pairs={{0,1},{1,0},{2,3},{3,2},{4,5},{5,4},{6,7},{7,6},{8,9},{9,8},{10,11... | collective-permute-start | bytes 417800 | tf_op jit(solution)/shard_map/ppermute | solution.py:361
  20.9 5.1 %collective-permute-start.8 = (bf16[272,256]{1,0:T(8,128)(2,1)S(1)}, bf16[272,256]{1,0:T(8,128)(2,1)S(1)}, u32[]{:S(2)}, u32[]{:S(2)}) collective-permute-start(bf16[272,256]{1,0:T(8,128)(2,1)S(1)} %after.1), channel_id=1, source_target_pairs={{0,1},{1,0},{2,3},{3,2},{4,5},{5,4},{6,7},{7,6},{8,9},{9,8},{10,11... | collective-permute-start | bytes 417800 | tf_op jit(solution)/shard_map/ppermute | solution.py:361
  24.9 10.2 %collective-permute-start.7 = (bf16[2,256,512]{2,1,0:T(8,128)(2,1)S(1)}, bf16[2,256,512]{2,1,0:T(8,128)(2,1)S(1)}, u32[]{:S(2)}, u32[]{:S(2)}) collective-permute-start(bf16[2,256,512]{2,1,0:T(8,128)(2,1)S(1)} %pack.2), channel_id=1, source_target_pairs={{0,8},{8,0},{16,24},{24,16},{1,9},{9,1},{17,25},{25,17},{2,10},{10... | collective-permute-start | bytes 1572872 | tf_op jit(solution)/shard_map/ppermute | solution.py:361
  28.5 5.0 %collective-permute-start.9 = (bf16[1,256,256]{2,1,0:T(8,128)(2,1)S(1)}, bf16[1,256,256]{2,1,0:T(8,128)(2,1)S(1)}, u32[]{:S(2)}, u32[]{:S(2)}) collective-permute-start(bf16[1,256,256]{2,1,0:T(8,128)(2,1)S(1)} %group_grad.1.refs_0_.refs_3_), channel_id=1, source_target_pairs={{0,16},{8,24},{16,0},{24,8},{1,17},{9,25},{17,1},{25,9},{2,18},{10... | collective-permute-start | bytes 393224 | tf_op jit(solution)/shard_map/ppermute | solution.py:361
  33.5 1.6 %collective-permute-start.10 = (bf16[2,256,256]{2,1,0:T(8,128)(2,1)S(1)}, bf16[2,256,256]{2,1,0:T(8,128)(2,1)S(1)}, u32[]{:S(2)}, u32[]{:S(2)}) collective-permute-start(bf16[2,256,256]{2,1,0:T(8,128)(2,1)S(1)} %pack.3), channel_id=1, source_target_pairs={{0,8},{8,0},{16,24},{24,16},{1,9},{9,1},{17,25},{25,17},{2,10},{10... | collective-permute-start | bytes 786440 | tf_op jit(solution)/shard_map/ppermute | solution.py:361
  35.6 5.6 %collective-permute-start.11 = (bf16[4,64,256]{2,1,0:T(8,128)(2,1)S(1)}, bf16[4,64,256]{2,1,0:T(8,128)(2,1)S(1)}, u32[]{:S(2)}, u32[]{:S(2)}) collective-permute-start(bf16[4,64,256]{2,1,0:T(8,128)(2,1)S(1)} %get-tuple-element.46), channel_id=1, source_target_pairs={{0,1},{1,0},{2,3},{3,2},{4,5},{5,4},{6,7},{7,6},{8,9},{9,8},{10,11... | collective-permute-start | bytes 393224 | tf_op jit(solution)/shard_map/ppermute | solution.py:361
  41.3 5.8 %collective-permute-start.12 = (bf16[64,256]{1,0:T(8,128)(2,1)S(1)}, bf16[64,256]{1,0:T(8,128)(2,1)S(1)}, u32[]{:S(2)}, u32[]{:S(2)}) collective-permute-start(bf16[64,256]{1,0:T(8,128)(2,1)S(1)} %get-tuple-element.48), channel_id=1, source_target_pairs={{0,6},{1,7},{2,4},{3,5},{4,2},{5,3},{6,0},{7,1},{8,14},{9,15},{10,... | collective-permute-start | bytes 98312 | tf_op jit(solution)/shard_map/ppermute | solution.py:361
  43.7 4.8 %collective-permute-start.13 = (bf16[64,256]{1,0:T(8,128)(2,1)S(1)}, bf16[64,256]{1,0:T(8,128)(2,1)S(1)}, u32[]{:S(2)}, u32[]{:S(2)}) collective-permute-start(bf16[64,256]{1,0:T(8,128)(2,1)S(1)} %get-tuple-element.49), channel_id=1, source_target_pairs={{0,4},{1,5},{2,6},{3,7},{4,0},{5,1},{6,2},{7,3},{8,12},{9,13},{10,... | collective-permute-start | bytes 98312 | tf_op jit(solution)/shard_map/ppermute | solution.py:361
  43.8 4.7 %collective-permute-start.14 = (bf16[64,256]{1,0:T(8,128)(2,1)S(1)}, bf16[64,256]{1,0:T(8,128)(2,1)S(1)}, u32[]{:S(2)}, u32[]{:S(2)}) collective-permute-start(bf16[64,256]{1,0:T(8,128)(2,1)S(1)} %get-tuple-element.50), channel_id=1, source_target_pairs={{0,2},{1,3},{2,0},{3,1},{4,6},{5,7},{6,4},{7,5},{8,10},{9,11},{10,... | collective-permute-start | bytes 98312 | tf_op jit(solution)/shard_map/ppermute | solution.py:361

commit v9 on v8

--- a/solution.py
+++ b/solution.py
@@ -298,16 +298,17 @@
 
 def weight_kernel(places, minor, inputs, *refs):
     arrays, outs, total = refs[:inputs], refs[inputs:-1], refs[-1]
-    majors, piece, _ = outs[0].shape
+    half, piece, _ = outs[0].shape
     me = lax.axis_index("pool")
     result = None
     for array, row, grad_array, grad_row in places:
         term = f32_dot(arrays[array][row], arrays[grad_array][grad_row], ((0,), (0,)))
         result = term if result is None else result + term
     total[...] = result
-    for near, out in enumerate(outs):
-        for far in range(majors):
-            first = pl.multiple_of((me ^ (far * minor + near)) * piece, piece)
+    for at, out in enumerate(outs):
+        near, start = at // 2, half * (1 - at % 2)
+        for far in range(half):
+            first = pl.multiple_of((me ^ ((start + far) * minor + near)) * piece, piece)
             out[far] = total[pl.ds(first, piece), :].astype(out.dtype)
 
 
@@ -318,13 +319,13 @@
     places = [(which[at], blocks[at][2], which[parts + at], grads[at][2]) for at in range(parts)]
     _, rows, cols = blocks[0][1].shape
     width = grads[0][1].shape[2]
-    pieces = (members // minor, cols // members, width)
+    pieces = (members // minor // 2, cols // members, width)
     return pl.pallas_call(
         functools.partial(weight_kernel, places, minor, len(arrays)),
-        out_shape=(jax.ShapeDtypeStruct(pieces, jnp.float32),)
-        + (jax.ShapeDtypeStruct(pieces, jnp.bfloat16),) * (minor - 1),
+        out_shape=(jax.ShapeDtypeStruct(pieces, jnp.float32),) * 2
+        + (jax.ShapeDtypeStruct(pieces, jnp.bfloat16),) * (2 * minor - 2),
         in_specs=[VMEM] * len(arrays),
-        out_specs=(VMEM,) * minor,
+        out_specs=(VMEM,) * (2 * minor),
         scratch_shapes=[pltpu.VMEM((cols, width), jnp.float32)],
         compiler_params=pltpu.CompilerParams(vmem_limit_bytes=VMEM_LIMIT),
         cost_estimate=pl.CostEstimate(
@@ -342,11 +343,11 @@
         out[...] = total.astype(out.dtype)
 
 
-def add_pieces(own, came):
+def add_pieces(own, came, first_type):
     majors, *piece = own.shape
     return pl.pallas_call(
         functools.partial(add_pieces_kernel, len(came)),
-        out_shape=(jax.ShapeDtypeStruct(piece, jnp.float32),)
+        out_shape=(jax.ShapeDtypeStruct(piece, first_type),)
         + (jax.ShapeDtypeStruct(piece, jnp.bfloat16),) * (majors - 1),
         in_specs=[VMEM] * (1 + len(came)),
         out_specs=(VMEM,) * majors,
@@ -354,6 +355,24 @@
         cost_estimate=pl.CostEstimate(flops=own.size, bytes_accessed=8 * own.size, transcendentals=0),
         name="add_pieces",
     )(own, *came)
+
+
+def add_all_kernel(*refs):
+    total = refs[0][...].astype(jnp.float32)
+    for ref in refs[1:-1]:
+        total = total + ref[...].astype(jnp.float32)
+    refs[-1][...] = total
+
+
+def add_all(pieces):
+    return pl.pallas_call(
+        add_all_kernel,
+        out_shape=jax.ShapeDtypeStruct(pieces[0].shape, jnp.float32),
+        in_specs=[VMEM] * len(pieces),
+        out_specs=VMEM,
+        compiler_params=pltpu.CompilerParams(vmem_limit_bytes=SMALL_VMEM_LIMIT),
+        name="add_all",
+    )(*pieces)
 
 
 def swap(value, axis, flip):
@@ -439,11 +458,18 @@
         grads += [(each[0] ^ bit, sent, at) for at, each in enumerate(grads)]
         bit //= 2
 
-    own, *pieces = weight_grad(blocks[0], grads, members, minor)
-    pieces = [swap(each, "pool", near + 1) for near, each in enumerate(pieces)]
-    total, *pieces = add_pieces(own, pieces)
-    for far in reversed(range(1, members // minor)):
-        total = total + swap(pieces[far - 1], "pool", far * minor).astype(jnp.float32)
+    own_far, own_near, *pieces = weight_grad(blocks[0], grads, members, minor)
+    far_came = [swap(each, "pool", at + 1) for at, each in enumerate(pieces[0::2])]
+    near_came = [swap(each, "pool", at + 1) for at, each in enumerate(pieces[1::2])]
+    far_sums = add_pieces(own_far, far_came, jnp.bfloat16)
+    total, *near_sums = add_pieces(own_near, near_came, jnp.float32)
+    half = members // minor // 2
+    far_came = [swap(each, "pool", (half + at) * minor) for at, each in enumerate(far_sums)]
+    near_came = [swap(each, "pool", (1 + at) * minor) for at, each in enumerate(near_sums)]
+    far_total = add_all(far_came)
+    total = total + far_total
+    for each in near_came:
+        total = total + after(each, far_total).astype(jnp.float32)
     return total
 
 

time: 49.3 us -> 49.2 us (level)
    ppermute x15 -> x16, starting transfers between devices: 20.3 us -> 20.1 us  [swap(): return lax.ppermute(value, axis, [(at, at ^ flip) for at in range(size)])]
    ppermute x15 -> x16, waiting for transfers between devices: 17.9 us -> 17.9 us  [swap(): return lax.ppermute(value, axis, [(at, at ^ flip) for at in range(size)])]
  transfers between devices with their start and end apart: 15 -> 16, of which waited for: 9 -> 9; matrix products, arithmetic and copies ran while one was open for 0% -> 0% of each run, Pallas kernels for 15% -> 15%
where the time goes in v9:
time: 49.2 us; the launch traced here: 49 us
  starting transfers between devices  20.1 us (41%)
  waiting for transfers between devices  17.9 us (36%)
  Pallas kernels  10.3 us (21%)
  other arithmetic  0.64 us (1%)
    ppermute x16, starting transfers between devices, swap(): return lax.ppermute(value, axis, [(at, at ^ flip) for at in range(size)])  20.1 us
    ppermute x16, waiting for transfers between devices, swap(): return lax.ppermute(value, axis, [(at, at ^ flip) for at in range(size)])  17.9 us
    pallas_call x4, Pallas kernels, add_pairs(): pl.pallas_call(functools.partial(pairs_kernel, seen, fresh), out_shape=(j...  4.9 us
    pallas_call x1, Pallas kernels, group_grad(): pl.pallas_call(functools.partial(grad_kernel, stages, fresh), out_shape=j...  2.47 us
    pallas_call x1, Pallas kernels, project(): pl.pallas_call(functools.partial(project_kernel, parts), out_shape=(jax.S...  2.27 us
  transfers between devices with their start and end apart: 16, of which 9 were waited for; matrix products, arithmetic and copies ran while one was open for 0% of the time, Pallas kernels for 15%

profile of v9, /device:TPU:0, one launch (start us, length us, event | category | flops | bytes accessed | tf_op | source)
XLA Modules:
  0.0 49.0 jit_solution(13677678548536005505)
XLA Ops:
  0.0 2.3 %project.1 = (bf16[272,256]{1,0:T(8,128)(2,1)S(1)}, f32[256,256]{1,0:T(8,128)S(1)}, f32[256,128]{1,0:T(8,128)S(1)}, bf16[2,256,512]{2,1,0:T(8,128)(2,1)S(1)}, bf16[2,256,512]{2,1,0:T(8,128)(2,1)S(1)}) custom-call(bf16[256,2048]{1,0:T(8,128)(2,1)} %feats_hbm.1, bf16[2048,256]{1,0:T(8,128)(2,1)} %w_hbm.1, s32[1,256]{1,0:T(1,128)} %bitcast.2, s32[1,256]{1,0:T(1,128)} %bitcast.3), custom_call_target="tpu_custom_call" | custom-call | flops 268435456 | bytes 2097152 | tf_op jit(solution)/shard_map/project/pallas_call | solution.py:81
  2.3 3.0 %collective-permute-start = (bf16[2,256,512]{2,1,0:T(8,128)(2,1)S(1)}, bf16[2,256,512]{2,1,0:T(8,128)(2,1)S(1)}, u32[]{:S(2)}, u32[]{:S(2)}) collective-permute-start(bf16[2,256,512]{2,1,0:T(8,128)(2,1)S(1)} %get-tuple-element.31), channel_id=1, source_target_pairs={{0,16},{8,24},{16,0},{24,8},{1,17},{9,25},{17,1},{25,9},{2,18},{10... | collective-permute-start | bytes 1572872 | tf_op jit(solution)/shard_map/ppermute | solution.py:380
  5.3 1.6 %collective-permute-start.1 = (bf16[272,256]{1,0:T(8,128)(2,1)S(1)}, bf16[272,256]{1,0:T(8,128)(2,1)S(1)}, u32[]{:S(2)}, u32[]{:S(2)}) collective-permute-start(bf16[272,256]{1,0:T(8,128)(2,1)S(1)} %get-tuple-element.32.refs_1_), channel_id=1, source_target_pairs={{0,2},{1,3},{2,0},{3,1},{4,6},{5,7},{6,4},{7,5},{8,10},{9,11},{10,... | collective-permute-start | bytes 417800 | tf_op jit(solution)/shard_map/ppermute | solution.py:380
  6.9 2.6 %collective-permute-start.2 = (bf16[272,256]{1,0:T(8,128)(2,1)S(1)}, bf16[272,256]{1,0:T(8,128)(2,1)S(1)}, u32[]{:S(2)}, u32[]{:S(2)}) collective-permute-start(bf16[272,256]{1,0:T(8,128)(2,1)S(1)} %get-tuple-element.32.refs_1_), channel_id=1, source_target_pairs={{0,4},{1,5},{2,6},{3,7},{4,0},{5,1},{6,2},{7,3},{8,12},{9,13},{10,... | collective-permute-start | bytes 417800 | tf_op jit(solution)/shard_map/ppermute | solution.py:380
  9.5 1.5 %collective-permute-start.3 = (bf16[272,256]{1,0:T(8,128)(2,1)S(1)}, bf16[272,256]{1,0:T(8,128)(2,1)S(1)}, u32[]{:S(2)}, u32[]{:S(2)}) collective-permute-start(bf16[272,256]{1,0:T(8,128)(2,1)S(1)} %get-tuple-element.32.refs_1_), channel_id=1, source_target_pairs={{0,1},{1,0},{2,3},{3,2},{4,5},{5,4},{6,7},{7,6},{8,9},{9,8},{10,11... | collective-permute-start | bytes 417800 | tf_op jit(solution)/shard_map/ppermute | solution.py:380
  11.0 1.5 %collective-permute-done.1.refs_2_ = bf16[272,256]{1,0:T(8,128)(2,1)S(1)} collective-permute-done((bf16[272,256]{1,0:T(8,128)(2,1)S(1)}, bf16[272,256]{1,0:T(8,128)(2,1)S(1)}, u32[]{:S(2)}, u32[]{:S(2)}) %collective-permute-start.1) | collective-permute-done | bytes 139296 | tf_op jit(solution)/shard_map/ppermute | solution.py:380
  12.5 1.5 %collective-permute-start.4 = (bf16[272,256]{1,0:T(8,128)(2,1)S(1)}, bf16[272,256]{1,0:T(8,128)(2,1)S(1)}, u32[]{:S(2)}, u32[]{:S(2)}) collective-permute-start(bf16[272,256]{1,0:T(8,128)(2,1)S(1)} %collective-permute-done.1.refs_2_), channel_id=1, source_target_pairs={{0,1},{1,0},{2,3},{3,2},{4,5},{5,4},{6,7},{7,6},{8,9},{9,8},{10,11... | collective-permute-start | bytes 417800 | tf_op jit(solution)/shard_map/ppermute | solution.py:380
  14.0 1.8 %collective-permute-done.2.refs_3_ = bf16[272,256]{1,0:T(8,128)(2,1)S(1)} collective-permute-done((bf16[272,256]{1,0:T(8,128)(2,1)S(1)}, bf16[272,256]{1,0:T(8,128)(2,1)S(1)}, u32[]{:S(2)}, u32[]{:S(2)}) %collective-permute-start.2) | collective-permute-done | bytes 139296 | tf_op jit(solution)/shard_map/ppermute | solution.py:380
  15.8 0.3 collective-permute-start.5
  16.1 1.5 %collective-permute-start.6 = (bf16[272,256]{1,0:T(8,128)(2,1)S(1)}, bf16[272,256]{1,0:T(8,128)(2,1)S(1)}, u32[]{:S(2)}, u32[]{:S(2)}) collective-permute-start(bf16[272,256]{1,0:T(8,128)(2,1)S(1)} %collective-permute-done.2.refs_3_), channel_id=1, source_target_pairs={{0,1},{1,0},{2,3},{3,2},{4,5},{5,4},{6,7},{7,6},{8,9},{9,8},{10,11... | collective-permute-start | bytes 417800 | tf_op jit(solution)/shard_map/ppermute | solution.py:380
  17.6 1.4 %add_pairs.4 = (f32[4,256]{1,0:T(4,128)S(1)}, f32[256,128]{1,0:T(8,128)S(1)}, f32[4,256,256]{2,1,0:T(8,128)S(1)}) custom-call(s32[4,8]{1,0:T(4,128)S(1)} %copy-done, bf16[272,256]{1,0:T(8,128)(2,1)S(1)} %get-tuple-element.32.refs_1_, bf16[272,256]{1,0:T(8,128)(2,1)S(1)} %collective-permute-done.1.refs_2_, ...), custom_call_target="tpu_custom_call" | custom-call | flops 335544320 | bytes 1572864 | tf_op jit(solution)/shard_map/add_pairs/pallas_call | solution.py:195
  19.0 1.1 %add_pairs.5 = (f32[5,256]{1,0:T(8,128)S(1)}, f32[256,128]{1,0:T(8,128)S(1)}, f32[1,256,256]{2,1,0:T(8,128)S(1)}) custom-call(s32[4,8]{1,0:T(4,128)S(1)} %copy-done, bf16[272,256]{1,0:T(8,128)(2,1)S(1)} %get-tuple-element.32.refs_1_, bf16[272,256]{1,0:T(8,128)(2,1)S(1)} %collective-permute-done.1.refs_2_, ...), custom_call_target="tpu_custom_call" | custom-call | flops 167772160 | bytes 917504 | tf_op jit(solution)/shard_map/add_pairs/pallas_call | solution.py:195
  20.1 0.7 %collective-permute-done.5.refs_6_.value_ref = bf16[272,256]{1,0:T(8,128)(2,1)S(1)} collective-permute-done((bf16[272,256]{1,0:T(8,128)(2,1)S(1)}, bf16[272,256]{1,0:T(8,128)(2,1)S(1)}, u32[]{:S(2)}, u32[]{:S(2)}) %collective-permute-start.5) | collective-permute-done | bytes 139296 | tf_op jit(solution)/shard_map/ppermute | solution.py:380
  20.9 1.6 %collective-permute-start.8 = (bf16[272,256]{1,0:T(8,128)(2,1)S(1)}, bf16[272,256]{1,0:T(8,128)(2,1)S(1)}, u32[]{:S(2)}, u32[]{:S(2)}) collective-permute-start(bf16[272,256]{1,0:T(8,128)(2,1)S(1)} %after.2), channel_id=1, source_target_pairs={{0,1},{1,0},{2,3},{3,2},{4,5},{5,4},{6,7},{7,6},{8,9},{9,8},{10,11... | collective-permute-start | bytes 417800 | tf_op jit(solution)/shard_map/ppermute | solution.py:380
  22.4 1.2 %add_pairs.6 = (f32[6,256]{1,0:T(8,128)S(1)}, f32[256,128]{1,0:T(8,128)S(1)}, f32[1,256,256]{2,1,0:T(8,128)S(1)}) custom-call(s32[4,8]{1,0:T(4,128)S(1)} %copy-done, bf16[272,256]{1,0:T(8,128)(2,1)S(1)} %get-tuple-element.32.refs_1_, bf16[272,256]{1,0:T(8,128)(2,1)S(1)} %collective-permute-done.1.refs_2_, ...), custom_call_target="tpu_custom_call" | custom-call | flops 201326592 | bytes 1048576 | tf_op jit(solution)/shard_map/add_pairs/pallas_call | solution.py:195
  23.6 1.2 %add_pairs.7 = (f32[7,256]{1,0:T(8,128)S(1)}, f32[256,128]{1,0:T(8,128)S(1)}, f32[1,256,256]{2,1,0:T(8,128)S(1)}) custom-call(s32[4,8]{1,0:T(4,128)S(1)} %copy-done, bf16[272,256]{1,0:T(8,128)(2,1)S(1)} %get-tuple-element.32.refs_1_, bf16[272,256]{1,0:T(8,128)(2,1)S(1)} %collective-permute-done.1.refs_2_, ...), custom_call_target="tpu_custom_call" | custom-call | flops 234881024 | bytes 1179648 | tf_op jit(solution)/shard_map/add_pairs/pallas_call | solution.py:195
  24.9 0.1 collective-permute-start.7
  25.0 1.0 %collective-permute-done.8.refs_8_ = bf16[272,256]{1,0:T(8,128)(2,1)S(1)} collective-permute-done((bf16[272,256]{1,0:T(8,128)(2,1)S(1)}, bf16[272,256]{1,0:T(8,128)(2,1)S(1)}, u32[]{:S(2)}, u32[]{:S(2)}) %collective-permute-start.8) | collective-permute-done | bytes 139296 | tf_op jit(solution)/shard_map/ppermute | solution.py:380
  26.0 2.5 %group_grad.1.refs_0_.refs_3_ = bf16[1,256,256]{2,1,0:T(8,128)(2,1)S(1)} custom-call(s32[4,8]{1,0:T(4,128)S(1)} %copy-done, bf16[272,256]{1,0:T(8,128)(2,1)S(1)} %get-tuple-element.32.refs_1_, bf16[272,256]{1,0:T(8,128)(2,1)S(1)} %collective-permute-done.1.refs_2_, bf16[272,256]{1,0:T(8,128)(2,1)S(1)} %collective-permute-done.2.refs_3_, ...), custom_call_target="tpu_custom_call" | custom-call | flops 268435456 | bytes 1310720 | tf_op jit(solution)/shard_map/group_grad/pallas_call | solution.py:260
  28.5 0.6 %collective-permute-start.9 = (bf16[1,256,256]{2,1,0:T(8,128)(2,1)S(1)}, bf16[1,256,256]{2,1,0:T(8,128)(2,1)S(1)}, u32[]{:S(2)}, u32[]{:S(2)}) collective-permute-start(bf16[1,256,256]{2,1,0:T(8,128)(2,1)S(1)} %group_grad.1.refs_0_.refs_3_), channel_id=1, source_target_pairs={{0,16},{8,24},{16,0},{24,8},{1,17},{9,25},{17,1},{25,9},{2,18},{10... | collective-permute-start | bytes 393224 | tf_op jit(solution)/shard_map/ppermute | solution.py:380
  29.0 4.5 %collective-permute-done.9.refs_1_.refs_5_ = bf16[1,256,256]{2,1,0:T(8,128)(2,1)S(1)} collective-permute-done((bf16[1,256,256]{2,1,0:T(8,128)(2,1)S(1)}, bf16[1,256,256]{2,1,0:T(8,128)(2,1)S(1)}, u32[]{:S(2)}, u32[]{:S(2)}) %collective-permute-start.9) | collective-permute-done | bytes 131104 | tf_op jit(solution)/shard_map/ppermute | solution.py:380
  33.5 0.1 collective-permute-start.10
  33.6 1.5 %collective-permute-done.10.refs_4_ = bf16[2,256,256]{2,1,0:T(8,128)(2,1)S(1)} collective-permute-done((bf16[2,256,256]{2,1,0:T(8,128)(2,1)S(1)}, bf16[2,256,256]{2,1,0:T(8,128)(2,1)S(1)}, u32[]{:S(2)}, u32[]{:S(2)}) %collective-permute-start.10) | collective-permute-done | bytes 262176 | tf_op jit(solution)/shard_map/ppermute | solution.py:380
  35.1 0.5 %weight_grad.1 = (f32[2,64,256]{2,1,0:T(8,128)S(1)}, f32[2,64,256]{2,1,0:T(8,128)S(1)}, bf16[2,64,256]{2,1,0:T(8,128)(2,1)S(1)}, bf16[2,64,256]{2,1,0:T(8,128)(2,1)S(1)}) custom-call(bf16[2,256,512]{2,1,0:T(8,128)(2,1)S(1)} %get-tuple-element.30.refs_0_, bf16[2,256,512]{2,1,0:T(8,128)(2,1)S(1)} %collective-permute-done.7.refs_1_, ...), custom_call_target="tpu_custom_call" | custom-call | flops 268435456 | bytes 1048576 | tf_op jit(solution)/shard_map/weight_grad/pallas_call | solution.py:323
  35.6 1.6 %collective-permute-start.12 = (bf16[2,64,256]{2,1,0:T(8,128)(2,1)S(1)}, bf16[2,64,256]{2,1,0:T(8,128)(2,1)S(1)}, u32[]{:S(2)}, u32[]{:S(2)}) collective-permute-start(bf16[2,64,256]{2,1,0:T(8,128)(2,1)S(1)} %get-tuple-element.51), channel_id=1, source_target_pairs={{0,1},{1,0},{2,3},{3,2},{4,5},{5,4},{6,7},{7,6},{8,9},{9,8},{10,11... | collective-permute-start | bytes 196616 | tf_op jit(solution)/shard_map/ppermute | solution.py:380
  37.2 0.5 %collective-permute-start.11 = (bf16[2,64,256]{2,1,0:T(8,128)(2,1)S(1)}, bf16[2,64,256]{2,1,0:T(8,128)(2,1)S(1)}, u32[]{:S(2)}, u32[]{:S(2)}) collective-permute-start(bf16[2,64,256]{2,1,0:T(8,128)(2,1)S(1)} %get-tuple-element.48), channel_id=1, source_target_pairs={{0,1},{1,0},{2,3},{3,2},{4,5},{5,4},{6,7},{7,6},{8,9},{9,8},{10,11... | collective-permute-start | bytes 196616 | tf_op jit(solution)/shard_map/ppermute | solution.py:380
  37.7 2.6 %collective-permute-done.12.refs_0_ = bf16[2,64,256]{2,1,0:T(8,128)(2,1)S(1)} collective-permute-done((bf16[2,64,256]{2,1,0:T(8,128)(2,1)S(1)}, bf16[2,64,256]{2,1,0:T(8,128)(2,1)S(1)}, u32[]{:S(2)}, u32[]{:S(2)}) %collective-permute-start.12) | collective-permute-done | bytes 65568 | tf_op jit(solution)/shard_map/ppermute | solution.py:380
  40.4 2.2 %collective-permute-start.13 = (bf16[64,256]{1,0:T(8,128)(2,1)S(1)}, bf16[64,256]{1,0:T(8,128)(2,1)S(1)}, u32[]{:S(2)}, u32[]{:S(2)}) collective-permute-start(bf16[64,256]{1,0:T(8,128)(2,1)S(1)} %get-tuple-element.52), channel_id=1, source_target_pairs={{0,4},{1,5},{2,6},{3,7},{4,0},{5,1},{6,2},{7,3},{8,12},{9,13},{10,... | collective-permute-start | bytes 98312 | tf_op jit(solution)/shard_map/ppermute | solution.py:380
  42.6 1.4 %collective-permute-start.14 = (bf16[64,256]{1,0:T(8,128)(2,1)S(1)}, bf16[64,256]{1,0:T(8,128)(2,1)S(1)}, u32[]{:S(2)}, u32[]{:S(2)}) collective-permute-start(bf16[64,256]{1,0:T(8,128)(2,1)S(1)} %get-tuple-element.53), channel_id=1, source_target_pairs={{0,6},{1,7},{2,4},{3,5},{4,2},{5,3},{6,0},{7,1},{8,14},{9,15},{10,... | collective-permute-start | bytes 98312 | tf_op jit(solution)/shard_map/ppermute | solution.py:380
  44.1 1.7 %collective-permute-done.13.refs_0_ = bf16[64,256]{1,0:T(8,128)(2,1)S(1)} collective-permute-done((bf16[64,256]{1,0:T(8,128)(2,1)S(1)}, bf16[64,256]{1,0:T(8,128)(2,1)S(1)}, u32[]{:S(2)}, u32[]{:S(2)}) %collective-permute-start.13) | collective-permute-done | bytes 32800 | tf_op jit(solution)/shard_map/ppermute | solution.py:380
  45.8 2.6 %collective-permute-done.14.refs_1_ = bf16[64,256]{1,0:T(8,128)(2,1)S(1)} collective-permute-done((bf16[64,256]{1,0:T(8,128)(2,1)S(1)}, bf16[64,256]{1,0:T(8,128)(2,1)S(1)}, u32[]{:S(2)}, u32[]{:S(2)}) %collective-permute-start.14) | collective-permute-done | bytes 32800 | tf_op jit(solution)/shard_map/ppermute | solution.py:380
  48.4 0.6 %convert_add_fusion = f32[64,256]{1,0:T(8,128)} fusion(bf16[64,256]{1,0:T(8,128)(2,1)S(1)} %after.3, f32[64,256]{1,0:T(8,128)S(1)} %get-tuple-element.49, f32[64,256]{1,0:T(8,128)S(1)} %add_all.1.refs_0_), kind=kLoop, calls=%fused_computation | loop fusion | flops 49152 | bytes 229376 | tf_op jit(solution)/shard_map/add | solution.py:472
  (17 shorter events, 0.2 us)
Async XLA Ops:
  2.3 15.4 %copy-start = (s32[4,8]{1,0:T(4,128)S(1)}, s32[4,8]{1,0:T(4,128)}, u32[]{:S(2)}) copy-start(s32[4,8]{1,0:T(4,128)} %refs_0_.9) | copy-start | bytes 388
  2.3 22.5 %collective-permute-start = (bf16[2,256,512]{2,1,0:T(8,128)(2,1)S(1)}, bf16[2,256,512]{2,1,0:T(8,128)(2,1)S(1)}, u32[]{:S(2)}, u32[]{:S(2)}) collective-permute-start(bf16[2,256,512]{2,1,0:T(8,128)(2,1)S(1)} %get-tuple-element.31), channel_id=1, source_target_pairs={{0,16},{8,24},{16,0},{24,8},{1,17},{9,25},{17,1},{25,9},{2,18},{10... | collective-permute-start | bytes 1572872 | tf_op jit(solution)/shard_map/ppermute | solution.py:380
  5.3 7.2 %collective-permute-start.1 = (bf16[272,256]{1,0:T(8,128)(2,1)S(1)}, bf16[272,256]{1,0:T(8,128)(2,1)S(1)}, u32[]{:S(2)}, u32[]{:S(2)}) collective-permute-start(bf16[272,256]{1,0:T(8,128)(2,1)S(1)} %get-tuple-element.32.refs_1_), channel_id=1, source_target_pairs={{0,2},{1,3},{2,0},{3,1},{4,6},{5,7},{6,4},{7,5},{8,10},{9,11},{10,... | collective-permute-start | bytes 417800 | tf_op jit(solution)/shard_map/ppermute | solution.py:380
  6.9 8.9 %collective-permute-start.2 = (bf16[272,256]{1,0:T(8,128)(2,1)S(1)}, bf16[272,256]{1,0:T(8,128)(2,1)S(1)}, u32[]{:S(2)}, u32[]{:S(2)}) collective-permute-start(bf16[272,256]{1,0:T(8,128)(2,1)S(1)} %get-tuple-element.32.refs_1_), channel_id=1, source_target_pairs={{0,4},{1,5},{2,6},{3,7},{4,0},{5,1},{6,2},{7,3},{8,12},{9,13},{10,... | collective-permute-start | bytes 417800 | tf_op jit(solution)/shard_map/ppermute | solution.py:380
  9.5 8.1 %collective-permute-start.3 = (bf16[272,256]{1,0:T(8,128)(2,1)S(1)}, bf16[272,256]{1,0:T(8,128)(2,1)S(1)}, u32[]{:S(2)}, u32[]{:S(2)}) collective-permute-start(bf16[272,256]{1,0:T(8,128)(2,1)S(1)} %get-tuple-element.32.refs_1_), channel_id=1, source_target_pairs={{0,1},{1,0},{2,3},{3,2},{4,5},{5,4},{6,7},{7,6},{8,9},{9,8},{10,11... | collective-permute-start | bytes 417800 | tf_op jit(solution)/shard_map/ppermute | solution.py:380
  12.5 6.5 %collective-permute-start.4 = (bf16[272,256]{1,0:T(8,128)(2,1)S(1)}, bf16[272,256]{1,0:T(8,128)(2,1)S(1)}, u32[]{:S(2)}, u32[]{:S(2)}) collective-permute-start(bf16[272,256]{1,0:T(8,128)(2,1)S(1)} %collective-permute-done.1.refs_2_), channel_id=1, source_target_pairs={{0,1},{1,0},{2,3},{3,2},{4,5},{5,4},{6,7},{7,6},{8,9},{9,8},{10,11... | collective-permute-start | bytes 417800 | tf_op jit(solution)/shard_map/ppermute | solution.py:380
  15.8 5.1 %collective-permute-start.5 = (bf16[272,256]{1,0:T(8,128)(2,1)S(1)}, bf16[272,256]{1,0:T(8,128)(2,1)S(1)}, u32[]{:S(2)}, u32[]{:S(2)}) collective-permute-start(bf16[272,256]{1,0:T(8,128)(2,1)S(1)} %collective-permute-done.2.refs_3_), channel_id=1, source_target_pairs={{0,2},{1,3},{2,0},{3,1},{4,6},{5,7},{6,4},{7,5},{8,10},{9,11},{10,... | collective-permute-start | bytes 417800 | tf_op jit(solution)/shard_map/ppermute | solution.py:380
  16.1 7.5 %collective-permute-start.6 = (bf16[272,256]{1,0:T(8,128)(2,1)S(1)}, bf16[272,256]{1,0:T(8,128)(2,1)S(1)}, u32[]{:S(2)}, u32[]{:S(2)}) collective-permute-start(bf16[272,256]{1,0:T(8,128)(2,1)S(1)} %collective-permute-done.2.refs_3_), channel_id=1, source_target_pairs={{0,1},{1,0},{2,3},{3,2},{4,5},{5,4},{6,7},{7,6},{8,9},{9,8},{10,11... | collective-permute-start | bytes 417800 | tf_op jit(solution)/shard_map/ppermute | solution.py:380
  20.9 5.1 %collective-permute-start.8 = (bf16[272,256]{1,0:T(8,128)(2,1)S(1)}, bf16[272,256]{1,0:T(8,128)(2,1)S(1)}, u32[]{:S(2)}, u32[]{:S(2)}) collective-permute-start(bf16[272,256]{1,0:T(8,128)(2,1)S(1)} %after.2), channel_id=1, source_target_pairs={{0,1},{1,0},{2,3},{3,2},{4,5},{5,4},{6,7},{7,6},{8,9},{9,8},{10,11... | collective-permute-start | bytes 417800 | tf_op jit(solution)/shard_map/ppermute | solution.py:380
  24.9 10.2 %collective-permute-start.7 = (bf16[2,256,512]{2,1,0:T(8,128)(2,1)S(1)}, bf16[2,256,512]{2,1,0:T(8,128)(2,1)S(1)}, u32[]{:S(2)}, u32[]{:S(2)}) collective-permute-start(bf16[2,256,512]{2,1,0:T(8,128)(2,1)S(1)} %pack.2), channel_id=1, source_target_pairs={{0,8},{8,0},{16,24},{24,16},{1,9},{9,1},{17,25},{25,17},{2,10},{10... | collective-permute-start | bytes 1572872 | tf_op jit(solution)/shard_map/ppermute | solution.py:380
  28.5 5.0 %collective-permute-start.9 = (bf16[1,256,256]{2,1,0:T(8,128)(2,1)S(1)}, bf16[1,256,256]{2,1,0:T(8,128)(2,1)S(1)}, u32[]{:S(2)}, u32[]{:S(2)}) collective-permute-start(bf16[1,256,256]{2,1,0:T(8,128)(2,1)S(1)} %group_grad.1.refs_0_.refs_3_), channel_id=1, source_target_pairs={{0,16},{8,24},{16,0},{24,8},{1,17},{9,25},{17,1},{25,9},{2,18},{10... | collective-permute-start | bytes 393224 | tf_op jit(solution)/shard_map/ppermute | solution.py:380
  33.5 1.6 %collective-permute-start.10 = (bf16[2,256,256]{2,1,0:T(8,128)(2,1)S(1)}, bf16[2,256,256]{2,1,0:T(8,128)(2,1)S(1)}, u32[]{:S(2)}, u32[]{:S(2)}) collective-permute-start(bf16[2,256,256]{2,1,0:T(8,128)(2,1)S(1)} %pack.3), channel_id=1, source_target_pairs={{0,8},{8,0},{16,24},{24,16},{1,9},{9,1},{17,25},{25,17},{2,10},{10... | collective-permute-start | bytes 786440 | tf_op jit(solution)/shard_map/ppermute | solution.py:380
  35.6 4.7 %collective-permute-start.12 = (bf16[2,64,256]{2,1,0:T(8,128)(2,1)S(1)}, bf16[2,64,256]{2,1,0:T(8,128)(2,1)S(1)}, u32[]{:S(2)}, u32[]{:S(2)}) collective-permute-start(bf16[2,64,256]{2,1,0:T(8,128)(2,1)S(1)} %get-tuple-element.51), channel_id=1, source_target_pairs={{0,1},{1,0},{2,3},{3,2},{4,5},{5,4},{6,7},{7,6},{8,9},{9,8},{10,11... | collective-permute-start | bytes 196616 | tf_op jit(solution)/shard_map/ppermute | solution.py:380
  37.2 6.8 %collective-permute-start.11 = (bf16[2,64,256]{2,1,0:T(8,128)(2,1)S(1)}, bf16[2,64,256]{2,1,0:T(8,128)(2,1)S(1)}, u32[]{:S(2)}, u32[]{:S(2)}) collective-permute-start(bf16[2,64,256]{2,1,0:T(8,128)(2,1)S(1)} %get-tuple-element.48), channel_id=1, source_target_pairs={{0,1},{1,0},{2,3},{3,2},{4,5},{5,4},{6,7},{7,6},{8,9},{9,8},{10,11... | collective-permute-start | bytes 196616 | tf_op jit(solution)/shard_map/ppermute | solution.py:380
  40.4 5.4 %collective-permute-start.13 = (bf16[64,256]{1,0:T(8,128)(2,1)S(1)}, bf16[64,256]{1,0:T(8,128)(2,1)S(1)}, u32[]{:S(2)}, u32[]{:S(2)}) collective-permute-start(bf16[64,256]{1,0:T(8,128)(2,1)S(1)} %get-tuple-element.52), channel_id=1, source_target_pairs={{0,4},{1,5},{2,6},{3,7},{4,0},{5,1},{6,2},{7,3},{8,12},{9,13},{10,... | collective-permute-start | bytes 98312 | tf_op jit(solution)/shard_map/ppermute | solution.py:380
  42.6 5.7 %collective-permute-start.14 = (bf16[64,256]{1,0:T(8,128)(2,1)S(1)}, bf16[64,256]{1,0:T(8,128)(2,1)S(1)}, u32[]{:S(2)}, u32[]{:S(2)}) collective-permute-start(bf16[64,256]{1,0:T(8,128)(2,1)S(1)} %get-tuple-element.53), channel_id=1, source_target_pairs={{0,6},{1,7},{2,4},{3,5},{4,2},{5,3},{6,0},{7,1},{8,14},{9,15},{10,... | collective-permute-start | bytes 98312 | tf_op jit(solution)/shard_map/ppermute | solution.py:380
  44.0 4.3 %collective-permute-start.15 = (bf16[64,256]{1,0:T(8,128)(2,1)S(1)}, bf16[64,256]{1,0:T(8,128)(2,1)S(1)}, u32[]{:S(2)}, u32[]{:S(2)}) collective-permute-start(bf16[64,256]{1,0:T(8,128)(2,1)S(1)} %get-tuple-element.54), channel_id=1, source_target_pairs={{0,2},{1,3},{2,0},{3,1},{4,6},{5,7},{6,4},{7,5},{8,10},{9,11},{10,... | collective-permute-start | bytes 98312 | tf_op jit(solution)/shard_map/ppermute | solution.py:380

commit v10 on v9

--- a/solution.py
+++ b/solution.py
@@ -460,7 +460,7 @@
 
     own_far, own_near, *pieces = weight_grad(blocks[0], grads, members, minor)
     far_came = [swap(each, "pool", at + 1) for at, each in enumerate(pieces[0::2])]
-    near_came = [swap(each, "pool", at + 1) for at, each in enumerate(pieces[1::2])]
+    near_came = [swap(after(each, *far_came), "pool", at + 1) for at, each in enumerate(pieces[1::2])]
     far_sums = add_pieces(own_far, far_came, jnp.bfloat16)
     total, *near_sums = add_pieces(own_near, near_came, jnp.float32)
     half = members // minor // 2

time: 49.2 us -> 49.5 us (level)
  starting transfers between devices: 20.1 us -> 21.2 us
  waiting for transfers between devices: 17.9 us -> 17.2 us
    ppermute x16, starting transfers between devices: 20.1 us -> 21.2 us  [swap(): return lax.ppermute(value, axis, [(at, at ^ flip) for at in range(size)])]
    ppermute x16, waiting for transfers between devices: 17.9 us -> 17.2 us  [swap(): return lax.ppermute(value, axis, [(at, at ^ flip) for at in range(size)])]
  transfers between devices with their start and end apart: 16 -> 16, of which waited for: 9 -> 10; matrix products, arithmetic and copies ran while one was open for 0% -> 0% of each run, Pallas kernels for 15% -> 15%
where the time goes in v10:
time: 49.5 us; the launch traced here: 49.4 us
  starting transfers between devices  21.2 us (43%)
  waiting for transfers between devices  17.2 us (35%)
  Pallas kernels  10.3 us (21%)
  other arithmetic  0.64 us (1%)
    ppermute x16, starting transfers between devices, swap(): return lax.ppermute(value, axis, [(at, at ^ flip) for at in range(size)])  21.2 us
    ppermute x16, waiting for transfers between devices, swap(): return lax.ppermute(value, axis, [(at, at ^ flip) for at in range(size)])  17.2 us
    pallas_call x4, Pallas kernels, add_pairs(): pl.pallas_call(functools.partial(pairs_kernel, seen, fresh), out_shape=(j...  4.9 us
    pallas_call x1, Pallas kernels, group_grad(): pl.pallas_call(functools.partial(grad_kernel, stages, fresh), out_shape=j...  2.47 us
    pallas_call x1, Pallas kernels, project(): pl.pallas_call(functools.partial(project_kernel, parts), out_shape=(jax.S...  2.27 us
  transfers between devices with their start and end apart: 16, of which 10 were waited for; matrix products, arithmetic and copies ran while one was open for 0% of the time, Pallas kernels for 15%

profile of v10, /device:TPU:0, one launch (start us, length us, event | category | flops | bytes accessed | tf_op | source)
XLA Modules:
  0.0 49.4 jit_solution(8767910764692808622)
XLA Ops:
  0.0 2.3 %project.1 = (bf16[272,256]{1,0:T(8,128)(2,1)S(1)}, f32[256,256]{1,0:T(8,128)S(1)}, f32[256,128]{1,0:T(8,128)S(1)}, bf16[2,256,512]{2,1,0:T(8,128)(2,1)S(1)}, bf16[2,256,512]{2,1,0:T(8,128)(2,1)S(1)}) custom-call(bf16[256,2048]{1,0:T(8,128)(2,1)} %feats_hbm.1, bf16[2048,256]{1,0:T(8,128)(2,1)} %w_hbm.1, s32[1,256]{1,0:T(1,128)} %bitcast.2, s32[1,256]{1,0:T(1,128)} %bitcast.3), custom_call_target="tpu_custom_call" | custom-call | flops 268435456 | bytes 2097152 | tf_op jit(solution)/shard_map/project/pallas_call | solution.py:81
  2.3 3.0 %collective-permute-start = (bf16[2,256,512]{2,1,0:T(8,128)(2,1)S(1)}, bf16[2,256,512]{2,1,0:T(8,128)(2,1)S(1)}, u32[]{:S(2)}, u32[]{:S(2)}) collective-permute-start(bf16[2,256,512]{2,1,0:T(8,128)(2,1)S(1)} %get-tuple-element.31), channel_id=1, source_target_pairs={{0,16},{8,24},{16,0},{24,8},{1,17},{9,25},{17,1},{25,9},{2,18},{10... | collective-permute-start | bytes 1572872 | tf_op jit(solution)/shard_map/ppermute | solution.py:380
  5.3 1.6 %collective-permute-start.1 = (bf16[272,256]{1,0:T(8,128)(2,1)S(1)}, bf16[272,256]{1,0:T(8,128)(2,1)S(1)}, u32[]{:S(2)}, u32[]{:S(2)}) collective-permute-start(bf16[272,256]{1,0:T(8,128)(2,1)S(1)} %get-tuple-element.32.refs_1_), channel_id=1, source_target_pairs={{0,2},{1,3},{2,0},{3,1},{4,6},{5,7},{6,4},{7,5},{8,10},{9,11},{10,... | collective-permute-start | bytes 417800 | tf_op jit(solution)/shard_map/ppermute | solution.py:380
  6.9 2.6 %collective-permute-start.2 = (bf16[272,256]{1,0:T(8,128)(2,1)S(1)}, bf16[272,256]{1,0:T(8,128)(2,1)S(1)}, u32[]{:S(2)}, u32[]{:S(2)}) collective-permute-start(bf16[272,256]{1,0:T(8,128)(2,1)S(1)} %get-tuple-element.32.refs_1_), channel_id=1, source_target_pairs={{0,4},{1,5},{2,6},{3,7},{4,0},{5,1},{6,2},{7,3},{8,12},{9,13},{10,... | collective-permute-start | bytes 417800 | tf_op jit(solution)/shard_map/ppermute | solution.py:380
  9.5 1.5 %collective-permute-start.3 = (bf16[272,256]{1,0:T(8,128)(2,1)S(1)}, bf16[272,256]{1,0:T(8,128)(2,1)S(1)}, u32[]{:S(2)}, u32[]{:S(2)}) collective-permute-start(bf16[272,256]{1,0:T(8,128)(2,1)S(1)} %get-tuple-element.32.refs_1_), channel_id=1, source_target_pairs={{0,1},{1,0},{2,3},{3,2},{4,5},{5,4},{6,7},{7,6},{8,9},{9,8},{10,11... | collective-permute-start | bytes 417800 | tf_op jit(solution)/shard_map/ppermute | solution.py:380
  11.0 1.5 %collective-permute-done.1.refs_2_ = bf16[272,256]{1,0:T(8,128)(2,1)S(1)} collective-permute-done((bf16[272,256]{1,0:T(8,128)(2,1)S(1)}, bf16[272,256]{1,0:T(8,128)(2,1)S(1)}, u32[]{:S(2)}, u32[]{:S(2)}) %collective-permute-start.1) | collective-permute-done | bytes 139296 | tf_op jit(solution)/shard_map/ppermute | solution.py:380
  12.5 1.5 %collective-permute-start.4 = (bf16[272,256]{1,0:T(8,128)(2,1)S(1)}, bf16[272,256]{1,0:T(8,128)(2,1)S(1)}, u32[]{:S(2)}, u32[]{:S(2)}) collective-permute-start(bf16[272,256]{1,0:T(8,128)(2,1)S(1)} %collective-permute-done.1.refs_2_), channel_id=1, source_target_pairs={{0,1},{1,0},{2,3},{3,2},{4,5},{5,4},{6,7},{7,6},{8,9},{9,8},{10,11... | collective-permute-start | bytes 417800 | tf_op jit(solution)/shard_map/ppermute | solution.py:380
  14.0 1.8 %collective-permute-done.2.refs_3_ = bf16[272,256]{1,0:T(8,128)(2,1)S(1)} collective-permute-done((bf16[272,256]{1,0:T(8,128)(2,1)S(1)}, bf16[272,256]{1,0:T(8,128)(2,1)S(1)}, u32[]{:S(2)}, u32[]{:S(2)}) %collective-permute-start.2) | collective-permute-done | bytes 139296 | tf_op jit(solution)/shard_map/ppermute | solution.py:380
  15.8 0.3 collective-permute-start.5
  16.1 1.5 %collective-permute-start.6 = (bf16[272,256]{1,0:T(8,128)(2,1)S(1)}, bf16[272,256]{1,0:T(8,128)(2,1)S(1)}, u32[]{:S(2)}, u32[]{:S(2)}) collective-permute-start(bf16[272,256]{1,0:T(8,128)(2,1)S(1)} %collective-permute-done.2.refs_3_), channel_id=1, source_target_pairs={{0,1},{1,0},{2,3},{3,2},{4,5},{5,4},{6,7},{7,6},{8,9},{9,8},{10,11... | collective-permute-start | bytes 417800 | tf_op jit(solution)/shard_map/ppermute | solution.py:380
  17.6 1.4 %add_pairs.4 = (f32[4,256]{1,0:T(4,128)S(1)}, f32[256,128]{1,0:T(8,128)S(1)}, f32[4,256,256]{2,1,0:T(8,128)S(1)}) custom-call(s32[4,8]{1,0:T(4,128)S(1)} %copy-done, bf16[272,256]{1,0:T(8,128)(2,1)S(1)} %get-tuple-element.32.refs_1_, bf16[272,256]{1,0:T(8,128)(2,1)S(1)} %collective-permute-done.1.refs_2_, ...), custom_call_target="tpu_custom_call" | custom-call | flops 335544320 | bytes 1572864 | tf_op jit(solution)/shard_map/add_pairs/pallas_call | solution.py:195
  19.0 1.1 %add_pairs.5 = (f32[5,256]{1,0:T(8,128)S(1)}, f32[256,128]{1,0:T(8,128)S(1)}, f32[1,256,256]{2,1,0:T(8,128)S(1)}) custom-call(s32[4,8]{1,0:T(4,128)S(1)} %copy-done, bf16[272,256]{1,0:T(8,128)(2,1)S(1)} %get-tuple-element.32.refs_1_, bf16[272,256]{1,0:T(8,128)(2,1)S(1)} %collective-permute-done.1.refs_2_, ...), custom_call_target="tpu_custom_call" | custom-call | flops 167772160 | bytes 917504 | tf_op jit(solution)/shard_map/add_pairs/pallas_call | solution.py:195
  20.1 0.7 %collective-permute-done.5.refs_6_.value_ref = bf16[272,256]{1,0:T(8,128)(2,1)S(1)} collective-permute-done((bf16[272,256]{1,0:T(8,128)(2,1)S(1)}, bf16[272,256]{1,0:T(8,128)(2,1)S(1)}, u32[]{:S(2)}, u32[]{:S(2)}) %collective-permute-start.5) | collective-permute-done | bytes 139296 | tf_op jit(solution)/shard_map/ppermute | solution.py:380
  20.9 1.6 %collective-permute-start.8 = (bf16[272,256]{1,0:T(8,128)(2,1)S(1)}, bf16[272,256]{1,0:T(8,128)(2,1)S(1)}, u32[]{:S(2)}, u32[]{:S(2)}) collective-permute-start(bf16[272,256]{1,0:T(8,128)(2,1)S(1)} %after.3), channel_id=1, source_target_pairs={{0,1},{1,0},{2,3},{3,2},{4,5},{5,4},{6,7},{7,6},{8,9},{9,8},{10,11... | collective-permute-start | bytes 417800 | tf_op jit(solution)/shard_map/ppermute | solution.py:380
  22.4 1.2 %add_pairs.6 = (f32[6,256]{1,0:T(8,128)S(1)}, f32[256,128]{1,0:T(8,128)S(1)}, f32[1,256,256]{2,1,0:T(8,128)S(1)}) custom-call(s32[4,8]{1,0:T(4,128)S(1)} %copy-done, bf16[272,256]{1,0:T(8,128)(2,1)S(1)} %get-tuple-element.32.refs_1_, bf16[272,256]{1,0:T(8,128)(2,1)S(1)} %collective-permute-done.1.refs_2_, ...), custom_call_target="tpu_custom_call" | custom-call | flops 201326592 | bytes 1048576 | tf_op jit(solution)/shard_map/add_pairs/pallas_call | solution.py:195
  23.6 1.2 %add_pairs.7 = (f32[7,256]{1,0:T(8,128)S(1)}, f32[256,128]{1,0:T(8,128)S(1)}, f32[1,256,256]{2,1,0:T(8,128)S(1)}) custom-call(s32[4,8]{1,0:T(4,128)S(1)} %copy-done, bf16[272,256]{1,0:T(8,128)(2,1)S(1)} %get-tuple-element.32.refs_1_, bf16[272,256]{1,0:T(8,128)(2,1)S(1)} %collective-permute-done.1.refs_2_, ...), custom_call_target="tpu_custom_call" | custom-call | flops 234881024 | bytes 1179648 | tf_op jit(solution)/shard_map/add_pairs/pallas_call | solution.py:195
  25.0 1.0 %collective-permute-done.8.refs_8_ = bf16[272,256]{1,0:T(8,128)(2,1)S(1)} collective-permute-done((bf16[272,256]{1,0:T(8,128)(2,1)S(1)}, bf16[272,256]{1,0:T(8,128)(2,1)S(1)}, u32[]{:S(2)}, u32[]{:S(2)}) %collective-permute-start.8) | collective-permute-done | bytes 139296 | tf_op jit(solution)/shard_map/ppermute | solution.py:380
  26.0 2.5 %group_grad.1.refs_0_.refs_3_ = bf16[1,256,256]{2,1,0:T(8,128)(2,1)S(1)} custom-call(s32[4,8]{1,0:T(4,128)S(1)} %copy-done, bf16[272,256]{1,0:T(8,128)(2,1)S(1)} %get-tuple-element.32.refs_1_, bf16[272,256]{1,0:T(8,128)(2,1)S(1)} %collective-permute-done.1.refs_2_, bf16[272,256]{1,0:T(8,128)(2,1)S(1)} %collective-permute-done.2.refs_3_, ...), custom_call_target="tpu_custom_call" | custom-call | flops 268435456 | bytes 1310720 | tf_op jit(solution)/shard_map/group_grad/pallas_call | solution.py:260
  28.5 0.6 %collective-permute-start.9 = (bf16[1,256,256]{2,1,0:T(8,128)(2,1)S(1)}, bf16[1,256,256]{2,1,0:T(8,128)(2,1)S(1)}, u32[]{:S(2)}, u32[]{:S(2)}) collective-permute-start(bf16[1,256,256]{2,1,0:T(8,128)(2,1)S(1)} %group_grad.1.refs_0_.refs_3_), channel_id=1, source_target_pairs={{0,16},{8,24},{16,0},{24,8},{1,17},{9,25},{17,1},{25,9},{2,18},{10... | collective-permute-start | bytes 393224 | tf_op jit(solution)/shard_map/ppermute | solution.py:380
  29.0 4.5 %collective-permute-done.9.refs_1_.refs_5_ = bf16[1,256,256]{2,1,0:T(8,128)(2,1)S(1)} collective-permute-done((bf16[1,256,256]{2,1,0:T(8,128)(2,1)S(1)}, bf16[1,256,256]{2,1,0:T(8,128)(2,1)S(1)}, u32[]{:S(2)}, u32[]{:S(2)}) %collective-permute-start.9) | collective-permute-done | bytes 131104 | tf_op jit(solution)/shard_map/ppermute | solution.py:380
  33.6 1.5 %collective-permute-done.10.refs_4_ = bf16[2,256,256]{2,1,0:T(8,128)(2,1)S(1)} collective-permute-done((bf16[2,256,256]{2,1,0:T(8,128)(2,1)S(1)}, bf16[2,256,256]{2,1,0:T(8,128)(2,1)S(1)}, u32[]{:S(2)}, u32[]{:S(2)}) %collective-permute-start.10) | collective-permute-done | bytes 262176 | tf_op jit(solution)/shard_map/ppermute | solution.py:380
  35.1 0.5 %weight_grad.1 = (f32[2,64,256]{2,1,0:T(8,128)S(1)}, f32[2,64,256]{2,1,0:T(8,128)S(1)}, bf16[2,64,256]{2,1,0:T(8,128)(2,1)S(1)}, bf16[2,64,256]{2,1,0:T(8,128)(2,1)S(1)}) custom-call(bf16[2,256,512]{2,1,0:T(8,128)(2,1)S(1)} %get-tuple-element.30.refs_0_, bf16[2,256,512]{2,1,0:T(8,128)(2,1)S(1)} %collective-permute-done.7.refs_1_, ...), custom_call_target="tpu_custom_call" | custom-call | flops 268435456 | bytes 1048576 | tf_op jit(solution)/shard_map/weight_grad/pallas_call | solution.py:323
  35.6 1.6 %collective-permute-start.11 = (bf16[2,64,256]{2,1,0:T(8,128)(2,1)S(1)}, bf16[2,64,256]{2,1,0:T(8,128)(2,1)S(1)}, u32[]{:S(2)}, u32[]{:S(2)}) collective-permute-start(bf16[2,64,256]{2,1,0:T(8,128)(2,1)S(1)} %get-tuple-element.49), channel_id=1, source_target_pairs={{0,1},{1,0},{2,3},{3,2},{4,5},{5,4},{6,7},{7,6},{8,9},{9,8},{10,11... | collective-permute-start | bytes 196616 | tf_op jit(solution)/shard_map/ppermute | solution.py:380
  37.2 2.8 %collective-permute-done.11.refs_0_ = bf16[2,64,256]{2,1,0:T(8,128)(2,1)S(1)} collective-permute-done((bf16[2,64,256]{2,1,0:T(8,128)(2,1)S(1)}, bf16[2,64,256]{2,1,0:T(8,128)(2,1)S(1)}, u32[]{:S(2)}, u32[]{:S(2)}) %collective-permute-start.11) | collective-permute-done | bytes 65568 | tf_op jit(solution)/shard_map/ppermute | solution.py:380
  40.0 1.5 %collective-permute-start.12 = (bf16[2,64,256]{2,1,0:T(8,128)(2,1)S(1)}, bf16[2,64,256]{2,1,0:T(8,128)(2,1)S(1)}, u32[]{:S(2)}, u32[]{:S(2)}) collective-permute-start(bf16[2,64,256]{2,1,0:T(8,128)(2,1)S(1)} %after.4), channel_id=1, source_target_pairs={{0,1},{1,0},{2,3},{3,2},{4,5},{5,4},{6,7},{7,6},{8,9},{9,8},{10,11... | collective-permute-start | bytes 196616 | tf_op jit(solution)/shard_map/ppermute | solution.py:380
  41.5 1.2 %collective-permute-start.13 = (bf16[64,256]{1,0:T(8,128)(2,1)S(1)}, bf16[64,256]{1,0:T(8,128)(2,1)S(1)}, u32[]{:S(2)}, u32[]{:S(2)}) collective-permute-start(bf16[64,256]{1,0:T(8,128)(2,1)S(1)} %get-tuple-element.52), channel_id=1, source_target_pairs={{0,4},{1,5},{2,6},{3,7},{4,0},{5,1},{6,2},{7,3},{8,12},{9,13},{10,... | collective-permute-start | bytes 98312 | tf_op jit(solution)/shard_map/ppermute | solution.py:380
  42.7 1.7 %collective-permute-start.14 = (bf16[64,256]{1,0:T(8,128)(2,1)S(1)}, bf16[64,256]{1,0:T(8,128)(2,1)S(1)}, u32[]{:S(2)}, u32[]{:S(2)}) collective-permute-start(bf16[64,256]{1,0:T(8,128)(2,1)S(1)} %get-tuple-element.53), channel_id=1, source_target_pairs={{0,6},{1,7},{2,4},{3,5},{4,2},{5,3},{6,0},{7,1},{8,14},{9,15},{10,... | collective-permute-start | bytes 98312 | tf_op jit(solution)/shard_map/ppermute | solution.py:380
  44.4 0.9 %collective-permute-start.15 = (bf16[64,256]{1,0:T(8,128)(2,1)S(1)}, bf16[64,256]{1,0:T(8,128)(2,1)S(1)}, u32[]{:S(2)}, u32[]{:S(2)}) collective-permute-start(bf16[64,256]{1,0:T(8,128)(2,1)S(1)} %get-tuple-element.54), channel_id=1, source_target_pairs={{0,2},{1,3},{2,0},{3,1},{4,6},{5,7},{6,4},{7,5},{8,10},{9,11},{10,... | collective-permute-start | bytes 98312 | tf_op jit(solution)/shard_map/ppermute | solution.py:380
  45.3 1.3 %collective-permute-done.13.refs_0_ = bf16[64,256]{1,0:T(8,128)(2,1)S(1)} collective-permute-done((bf16[64,256]{1,0:T(8,128)(2,1)S(1)}, bf16[64,256]{1,0:T(8,128)(2,1)S(1)}, u32[]{:S(2)}, u32[]{:S(2)}) %collective-permute-start.13) | collective-permute-done | bytes 32800 | tf_op jit(solution)/shard_map/ppermute | solution.py:380
  46.7 1.8 %collective-permute-done.14.refs_1_ = bf16[64,256]{1,0:T(8,128)(2,1)S(1)} collective-permute-done((bf16[64,256]{1,0:T(8,128)(2,1)S(1)}, bf16[64,256]{1,0:T(8,128)(2,1)S(1)}, u32[]{:S(2)}, u32[]{:S(2)}) %collective-permute-start.14) | collective-permute-done | bytes 32800 | tf_op jit(solution)/shard_map/ppermute | solution.py:380
  48.4 0.3 collective-permute-done.15.value_ref
  48.8 0.6 %convert_add_fusion = f32[64,256]{1,0:T(8,128)} fusion(bf16[64,256]{1,0:T(8,128)(2,1)S(1)} %after.5, f32[64,256]{1,0:T(8,128)S(1)} %get-tuple-element.50, f32[64,256]{1,0:T(8,128)S(1)} %add_all.1.refs_0_), kind=kLoop, calls=%fused_computation | loop fusion | flops 49152 | bytes 229376 | tf_op jit(solution)/shard_map/add | solution.py:472
  (18 shorter events, 0.3 us)
Async XLA Ops:
  2.3 15.4 %copy-start = (s32[4,8]{1,0:T(4,128)S(1)}, s32[4,8]{1,0:T(4,128)}, u32[]{:S(2)}) copy-start(s32[4,8]{1,0:T(4,128)} %refs_0_.9) | copy-start | bytes 388
  2.3 22.5 %collective-permute-start = (bf16[2,256,512]{2,1,0:T(8,128)(2,1)S(1)}, bf16[2,256,512]{2,1,0:T(8,128)(2,1)S(1)}, u32[]{:S(2)}, u32[]{:S(2)}) collective-permute-start(bf16[2,256,512]{2,1,0:T(8,128)(2,1)S(1)} %get-tuple-element.31), channel_id=1, source_target_pairs={{0,16},{8,24},{16,0},{24,8},{1,17},{9,25},{17,1},{25,9},{2,18},{10... | collective-permute-start | bytes 1572872 | tf_op jit(solution)/shard_map/ppermute | solution.py:380
  5.3 7.2 %collective-permute-start.1 = (bf16[272,256]{1,0:T(8,128)(2,1)S(1)}, bf16[272,256]{1,0:T(8,128)(2,1)S(1)}, u32[]{:S(2)}, u32[]{:S(2)}) collective-permute-start(bf16[272,256]{1,0:T(8,128)(2,1)S(1)} %get-tuple-element.32.refs_1_), channel_id=1, source_target_pairs={{0,2},{1,3},{2,0},{3,1},{4,6},{5,7},{6,4},{7,5},{8,10},{9,11},{10,... | collective-permute-start | bytes 417800 | tf_op jit(solution)/shard_map/ppermute | solution.py:380
  6.9 8.9 %collective-permute-start.2 = (bf16[272,256]{1,0:T(8,128)(2,1)S(1)}, bf16[272,256]{1,0:T(8,128)(2,1)S(1)}, u32[]{:S(2)}, u32[]{:S(2)}) collective-permute-start(bf16[272,256]{1,0:T(8,128)(2,1)S(1)} %get-tuple-element.32.refs_1_), channel_id=1, source_target_pairs={{0,4},{1,5},{2,6},{3,7},{4,0},{5,1},{6,2},{7,3},{8,12},{9,13},{10,... | collective-permute-start | bytes 417800 | tf_op jit(solution)/shard_map/ppermute | solution.py:380
  9.5 8.1 %collective-permute-start.3 = (bf16[272,256]{1,0:T(8,128)(2,1)S(1)}, bf16[272,256]{1,0:T(8,128)(2,1)S(1)}, u32[]{:S(2)}, u32[]{:S(2)}) collective-permute-start(bf16[272,256]{1,0:T(8,128)(2,1)S(1)} %get-tuple-element.32.refs_1_), channel_id=1, source_target_pairs={{0,1},{1,0},{2,3},{3,2},{4,5},{5,4},{6,7},{7,6},{8,9},{9,8},{10,11... | collective-permute-start | bytes 417800 | tf_op jit(solution)/shard_map/ppermute | solution.py:380
  12.5 6.5 %collective-permute-start.4 = (bf16[272,256]{1,0:T(8,128)(2,1)S(1)}, bf16[272,256]{1,0:T(8,128)(2,1)S(1)}, u32[]{:S(2)}, u32[]{:S(2)}) collective-permute-start(bf16[272,256]{1,0:T(8,128)(2,1)S(1)} %collective-permute-done.1.refs_2_), channel_id=1, source_target_pairs={{0,1},{1,0},{2,3},{3,2},{4,5},{5,4},{6,7},{7,6},{8,9},{9,8},{10,11... | collective-permute-start | bytes 417800 | tf_op jit(solution)/shard_map/ppermute | solution.py:380
  15.8 5.1 %collective-permute-start.5 = (bf16[272,256]{1,0:T(8,128)(2,1)S(1)}, bf16[272,256]{1,0:T(8,128)(2,1)S(1)}, u32[]{:S(2)}, u32[]{:S(2)}) collective-permute-start(bf16[272,256]{1,0:T(8,128)(2,1)S(1)} %collective-permute-done.2.refs_3_), channel_id=1, source_target_pairs={{0,2},{1,3},{2,0},{3,1},{4,6},{5,7},{6,4},{7,5},{8,10},{9,11},{10,... | collective-permute-start | bytes 417800 | tf_op jit(solution)/shard_map/ppermute | solution.py:380
  16.1 7.5 %collective-permute-start.6 = (bf16[272,256]{1,0:T(8,128)(2,1)S(1)}, bf16[272,256]{1,0:T(8,128)(2,1)S(1)}, u32[]{:S(2)}, u32[]{:S(2)}) collective-permute-start(bf16[272,256]{1,0:T(8,128)(2,1)S(1)} %collective-permute-done.2.refs_3_), channel_id=1, source_target_pairs={{0,1},{1,0},{2,3},{3,2},{4,5},{5,4},{6,7},{7,6},{8,9},{9,8},{10,11... | collective-permute-start | bytes 417800 | tf_op jit(solution)/shard_map/ppermute | solution.py:380
  20.9 5.1 %collective-permute-start.8 = (bf16[272,256]{1,0:T(8,128)(2,1)S(1)}, bf16[272,256]{1,0:T(8,128)(2,1)S(1)}, u32[]{:S(2)}, u32[]{:S(2)}) collective-permute-start(bf16[272,256]{1,0:T(8,128)(2,1)S(1)} %after.3), channel_id=1, source_target_pairs={{0,1},{1,0},{2,3},{3,2},{4,5},{5,4},{6,7},{7,6},{8,9},{9,8},{10,11... | collective-permute-start | bytes 417800 | tf_op jit(solution)/shard_map/ppermute | solution.py:380
  24.9 10.2 %collective-permute-start.7 = (bf16[2,256,512]{2,1,0:T(8,128)(2,1)S(1)}, bf16[2,256,512]{2,1,0:T(8,128)(2,1)S(1)}, u32[]{:S(2)}, u32[]{:S(2)}) collective-permute-start(bf16[2,256,512]{2,1,0:T(8,128)(2,1)S(1)} %pack.2), channel_id=1, source_target_pairs={{0,8},{8,0},{16,24},{24,16},{1,9},{9,1},{17,25},{25,17},{2,10},{10... | collective-permute-start | bytes 1572872 | tf_op jit(solution)/shard_map/ppermute | solution.py:380
  28.5 5.0 %collective-permute-start.9 = (bf16[1,256,256]{2,1,0:T(8,128)(2,1)S(1)}, bf16[1,256,256]{2,1,0:T(8,128)(2,1)S(1)}, u32[]{:S(2)}, u32[]{:S(2)}) collective-permute-start(bf16[1,256,256]{2,1,0:T(8,128)(2,1)S(1)} %group_grad.1.refs_0_.refs_3_), channel_id=1, source_target_pairs={{0,16},{8,24},{16,0},{24,8},{1,17},{9,25},{17,1},{25,9},{2,18},{10... | collective-permute-start | bytes 393224 | tf_op jit(solution)/shard_map/ppermute | solution.py:380
  33.5 1.6 %collective-permute-start.10 = (bf16[2,256,256]{2,1,0:T(8,128)(2,1)S(1)}, bf16[2,256,256]{2,1,0:T(8,128)(2,1)S(1)}, u32[]{:S(2)}, u32[]{:S(2)}) collective-permute-start(bf16[2,256,256]{2,1,0:T(8,128)(2,1)S(1)} %pack.3), channel_id=1, source_target_pairs={{0,8},{8,0},{16,24},{24,16},{1,9},{9,1},{17,25},{25,17},{2,10},{10... | collective-permute-start | bytes 786440 | tf_op jit(solution)/shard_map/ppermute | solution.py:380
  35.6 4.3 %collective-permute-start.11 = (bf16[2,64,256]{2,1,0:T(8,128)(2,1)S(1)}, bf16[2,64,256]{2,1,0:T(8,128)(2,1)S(1)}, u32[]{:S(2)}, u32[]{:S(2)}) collective-permute-start(bf16[2,64,256]{2,1,0:T(8,128)(2,1)S(1)} %get-tuple-element.49), channel_id=1, source_target_pairs={{0,1},{1,0},{2,3},{3,2},{4,5},{5,4},{6,7},{7,6},{8,9},{9,8},{10,11... | collective-permute-start | bytes 196616 | tf_op jit(solution)/shard_map/ppermute | solution.py:380
  40.0 4.5 %collective-permute-start.12 = (bf16[2,64,256]{2,1,0:T(8,128)(2,1)S(1)}, bf16[2,64,256]{2,1,0:T(8,128)(2,1)S(1)}, u32[]{:S(2)}, u32[]{:S(2)}) collective-permute-start(bf16[2,64,256]{2,1,0:T(8,128)(2,1)S(1)} %after.4), channel_id=1, source_target_pairs={{0,1},{1,0},{2,3},{3,2},{4,5},{5,4},{6,7},{7,6},{8,9},{9,8},{10,11... | collective-permute-start | bytes 196616 | tf_op jit(solution)/shard_map/ppermute | solution.py:380
  41.5 5.2 %collective-permute-start.13 = (bf16[64,256]{1,0:T(8,128)(2,1)S(1)}, bf16[64,256]{1,0:T(8,128)(2,1)S(1)}, u32[]{:S(2)}, u32[]{:S(2)}) collective-permute-start(bf16[64,256]{1,0:T(8,128)(2,1)S(1)} %get-tuple-element.52), channel_id=1, source_target_pairs={{0,4},{1,5},{2,6},{3,7},{4,0},{5,1},{6,2},{7,3},{8,12},{9,13},{10,... | collective-permute-start | bytes 98312 | tf_op jit(solution)/shard_map/ppermute | solution.py:380
  42.7 5.7 %collective-permute-start.14 = (bf16[64,256]{1,0:T(8,128)(2,1)S(1)}, bf16[64,256]{1,0:T(8,128)(2,1)S(1)}, u32[]{:S(2)}, u32[]{:S(2)}) collective-permute-start(bf16[64,256]{1,0:T(8,128)(2,1)S(1)} %get-tuple-element.53), channel_id=1, source_target_pairs={{0,6},{1,7},{2,4},{3,5},{4,2},{5,3},{6,0},{7,1},{8,14},{9,15},{10,... | collective-permute-start | bytes 98312 | tf_op jit(solution)/shard_map/ppermute | solution.py:380
  44.4 4.3 %collective-permute-start.15 = (bf16[64,256]{1,0:T(8,128)(2,1)S(1)}, bf16[64,256]{1,0:T(8,128)(2,1)S(1)}, u32[]{:S(2)}, u32[]{:S(2)}) collective-permute-start(bf16[64,256]{1,0:T(8,128)(2,1)S(1)} %get-tuple-element.54), channel_id=1, source_target_pairs={{0,2},{1,3},{2,0},{3,1},{4,6},{5,7},{6,4},{7,5},{8,10},{9,11},{10,... | collective-permute-start | bytes 98312 | tf_op jit(solution)/shard_map/ppermute | solution.py:380

commit v11 on v9

--- a/solution.py
+++ b/solution.py
@@ -431,11 +431,9 @@
         stages.append(fresh)
 
     add(majors[:-1] + list(range(1, minor)))
-    add([far + near for far in majors[1:-2] for near in range(1, minor)])
-    msgs3 = after(msgs[majors[-1]], state[1])
     for near in range(1, minor):
-        msgs[majors[-1] + near] = swap(msgs3, "pool", near)
-    add([majors[-1]])
+        msgs[majors[-1] + near] = swap(msgs[majors[-1]], "pool", near)
+    add([far + near for far in majors[1:-2] for near in range(1, minor)] + [majors[-1]])
     add([majors[-2] + near for near in range(1, minor)])
     bit = parts // 2
     blocks = {k: [(0, near_cuts, k), (bit, came, k)] for k in range(bit)}

time: 49.2 us -> 51.3 us (1.043)
  waiting for transfers between devices: 17.9 us -> 21.2 us
  Pallas kernels: 10.3 us -> 9.41 us
    ppermute x16, waiting for transfers between devices: 17.9 us -> 21.2 us  [swap(): return lax.ppermute(value, axis, [(at, at ^ flip) for at in range(size)])]
    pallas_call x4 -> x3, Pallas kernels: 4.9 us -> 4.07 us  [add_pairs(): pl.pallas_call(functools.partial(pairs_kernel, seen, fresh), out_shape=(j...]
  transfers between devices with their start and end apart: 16 -> 16, of which waited for: 9 -> 10; matrix products, arithmetic and copies ran while one was open for 0% -> 0% of each run, Pallas kernels for 15% -> 13%
where the time goes in v11:
time: 51.3 us; the launch traced here: 51.1 us
  waiting for transfers between devices  21.2 us (41%)
  starting transfers between devices  19.7 us (38%)
  Pallas kernels  9.41 us (18%)
  other arithmetic  0.64 us (1%)
    ppermute x16, waiting for transfers between devices, swap(): return lax.ppermute(value, axis, [(at, at ^ flip) for at in range(size)])  21.2 us
    ppermute x16, starting transfers between devices, swap(): return lax.ppermute(value, axis, [(at, at ^ flip) for at in range(size)])  19.7 us
    pallas_call x3, Pallas kernels, add_pairs(): pl.pallas_call(functools.partial(pairs_kernel, seen, fresh), out_shape=(j...  4.07 us
    pallas_call x1, Pallas kernels, group_grad(): pl.pallas_call(functools.partial(grad_kernel, stages, fresh), out_shape=j...  2.45 us
    pallas_call x1, Pallas kernels, project(): pl.pallas_call(functools.partial(project_kernel, parts), out_shape=(jax.S...  2.27 us
  transfers between devices with their start and end apart: 16, of which 10 were waited for; matrix products, arithmetic and copies ran while one was open for 0% of the time, Pallas kernels for 13%

profile of v11, /device:TPU:0, one launch (start us, length us, event | category | flops | bytes accessed | tf_op | source)
XLA Modules:
  0.0 51.1 jit_solution(12640892449842934336)
XLA Ops:
  0.0 2.3 %project.1 = (bf16[272,256]{1,0:T(8,128)(2,1)S(1)}, f32[256,256]{1,0:T(8,128)S(1)}, f32[256,128]{1,0:T(8,128)S(1)}, bf16[2,256,512]{2,1,0:T(8,128)(2,1)S(1)}, bf16[2,256,512]{2,1,0:T(8,128)(2,1)S(1)}) custom-call(bf16[256,2048]{1,0:T(8,128)(2,1)} %feats_hbm.1, bf16[2048,256]{1,0:T(8,128)(2,1)} %w_hbm.1, s32[1,256]{1,0:T(1,128)} %bitcast.2, s32[1,256]{1,0:T(1,128)} %bitcast.3), custom_call_target="tpu_custom_call" | custom-call | flops 268435456 | bytes 2097152 | tf_op jit(solution)/shard_map/project/pallas_call | solution.py:81
  2.3 3.0 %collective-permute-start = (bf16[2,256,512]{2,1,0:T(8,128)(2,1)S(1)}, bf16[2,256,512]{2,1,0:T(8,128)(2,1)S(1)}, u32[]{:S(2)}, u32[]{:S(2)}) collective-permute-start(bf16[2,256,512]{2,1,0:T(8,128)(2,1)S(1)} %get-tuple-element.28), channel_id=1, source_target_pairs={{0,16},{8,24},{16,0},{24,8},{1,17},{9,25},{17,1},{25,9},{2,18},{10... | collective-permute-start | bytes 1572872 | tf_op jit(solution)/shard_map/ppermute | solution.py:380
  5.3 2.6 %collective-permute-start.2 = (bf16[272,256]{1,0:T(8,128)(2,1)S(1)}, bf16[272,256]{1,0:T(8,128)(2,1)S(1)}, u32[]{:S(2)}, u32[]{:S(2)}) collective-permute-start(bf16[272,256]{1,0:T(8,128)(2,1)S(1)} %get-tuple-element.29.refs_1_), channel_id=1, source_target_pairs={{0,4},{1,5},{2,6},{3,7},{4,0},{5,1},{6,2},{7,3},{8,12},{9,13},{10,... | collective-permute-start | bytes 417800 | tf_op jit(solution)/shard_map/ppermute | solution.py:380
  7.9 1.6 %collective-permute-start.1 = (bf16[272,256]{1,0:T(8,128)(2,1)S(1)}, bf16[272,256]{1,0:T(8,128)(2,1)S(1)}, u32[]{:S(2)}, u32[]{:S(2)}) collective-permute-start(bf16[272,256]{1,0:T(8,128)(2,1)S(1)} %get-tuple-element.29.refs_1_), channel_id=1, source_target_pairs={{0,2},{1,3},{2,0},{3,1},{4,6},{5,7},{6,4},{7,5},{8,10},{9,11},{10,... | collective-permute-start | bytes 417800 | tf_op jit(solution)/shard_map/ppermute | solution.py:380
  9.5 1.5 %collective-permute-start.3 = (bf16[272,256]{1,0:T(8,128)(2,1)S(1)}, bf16[272,256]{1,0:T(8,128)(2,1)S(1)}, u32[]{:S(2)}, u32[]{:S(2)}) collective-permute-start(bf16[272,256]{1,0:T(8,128)(2,1)S(1)} %get-tuple-element.29.refs_1_), channel_id=1, source_target_pairs={{0,1},{1,0},{2,3},{3,2},{4,5},{5,4},{6,7},{7,6},{8,9},{9,8},{10,11... | collective-permute-start | bytes 417800 | tf_op jit(solution)/shard_map/ppermute | solution.py:380
  11.0 3.5 %collective-permute-done.2.refs_3_ = bf16[272,256]{1,0:T(8,128)(2,1)S(1)} collective-permute-done((bf16[272,256]{1,0:T(8,128)(2,1)S(1)}, bf16[272,256]{1,0:T(8,128)(2,1)S(1)}, u32[]{:S(2)}, u32[]{:S(2)}) %collective-permute-start.2) | collective-permute-done | bytes 139296 | tf_op jit(solution)/shard_map/ppermute | solution.py:380
  14.4 0.6 %collective-permute-start.5 = (bf16[272,256]{1,0:T(8,128)(2,1)S(1)}, bf16[272,256]{1,0:T(8,128)(2,1)S(1)}, u32[]{:S(2)}, u32[]{:S(2)}) collective-permute-start(bf16[272,256]{1,0:T(8,128)(2,1)S(1)} %collective-permute-done.2.refs_3_), channel_id=1, source_target_pairs={{0,2},{1,3},{2,0},{3,1},{4,6},{5,7},{6,4},{7,5},{8,10},{9,11},{10,... | collective-permute-start | bytes 417800 | tf_op jit(solution)/shard_map/ppermute | solution.py:380
  15.0 1.5 %collective-permute-start.4 = (bf16[272,256]{1,0:T(8,128)(2,1)S(1)}, bf16[272,256]{1,0:T(8,128)(2,1)S(1)}, u32[]{:S(2)}, u32[]{:S(2)}) collective-permute-start(bf16[272,256]{1,0:T(8,128)(2,1)S(1)} %collective-permute-done.1.refs_2_), channel_id=1, source_target_pairs={{0,1},{1,0},{2,3},{3,2},{4,5},{5,4},{6,7},{7,6},{8,9},{9,8},{10,11... | collective-permute-start | bytes 417800 | tf_op jit(solution)/shard_map/ppermute | solution.py:380
  16.5 0.5 %collective-permute-start.6 = (bf16[272,256]{1,0:T(8,128)(2,1)S(1)}, bf16[272,256]{1,0:T(8,128)(2,1)S(1)}, u32[]{:S(2)}, u32[]{:S(2)}) collective-permute-start(bf16[272,256]{1,0:T(8,128)(2,1)S(1)} %collective-permute-done.2.refs_3_), channel_id=1, source_target_pairs={{0,1},{1,0},{2,3},{3,2},{4,5},{5,4},{6,7},{7,6},{8,9},{9,8},{10,11... | collective-permute-start | bytes 417800 | tf_op jit(solution)/shard_map/ppermute | solution.py:380
  17.0 1.4 %add_pairs.3 = (f32[4,256]{1,0:T(4,128)S(1)}, f32[256,128]{1,0:T(8,128)S(1)}, f32[4,256,256]{2,1,0:T(8,128)S(1)}) custom-call(s32[4,8]{1,0:T(4,128)S(1)} %copy-done, bf16[272,256]{1,0:T(8,128)(2,1)S(1)} %get-tuple-element.29.refs_1_, bf16[272,256]{1,0:T(8,128)(2,1)S(1)} %collective-permute-done.1.refs_2_, ...), custom_call_target="tpu_custom_call" | custom-call | flops 335544320 | bytes 1572864 | tf_op jit(solution)/shard_map/add_pairs/pallas_call | solution.py:195
  18.4 1.1 %collective-permute-done.5.refs_6_ = bf16[272,256]{1,0:T(8,128)(2,1)S(1)} collective-permute-done((bf16[272,256]{1,0:T(8,128)(2,1)S(1)}, bf16[272,256]{1,0:T(8,128)(2,1)S(1)}, u32[]{:S(2)}, u32[]{:S(2)}) %collective-permute-start.5) | collective-permute-done | bytes 139296 | tf_op jit(solution)/shard_map/ppermute | solution.py:380
  19.5 1.5 %collective-permute-start.8 = (bf16[272,256]{1,0:T(8,128)(2,1)S(1)}, bf16[272,256]{1,0:T(8,128)(2,1)S(1)}, u32[]{:S(2)}, u32[]{:S(2)}) collective-permute-start(bf16[272,256]{1,0:T(8,128)(2,1)S(1)} %collective-permute-done.5.refs_6_), channel_id=1, source_target_pairs={{0,1},{1,0},{2,3},{3,2},{4,5},{5,4},{6,7},{7,6},{8,9},{9,8},{10,11... | collective-permute-start | bytes 417800 | tf_op jit(solution)/shard_map/ppermute | solution.py:380
  21.0 0.6 %collective-permute-done.4.refs_5_ = bf16[272,256]{1,0:T(8,128)(2,1)S(1)} collective-permute-done((bf16[272,256]{1,0:T(8,128)(2,1)S(1)}, bf16[272,256]{1,0:T(8,128)(2,1)S(1)}, u32[]{:S(2)}, u32[]{:S(2)}) %collective-permute-start.4) | collective-permute-done | bytes 139296 | tf_op jit(solution)/shard_map/ppermute | solution.py:380
  21.6 1.5 %add_pairs.4 = (f32[6,256]{1,0:T(8,128)S(1)}, f32[256,128]{1,0:T(8,128)S(1)}, f32[2,256,256]{2,1,0:T(8,128)S(1)}) custom-call(s32[4,8]{1,0:T(4,128)S(1)} %copy-done, bf16[272,256]{1,0:T(8,128)(2,1)S(1)} %get-tuple-element.29.refs_1_, bf16[272,256]{1,0:T(8,128)(2,1)S(1)} %collective-permute-done.1.refs_2_, ...), custom_call_target="tpu_custom_call" | custom-call | flops 369098752 | bytes 1310720 | tf_op jit(solution)/shard_map/add_pairs/pallas_call | solution.py:195
  23.1 1.5 %collective-permute-done.6.refs_7_ = bf16[272,256]{1,0:T(8,128)(2,1)S(1)} collective-permute-done((bf16[272,256]{1,0:T(8,128)(2,1)S(1)}, bf16[272,256]{1,0:T(8,128)(2,1)S(1)}, u32[]{:S(2)}, u32[]{:S(2)}) %collective-permute-start.6) | collective-permute-done | bytes 139296 | tf_op jit(solution)/shard_map/ppermute | solution.py:380
  24.6 1.2 %add_pairs.5 = (f32[7,256]{1,0:T(8,128)S(1)}, f32[256,128]{1,0:T(8,128)S(1)}, f32[1,256,256]{2,1,0:T(8,128)S(1)}) custom-call(s32[4,8]{1,0:T(4,128)S(1)} %copy-done, bf16[272,256]{1,0:T(8,128)(2,1)S(1)} %get-tuple-element.29.refs_1_, bf16[272,256]{1,0:T(8,128)(2,1)S(1)} %collective-permute-done.1.refs_2_, ...), custom_call_target="tpu_custom_call" | custom-call | flops 234881024 | bytes 1179648 | tf_op jit(solution)/shard_map/add_pairs/pallas_call | solution.py:195
  25.9 0.1 collective-permute-start.7
  25.9 0.4 collective-permute-done.8.refs_8_
  26.3 2.5 %group_grad.1.refs_0_.refs_3_ = bf16[1,256,256]{2,1,0:T(8,128)(2,1)S(1)} custom-call(s32[4,8]{1,0:T(4,128)S(1)} %copy-done, bf16[272,256]{1,0:T(8,128)(2,1)S(1)} %get-tuple-element.29.refs_1_, bf16[272,256]{1,0:T(8,128)(2,1)S(1)} %collective-permute-done.1.refs_2_, bf16[272,256]{1,0:T(8,128)(2,1)S(1)} %collective-permute-done.2.refs_3_, ...), custom_call_target="tpu_custom_call" | custom-call | flops 268435456 | bytes 1310720 | tf_op jit(solution)/shard_map/group_grad/pallas_call | solution.py:260
  28.8 0.6 %collective-permute-start.9 = (bf16[1,256,256]{2,1,0:T(8,128)(2,1)S(1)}, bf16[1,256,256]{2,1,0:T(8,128)(2,1)S(1)}, u32[]{:S(2)}, u32[]{:S(2)}) collective-permute-start(bf16[1,256,256]{2,1,0:T(8,128)(2,1)S(1)} %group_grad.1.refs_0_.refs_3_), channel_id=1, source_target_pairs={{0,16},{8,24},{16,0},{24,8},{1,17},{9,25},{17,1},{25,9},{2,18},{10... | collective-permute-start | bytes 393224 | tf_op jit(solution)/shard_map/ppermute | solution.py:380
  29.3 5.0 %collective-permute-done.9.refs_1_.refs_5_ = bf16[1,256,256]{2,1,0:T(8,128)(2,1)S(1)} collective-permute-done((bf16[1,256,256]{2,1,0:T(8,128)(2,1)S(1)}, bf16[1,256,256]{2,1,0:T(8,128)(2,1)S(1)}, u32[]{:S(2)}, u32[]{:S(2)}) %collective-permute-start.9) | collective-permute-done | bytes 131104 | tf_op jit(solution)/shard_map/ppermute | solution.py:380
  34.4 0.1 collective-permute-start.10
  34.5 1.5 %collective-permute-done.10.refs_4_ = bf16[2,256,256]{2,1,0:T(8,128)(2,1)S(1)} collective-permute-done((bf16[2,256,256]{2,1,0:T(8,128)(2,1)S(1)}, bf16[2,256,256]{2,1,0:T(8,128)(2,1)S(1)}, u32[]{:S(2)}, u32[]{:S(2)}) %collective-permute-start.10) | collective-permute-done | bytes 262176 | tf_op jit(solution)/shard_map/ppermute | solution.py:380
  36.0 0.5 %weight_grad.1 = (f32[2,64,256]{2,1,0:T(8,128)S(1)}, f32[2,64,256]{2,1,0:T(8,128)S(1)}, bf16[2,64,256]{2,1,0:T(8,128)(2,1)S(1)}, bf16[2,64,256]{2,1,0:T(8,128)(2,1)S(1)}) custom-call(bf16[2,256,512]{2,1,0:T(8,128)(2,1)S(1)} %get-tuple-element.27.refs_0_, bf16[2,256,512]{2,1,0:T(8,128)(2,1)S(1)} %collective-permute-done.7.refs_1_, ...), custom_call_target="tpu_custom_call" | custom-call | flops 268435456 | bytes 1048576 | tf_op jit(solution)/shard_map/weight_grad/pallas_call | solution.py:323
  36.5 1.6 %collective-permute-start.12 = (bf16[2,64,256]{2,1,0:T(8,128)(2,1)S(1)}, bf16[2,64,256]{2,1,0:T(8,128)(2,1)S(1)}, u32[]{:S(2)}, u32[]{:S(2)}) collective-permute-start(bf16[2,64,256]{2,1,0:T(8,128)(2,1)S(1)} %get-tuple-element.45), channel_id=1, source_target_pairs={{0,1},{1,0},{2,3},{3,2},{4,5},{5,4},{6,7},{7,6},{8,9},{9,8},{10,11... | collective-permute-start | bytes 196616 | tf_op jit(solution)/shard_map/ppermute | solution.py:380
  38.1 0.5 collective-permute-start.11
  38.6 2.6 %collective-permute-done.12.refs_0_ = bf16[2,64,256]{2,1,0:T(8,128)(2,1)S(1)} collective-permute-done((bf16[2,64,256]{2,1,0:T(8,128)(2,1)S(1)}, bf16[2,64,256]{2,1,0:T(8,128)(2,1)S(1)}, u32[]{:S(2)}, u32[]{:S(2)}) %collective-permute-start.12) | collective-permute-done | bytes 65568 | tf_op jit(solution)/shard_map/ppermute | solution.py:380
  41.3 3.5 %collective-permute-start.13 = (bf16[64,256]{1,0:T(8,128)(2,1)S(1)}, bf16[64,256]{1,0:T(8,128)(2,1)S(1)}, u32[]{:S(2)}, u32[]{:S(2)}) collective-permute-start(bf16[64,256]{1,0:T(8,128)(2,1)S(1)} %get-tuple-element.46), channel_id=1, source_target_pairs={{0,4},{1,5},{2,6},{3,7},{4,0},{5,1},{6,2},{7,3},{8,12},{9,13},{10,... | collective-permute-start | bytes 98312 | tf_op jit(solution)/shard_map/ppermute | solution.py:380
  44.8 0.7 %collective-permute-start.15 = (bf16[64,256]{1,0:T(8,128)(2,1)S(1)}, bf16[64,256]{1,0:T(8,128)(2,1)S(1)}, u32[]{:S(2)}, u32[]{:S(2)}) collective-permute-start(bf16[64,256]{1,0:T(8,128)(2,1)S(1)} %get-tuple-element.48), channel_id=1, source_target_pairs={{0,2},{1,3},{2,0},{3,1},{4,6},{5,7},{6,4},{7,5},{8,10},{9,11},{10,... | collective-permute-start | bytes 98312 | tf_op jit(solution)/shard_map/ppermute | solution.py:380
  45.5 1.2 %collective-permute-done.13.refs_0_ = bf16[64,256]{1,0:T(8,128)(2,1)S(1)} collective-permute-done((bf16[64,256]{1,0:T(8,128)(2,1)S(1)}, bf16[64,256]{1,0:T(8,128)(2,1)S(1)}, u32[]{:S(2)}, u32[]{:S(2)}) %collective-permute-start.13) | collective-permute-done | bytes 32800 | tf_op jit(solution)/shard_map/ppermute | solution.py:380
  46.6 3.8 %collective-permute-done.14.refs_1_ = bf16[64,256]{1,0:T(8,128)(2,1)S(1)} collective-permute-done((bf16[64,256]{1,0:T(8,128)(2,1)S(1)}, bf16[64,256]{1,0:T(8,128)(2,1)S(1)}, u32[]{:S(2)}, u32[]{:S(2)}) %collective-permute-start.14) | collective-permute-done | bytes 32800 | tf_op jit(solution)/shard_map/ppermute | solution.py:380
  50.5 0.6 %convert_add_fusion = f32[64,256]{1,0:T(8,128)} fusion(bf16[64,256]{1,0:T(8,128)(2,1)S(1)} %after.1, f32[64,256]{1,0:T(8,128)S(1)} %get-tuple-element.43, f32[64,256]{1,0:T(8,128)S(1)} %add_all.1.refs_0_), kind=kLoop, calls=%fused_computation | loop fusion | flops 49152 | bytes 229376 | tf_op jit(solution)/shard_map/add | solution.py:470
  (15 shorter events, 0.1 us)
Async XLA Ops:
  2.3 14.8 %copy-start = (s32[4,8]{1,0:T(4,128)S(1)}, s32[4,8]{1,0:T(4,128)}, u32[]{:S(2)}) copy-start(s32[4,8]{1,0:T(4,128)} %refs_0_.7) | copy-start | bytes 388
  2.3 23.5 %collective-permute-start = (bf16[2,256,512]{2,1,0:T(8,128)(2,1)S(1)}, bf16[2,256,512]{2,1,0:T(8,128)(2,1)S(1)}, u32[]{:S(2)}, u32[]{:S(2)}) collective-permute-start(bf16[2,256,512]{2,1,0:T(8,128)(2,1)S(1)} %get-tuple-element.28), channel_id=1, source_target_pairs={{0,16},{8,24},{16,0},{24,8},{1,17},{9,25},{17,1},{25,9},{2,18},{10... | collective-permute-start | bytes 1572872 | tf_op jit(solution)/shard_map/ppermute | solution.py:380
  5.3 9.1 %collective-permute-start.2 = (bf16[272,256]{1,0:T(8,128)(2,1)S(1)}, bf16[272,256]{1,0:T(8,128)(2,1)S(1)}, u32[]{:S(2)}, u32[]{:S(2)}) collective-permute-start(bf16[272,256]{1,0:T(8,128)(2,1)S(1)} %get-tuple-element.29.refs_1_), channel_id=1, source_target_pairs={{0,4},{1,5},{2,6},{3,7},{4,0},{5,1},{6,2},{7,3},{8,12},{9,13},{10,... | collective-permute-start | bytes 417800 | tf_op jit(solution)/shard_map/ppermute | solution.py:380
  7.9 7.1 %collective-permute-start.1 = (bf16[272,256]{1,0:T(8,128)(2,1)S(1)}, bf16[272,256]{1,0:T(8,128)(2,1)S(1)}, u32[]{:S(2)}, u32[]{:S(2)}) collective-permute-start(bf16[272,256]{1,0:T(8,128)(2,1)S(1)} %get-tuple-element.29.refs_1_), channel_id=1, source_target_pairs={{0,2},{1,3},{2,0},{3,1},{4,6},{5,7},{6,4},{7,5},{8,10},{9,11},{10,... | collective-permute-start | bytes 417800 | tf_op jit(solution)/shard_map/ppermute | solution.py:380
  9.5 7.6 %collective-permute-start.3 = (bf16[272,256]{1,0:T(8,128)(2,1)S(1)}, bf16[272,256]{1,0:T(8,128)(2,1)S(1)}, u32[]{:S(2)}, u32[]{:S(2)}) collective-permute-start(bf16[272,256]{1,0:T(8,128)(2,1)S(1)} %get-tuple-element.29.refs_1_), channel_id=1, source_target_pairs={{0,1},{1,0},{2,3},{3,2},{4,5},{5,4},{6,7},{7,6},{8,9},{9,8},{10,11... | collective-permute-start | bytes 417800 | tf_op jit(solution)/shard_map/ppermute | solution.py:380
  14.4 5.1 %collective-permute-start.5 = (bf16[272,256]{1,0:T(8,128)(2,1)S(1)}, bf16[272,256]{1,0:T(8,128)(2,1)S(1)}, u32[]{:S(2)}, u32[]{:S(2)}) collective-permute-start(bf16[272,256]{1,0:T(8,128)(2,1)S(1)} %collective-permute-done.2.refs_3_), channel_id=1, source_target_pairs={{0,2},{1,3},{2,0},{3,1},{4,6},{5,7},{6,4},{7,5},{8,10},{9,11},{10,... | collective-permute-start | bytes 417800 | tf_op jit(solution)/shard_map/ppermute | solution.py:380
  15.0 6.6 %collective-permute-start.4 = (bf16[272,256]{1,0:T(8,128)(2,1)S(1)}, bf16[272,256]{1,0:T(8,128)(2,1)S(1)}, u32[]{:S(2)}, u32[]{:S(2)}) collective-permute-start(bf16[272,256]{1,0:T(8,128)(2,1)S(1)} %collective-permute-done.1.refs_2_), channel_id=1, source_target_pairs={{0,1},{1,0},{2,3},{3,2},{4,5},{5,4},{6,7},{7,6},{8,9},{9,8},{10,11... | collective-permute-start | bytes 417800 | tf_op jit(solution)/shard_map/ppermute | solution.py:380
  16.5 8.1 %collective-permute-start.6 = (bf16[272,256]{1,0:T(8,128)(2,1)S(1)}, bf16[272,256]{1,0:T(8,128)(2,1)S(1)}, u32[]{:S(2)}, u32[]{:S(2)}) collective-permute-start(bf16[272,256]{1,0:T(8,128)(2,1)S(1)} %collective-permute-done.2.refs_3_), channel_id=1, source_target_pairs={{0,1},{1,0},{2,3},{3,2},{4,5},{5,4},{6,7},{7,6},{8,9},{9,8},{10,11... | collective-permute-start | bytes 417800 | tf_op jit(solution)/shard_map/ppermute | solution.py:380
  19.5 6.8 %collective-permute-start.8 = (bf16[272,256]{1,0:T(8,128)(2,1)S(1)}, bf16[272,256]{1,0:T(8,128)(2,1)S(1)}, u32[]{:S(2)}, u32[]{:S(2)}) collective-permute-start(bf16[272,256]{1,0:T(8,128)(2,1)S(1)} %collective-permute-done.5.refs_6_), channel_id=1, source_target_pairs={{0,1},{1,0},{2,3},{3,2},{4,5},{5,4},{6,7},{7,6},{8,9},{9,8},{10,11... | collective-permute-start | bytes 417800 | tf_op jit(solution)/shard_map/ppermute | solution.py:380
  25.9 10.1 %collective-permute-start.7 = (bf16[2,256,512]{2,1,0:T(8,128)(2,1)S(1)}, bf16[2,256,512]{2,1,0:T(8,128)(2,1)S(1)}, u32[]{:S(2)}, u32[]{:S(2)}) collective-permute-start(bf16[2,256,512]{2,1,0:T(8,128)(2,1)S(1)} %pack.2), channel_id=1, source_target_pairs={{0,8},{8,0},{16,24},{24,16},{1,9},{9,1},{17,25},{25,17},{2,10},{10... | collective-permute-start | bytes 1572872 | tf_op jit(solution)/shard_map/ppermute | solution.py:380
  28.8 5.6 %collective-permute-start.9 = (bf16[1,256,256]{2,1,0:T(8,128)(2,1)S(1)}, bf16[1,256,256]{2,1,0:T(8,128)(2,1)S(1)}, u32[]{:S(2)}, u32[]{:S(2)}) collective-permute-start(bf16[1,256,256]{2,1,0:T(8,128)(2,1)S(1)} %group_grad.1.refs_0_.refs_3_), channel_id=1, source_target_pairs={{0,16},{8,24},{16,0},{24,8},{1,17},{9,25},{17,1},{25,9},{2,18},{10... | collective-permute-start | bytes 393224 | tf_op jit(solution)/shard_map/ppermute | solution.py:380
  34.4 1.6 %collective-permute-start.10 = (bf16[2,256,256]{2,1,0:T(8,128)(2,1)S(1)}, bf16[2,256,256]{2,1,0:T(8,128)(2,1)S(1)}, u32[]{:S(2)}, u32[]{:S(2)}) collective-permute-start(bf16[2,256,256]{2,1,0:T(8,128)(2,1)S(1)} %pack.3), channel_id=1, source_target_pairs={{0,8},{8,0},{16,24},{24,16},{1,9},{9,1},{17,25},{25,17},{2,10},{10... | collective-permute-start | bytes 786440 | tf_op jit(solution)/shard_map/ppermute | solution.py:380
  36.5 4.7 %collective-permute-start.12 = (bf16[2,64,256]{2,1,0:T(8,128)(2,1)S(1)}, bf16[2,64,256]{2,1,0:T(8,128)(2,1)S(1)}, u32[]{:S(2)}, u32[]{:S(2)}) collective-permute-start(bf16[2,64,256]{2,1,0:T(8,128)(2,1)S(1)} %get-tuple-element.45), channel_id=1, source_target_pairs={{0,1},{1,0},{2,3},{3,2},{4,5},{5,4},{6,7},{7,6},{8,9},{9,8},{10,11... | collective-permute-start | bytes 196616 | tf_op jit(solution)/shard_map/ppermute | solution.py:380
  38.1 6.6 %collective-permute-start.11 = (bf16[2,64,256]{2,1,0:T(8,128)(2,1)S(1)}, bf16[2,64,256]{2,1,0:T(8,128)(2,1)S(1)}, u32[]{:S(2)}, u32[]{:S(2)}) collective-permute-start(bf16[2,64,256]{2,1,0:T(8,128)(2,1)S(1)} %get-tuple-element.42), channel_id=1, source_target_pairs={{0,1},{1,0},{2,3},{3,2},{4,5},{5,4},{6,7},{7,6},{8,9},{9,8},{10,11... | collective-permute-start | bytes 196616 | tf_op jit(solution)/shard_map/ppermute | solution.py:380
  41.3 5.3 %collective-permute-start.13 = (bf16[64,256]{1,0:T(8,128)(2,1)S(1)}, bf16[64,256]{1,0:T(8,128)(2,1)S(1)}, u32[]{:S(2)}, u32[]{:S(2)}) collective-permute-start(bf16[64,256]{1,0:T(8,128)(2,1)S(1)} %get-tuple-element.46), channel_id=1, source_target_pairs={{0,4},{1,5},{2,6},{3,7},{4,0},{5,1},{6,2},{7,3},{8,12},{9,13},{10,... | collective-permute-start | bytes 98312 | tf_op jit(solution)/shard_map/ppermute | solution.py:380
  44.7 5.7 %collective-permute-start.14 = (bf16[64,256]{1,0:T(8,128)(2,1)S(1)}, bf16[64,256]{1,0:T(8,128)(2,1)S(1)}, u32[]{:S(2)}, u32[]{:S(2)}) collective-permute-start(bf16[64,256]{1,0:T(8,128)(2,1)S(1)} %get-tuple-element.47), channel_id=1, source_target_pairs={{0,6},{1,7},{2,4},{3,5},{4,2},{5,3},{6,0},{7,1},{8,14},{9,15},{10,... | collective-permute-start | bytes 98312 | tf_op jit(solution)/shard_map/ppermute | solution.py:380
  44.8 5.7 %collective-permute-start.15 = (bf16[64,256]{1,0:T(8,128)(2,1)S(1)}, bf16[64,256]{1,0:T(8,128)(2,1)S(1)}, u32[]{:S(2)}, u32[]{:S(2)}) collective-permute-start(bf16[64,256]{1,0:T(8,128)(2,1)S(1)} %get-tuple-element.48), channel_id=1, source_target_pairs={{0,2},{1,3},{2,0},{3,1},{4,6},{5,7},{6,4},{7,5},{8,10},{9,11},{10,... | collective-permute-start | bytes 98312 | tf_op jit(solution)/shard_map/ppermute | solution.py:380

commit v12 on v9

--- a/solution.py
+++ b/solution.py
@@ -437,24 +437,23 @@
         msgs[majors[-1] + near] = swap(msgs3, "pool", near)
     add([majors[-1]])
     add([majors[-2] + near for near in range(1, minor)])
+    final = [majors[-1] + near for near in range(1, minor)]
+    grad_proj = group_grad(stages, final, row_counts, msgs, state, kept, [], normed, inv)
+
     bit = parts // 2
+    grads = [(0, grad_proj, 0), (bit, swap(grad_proj, "dp", bit), 0)]
     blocks = {k: [(0, near_cuts, k), (bit, came, k)] for k in range(bit)}
     bit //= 2
     while bit:
         moving = [(k ^ bit, source ^ bit, array, at) for k in blocks if k & bit for source, array, at in blocks[k]]
         blocks = {k: blocks[k] for k in blocks if not k & bit}
-        passed = swap(pack([each[2:] for each in moving], [state[1]]), "dp", bit)
+        passed = swap(pack([each[2:] for each in moving], [grads[-1][1]]), "dp", bit)
         for at, (k, source, _, _) in enumerate(moving):
             blocks[k].append((source, passed, at))
         bit //= 2
-
-    final = [majors[-1] + near for near in range(1, minor)]
-    grad_proj = group_grad(stages, final, row_counts, msgs, state, kept, [], normed, inv)
-
-    bit = parts // 2
-    grads = [(0, grad_proj, 0)]
+    bit = parts // 4
     while bit:
-        sent = swap(grad_proj if len(grads) == 1 else pack([each[1:] for each in grads]), "dp", bit)
+        sent = swap(pack([each[1:] for each in grads]), "dp", bit)
         grads += [(each[0] ^ bit, sent, at) for at, each in enumerate(grads)]
         bit //= 2
 

time: 49.2 us -> 48.7 us (0.990)
  waiting for transfers between devices: 17.9 us -> 15.5 us
  starting transfers between devices: 20.1 us -> 22 us
    ppermute x16, waiting for transfers between devices: 17.9 us -> 15.5 us  [swap(): return lax.ppermute(value, axis, [(at, at ^ flip) for at in range(size)])]
    ppermute x16, starting transfers between devices: 20.1 us -> 22 us  [swap(): return lax.ppermute(value, axis, [(at, at ^ flip) for at in range(size)])]
  transfers between devices with their start and end apart: 16 -> 16, of which waited for: 9 -> 10; matrix products, arithmetic and copies ran while one was open for 0% -> 0% of each run, Pallas kernels for 15% -> 15%
where the time goes in v12:
time: 48.7 us; the launch traced here: 48.5 us
  starting transfers between devices  22 us (45%)
  waiting for transfers between devices  15.5 us (32%)
  Pallas kernels  10.3 us (21%)
  other arithmetic  0.64 us (1%)
    ppermute x16, starting transfers between devices, swap(): return lax.ppermute(value, axis, [(at, at ^ flip) for at in range(size)])  22 us
    ppermute x16, waiting for transfers between devices, swap(): return lax.ppermute(value, axis, [(at, at ^ flip) for at in range(size)])  15.5 us
    pallas_call x4, Pallas kernels, add_pairs(): pl.pallas_call(functools.partial(pairs_kernel, seen, fresh), out_shape=(j...  4.9 us
    pallas_call x1, Pallas kernels, group_grad(): pl.pallas_call(functools.partial(grad_kernel, stages, fresh), out_shape=j...  2.49 us
    pallas_call x1, Pallas kernels, project(): pl.pallas_call(functools.partial(project_kernel, parts), out_shape=(jax.S...  2.27 us
  transfers between devices with their start and end apart: 16, of which 10 were waited for; matrix products, arithmetic and copies ran while one was open for 0% of the time, Pallas kernels for 15%

profile of v12, /device:TPU:0, one launch (start us, length us, event | category | flops | bytes accessed | tf_op | source)
XLA Modules:
  0.0 48.5 jit_solution(8930460443309829693)
XLA Ops:
  0.0 2.3 %project.1 = (bf16[272,256]{1,0:T(8,128)(2,1)S(1)}, f32[256,256]{1,0:T(8,128)S(1)}, f32[256,128]{1,0:T(8,128)S(1)}, bf16[2,256,512]{2,1,0:T(8,128)(2,1)S(1)}, bf16[2,256,512]{2,1,0:T(8,128)(2,1)S(1)}) custom-call(bf16[256,2048]{1,0:T(8,128)(2,1)} %feats_hbm.1, bf16[2048,256]{1,0:T(8,128)(2,1)} %w_hbm.1, s32[1,256]{1,0:T(1,128)} %bitcast.2, s32[1,256]{1,0:T(1,128)} %bitcast.3), custom_call_target="tpu_custom_call" | custom-call | flops 268435456 | bytes 2097152 | tf_op jit(solution)/shard_map/project/pallas_call | solution.py:81
  2.3 3.1 %collective-permute-start.1 = (bf16[272,256]{1,0:T(8,128)(2,1)S(1)}, bf16[272,256]{1,0:T(8,128)(2,1)S(1)}, u32[]{:S(2)}, u32[]{:S(2)}) collective-permute-start(bf16[272,256]{1,0:T(8,128)(2,1)S(1)} %get-tuple-element.32.refs_1_), channel_id=1, source_target_pairs={{0,2},{1,3},{2,0},{3,1},{4,6},{5,7},{6,4},{7,5},{8,10},{9,11},{10,... | collective-permute-start | bytes 417800 | tf_op jit(solution)/shard_map/ppermute | solution.py:380
  5.4 2.6 %collective-permute-start.2 = (bf16[272,256]{1,0:T(8,128)(2,1)S(1)}, bf16[272,256]{1,0:T(8,128)(2,1)S(1)}, u32[]{:S(2)}, u32[]{:S(2)}) collective-permute-start(bf16[272,256]{1,0:T(8,128)(2,1)S(1)} %get-tuple-element.32.refs_1_), channel_id=1, source_target_pairs={{0,4},{1,5},{2,6},{3,7},{4,0},{5,1},{6,2},{7,3},{8,12},{9,13},{10,... | collective-permute-start | bytes 417800 | tf_op jit(solution)/shard_map/ppermute | solution.py:380
  8.0 1.5 %collective-permute-start = (bf16[2,256,512]{2,1,0:T(8,128)(2,1)S(1)}, bf16[2,256,512]{2,1,0:T(8,128)(2,1)S(1)}, u32[]{:S(2)}, u32[]{:S(2)}) collective-permute-start(bf16[2,256,512]{2,1,0:T(8,128)(2,1)S(1)} %get-tuple-element.31), channel_id=1, source_target_pairs={{0,16},{8,24},{16,0},{24,8},{1,17},{9,25},{17,1},{25,9},{2,18},{10... | collective-permute-start | bytes 1572872 | tf_op jit(solution)/shard_map/ppermute | solution.py:380
  9.5 1.5 %collective-permute-start.3 = (bf16[272,256]{1,0:T(8,128)(2,1)S(1)}, bf16[272,256]{1,0:T(8,128)(2,1)S(1)}, u32[]{:S(2)}, u32[]{:S(2)}) collective-permute-start(bf16[272,256]{1,0:T(8,128)(2,1)S(1)} %get-tuple-element.32.refs_1_), channel_id=1, source_target_pairs={{0,1},{1,0},{2,3},{3,2},{4,5},{5,4},{6,7},{7,6},{8,9},{9,8},{10,11... | collective-permute-start | bytes 417800 | tf_op jit(solution)/shard_map/ppermute | solution.py:380
  11.0 0.3 collective-permute-done.1.refs_2_
  11.2 1.8 %collective-permute-start.4 = (bf16[272,256]{1,0:T(8,128)(2,1)S(1)}, bf16[272,256]{1,0:T(8,128)(2,1)S(1)}, u32[]{:S(2)}, u32[]{:S(2)}) collective-permute-start(bf16[272,256]{1,0:T(8,128)(2,1)S(1)} %collective-permute-done.1.refs_2_), channel_id=1, source_target_pairs={{0,1},{1,0},{2,3},{3,2},{4,5},{5,4},{6,7},{7,6},{8,9},{9,8},{10,11... | collective-permute-start | bytes 417800 | tf_op jit(solution)/shard_map/ppermute | solution.py:380
  13.1 1.4 %collective-permute-done.2.refs_3_ = bf16[272,256]{1,0:T(8,128)(2,1)S(1)} collective-permute-done((bf16[272,256]{1,0:T(8,128)(2,1)S(1)}, bf16[272,256]{1,0:T(8,128)(2,1)S(1)}, u32[]{:S(2)}, u32[]{:S(2)}) %collective-permute-start.2) | collective-permute-done | bytes 139296 | tf_op jit(solution)/shard_map/ppermute | solution.py:380
  14.4 0.4 collective-permute-start.5
  14.9 1.5 %collective-permute-start.6 = (bf16[272,256]{1,0:T(8,128)(2,1)S(1)}, bf16[272,256]{1,0:T(8,128)(2,1)S(1)}, u32[]{:S(2)}, u32[]{:S(2)}) collective-permute-start(bf16[272,256]{1,0:T(8,128)(2,1)S(1)} %collective-permute-done.2.refs_3_), channel_id=1, source_target_pairs={{0,1},{1,0},{2,3},{3,2},{4,5},{5,4},{6,7},{7,6},{8,9},{9,8},{10,11... | collective-permute-start | bytes 417800 | tf_op jit(solution)/shard_map/ppermute | solution.py:380
  16.4 1.4 %add_pairs.4 = (f32[4,256]{1,0:T(4,128)S(1)}, f32[256,128]{1,0:T(8,128)S(1)}, f32[4,256,256]{2,1,0:T(8,128)S(1)}) custom-call(s32[4,8]{1,0:T(4,128)S(1)} %copy-done, bf16[272,256]{1,0:T(8,128)(2,1)S(1)} %get-tuple-element.32.refs_1_, bf16[272,256]{1,0:T(8,128)(2,1)S(1)} %collective-permute-done.1.refs_2_, ...), custom_call_target="tpu_custom_call" | custom-call | flops 335544320 | bytes 1572864 | tf_op jit(solution)/shard_map/add_pairs/pallas_call | solution.py:195
  17.8 0.2 collective-permute-done.4.refs_5_
  18.0 1.1 %add_pairs.5 = (f32[5,256]{1,0:T(8,128)S(1)}, f32[256,128]{1,0:T(8,128)S(1)}, f32[1,256,256]{2,1,0:T(8,128)S(1)}) custom-call(s32[4,8]{1,0:T(4,128)S(1)} %copy-done, bf16[272,256]{1,0:T(8,128)(2,1)S(1)} %get-tuple-element.32.refs_1_, bf16[272,256]{1,0:T(8,128)(2,1)S(1)} %collective-permute-done.1.refs_2_, ...), custom_call_target="tpu_custom_call" | custom-call | flops 167772160 | bytes 917504 | tf_op jit(solution)/shard_map/add_pairs/pallas_call | solution.py:195
  19.1 0.4 collective-permute-done.5.value_ref.refs_6_
  19.5 1.6 %collective-permute-start.7 = (bf16[272,256]{1,0:T(8,128)(2,1)S(1)}, bf16[272,256]{1,0:T(8,128)(2,1)S(1)}, u32[]{:S(2)}, u32[]{:S(2)}) collective-permute-start(bf16[272,256]{1,0:T(8,128)(2,1)S(1)} %after.2), channel_id=1, source_target_pairs={{0,1},{1,0},{2,3},{3,2},{4,5},{5,4},{6,7},{7,6},{8,9},{9,8},{10,11... | collective-permute-start | bytes 417800 | tf_op jit(solution)/shard_map/ppermute | solution.py:380
  21.1 1.2 %add_pairs.6 = (f32[6,256]{1,0:T(8,128)S(1)}, f32[256,128]{1,0:T(8,128)S(1)}, f32[1,256,256]{2,1,0:T(8,128)S(1)}) custom-call(s32[4,8]{1,0:T(4,128)S(1)} %copy-done, bf16[272,256]{1,0:T(8,128)(2,1)S(1)} %get-tuple-element.32.refs_1_, bf16[272,256]{1,0:T(8,128)(2,1)S(1)} %collective-permute-done.1.refs_2_, ...), custom_call_target="tpu_custom_call" | custom-call | flops 201326592 | bytes 1048576 | tf_op jit(solution)/shard_map/add_pairs/pallas_call | solution.py:195
  22.3 1.2 %add_pairs.7 = (f32[7,256]{1,0:T(8,128)S(1)}, f32[256,128]{1,0:T(8,128)S(1)}, f32[1,256,256]{2,1,0:T(8,128)S(1)}) custom-call(s32[4,8]{1,0:T(4,128)S(1)} %copy-done, bf16[272,256]{1,0:T(8,128)(2,1)S(1)} %get-tuple-element.32.refs_1_, bf16[272,256]{1,0:T(8,128)(2,1)S(1)} %collective-permute-done.1.refs_2_, ...), custom_call_target="tpu_custom_call" | custom-call | flops 234881024 | bytes 1179648 | tf_op jit(solution)/shard_map/add_pairs/pallas_call | solution.py:195
  23.5 1.2 %collective-permute-done.7.refs_8_ = bf16[272,256]{1,0:T(8,128)(2,1)S(1)} collective-permute-done((bf16[272,256]{1,0:T(8,128)(2,1)S(1)}, bf16[272,256]{1,0:T(8,128)(2,1)S(1)}, u32[]{:S(2)}, u32[]{:S(2)}) %collective-permute-start.7) | collective-permute-done | bytes 139296 | tf_op jit(solution)/shard_map/ppermute | solution.py:380
  24.6 2.5 %group_grad.1.refs_0_.refs_3_ = bf16[1,256,256]{2,1,0:T(8,128)(2,1)S(1)} custom-call(s32[4,8]{1,0:T(4,128)S(1)} %copy-done, bf16[272,256]{1,0:T(8,128)(2,1)S(1)} %get-tuple-element.32.refs_1_, bf16[272,256]{1,0:T(8,128)(2,1)S(1)} %collective-permute-done.1.refs_2_, bf16[272,256]{1,0:T(8,128)(2,1)S(1)} %collective-permute-done.2.refs_3_, ...), custom_call_target="tpu_custom_call" | custom-call | flops 268435456 | bytes 1310720 | tf_op jit(solution)/shard_map/group_grad/pallas_call | solution.py:260
  27.1 1.6 %collective-permute-start.8 = (bf16[1,256,256]{2,1,0:T(8,128)(2,1)S(1)}, bf16[1,256,256]{2,1,0:T(8,128)(2,1)S(1)}, u32[]{:S(2)}, u32[]{:S(2)}) collective-permute-start(bf16[1,256,256]{2,1,0:T(8,128)(2,1)S(1)} %group_grad.1.refs_0_.refs_3_), channel_id=1, source_target_pairs={{0,16},{8,24},{16,0},{24,8},{1,17},{9,25},{17,1},{25,9},{2,18},{10... | collective-permute-start | bytes 393224 | tf_op jit(solution)/shard_map/ppermute | solution.py:380
  28.7 3.4 %collective-permute-done.8.refs_2_.refs_1_.refs_5_ = bf16[1,256,256]{2,1,0:T(8,128)(2,1)S(1)} collective-permute-done((bf16[1,256,256]{2,1,0:T(8,128)(2,1)S(1)}, bf16[1,256,256]{2,1,0:T(8,128)(2,1)S(1)}, u32[]{:S(2)}, u32[]{:S(2)}) %collective-permute-start.8) | collective-permute-done | bytes 131104 | tf_op jit(solution)/shard_map/ppermute | solution.py:380
  32.3 0.6 %collective-permute-start.10 = (bf16[2,256,256]{2,1,0:T(8,128)(2,1)S(1)}, bf16[2,256,256]{2,1,0:T(8,128)(2,1)S(1)}, u32[]{:S(2)}, u32[]{:S(2)}) collective-permute-start(bf16[2,256,256]{2,1,0:T(8,128)(2,1)S(1)} %pack.3), channel_id=1, source_target_pairs={{0,8},{8,0},{16,24},{24,16},{1,9},{9,1},{17,25},{25,17},{2,10},{10... | collective-permute-start | bytes 786440 | tf_op jit(solution)/shard_map/ppermute | solution.py:380
  32.9 1.7 %collective-permute-done.10.refs_4_ = bf16[2,256,256]{2,1,0:T(8,128)(2,1)S(1)} collective-permute-done((bf16[2,256,256]{2,1,0:T(8,128)(2,1)S(1)}, bf16[2,256,256]{2,1,0:T(8,128)(2,1)S(1)}, u32[]{:S(2)}, u32[]{:S(2)}) %collective-permute-start.10) | collective-permute-done | bytes 262176 | tf_op jit(solution)/shard_map/ppermute | solution.py:380
  34.6 0.5 %weight_grad.1 = (f32[2,64,256]{2,1,0:T(8,128)S(1)}, f32[2,64,256]{2,1,0:T(8,128)S(1)}, bf16[2,64,256]{2,1,0:T(8,128)(2,1)S(1)}, bf16[2,64,256]{2,1,0:T(8,128)(2,1)S(1)}) custom-call(bf16[2,256,512]{2,1,0:T(8,128)(2,1)S(1)} %get-tuple-element.30.refs_0_, bf16[2,256,512]{2,1,0:T(8,128)(2,1)S(1)} %collective-permute-done.9.refs_1_, ...), custom_call_target="tpu_custom_call" | custom-call | flops 268435456 | bytes 1048576 | tf_op jit(solution)/shard_map/weight_grad/pallas_call | solution.py:323
  35.1 1.6 %collective-permute-start.12 = (bf16[2,64,256]{2,1,0:T(8,128)(2,1)S(1)}, bf16[2,64,256]{2,1,0:T(8,128)(2,1)S(1)}, u32[]{:S(2)}, u32[]{:S(2)}) collective-permute-start(bf16[2,64,256]{2,1,0:T(8,128)(2,1)S(1)} %get-tuple-element.51), channel_id=1, source_target_pairs={{0,1},{1,0},{2,3},{3,2},{4,5},{5,4},{6,7},{7,6},{8,9},{9,8},{10,11... | collective-permute-start | bytes 196616 | tf_op jit(solution)/shard_map/ppermute | solution.py:380
  36.6 0.5 %collective-permute-start.11 = (bf16[2,64,256]{2,1,0:T(8,128)(2,1)S(1)}, bf16[2,64,256]{2,1,0:T(8,128)(2,1)S(1)}, u32[]{:S(2)}, u32[]{:S(2)}) collective-permute-start(bf16[2,64,256]{2,1,0:T(8,128)(2,1)S(1)} %get-tuple-element.48), channel_id=1, source_target_pairs={{0,1},{1,0},{2,3},{3,2},{4,5},{5,4},{6,7},{7,6},{8,9},{9,8},{10,11... | collective-permute-start | bytes 196616 | tf_op jit(solution)/shard_map/ppermute | solution.py:380
  37.2 2.6 %collective-permute-done.12.refs_0_ = bf16[2,64,256]{2,1,0:T(8,128)(2,1)S(1)} collective-permute-done((bf16[2,64,256]{2,1,0:T(8,128)(2,1)S(1)}, bf16[2,64,256]{2,1,0:T(8,128)(2,1)S(1)}, u32[]{:S(2)}, u32[]{:S(2)}) %collective-permute-start.12) | collective-permute-done | bytes 65568 | tf_op jit(solution)/shard_map/ppermute | solution.py:380
  39.8 2.3 %collective-permute-start.13 = (bf16[64,256]{1,0:T(8,128)(2,1)S(1)}, bf16[64,256]{1,0:T(8,128)(2,1)S(1)}, u32[]{:S(2)}, u32[]{:S(2)}) collective-permute-start(bf16[64,256]{1,0:T(8,128)(2,1)S(1)} %get-tuple-element.52), channel_id=1, source_target_pairs={{0,4},{1,5},{2,6},{3,7},{4,0},{5,1},{6,2},{7,3},{8,12},{9,13},{10,... | collective-permute-start | bytes 98312 | tf_op jit(solution)/shard_map/ppermute | solution.py:380
  42.1 1.3 %collective-permute-start.14 = (bf16[64,256]{1,0:T(8,128)(2,1)S(1)}, bf16[64,256]{1,0:T(8,128)(2,1)S(1)}, u32[]{:S(2)}, u32[]{:S(2)}) collective-permute-start(bf16[64,256]{1,0:T(8,128)(2,1)S(1)} %get-tuple-element.53), channel_id=1, source_target_pairs={{0,6},{1,7},{2,4},{3,5},{4,2},{5,3},{6,0},{7,1},{8,14},{9,15},{10,... | collective-permute-start | bytes 98312 | tf_op jit(solution)/shard_map/ppermute | solution.py:380
  43.5 1.2 %collective-permute-done.13.refs_0_ = bf16[64,256]{1,0:T(8,128)(2,1)S(1)} collective-permute-done((bf16[64,256]{1,0:T(8,128)(2,1)S(1)}, bf16[64,256]{1,0:T(8,128)(2,1)S(1)}, u32[]{:S(2)}, u32[]{:S(2)}) %collective-permute-start.13) | collective-permute-done | bytes 32800 | tf_op jit(solution)/shard_map/ppermute | solution.py:380
  44.7 3.1 %collective-permute-done.14.refs_1_ = bf16[64,256]{1,0:T(8,128)(2,1)S(1)} collective-permute-done((bf16[64,256]{1,0:T(8,128)(2,1)S(1)}, bf16[64,256]{1,0:T(8,128)(2,1)S(1)}, u32[]{:S(2)}, u32[]{:S(2)}) %collective-permute-start.14) | collective-permute-done | bytes 32800 | tf_op jit(solution)/shard_map/ppermute | solution.py:380
  47.9 0.6 %convert_add_fusion = f32[64,256]{1,0:T(8,128)} fusion(bf16[64,256]{1,0:T(8,128)(2,1)S(1)} %after.3, f32[64,256]{1,0:T(8,128)S(1)} %get-tuple-element.49, f32[64,256]{1,0:T(8,128)S(1)} %add_all.1.refs_0_), kind=kLoop, calls=%fused_computation | loop fusion | flops 49152 | bytes 229376 | tf_op jit(solution)/shard_map/add | solution.py:471
  (17 shorter events, 0.3 us)
Async XLA Ops:
  2.3 14.1 %copy-start = (s32[4,8]{1,0:T(4,128)S(1)}, s32[4,8]{1,0:T(4,128)}, u32[]{:S(2)}) copy-start(s32[4,8]{1,0:T(4,128)} %refs_0_.9) | copy-start | bytes 388
  2.3 9.0 %collective-permute-start.1 = (bf16[272,256]{1,0:T(8,128)(2,1)S(1)}, bf16[272,256]{1,0:T(8,128)(2,1)S(1)}, u32[]{:S(2)}, u32[]{:S(2)}) collective-permute-start(bf16[272,256]{1,0:T(8,128)(2,1)S(1)} %get-tuple-element.32.refs_1_), channel_id=1, source_target_pairs={{0,2},{1,3},{2,0},{3,1},{4,6},{5,7},{6,4},{7,5},{8,10},{9,11},{10,... | collective-permute-start | bytes 417800 | tf_op jit(solution)/shard_map/ppermute | solution.py:380
  5.4 9.1 %collective-permute-start.2 = (bf16[272,256]{1,0:T(8,128)(2,1)S(1)}, bf16[272,256]{1,0:T(8,128)(2,1)S(1)}, u32[]{:S(2)}, u32[]{:S(2)}) collective-permute-start(bf16[272,256]{1,0:T(8,128)(2,1)S(1)} %get-tuple-element.32.refs_1_), channel_id=1, source_target_pairs={{0,4},{1,5},{2,6},{3,7},{4,0},{5,1},{6,2},{7,3},{8,12},{9,13},{10,... | collective-permute-start | bytes 417800 | tf_op jit(solution)/shard_map/ppermute | solution.py:380
  8.0 20.7 %collective-permute-start = (bf16[2,256,512]{2,1,0:T(8,128)(2,1)S(1)}, bf16[2,256,512]{2,1,0:T(8,128)(2,1)S(1)}, u32[]{:S(2)}, u32[]{:S(2)}) collective-permute-start(bf16[2,256,512]{2,1,0:T(8,128)(2,1)S(1)} %get-tuple-element.31), channel_id=1, source_target_pairs={{0,16},{8,24},{16,0},{24,8},{1,17},{9,25},{17,1},{25,9},{2,18},{10... | collective-permute-start | bytes 1572872 | tf_op jit(solution)/shard_map/ppermute | solution.py:380
  9.5 6.9 %collective-permute-start.3 = (bf16[272,256]{1,0:T(8,128)(2,1)S(1)}, bf16[272,256]{1,0:T(8,128)(2,1)S(1)}, u32[]{:S(2)}, u32[]{:S(2)}) collective-permute-start(bf16[272,256]{1,0:T(8,128)(2,1)S(1)} %get-tuple-element.32.refs_1_), channel_id=1, source_target_pairs={{0,1},{1,0},{2,3},{3,2},{4,5},{5,4},{6,7},{7,6},{8,9},{9,8},{10,11... | collective-permute-start | bytes 417800 | tf_op jit(solution)/shard_map/ppermute | solution.py:380
  11.2 6.7 %collective-permute-start.4 = (bf16[272,256]{1,0:T(8,128)(2,1)S(1)}, bf16[272,256]{1,0:T(8,128)(2,1)S(1)}, u32[]{:S(2)}, u32[]{:S(2)}) collective-permute-start(bf16[272,256]{1,0:T(8,128)(2,1)S(1)} %collective-permute-done.1.refs_2_), channel_id=1, source_target_pairs={{0,1},{1,0},{2,3},{3,2},{4,5},{5,4},{6,7},{7,6},{8,9},{9,8},{10,11... | collective-permute-start | bytes 417800 | tf_op jit(solution)/shard_map/ppermute | solution.py:380
  14.4 5.1 %collective-permute-start.5 = (bf16[272,256]{1,0:T(8,128)(2,1)S(1)}, bf16[272,256]{1,0:T(8,128)(2,1)S(1)}, u32[]{:S(2)}, u32[]{:S(2)}) collective-permute-start(bf16[272,256]{1,0:T(8,128)(2,1)S(1)} %collective-permute-done.2.refs_3_), channel_id=1, source_target_pairs={{0,2},{1,3},{2,0},{3,1},{4,6},{5,7},{6,4},{7,5},{8,10},{9,11},{10,... | collective-permute-start | bytes 417800 | tf_op jit(solution)/shard_map/ppermute | solution.py:380
  14.9 7.4 %collective-permute-start.6 = (bf16[272,256]{1,0:T(8,128)(2,1)S(1)}, bf16[272,256]{1,0:T(8,128)(2,1)S(1)}, u32[]{:S(2)}, u32[]{:S(2)}) collective-permute-start(bf16[272,256]{1,0:T(8,128)(2,1)S(1)} %collective-permute-done.2.refs_3_), channel_id=1, source_target_pairs={{0,1},{1,0},{2,3},{3,2},{4,5},{5,4},{6,7},{7,6},{8,9},{9,8},{10,11... | collective-permute-start | bytes 417800 | tf_op jit(solution)/shard_map/ppermute | solution.py:380
  19.5 5.1 %collective-permute-start.7 = (bf16[272,256]{1,0:T(8,128)(2,1)S(1)}, bf16[272,256]{1,0:T(8,128)(2,1)S(1)}, u32[]{:S(2)}, u32[]{:S(2)}) collective-permute-start(bf16[272,256]{1,0:T(8,128)(2,1)S(1)} %after.2), channel_id=1, source_target_pairs={{0,1},{1,0},{2,3},{3,2},{4,5},{5,4},{6,7},{7,6},{8,9},{9,8},{10,11... | collective-permute-start | bytes 417800 | tf_op jit(solution)/shard_map/ppermute | solution.py:380
  27.1 5.0 %collective-permute-start.8 = (bf16[1,256,256]{2,1,0:T(8,128)(2,1)S(1)}, bf16[1,256,256]{2,1,0:T(8,128)(2,1)S(1)}, u32[]{:S(2)}, u32[]{:S(2)}) collective-permute-start(bf16[1,256,256]{2,1,0:T(8,128)(2,1)S(1)} %group_grad.1.refs_0_.refs_3_), channel_id=1, source_target_pairs={{0,16},{8,24},{16,0},{24,8},{1,17},{9,25},{17,1},{25,9},{2,18},{10... | collective-permute-start | bytes 393224 | tf_op jit(solution)/shard_map/ppermute | solution.py:380
  32.2 2.4 %collective-permute-start.9 = (bf16[2,256,512]{2,1,0:T(8,128)(2,1)S(1)}, bf16[2,256,512]{2,1,0:T(8,128)(2,1)S(1)}, u32[]{:S(2)}, u32[]{:S(2)}) collective-permute-start(bf16[2,256,512]{2,1,0:T(8,128)(2,1)S(1)} %pack.2), channel_id=1, source_target_pairs={{0,8},{8,0},{16,24},{24,16},{1,9},{9,1},{17,25},{25,17},{2,10},{10... | collective-permute-start | bytes 1572872 | tf_op jit(solution)/shard_map/ppermute | solution.py:380
  32.3 2.2 %collective-permute-start.10 = (bf16[2,256,256]{2,1,0:T(8,128)(2,1)S(1)}, bf16[2,256,256]{2,1,0:T(8,128)(2,1)S(1)}, u32[]{:S(2)}, u32[]{:S(2)}) collective-permute-start(bf16[2,256,256]{2,1,0:T(8,128)(2,1)S(1)} %pack.3), channel_id=1, source_target_pairs={{0,8},{8,0},{16,24},{24,16},{1,9},{9,1},{17,25},{25,17},{2,10},{10... | collective-permute-start | bytes 786440 | tf_op jit(solution)/shard_map/ppermute | solution.py:380
  35.1 4.7 %collective-permute-start.12 = (bf16[2,64,256]{2,1,0:T(8,128)(2,1)S(1)}, bf16[2,64,256]{2,1,0:T(8,128)(2,1)S(1)}, u32[]{:S(2)}, u32[]{:S(2)}) collective-permute-start(bf16[2,64,256]{2,1,0:T(8,128)(2,1)S(1)} %get-tuple-element.51), channel_id=1, source_target_pairs={{0,1},{1,0},{2,3},{3,2},{4,5},{5,4},{6,7},{7,6},{8,9},{9,8},{10,11... | collective-permute-start | bytes 196616 | tf_op jit(solution)/shard_map/ppermute | solution.py:380
  36.6 6.8 %collective-permute-start.11 = (bf16[2,64,256]{2,1,0:T(8,128)(2,1)S(1)}, bf16[2,64,256]{2,1,0:T(8,128)(2,1)S(1)}, u32[]{:S(2)}, u32[]{:S(2)}) collective-permute-start(bf16[2,64,256]{2,1,0:T(8,128)(2,1)S(1)} %get-tuple-element.48), channel_id=1, source_target_pairs={{0,1},{1,0},{2,3},{3,2},{4,5},{5,4},{6,7},{7,6},{8,9},{9,8},{10,11... | collective-permute-start | bytes 196616 | tf_op jit(solution)/shard_map/ppermute | solution.py:380
  39.8 4.9 %collective-permute-start.13 = (bf16[64,256]{1,0:T(8,128)(2,1)S(1)}, bf16[64,256]{1,0:T(8,128)(2,1)S(1)}, u32[]{:S(2)}, u32[]{:S(2)}) collective-permute-start(bf16[64,256]{1,0:T(8,128)(2,1)S(1)} %get-tuple-element.52), channel_id=1, source_target_pairs={{0,4},{1,5},{2,6},{3,7},{4,0},{5,1},{6,2},{7,3},{8,12},{9,13},{10,... | collective-permute-start | bytes 98312 | tf_op jit(solution)/shard_map/ppermute | solution.py:380
  42.1 5.7 %collective-permute-start.14 = (bf16[64,256]{1,0:T(8,128)(2,1)S(1)}, bf16[64,256]{1,0:T(8,128)(2,1)S(1)}, u32[]{:S(2)}, u32[]{:S(2)}) collective-permute-start(bf16[64,256]{1,0:T(8,128)(2,1)S(1)} %get-tuple-element.53), channel_id=1, source_target_pairs={{0,6},{1,7},{2,4},{3,5},{4,2},{5,3},{6,0},{7,1},{8,14},{9,15},{10,... | collective-permute-start | bytes 98312 | tf_op jit(solution)/shard_map/ppermute | solution.py:380
  43.4 4.4 %collective-permute-start.15 = (bf16[64,256]{1,0:T(8,128)(2,1)S(1)}, bf16[64,256]{1,0:T(8,128)(2,1)S(1)}, u32[]{:S(2)}, u32[]{:S(2)}) collective-permute-start(bf16[64,256]{1,0:T(8,128)(2,1)S(1)} %get-tuple-element.54), channel_id=1, source_target_pairs={{0,2},{1,3},{2,0},{3,1},{4,6},{5,7},{6,4},{7,5},{8,10},{9,11},{10,... | collective-permute-start | bytes 98312 | tf_op jit(solution)/shard_map/ppermute | solution.py:380

commit v13 on v12

--- a/solution.py
+++ b/solution.py
@@ -214,7 +214,7 @@
     msgs, refs = dict(zip(known, refs)), refs[len(known):]
     sums_ref, own_ref, refs = refs[0], refs[1], refs[2:]
     stage_refs, refs = refs[:len(stages)], refs[len(stages):]
-    normed_ref, inv_ref, out_ref, kept = refs[-4:]
+    normed_ref, inv_ref, first_ref, second_ref, kept = refs[-5:]
     rows, width = normed_ref.shape
     before = {k: sums_ref[at:at + 1, :] for at, k in enumerate(seen)}
     sums, own_sums, weight, own_weight = pair_sums(
@@ -250,7 +250,9 @@
     grad = both[:rows] + both[rows:]
     normed = normed_ref[...]
     inward = jnp.sum(normed * grad, axis=1, keepdims=True)
-    out_ref[0] = ((grad - normed * inward) * inv_ref[:, 0:1]).astype(jnp.bfloat16)
+    result = ((grad - normed * inward) * inv_ref[:, 0:1]).astype(jnp.bfloat16)
+    first_ref[...] = result[:rows // 2]
+    second_ref[...] = result[rows // 2:]
 
 
 def group_grad(stages, fresh, counts, msgs, state, kept, earlier, normed, inv):
@@ -259,9 +261,9 @@
     rows, width = normed.shape
     return pl.pallas_call(
         functools.partial(grad_kernel, stages, fresh),
-        out_shape=jax.ShapeDtypeStruct((1, rows, width), jnp.bfloat16),
+        out_shape=(jax.ShapeDtypeStruct((rows // 2, width), jnp.bfloat16),) * 2,
         in_specs=[SMEM] + [VMEM] * (len(known) + len(state) + len(kept) + len(earlier) + 2),
-        out_specs=VMEM,
+        out_specs=(VMEM, VMEM),
         scratch_shapes=[pltpu.VMEM((len(fresh), rows, rows), jnp.float32)],
         compiler_params=pltpu.CompilerParams(vmem_limit_bytes=VMEM_LIMIT),
         cost_estimate=pairs_cost(seen, fresh, rows, width),
@@ -275,6 +277,24 @@
         if all(array is not other for other in found):
             found.append(array)
     return found, [next(at for at, other in enumerate(found) if array is other) for array in arrays]
+
+
+def join_kernel(*refs):
+    half = refs[0].shape[0]
+    for at, ref in enumerate(refs[:-1]):
+        refs[-1][at // 2, pl.ds(at % 2 * half, half), :] = ref[...]
+
+
+def join(halves):
+    half, width = halves[0].shape
+    return pl.pallas_call(
+        join_kernel,
+        out_shape=jax.ShapeDtypeStruct((len(halves) // 2, 2 * half, width), halves[0].dtype),
+        in_specs=[VMEM] * len(halves),
+        out_specs=VMEM,
+        compiler_params=pltpu.CompilerParams(vmem_limit_bytes=SMALL_VMEM_LIMIT),
+        name="join",
+    )(*halves)
 
 
 def pack_kernel(places, *refs):
@@ -438,16 +458,18 @@
     add([majors[-1]])
     add([majors[-2] + near for near in range(1, minor)])
     final = [majors[-1] + near for near in range(1, minor)]
-    grad_proj = group_grad(stages, final, row_counts, msgs, state, kept, [], normed, inv)
+    halves = group_grad(stages, final, row_counts, msgs, state, kept, [], normed, inv)
 
     bit = parts // 2
-    grads = [(0, grad_proj, 0), (bit, swap(grad_proj, "dp", bit), 0)]
+    came_halves = [swap(each, "dp", bit) for each in halves]
+    joined = join([*halves, *came_halves])
+    grads = [(0, joined, 0), (bit, joined, 1)]
     blocks = {k: [(0, near_cuts, k), (bit, came, k)] for k in range(bit)}
     bit //= 2
     while bit:
         moving = [(k ^ bit, source ^ bit, array, at) for k in blocks if k & bit for source, array, at in blocks[k]]
         blocks = {k: blocks[k] for k in blocks if not k & bit}
-        passed = swap(pack([each[2:] for each in moving], [grads[-1][1]]), "dp", bit)
+        passed = swap(pack([each[2:] for each in moving], list(came_halves)), "dp", bit)
         for at, (k, source, _, _) in enumerate(moving):
             blocks[k].append((source, passed, at))
         bit //= 2

time: 48.7 us -> 49.9 us (1.025)
  waiting for transfers between devices: 15.5 us -> 17.9 us
  starting transfers between devices: 22 us -> 20.7 us
    ppermute x16 -> x17, waiting for transfers between devices: 15.5 us -> 17.9 us  [swap(): return lax.ppermute(value, axis, [(at, at ^ flip) for at in range(size)])]
    ppermute x16 -> x17, starting transfers between devices: 22 us -> 20.7 us  [swap(): return lax.ppermute(value, axis, [(at, at ^ flip) for at in range(size)])]
    pallas_call x1 -> x2, Pallas kernels: 2.49 us -> 2.5 us  [the longest x1 2.48 us: group_grad(): pl.pallas_call(functools.partial(grad_kernel, stages, fresh), out_shape=(...]
  transfers between devices with their start and end apart: 16 -> 17, of which waited for: 10 -> 9; matrix products, arithmetic and copies ran while one was open for 0% -> 0% of each run, Pallas kernels for 15% -> 15%
where the time goes in v13:
time: 49.9 us; the launch traced here: 49.7 us
  starting transfers between devices  20.7 us (41%)
  waiting for transfers between devices  17.9 us (36%)
  Pallas kernels  10.3 us (21%)
  other arithmetic  0.64 us (1%)
    ppermute x17, starting transfers between devices, swap(): return lax.ppermute(value, axis, [(at, at ^ flip) for at in range(size)])  20.7 us
    ppermute x17, waiting for transfers between devices, swap(): return lax.ppermute(value, axis, [(at, at ^ flip) for at in range(size)])  17.9 us
    pallas_call x4, Pallas kernels, add_pairs(): pl.pallas_call(functools.partial(pairs_kernel, seen, fresh), out_shape=(j...  4.9 us
    pallas_call x1, Pallas kernels, group_grad(): pl.pallas_call(functools.partial(grad_kernel, stages, fresh), out_shape=(...  2.48 us
    pallas_call x1, Pallas kernels, project(): pl.pallas_call(functools.partial(project_kernel, parts), out_shape=(jax.S...  2.27 us
  transfers between devices with their start and end apart: 17, of which 9 were waited for; matrix products, arithmetic and copies ran while one was open for 0% of the time, Pallas kernels for 15%

profile of v13, /device:TPU:0, one launch (start us, length us, event | category | flops | bytes accessed | tf_op | source)
XLA Modules:
  0.0 49.7 jit_solution(8023717370059807117)
XLA Ops:
  0.0 2.3 %project.1 = (bf16[272,256]{1,0:T(8,128)(2,1)S(1)}, f32[256,256]{1,0:T(8,128)S(1)}, f32[256,128]{1,0:T(8,128)S(1)}, bf16[2,256,512]{2,1,0:T(8,128)(2,1)S(1)}, bf16[2,256,512]{2,1,0:T(8,128)(2,1)S(1)}) custom-call(bf16[256,2048]{1,0:T(8,128)(2,1)} %feats_hbm.1, bf16[2048,256]{1,0:T(8,128)(2,1)} %w_hbm.1, s32[1,256]{1,0:T(1,128)} %bitcast.2, s32[1,256]{1,0:T(1,128)} %bitcast.3), custom_call_target="tpu_custom_call" | custom-call | flops 268435456 | bytes 2097152 | tf_op jit(solution)/shard_map/project/pallas_call | solution.py:81
  2.3 3.1 %collective-permute-start.1 = (bf16[272,256]{1,0:T(8,128)(2,1)S(1)}, bf16[272,256]{1,0:T(8,128)(2,1)S(1)}, u32[]{:S(2)}, u32[]{:S(2)}) collective-permute-start(bf16[272,256]{1,0:T(8,128)(2,1)S(1)} %get-tuple-element.34.refs_1_), channel_id=1, source_target_pairs={{0,2},{1,3},{2,0},{3,1},{4,6},{5,7},{6,4},{7,5},{8,10},{9,11},{10,... | collective-permute-start | bytes 417800 | tf_op jit(solution)/shard_map/ppermute | solution.py:400
  5.4 1.5 %collective-permute-start = (bf16[2,256,512]{2,1,0:T(8,128)(2,1)S(1)}, bf16[2,256,512]{2,1,0:T(8,128)(2,1)S(1)}, u32[]{:S(2)}, u32[]{:S(2)}) collective-permute-start(bf16[2,256,512]{2,1,0:T(8,128)(2,1)S(1)} %get-tuple-element.33), channel_id=1, source_target_pairs={{0,16},{8,24},{16,0},{24,8},{1,17},{9,25},{17,1},{25,9},{2,18},{10... | collective-permute-start | bytes 1572872 | tf_op jit(solution)/shard_map/ppermute | solution.py:400
  6.9 2.6 %collective-permute-start.2 = (bf16[272,256]{1,0:T(8,128)(2,1)S(1)}, bf16[272,256]{1,0:T(8,128)(2,1)S(1)}, u32[]{:S(2)}, u32[]{:S(2)}) collective-permute-start(bf16[272,256]{1,0:T(8,128)(2,1)S(1)} %get-tuple-element.34.refs_1_), channel_id=1, source_target_pairs={{0,4},{1,5},{2,6},{3,7},{4,0},{5,1},{6,2},{7,3},{8,12},{9,13},{10,... | collective-permute-start | bytes 417800 | tf_op jit(solution)/shard_map/ppermute | solution.py:400
  9.5 1.5 %collective-permute-start.3 = (bf16[272,256]{1,0:T(8,128)(2,1)S(1)}, bf16[272,256]{1,0:T(8,128)(2,1)S(1)}, u32[]{:S(2)}, u32[]{:S(2)}) collective-permute-start(bf16[272,256]{1,0:T(8,128)(2,1)S(1)} %get-tuple-element.34.refs_1_), channel_id=1, source_target_pairs={{0,1},{1,0},{2,3},{3,2},{4,5},{5,4},{6,7},{7,6},{8,9},{9,8},{10,11... | collective-permute-start | bytes 417800 | tf_op jit(solution)/shard_map/ppermute | solution.py:400
  11.0 0.5 %collective-permute-start.4 = (bf16[272,256]{1,0:T(8,128)(2,1)S(1)}, bf16[272,256]{1,0:T(8,128)(2,1)S(1)}, u32[]{:S(2)}, u32[]{:S(2)}) collective-permute-start(bf16[272,256]{1,0:T(8,128)(2,1)S(1)} %collective-permute-done.1.refs_2_), channel_id=1, source_target_pairs={{0,1},{1,0},{2,3},{3,2},{4,5},{5,4},{6,7},{7,6},{8,9},{9,8},{10,11... | collective-permute-start | bytes 417800 | tf_op jit(solution)/shard_map/ppermute | solution.py:400
  11.5 4.1 %collective-permute-done.2.refs_3_ = bf16[272,256]{1,0:T(8,128)(2,1)S(1)} collective-permute-done((bf16[272,256]{1,0:T(8,128)(2,1)S(1)}, bf16[272,256]{1,0:T(8,128)(2,1)S(1)}, u32[]{:S(2)}, u32[]{:S(2)}) %collective-permute-start.2) | collective-permute-done | bytes 139296 | tf_op jit(solution)/shard_map/ppermute | solution.py:400
  15.6 1.5 %collective-permute-start.6 = (bf16[272,256]{1,0:T(8,128)(2,1)S(1)}, bf16[272,256]{1,0:T(8,128)(2,1)S(1)}, u32[]{:S(2)}, u32[]{:S(2)}) collective-permute-start(bf16[272,256]{1,0:T(8,128)(2,1)S(1)} %collective-permute-done.2.refs_3_), channel_id=1, source_target_pairs={{0,1},{1,0},{2,3},{3,2},{4,5},{5,4},{6,7},{7,6},{8,9},{9,8},{10,11... | collective-permute-start | bytes 417800 | tf_op jit(solution)/shard_map/ppermute | solution.py:400
  17.1 1.4 %add_pairs.4 = (f32[4,256]{1,0:T(4,128)S(1)}, f32[256,128]{1,0:T(8,128)S(1)}, f32[4,256,256]{2,1,0:T(8,128)S(1)}) custom-call(s32[4,8]{1,0:T(4,128)S(1)} %copy-done, bf16[272,256]{1,0:T(8,128)(2,1)S(1)} %get-tuple-element.34.refs_1_, bf16[272,256]{1,0:T(8,128)(2,1)S(1)} %collective-permute-done.1.refs_2_, ...), custom_call_target="tpu_custom_call" | custom-call | flops 335544320 | bytes 1572864 | tf_op jit(solution)/shard_map/add_pairs/pallas_call | solution.py:195
  18.5 1.1 %add_pairs.5 = (f32[5,256]{1,0:T(8,128)S(1)}, f32[256,128]{1,0:T(8,128)S(1)}, f32[1,256,256]{2,1,0:T(8,128)S(1)}) custom-call(s32[4,8]{1,0:T(4,128)S(1)} %copy-done, bf16[272,256]{1,0:T(8,128)(2,1)S(1)} %get-tuple-element.34.refs_1_, bf16[272,256]{1,0:T(8,128)(2,1)S(1)} %collective-permute-done.1.refs_2_, ...), custom_call_target="tpu_custom_call" | custom-call | flops 167772160 | bytes 917504 | tf_op jit(solution)/shard_map/add_pairs/pallas_call | solution.py:195
  19.7 1.0 %collective-permute-done.5.value_ref.refs_6_ = bf16[272,256]{1,0:T(8,128)(2,1)S(1)} collective-permute-done((bf16[272,256]{1,0:T(8,128)(2,1)S(1)}, bf16[272,256]{1,0:T(8,128)(2,1)S(1)}, u32[]{:S(2)}, u32[]{:S(2)}) %collective-permute-start.5) | collective-permute-done | bytes 139296 | tf_op jit(solution)/shard_map/ppermute | solution.py:400
  20.7 1.6 %collective-permute-start.7 = (bf16[272,256]{1,0:T(8,128)(2,1)S(1)}, bf16[272,256]{1,0:T(8,128)(2,1)S(1)}, u32[]{:S(2)}, u32[]{:S(2)}) collective-permute-start(bf16[272,256]{1,0:T(8,128)(2,1)S(1)} %after.2), channel_id=1, source_target_pairs={{0,1},{1,0},{2,3},{3,2},{4,5},{5,4},{6,7},{7,6},{8,9},{9,8},{10,11... | collective-permute-start | bytes 417800 | tf_op jit(solution)/shard_map/ppermute | solution.py:400
  22.3 1.2 %add_pairs.6 = (f32[6,256]{1,0:T(8,128)S(1)}, f32[256,128]{1,0:T(8,128)S(1)}, f32[1,256,256]{2,1,0:T(8,128)S(1)}) custom-call(s32[4,8]{1,0:T(4,128)S(1)} %copy-done, bf16[272,256]{1,0:T(8,128)(2,1)S(1)} %get-tuple-element.34.refs_1_, bf16[272,256]{1,0:T(8,128)(2,1)S(1)} %collective-permute-done.1.refs_2_, ...), custom_call_target="tpu_custom_call" | custom-call | flops 201326592 | bytes 1048576 | tf_op jit(solution)/shard_map/add_pairs/pallas_call | solution.py:195
  23.4 1.2 %add_pairs.7 = (f32[7,256]{1,0:T(8,128)S(1)}, f32[256,128]{1,0:T(8,128)S(1)}, f32[1,256,256]{2,1,0:T(8,128)S(1)}) custom-call(s32[4,8]{1,0:T(4,128)S(1)} %copy-done, bf16[272,256]{1,0:T(8,128)(2,1)S(1)} %get-tuple-element.34.refs_1_, bf16[272,256]{1,0:T(8,128)(2,1)S(1)} %collective-permute-done.1.refs_2_, ...), custom_call_target="tpu_custom_call" | custom-call | flops 234881024 | bytes 1179648 | tf_op jit(solution)/shard_map/add_pairs/pallas_call | solution.py:195
  24.7 1.2 %collective-permute-done.7.refs_8_ = bf16[272,256]{1,0:T(8,128)(2,1)S(1)} collective-permute-done((bf16[272,256]{1,0:T(8,128)(2,1)S(1)}, bf16[272,256]{1,0:T(8,128)(2,1)S(1)}, u32[]{:S(2)}, u32[]{:S(2)}) %collective-permute-start.7) | collective-permute-done | bytes 139296 | tf_op jit(solution)/shard_map/ppermute | solution.py:400
  25.8 2.5 %group_grad.1 = (bf16[128,256]{1,0:T(8,128)(2,1)S(1)}, bf16[128,256]{1,0:T(8,128)(2,1)S(1)}) custom-call(s32[4,8]{1,0:T(4,128)S(1)} %copy-done, bf16[272,256]{1,0:T(8,128)(2,1)S(1)} %get-tuple-element.34.refs_1_, bf16[272,256]{1,0:T(8,128)(2,1)S(1)} %collective-permute-done.1.refs_2_, bf16[272,256]{1,0:T(8,128)(2,1)S(1)} %collective-permute-done.2.refs_3_, ...), custom_call_target="tpu_custom_call" | custom-call | flops 268435456 | bytes 1310720 | tf_op jit(solution)/shard_map/group_grad/pallas_call | solution.py:262
  28.3 0.7 %collective-permute-start.8 = (bf16[128,256]{1,0:T(8,128)(2,1)S(1)}, bf16[128,256]{1,0:T(8,128)(2,1)S(1)}, u32[]{:S(2)}, u32[]{:S(2)}) collective-permute-start(bf16[128,256]{1,0:T(8,128)(2,1)S(1)} %get-tuple-element.49.refs_0_), channel_id=1, source_target_pairs={{0,16},{8,24},{16,0},{24,8},{1,17},{9,25},{17,1},{25,9},{2,18},{10... | collective-permute-start | bytes 196616 | tf_op jit(solution)/shard_map/ppermute | solution.py:400
  29.0 1.4 %collective-permute-start.9 = (bf16[128,256]{1,0:T(8,128)(2,1)S(1)}, bf16[128,256]{1,0:T(8,128)(2,1)S(1)}, u32[]{:S(2)}, u32[]{:S(2)}) collective-permute-start(bf16[128,256]{1,0:T(8,128)(2,1)S(1)} %get-tuple-element.50.refs_1_), channel_id=1, source_target_pairs={{0,16},{8,24},{16,0},{24,8},{1,17},{9,25},{17,1},{25,9},{2,18},{10... | collective-permute-start | bytes 196616 | tf_op jit(solution)/shard_map/ppermute | solution.py:400
  30.4 2.2 %collective-permute-done.8.refs_2_ = bf16[128,256]{1,0:T(8,128)(2,1)S(1)} collective-permute-done((bf16[128,256]{1,0:T(8,128)(2,1)S(1)}, bf16[128,256]{1,0:T(8,128)(2,1)S(1)}, u32[]{:S(2)}, u32[]{:S(2)}) %collective-permute-start.8) | collective-permute-done | bytes 65568 | tf_op jit(solution)/shard_map/ppermute | solution.py:400
  32.7 0.7 %collective-permute-done.9.refs_3_ = bf16[128,256]{1,0:T(8,128)(2,1)S(1)} collective-permute-done((bf16[128,256]{1,0:T(8,128)(2,1)S(1)}, bf16[128,256]{1,0:T(8,128)(2,1)S(1)}, u32[]{:S(2)}, u32[]{:S(2)}) %collective-permute-start.9) | collective-permute-done | bytes 65568 | tf_op jit(solution)/shard_map/ppermute | solution.py:400
  33.5 0.6 %collective-permute-start.11 = (bf16[2,256,256]{2,1,0:T(8,128)(2,1)S(1)}, bf16[2,256,256]{2,1,0:T(8,128)(2,1)S(1)}, u32[]{:S(2)}, u32[]{:S(2)}) collective-permute-start(bf16[2,256,256]{2,1,0:T(8,128)(2,1)S(1)} %pack.3), channel_id=1, source_target_pairs={{0,8},{8,0},{16,24},{24,16},{1,9},{9,1},{17,25},{25,17},{2,10},{10... | collective-permute-start | bytes 786440 | tf_op jit(solution)/shard_map/ppermute | solution.py:400
  34.1 1.7 %collective-permute-done.11.refs_4_ = bf16[2,256,256]{2,1,0:T(8,128)(2,1)S(1)} collective-permute-done((bf16[2,256,256]{2,1,0:T(8,128)(2,1)S(1)}, bf16[2,256,256]{2,1,0:T(8,128)(2,1)S(1)}, u32[]{:S(2)}, u32[]{:S(2)}) %collective-permute-start.11) | collective-permute-done | bytes 262176 | tf_op jit(solution)/shard_map/ppermute | solution.py:400
  35.8 0.5 %weight_grad.1 = (f32[2,64,256]{2,1,0:T(8,128)S(1)}, f32[2,64,256]{2,1,0:T(8,128)S(1)}, bf16[2,64,256]{2,1,0:T(8,128)(2,1)S(1)}, bf16[2,64,256]{2,1,0:T(8,128)(2,1)S(1)}) custom-call(bf16[2,256,512]{2,1,0:T(8,128)(2,1)S(1)} %get-tuple-element.32.refs_0_, bf16[2,256,512]{2,1,0:T(8,128)(2,1)S(1)} %collective-permute-done.10.refs_1_, ...), custom_call_target="tpu_custom_call" | custom-call | flops 268435456 | bytes 1048576 | tf_op jit(solution)/shard_map/weight_grad/pallas_call | solution.py:343
  36.3 1.6 %collective-permute-start.13 = (bf16[2,64,256]{2,1,0:T(8,128)(2,1)S(1)}, bf16[2,64,256]{2,1,0:T(8,128)(2,1)S(1)}, u32[]{:S(2)}, u32[]{:S(2)}) collective-permute-start(bf16[2,64,256]{2,1,0:T(8,128)(2,1)S(1)} %get-tuple-element.55), channel_id=1, source_target_pairs={{0,1},{1,0},{2,3},{3,2},{4,5},{5,4},{6,7},{7,6},{8,9},{9,8},{10,11... | collective-permute-start | bytes 196616 | tf_op jit(solution)/shard_map/ppermute | solution.py:400
  37.9 0.5 %collective-permute-start.12 = (bf16[2,64,256]{2,1,0:T(8,128)(2,1)S(1)}, bf16[2,64,256]{2,1,0:T(8,128)(2,1)S(1)}, u32[]{:S(2)}, u32[]{:S(2)}) collective-permute-start(bf16[2,64,256]{2,1,0:T(8,128)(2,1)S(1)} %get-tuple-element.52), channel_id=1, source_target_pairs={{0,1},{1,0},{2,3},{3,2},{4,5},{5,4},{6,7},{7,6},{8,9},{9,8},{10,11... | collective-permute-start | bytes 196616 | tf_op jit(solution)/shard_map/ppermute | solution.py:400
  38.4 2.6 %collective-permute-done.13.refs_0_ = bf16[2,64,256]{2,1,0:T(8,128)(2,1)S(1)} collective-permute-done((bf16[2,64,256]{2,1,0:T(8,128)(2,1)S(1)}, bf16[2,64,256]{2,1,0:T(8,128)(2,1)S(1)}, u32[]{:S(2)}, u32[]{:S(2)}) %collective-permute-start.13) | collective-permute-done | bytes 65568 | tf_op jit(solution)/shard_map/ppermute | solution.py:400
  41.0 2.3 %collective-permute-start.14 = (bf16[64,256]{1,0:T(8,128)(2,1)S(1)}, bf16[64,256]{1,0:T(8,128)(2,1)S(1)}, u32[]{:S(2)}, u32[]{:S(2)}) collective-permute-start(bf16[64,256]{1,0:T(8,128)(2,1)S(1)} %get-tuple-element.56), channel_id=1, source_target_pairs={{0,4},{1,5},{2,6},{3,7},{4,0},{5,1},{6,2},{7,3},{8,12},{9,13},{10,... | collective-permute-start | bytes 98312 | tf_op jit(solution)/shard_map/ppermute | solution.py:400
  43.3 1.3 %collective-permute-start.15 = (bf16[64,256]{1,0:T(8,128)(2,1)S(1)}, bf16[64,256]{1,0:T(8,128)(2,1)S(1)}, u32[]{:S(2)}, u32[]{:S(2)}) collective-permute-start(bf16[64,256]{1,0:T(8,128)(2,1)S(1)} %get-tuple-element.57), channel_id=1, source_target_pairs={{0,6},{1,7},{2,4},{3,5},{4,2},{5,3},{6,0},{7,1},{8,14},{9,15},{10,... | collective-permute-start | bytes 98312 | tf_op jit(solution)/shard_map/ppermute | solution.py:400
  44.6 0.1 collective-permute-start.16
  44.7 1.2 %collective-permute-done.14.refs_0_ = bf16[64,256]{1,0:T(8,128)(2,1)S(1)} collective-permute-done((bf16[64,256]{1,0:T(8,128)(2,1)S(1)}, bf16[64,256]{1,0:T(8,128)(2,1)S(1)}, u32[]{:S(2)}, u32[]{:S(2)}) %collective-permute-start.14) | collective-permute-done | bytes 32800 | tf_op jit(solution)/shard_map/ppermute | solution.py:400
  45.9 3.1 %collective-permute-done.15.refs_1_ = bf16[64,256]{1,0:T(8,128)(2,1)S(1)} collective-permute-done((bf16[64,256]{1,0:T(8,128)(2,1)S(1)}, bf16[64,256]{1,0:T(8,128)(2,1)S(1)}, u32[]{:S(2)}, u32[]{:S(2)}) %collective-permute-start.15) | collective-permute-done | bytes 32800 | tf_op jit(solution)/shard_map/ppermute | solution.py:400
  49.1 0.6 %convert_add_fusion = f32[64,256]{1,0:T(8,128)} fusion(bf16[64,256]{1,0:T(8,128)(2,1)S(1)} %after.3, f32[64,256]{1,0:T(8,128)S(1)} %get-tuple-element.53, f32[64,256]{1,0:T(8,128)S(1)} %add_all.1.refs_0_), kind=kLoop, calls=%fused_computation | loop fusion | flops 49152 | bytes 229376 | tf_op jit(solution)/shard_map/add | solution.py:493
  (20 shorter events, 0.2 us)
Async XLA Ops:
  2.3 14.9 %copy-start = (s32[4,8]{1,0:T(4,128)S(1)}, s32[4,8]{1,0:T(4,128)}, u32[]{:S(2)}) copy-start(s32[4,8]{1,0:T(4,128)} %refs_0_.9) | copy-start | bytes 388
  2.3 8.7 %collective-permute-start.1 = (bf16[272,256]{1,0:T(8,128)(2,1)S(1)}, bf16[272,256]{1,0:T(8,128)(2,1)S(1)}, u32[]{:S(2)}, u32[]{:S(2)}) collective-permute-start(bf16[272,256]{1,0:T(8,128)(2,1)S(1)} %get-tuple-element.34.refs_1_), channel_id=1, source_target_pairs={{0,2},{1,3},{2,0},{3,1},{4,6},{5,7},{6,4},{7,5},{8,10},{9,11},{10,... | collective-permute-start | bytes 417800 | tf_op jit(solution)/shard_map/ppermute | solution.py:400
  5.4 28.0 %collective-permute-start = (bf16[2,256,512]{2,1,0:T(8,128)(2,1)S(1)}, bf16[2,256,512]{2,1,0:T(8,128)(2,1)S(1)}, u32[]{:S(2)}, u32[]{:S(2)}) collective-permute-start(bf16[2,256,512]{2,1,0:T(8,128)(2,1)S(1)} %get-tuple-element.33), channel_id=1, source_target_pairs={{0,16},{8,24},{16,0},{24,8},{1,17},{9,25},{17,1},{25,9},{2,18},{10... | collective-permute-start | bytes 1572872 | tf_op jit(solution)/shard_map/ppermute | solution.py:400
  6.9 8.7 %collective-permute-start.2 = (bf16[272,256]{1,0:T(8,128)(2,1)S(1)}, bf16[272,256]{1,0:T(8,128)(2,1)S(1)}, u32[]{:S(2)}, u32[]{:S(2)}) collective-permute-start(bf16[272,256]{1,0:T(8,128)(2,1)S(1)} %get-tuple-element.34.refs_1_), channel_id=1, source_target_pairs={{0,4},{1,5},{2,6},{3,7},{4,0},{5,1},{6,2},{7,3},{8,12},{9,13},{10,... | collective-permute-start | bytes 417800 | tf_op jit(solution)/shard_map/ppermute | solution.py:400
  9.5 7.6 %collective-permute-start.3 = (bf16[272,256]{1,0:T(8,128)(2,1)S(1)}, bf16[272,256]{1,0:T(8,128)(2,1)S(1)}, u32[]{:S(2)}, u32[]{:S(2)}) collective-permute-start(bf16[272,256]{1,0:T(8,128)(2,1)S(1)} %get-tuple-element.34.refs_1_), channel_id=1, source_target_pairs={{0,1},{1,0},{2,3},{3,2},{4,5},{5,4},{6,7},{7,6},{8,9},{9,8},{10,11... | collective-permute-start | bytes 417800 | tf_op jit(solution)/shard_map/ppermute | solution.py:400
  11.0 7.6 %collective-permute-start.4 = (bf16[272,256]{1,0:T(8,128)(2,1)S(1)}, bf16[272,256]{1,0:T(8,128)(2,1)S(1)}, u32[]{:S(2)}, u32[]{:S(2)}) collective-permute-start(bf16[272,256]{1,0:T(8,128)(2,1)S(1)} %collective-permute-done.1.refs_2_), channel_id=1, source_target_pairs={{0,1},{1,0},{2,3},{3,2},{4,5},{5,4},{6,7},{7,6},{8,9},{9,8},{10,11... | collective-permute-start | bytes 417800 | tf_op jit(solution)/shard_map/ppermute | solution.py:400
  15.6 5.1 %collective-permute-start.5 = (bf16[272,256]{1,0:T(8,128)(2,1)S(1)}, bf16[272,256]{1,0:T(8,128)(2,1)S(1)}, u32[]{:S(2)}, u32[]{:S(2)}) collective-permute-start(bf16[272,256]{1,0:T(8,128)(2,1)S(1)} %collective-permute-done.2.refs_3_), channel_id=1, source_target_pairs={{0,2},{1,3},{2,0},{3,1},{4,6},{5,7},{6,4},{7,5},{8,10},{9,11},{10,... | collective-permute-start | bytes 417800 | tf_op jit(solution)/shard_map/ppermute | solution.py:400
  15.6 7.8 %collective-permute-start.6 = (bf16[272,256]{1,0:T(8,128)(2,1)S(1)}, bf16[272,256]{1,0:T(8,128)(2,1)S(1)}, u32[]{:S(2)}, u32[]{:S(2)}) collective-permute-start(bf16[272,256]{1,0:T(8,128)(2,1)S(1)} %collective-permute-done.2.refs_3_), channel_id=1, source_target_pairs={{0,1},{1,0},{2,3},{3,2},{4,5},{5,4},{6,7},{7,6},{8,9},{9,8},{10,11... | collective-permute-start | bytes 417800 | tf_op jit(solution)/shard_map/ppermute | solution.py:400
  20.7 5.1 %collective-permute-start.7 = (bf16[272,256]{1,0:T(8,128)(2,1)S(1)}, bf16[272,256]{1,0:T(8,128)(2,1)S(1)}, u32[]{:S(2)}, u32[]{:S(2)}) collective-permute-start(bf16[272,256]{1,0:T(8,128)(2,1)S(1)} %after.2), channel_id=1, source_target_pairs={{0,1},{1,0},{2,3},{3,2},{4,5},{5,4},{6,7},{7,6},{8,9},{9,8},{10,11... | collective-permute-start | bytes 417800 | tf_op jit(solution)/shard_map/ppermute | solution.py:400
  28.3 4.3 %collective-permute-start.8 = (bf16[128,256]{1,0:T(8,128)(2,1)S(1)}, bf16[128,256]{1,0:T(8,128)(2,1)S(1)}, u32[]{:S(2)}, u32[]{:S(2)}) collective-permute-start(bf16[128,256]{1,0:T(8,128)(2,1)S(1)} %get-tuple-element.49.refs_0_), channel_id=1, source_target_pairs={{0,16},{8,24},{16,0},{24,8},{1,17},{9,25},{17,1},{25,9},{2,18},{10... | collective-permute-start | bytes 196616 | tf_op jit(solution)/shard_map/ppermute | solution.py:400
  29.0 4.4 %collective-permute-start.9 = (bf16[128,256]{1,0:T(8,128)(2,1)S(1)}, bf16[128,256]{1,0:T(8,128)(2,1)S(1)}, u32[]{:S(2)}, u32[]{:S(2)}) collective-permute-start(bf16[128,256]{1,0:T(8,128)(2,1)S(1)} %get-tuple-element.50.refs_1_), channel_id=1, source_target_pairs={{0,16},{8,24},{16,0},{24,8},{1,17},{9,25},{17,1},{25,9},{2,18},{10... | collective-permute-start | bytes 196616 | tf_op jit(solution)/shard_map/ppermute | solution.py:400
  33.4 2.4 %collective-permute-start.10 = (bf16[2,256,512]{2,1,0:T(8,128)(2,1)S(1)}, bf16[2,256,512]{2,1,0:T(8,128)(2,1)S(1)}, u32[]{:S(2)}, u32[]{:S(2)}) collective-permute-start(bf16[2,256,512]{2,1,0:T(8,128)(2,1)S(1)} %pack.2), channel_id=1, source_target_pairs={{0,8},{8,0},{16,24},{24,16},{1,9},{9,1},{17,25},{25,17},{2,10},{10... | collective-permute-start | bytes 1572872 | tf_op jit(solution)/shard_map/ppermute | solution.py:400
  33.5 2.2 %collective-permute-start.11 = (bf16[2,256,256]{2,1,0:T(8,128)(2,1)S(1)}, bf16[2,256,256]{2,1,0:T(8,128)(2,1)S(1)}, u32[]{:S(2)}, u32[]{:S(2)}) collective-permute-start(bf16[2,256,256]{2,1,0:T(8,128)(2,1)S(1)} %pack.3), channel_id=1, source_target_pairs={{0,8},{8,0},{16,24},{24,16},{1,9},{9,1},{17,25},{25,17},{2,10},{10... | collective-permute-start | bytes 786440 | tf_op jit(solution)/shard_map/ppermute | solution.py:400
  36.3 4.7 %collective-permute-start.13 = (bf16[2,64,256]{2,1,0:T(8,128)(2,1)S(1)}, bf16[2,64,256]{2,1,0:T(8,128)(2,1)S(1)}, u32[]{:S(2)}, u32[]{:S(2)}) collective-permute-start(bf16[2,64,256]{2,1,0:T(8,128)(2,1)S(1)} %get-tuple-element.55), channel_id=1, source_target_pairs={{0,1},{1,0},{2,3},{3,2},{4,5},{5,4},{6,7},{7,6},{8,9},{9,8},{10,11... | collective-permute-start | bytes 196616 | tf_op jit(solution)/shard_map/ppermute | solution.py:400
  37.9 6.8 %collective-permute-start.12 = (bf16[2,64,256]{2,1,0:T(8,128)(2,1)S(1)}, bf16[2,64,256]{2,1,0:T(8,128)(2,1)S(1)}, u32[]{:S(2)}, u32[]{:S(2)}) collective-permute-start(bf16[2,64,256]{2,1,0:T(8,128)(2,1)S(1)} %get-tuple-element.52), channel_id=1, source_target_pairs={{0,1},{1,0},{2,3},{3,2},{4,5},{5,4},{6,7},{7,6},{8,9},{9,8},{10,11... | collective-permute-start | bytes 196616 | tf_op jit(solution)/shard_map/ppermute | solution.py:400
  41.0 4.9 %collective-permute-start.14 = (bf16[64,256]{1,0:T(8,128)(2,1)S(1)}, bf16[64,256]{1,0:T(8,128)(2,1)S(1)}, u32[]{:S(2)}, u32[]{:S(2)}) collective-permute-start(bf16[64,256]{1,0:T(8,128)(2,1)S(1)} %get-tuple-element.56), channel_id=1, source_target_pairs={{0,4},{1,5},{2,6},{3,7},{4,0},{5,1},{6,2},{7,3},{8,12},{9,13},{10,... | collective-permute-start | bytes 98312 | tf_op jit(solution)/shard_map/ppermute | solution.py:400
  43.3 5.7 %collective-permute-start.15 = (bf16[64,256]{1,0:T(8,128)(2,1)S(1)}, bf16[64,256]{1,0:T(8,128)(2,1)S(1)}, u32[]{:S(2)}, u32[]{:S(2)}) collective-permute-start(bf16[64,256]{1,0:T(8,128)(2,1)S(1)} %get-tuple-element.57), channel_id=1, source_target_pairs={{0,6},{1,7},{2,4},{3,5},{4,2},{5,3},{6,0},{7,1},{8,14},{9,15},{10,... | collective-permute-start | bytes 98312 | tf_op jit(solution)/shard_map/ppermute | solution.py:400
  44.6 4.4 %collective-permute-start.16 = (bf16[64,256]{1,0:T(8,128)(2,1)S(1)}, bf16[64,256]{1,0:T(8,128)(2,1)S(1)}, u32[]{:S(2)}, u32[]{:S(2)}) collective-permute-start(bf16[64,256]{1,0:T(8,128)(2,1)S(1)} %get-tuple-element.58), channel_id=1, source_target_pairs={{0,2},{1,3},{2,0},{3,1},{4,6},{5,7},{6,4},{7,5},{8,10},{9,11},{10,... | collective-permute-start | bytes 98312 | tf_op jit(solution)/shard_map/ppermute | solution.py:400

commit v14 on v12

--- a/solution.py
+++ b/solution.py
@@ -43,22 +43,26 @@
     )
     for copy in small:
         copy.start()
+    halves = sems.shape[1] // parts
+    part = step // halves
     copies = []
-    for k in range(parts):
-        first = pl.multiple_of((me ^ k) * step, step)
-        cut = pl.ds(first, step)
+    for at in range(parts * halves):
+        k, half = at // halves, at % halves
+        first = pl.multiple_of((me ^ k) * step + half * part, part)
+        feats_part = cuts[k].at[:, pl.ds(half * part, part)]
+        w_part = w_v.at[pl.ds(at * part, part), :]
         pair = (
-            pltpu.make_async_copy(feats_hbm.at[:, cut], cuts[k], sems.at[0, k]),
-            pltpu.make_async_copy(w_hbm.at[cut, :], w_v.at[pl.ds(k * step, step), :], sems.at[1, k]),
+            pltpu.make_async_copy(feats_hbm.at[:, pl.ds(first, part)], feats_part, sems.at[0, at]),
+            pltpu.make_async_copy(w_hbm.at[pl.ds(first, part), :], w_part, sems.at[1, at]),
         )
         pair[0].start()
         pair[1].start()
-        copies.append(pair)
+        copies.append((pair, feats_part, w_part))
     projected = jnp.zeros((rows, width), jnp.float32)
-    for k in range(parts):
-        copies[k][0].wait()
-        copies[k][1].wait()
-        projected = projected + f32_dot(cuts[k][...], w_v[pl.ds(k * step, step), :], ((1,), (0,)))
+    for pair, feats_part, w_part in copies:
+        pair[0].wait()
+        pair[1].wait()
+        projected = projected + f32_dot(feats_part[...], w_part[...], ((1,), (0,)))
     for copy in small:
         copy.wait()
     partners = partners_ref[...]
@@ -78,6 +82,7 @@
 def project(feats, tower_w, partners, buckets, parts):
     rows, din = feats.shape
     width = tower_w.shape[1]
+    halves = 2 if din // parts % 256 == 0 else 1
     return pl.pallas_call(
         functools.partial(project_kernel, parts),
         out_shape=(
@@ -92,7 +97,7 @@
             pltpu.VMEM((din, width), jnp.bfloat16),
             pltpu.VMEM((1, rows), jnp.int32),
             pltpu.VMEM((1, rows), jnp.int32),
-            pltpu.SemaphoreType.DMA((2, parts)),
+            pltpu.SemaphoreType.DMA((2, parts * halves)),
             pltpu.SemaphoreType.DMA((2,)),
         ],
         compiler_params=pltpu.CompilerParams(vmem_limit_bytes=VMEM_LIMIT),

time: 48.7 us -> 48.8 us (level)
  no operation moved by 1% of the time
where the time goes in v14:
time: 48.8 us; the launch traced here: 48.6 us
  starting transfers between devices  21.9 us (45%)
  waiting for transfers between devices  15.5 us (32%)
  Pallas kernels  10.4 us (21%)
  other arithmetic  0.64 us (1%)
    ppermute x16, starting transfers between devices, swap(): return lax.ppermute(value, axis, [(at, at ^ flip) for at in range(size)])  21.9 us
    ppermute x16, waiting for transfers between devices, swap(): return lax.ppermute(value, axis, [(at, at ^ flip) for at in range(size)])  15.5 us
    pallas_call x4, Pallas kernels, add_pairs(): pl.pallas_call(functools.partial(pairs_kernel, seen, fresh), out_shape=(j...  4.89 us
    pallas_call x1, Pallas kernels, group_grad(): pl.pallas_call(functools.partial(grad_kernel, stages, fresh), out_shape=j...  2.49 us
    pallas_call x1, Pallas kernels, project(): pl.pallas_call(functools.partial(project_kernel, parts), out_shape=(jax.S...  2.39 us
  transfers between devices with their start and end apart: 16, of which 10 were waited for; matrix products, arithmetic and copies ran while one was open for 0% of the time, Pallas kernels for 15%

profile of v14, /device:TPU:0, one launch (start us, length us, event | category | flops | bytes accessed | tf_op | source)
XLA Modules:
  0.0 48.6 jit_solution(11923195396383116134)
XLA Ops:
  0.0 2.4 %project.1 = (bf16[272,256]{1,0:T(8,128)(2,1)S(1)}, f32[256,256]{1,0:T(8,128)S(1)}, f32[256,128]{1,0:T(8,128)S(1)}, bf16[2,256,512]{2,1,0:T(8,128)(2,1)S(1)}, bf16[2,256,512]{2,1,0:T(8,128)(2,1)S(1)}) custom-call(bf16[256,2048]{1,0:T(8,128)(2,1)} %feats_hbm.1, bf16[2048,256]{1,0:T(8,128)(2,1)} %w_hbm.1, s32[1,256]{1,0:T(1,128)} %bitcast.2, s32[1,256]{1,0:T(1,128)} %bitcast.3), custom_call_target="tpu_custom_call" | custom-call | flops 268435456 | bytes 2097152 | tf_op jit(solution)/shard_map/project/pallas_call | solution.py:86
  2.4 3.1 %collective-permute-start.1 = (bf16[272,256]{1,0:T(8,128)(2,1)S(1)}, bf16[272,256]{1,0:T(8,128)(2,1)S(1)}, u32[]{:S(2)}, u32[]{:S(2)}) collective-permute-start(bf16[272,256]{1,0:T(8,128)(2,1)S(1)} %get-tuple-element.32.refs_1_), channel_id=1, source_target_pairs={{0,2},{1,3},{2,0},{3,1},{4,6},{5,7},{6,4},{7,5},{8,10},{9,11},{10,... | collective-permute-start | bytes 417800 | tf_op jit(solution)/shard_map/ppermute | solution.py:385
  5.5 2.6 %collective-permute-start.2 = (bf16[272,256]{1,0:T(8,128)(2,1)S(1)}, bf16[272,256]{1,0:T(8,128)(2,1)S(1)}, u32[]{:S(2)}, u32[]{:S(2)}) collective-permute-start(bf16[272,256]{1,0:T(8,128)(2,1)S(1)} %get-tuple-element.32.refs_1_), channel_id=1, source_target_pairs={{0,4},{1,5},{2,6},{3,7},{4,0},{5,1},{6,2},{7,3},{8,12},{9,13},{10,... | collective-permute-start | bytes 417800 | tf_op jit(solution)/shard_map/ppermute | solution.py:385
  8.1 1.5 %collective-permute-start = (bf16[2,256,512]{2,1,0:T(8,128)(2,1)S(1)}, bf16[2,256,512]{2,1,0:T(8,128)(2,1)S(1)}, u32[]{:S(2)}, u32[]{:S(2)}) collective-permute-start(bf16[2,256,512]{2,1,0:T(8,128)(2,1)S(1)} %get-tuple-element.31), channel_id=1, source_target_pairs={{0,16},{8,24},{16,0},{24,8},{1,17},{9,25},{17,1},{25,9},{2,18},{10... | collective-permute-start | bytes 1572872 | tf_op jit(solution)/shard_map/ppermute | solution.py:385
  9.6 1.5 %collective-permute-start.3 = (bf16[272,256]{1,0:T(8,128)(2,1)S(1)}, bf16[272,256]{1,0:T(8,128)(2,1)S(1)}, u32[]{:S(2)}, u32[]{:S(2)}) collective-permute-start(bf16[272,256]{1,0:T(8,128)(2,1)S(1)} %get-tuple-element.32.refs_1_), channel_id=1, source_target_pairs={{0,1},{1,0},{2,3},{3,2},{4,5},{5,4},{6,7},{7,6},{8,9},{9,8},{10,11... | collective-permute-start | bytes 417800 | tf_op jit(solution)/shard_map/ppermute | solution.py:385
  11.1 0.3 collective-permute-done.1.refs_2_
  11.4 1.8 %collective-permute-start.4 = (bf16[272,256]{1,0:T(8,128)(2,1)S(1)}, bf16[272,256]{1,0:T(8,128)(2,1)S(1)}, u32[]{:S(2)}, u32[]{:S(2)}) collective-permute-start(bf16[272,256]{1,0:T(8,128)(2,1)S(1)} %collective-permute-done.1.refs_2_), channel_id=1, source_target_pairs={{0,1},{1,0},{2,3},{3,2},{4,5},{5,4},{6,7},{7,6},{8,9},{9,8},{10,11... | collective-permute-start | bytes 417800 | tf_op jit(solution)/shard_map/ppermute | solution.py:385
  13.2 1.4 %collective-permute-done.2.refs_3_ = bf16[272,256]{1,0:T(8,128)(2,1)S(1)} collective-permute-done((bf16[272,256]{1,0:T(8,128)(2,1)S(1)}, bf16[272,256]{1,0:T(8,128)(2,1)S(1)}, u32[]{:S(2)}, u32[]{:S(2)}) %collective-permute-start.2) | collective-permute-done | bytes 139296 | tf_op jit(solution)/shard_map/ppermute | solution.py:385
  14.6 0.4 collective-permute-start.5
  15.0 1.5 %collective-permute-start.6 = (bf16[272,256]{1,0:T(8,128)(2,1)S(1)}, bf16[272,256]{1,0:T(8,128)(2,1)S(1)}, u32[]{:S(2)}, u32[]{:S(2)}) collective-permute-start(bf16[272,256]{1,0:T(8,128)(2,1)S(1)} %collective-permute-done.2.refs_3_), channel_id=1, source_target_pairs={{0,1},{1,0},{2,3},{3,2},{4,5},{5,4},{6,7},{7,6},{8,9},{9,8},{10,11... | collective-permute-start | bytes 417800 | tf_op jit(solution)/shard_map/ppermute | solution.py:385
  16.5 1.4 %add_pairs.4 = (f32[4,256]{1,0:T(4,128)S(1)}, f32[256,128]{1,0:T(8,128)S(1)}, f32[4,256,256]{2,1,0:T(8,128)S(1)}) custom-call(s32[4,8]{1,0:T(4,128)S(1)} %copy-done, bf16[272,256]{1,0:T(8,128)(2,1)S(1)} %get-tuple-element.32.refs_1_, bf16[272,256]{1,0:T(8,128)(2,1)S(1)} %collective-permute-done.1.refs_2_, ...), custom_call_target="tpu_custom_call" | custom-call | flops 335544320 | bytes 1572864 | tf_op jit(solution)/shard_map/add_pairs/pallas_call | solution.py:200
  17.9 0.2 collective-permute-done.4.refs_5_
  18.1 1.1 %add_pairs.5 = (f32[5,256]{1,0:T(8,128)S(1)}, f32[256,128]{1,0:T(8,128)S(1)}, f32[1,256,256]{2,1,0:T(8,128)S(1)}) custom-call(s32[4,8]{1,0:T(4,128)S(1)} %copy-done, bf16[272,256]{1,0:T(8,128)(2,1)S(1)} %get-tuple-element.32.refs_1_, bf16[272,256]{1,0:T(8,128)(2,1)S(1)} %collective-permute-done.1.refs_2_, ...), custom_call_target="tpu_custom_call" | custom-call | flops 167772160 | bytes 917504 | tf_op jit(solution)/shard_map/add_pairs/pallas_call | solution.py:200
  19.2 0.4 collective-permute-done.5.value_ref.refs_6_
  19.6 1.6 %collective-permute-start.7 = (bf16[272,256]{1,0:T(8,128)(2,1)S(1)}, bf16[272,256]{1,0:T(8,128)(2,1)S(1)}, u32[]{:S(2)}, u32[]{:S(2)}) collective-permute-start(bf16[272,256]{1,0:T(8,128)(2,1)S(1)} %after.2), channel_id=1, source_target_pairs={{0,1},{1,0},{2,3},{3,2},{4,5},{5,4},{6,7},{7,6},{8,9},{9,8},{10,11... | collective-permute-start | bytes 417800 | tf_op jit(solution)/shard_map/ppermute | solution.py:385
  21.2 1.2 %add_pairs.6 = (f32[6,256]{1,0:T(8,128)S(1)}, f32[256,128]{1,0:T(8,128)S(1)}, f32[1,256,256]{2,1,0:T(8,128)S(1)}) custom-call(s32[4,8]{1,0:T(4,128)S(1)} %copy-done, bf16[272,256]{1,0:T(8,128)(2,1)S(1)} %get-tuple-element.32.refs_1_, bf16[272,256]{1,0:T(8,128)(2,1)S(1)} %collective-permute-done.1.refs_2_, ...), custom_call_target="tpu_custom_call" | custom-call | flops 201326592 | bytes 1048576 | tf_op jit(solution)/shard_map/add_pairs/pallas_call | solution.py:200
  22.4 1.2 %add_pairs.7 = (f32[7,256]{1,0:T(8,128)S(1)}, f32[256,128]{1,0:T(8,128)S(1)}, f32[1,256,256]{2,1,0:T(8,128)S(1)}) custom-call(s32[4,8]{1,0:T(4,128)S(1)} %copy-done, bf16[272,256]{1,0:T(8,128)(2,1)S(1)} %get-tuple-element.32.refs_1_, bf16[272,256]{1,0:T(8,128)(2,1)S(1)} %collective-permute-done.1.refs_2_, ...), custom_call_target="tpu_custom_call" | custom-call | flops 234881024 | bytes 1179648 | tf_op jit(solution)/shard_map/add_pairs/pallas_call | solution.py:200
  23.6 1.2 %collective-permute-done.7.refs_8_ = bf16[272,256]{1,0:T(8,128)(2,1)S(1)} collective-permute-done((bf16[272,256]{1,0:T(8,128)(2,1)S(1)}, bf16[272,256]{1,0:T(8,128)(2,1)S(1)}, u32[]{:S(2)}, u32[]{:S(2)}) %collective-permute-start.7) | collective-permute-done | bytes 139296 | tf_op jit(solution)/shard_map/ppermute | solution.py:385
  24.8 2.5 %group_grad.1.refs_0_.refs_3_ = bf16[1,256,256]{2,1,0:T(8,128)(2,1)S(1)} custom-call(s32[4,8]{1,0:T(4,128)S(1)} %copy-done, bf16[272,256]{1,0:T(8,128)(2,1)S(1)} %get-tuple-element.32.refs_1_, bf16[272,256]{1,0:T(8,128)(2,1)S(1)} %collective-permute-done.1.refs_2_, bf16[272,256]{1,0:T(8,128)(2,1)S(1)} %collective-permute-done.2.refs_3_, ...), custom_call_target="tpu_custom_call" | custom-call | flops 268435456 | bytes 1310720 | tf_op jit(solution)/shard_map/group_grad/pallas_call | solution.py:265
  27.3 1.6 %collective-permute-start.8 = (bf16[1,256,256]{2,1,0:T(8,128)(2,1)S(1)}, bf16[1,256,256]{2,1,0:T(8,128)(2,1)S(1)}, u32[]{:S(2)}, u32[]{:S(2)}) collective-permute-start(bf16[1,256,256]{2,1,0:T(8,128)(2,1)S(1)} %group_grad.1.refs_0_.refs_3_), channel_id=1, source_target_pairs={{0,16},{8,24},{16,0},{24,8},{1,17},{9,25},{17,1},{25,9},{2,18},{10... | collective-permute-start | bytes 393224 | tf_op jit(solution)/shard_map/ppermute | solution.py:385
  28.8 3.5 %collective-permute-done.8.refs_2_.refs_1_.refs_5_ = bf16[1,256,256]{2,1,0:T(8,128)(2,1)S(1)} collective-permute-done((bf16[1,256,256]{2,1,0:T(8,128)(2,1)S(1)}, bf16[1,256,256]{2,1,0:T(8,128)(2,1)S(1)}, u32[]{:S(2)}, u32[]{:S(2)}) %collective-permute-start.8) | collective-permute-done | bytes 131104 | tf_op jit(solution)/shard_map/ppermute | solution.py:385
  32.4 0.6 %collective-permute-start.10 = (bf16[2,256,256]{2,1,0:T(8,128)(2,1)S(1)}, bf16[2,256,256]{2,1,0:T(8,128)(2,1)S(1)}, u32[]{:S(2)}, u32[]{:S(2)}) collective-permute-start(bf16[2,256,256]{2,1,0:T(8,128)(2,1)S(1)} %pack.3), channel_id=1, source_target_pairs={{0,8},{8,0},{16,24},{24,16},{1,9},{9,1},{17,25},{25,17},{2,10},{10... | collective-permute-start | bytes 786440 | tf_op jit(solution)/shard_map/ppermute | solution.py:385
  33.0 1.7 %collective-permute-done.10.refs_4_ = bf16[2,256,256]{2,1,0:T(8,128)(2,1)S(1)} collective-permute-done((bf16[2,256,256]{2,1,0:T(8,128)(2,1)S(1)}, bf16[2,256,256]{2,1,0:T(8,128)(2,1)S(1)}, u32[]{:S(2)}, u32[]{:S(2)}) %collective-permute-start.10) | collective-permute-done | bytes 262176 | tf_op jit(solution)/shard_map/ppermute | solution.py:385
  34.7 0.5 %weight_grad.1 = (f32[2,64,256]{2,1,0:T(8,128)S(1)}, f32[2,64,256]{2,1,0:T(8,128)S(1)}, bf16[2,64,256]{2,1,0:T(8,128)(2,1)S(1)}, bf16[2,64,256]{2,1,0:T(8,128)(2,1)S(1)}) custom-call(bf16[2,256,512]{2,1,0:T(8,128)(2,1)S(1)} %get-tuple-element.30.refs_0_, bf16[2,256,512]{2,1,0:T(8,128)(2,1)S(1)} %collective-permute-done.9.refs_1_, ...), custom_call_target="tpu_custom_call" | custom-call | flops 268435456 | bytes 1048576 | tf_op jit(solution)/shard_map/weight_grad/pallas_call | solution.py:328
  35.2 1.5 %collective-permute-start.12 = (bf16[2,64,256]{2,1,0:T(8,128)(2,1)S(1)}, bf16[2,64,256]{2,1,0:T(8,128)(2,1)S(1)}, u32[]{:S(2)}, u32[]{:S(2)}) collective-permute-start(bf16[2,64,256]{2,1,0:T(8,128)(2,1)S(1)} %get-tuple-element.51), channel_id=1, source_target_pairs={{0,1},{1,0},{2,3},{3,2},{4,5},{5,4},{6,7},{7,6},{8,9},{9,8},{10,11... | collective-permute-start | bytes 196616 | tf_op jit(solution)/shard_map/ppermute | solution.py:385
  36.7 0.5 %collective-permute-start.11 = (bf16[2,64,256]{2,1,0:T(8,128)(2,1)S(1)}, bf16[2,64,256]{2,1,0:T(8,128)(2,1)S(1)}, u32[]{:S(2)}, u32[]{:S(2)}) collective-permute-start(bf16[2,64,256]{2,1,0:T(8,128)(2,1)S(1)} %get-tuple-element.48), channel_id=1, source_target_pairs={{0,1},{1,0},{2,3},{3,2},{4,5},{5,4},{6,7},{7,6},{8,9},{9,8},{10,11... | collective-permute-start | bytes 196616 | tf_op jit(solution)/shard_map/ppermute | solution.py:385
  37.3 2.7 %collective-permute-done.12.refs_0_ = bf16[2,64,256]{2,1,0:T(8,128)(2,1)S(1)} collective-permute-done((bf16[2,64,256]{2,1,0:T(8,128)(2,1)S(1)}, bf16[2,64,256]{2,1,0:T(8,128)(2,1)S(1)}, u32[]{:S(2)}, u32[]{:S(2)}) %collective-permute-start.12) | collective-permute-done | bytes 65568 | tf_op jit(solution)/shard_map/ppermute | solution.py:385
  40.0 2.3 %collective-permute-start.13 = (bf16[64,256]{1,0:T(8,128)(2,1)S(1)}, bf16[64,256]{1,0:T(8,128)(2,1)S(1)}, u32[]{:S(2)}, u32[]{:S(2)}) collective-permute-start(bf16[64,256]{1,0:T(8,128)(2,1)S(1)} %get-tuple-element.52), channel_id=1, source_target_pairs={{0,4},{1,5},{2,6},{3,7},{4,0},{5,1},{6,2},{7,3},{8,12},{9,13},{10,... | collective-permute-start | bytes 98312 | tf_op jit(solution)/shard_map/ppermute | solution.py:385
  42.2 1.3 %collective-permute-start.14 = (bf16[64,256]{1,0:T(8,128)(2,1)S(1)}, bf16[64,256]{1,0:T(8,128)(2,1)S(1)}, u32[]{:S(2)}, u32[]{:S(2)}) collective-permute-start(bf16[64,256]{1,0:T(8,128)(2,1)S(1)} %get-tuple-element.53), channel_id=1, source_target_pairs={{0,6},{1,7},{2,4},{3,5},{4,2},{5,3},{6,0},{7,1},{8,14},{9,15},{10,... | collective-permute-start | bytes 98312 | tf_op jit(solution)/shard_map/ppermute | solution.py:385
  43.6 1.2 %collective-permute-done.13.refs_0_ = bf16[64,256]{1,0:T(8,128)(2,1)S(1)} collective-permute-done((bf16[64,256]{1,0:T(8,128)(2,1)S(1)}, bf16[64,256]{1,0:T(8,128)(2,1)S(1)}, u32[]{:S(2)}, u32[]{:S(2)}) %collective-permute-start.13) | collective-permute-done | bytes 32800 | tf_op jit(solution)/shard_map/ppermute | solution.py:385
  44.9 3.1 %collective-permute-done.14.refs_1_ = bf16[64,256]{1,0:T(8,128)(2,1)S(1)} collective-permute-done((bf16[64,256]{1,0:T(8,128)(2,1)S(1)}, bf16[64,256]{1,0:T(8,128)(2,1)S(1)}, u32[]{:S(2)}, u32[]{:S(2)}) %collective-permute-start.14) | collective-permute-done | bytes 32800 | tf_op jit(solution)/shard_map/ppermute | solution.py:385
  48.0 0.6 %convert_add_fusion = f32[64,256]{1,0:T(8,128)} fusion(bf16[64,256]{1,0:T(8,128)(2,1)S(1)} %after.3, f32[64,256]{1,0:T(8,128)S(1)} %get-tuple-element.49, f32[64,256]{1,0:T(8,128)S(1)} %add_all.1.refs_0_), kind=kLoop, calls=%fused_computation | loop fusion | flops 49152 | bytes 229376 | tf_op jit(solution)/shard_map/add | solution.py:476
  (17 shorter events, 0.3 us)
Async XLA Ops:
  2.4 14.1 %copy-start = (s32[4,8]{1,0:T(4,128)S(1)}, s32[4,8]{1,0:T(4,128)}, u32[]{:S(2)}) copy-start(s32[4,8]{1,0:T(4,128)} %refs_0_.9) | copy-start | bytes 388
  2.4 9.0 %collective-permute-start.1 = (bf16[272,256]{1,0:T(8,128)(2,1)S(1)}, bf16[272,256]{1,0:T(8,128)(2,1)S(1)}, u32[]{:S(2)}, u32[]{:S(2)}) collective-permute-start(bf16[272,256]{1,0:T(8,128)(2,1)S(1)} %get-tuple-element.32.refs_1_), channel_id=1, source_target_pairs={{0,2},{1,3},{2,0},{3,1},{4,6},{5,7},{6,4},{7,5},{8,10},{9,11},{10,... | collective-permute-start | bytes 417800 | tf_op jit(solution)/shard_map/ppermute | solution.py:385
  5.5 9.1 %collective-permute-start.2 = (bf16[272,256]{1,0:T(8,128)(2,1)S(1)}, bf16[272,256]{1,0:T(8,128)(2,1)S(1)}, u32[]{:S(2)}, u32[]{:S(2)}) collective-permute-start(bf16[272,256]{1,0:T(8,128)(2,1)S(1)} %get-tuple-element.32.refs_1_), channel_id=1, source_target_pairs={{0,4},{1,5},{2,6},{3,7},{4,0},{5,1},{6,2},{7,3},{8,12},{9,13},{10,... | collective-permute-start | bytes 417800 | tf_op jit(solution)/shard_map/ppermute | solution.py:385
  8.1 20.7 %collective-permute-start = (bf16[2,256,512]{2,1,0:T(8,128)(2,1)S(1)}, bf16[2,256,512]{2,1,0:T(8,128)(2,1)S(1)}, u32[]{:S(2)}, u32[]{:S(2)}) collective-permute-start(bf16[2,256,512]{2,1,0:T(8,128)(2,1)S(1)} %get-tuple-element.31), channel_id=1, source_target_pairs={{0,16},{8,24},{16,0},{24,8},{1,17},{9,25},{17,1},{25,9},{2,18},{10... | collective-permute-start | bytes 1572872 | tf_op jit(solution)/shard_map/ppermute | solution.py:385
  9.6 6.9 %collective-permute-start.3 = (bf16[272,256]{1,0:T(8,128)(2,1)S(1)}, bf16[272,256]{1,0:T(8,128)(2,1)S(1)}, u32[]{:S(2)}, u32[]{:S(2)}) collective-permute-start(bf16[272,256]{1,0:T(8,128)(2,1)S(1)} %get-tuple-element.32.refs_1_), channel_id=1, source_target_pairs={{0,1},{1,0},{2,3},{3,2},{4,5},{5,4},{6,7},{7,6},{8,9},{9,8},{10,11... | collective-permute-start | bytes 417800 | tf_op jit(solution)/shard_map/ppermute | solution.py:385
  11.4 6.7 %collective-permute-start.4 = (bf16[272,256]{1,0:T(8,128)(2,1)S(1)}, bf16[272,256]{1,0:T(8,128)(2,1)S(1)}, u32[]{:S(2)}, u32[]{:S(2)}) collective-permute-start(bf16[272,256]{1,0:T(8,128)(2,1)S(1)} %collective-permute-done.1.refs_2_), channel_id=1, source_target_pairs={{0,1},{1,0},{2,3},{3,2},{4,5},{5,4},{6,7},{7,6},{8,9},{9,8},{10,11... | collective-permute-start | bytes 417800 | tf_op jit(solution)/shard_map/ppermute | solution.py:385
  14.6 5.1 %collective-permute-start.5 = (bf16[272,256]{1,0:T(8,128)(2,1)S(1)}, bf16[272,256]{1,0:T(8,128)(2,1)S(1)}, u32[]{:S(2)}, u32[]{:S(2)}) collective-permute-start(bf16[272,256]{1,0:T(8,128)(2,1)S(1)} %collective-permute-done.2.refs_3_), channel_id=1, source_target_pairs={{0,2},{1,3},{2,0},{3,1},{4,6},{5,7},{6,4},{7,5},{8,10},{9,11},{10,... | collective-permute-start | bytes 417800 | tf_op jit(solution)/shard_map/ppermute | solution.py:385
  15.0 7.3 %collective-permute-start.6 = (bf16[272,256]{1,0:T(8,128)(2,1)S(1)}, bf16[272,256]{1,0:T(8,128)(2,1)S(1)}, u32[]{:S(2)}, u32[]{:S(2)}) collective-permute-start(bf16[272,256]{1,0:T(8,128)(2,1)S(1)} %collective-permute-done.2.refs_3_), channel_id=1, source_target_pairs={{0,1},{1,0},{2,3},{3,2},{4,5},{5,4},{6,7},{7,6},{8,9},{9,8},{10,11... | collective-permute-start | bytes 417800 | tf_op jit(solution)/shard_map/ppermute | solution.py:385
  19.6 5.1 %collective-permute-start.7 = (bf16[272,256]{1,0:T(8,128)(2,1)S(1)}, bf16[272,256]{1,0:T(8,128)(2,1)S(1)}, u32[]{:S(2)}, u32[]{:S(2)}) collective-permute-start(bf16[272,256]{1,0:T(8,128)(2,1)S(1)} %after.2), channel_id=1, source_target_pairs={{0,1},{1,0},{2,3},{3,2},{4,5},{5,4},{6,7},{7,6},{8,9},{9,8},{10,11... | collective-permute-start | bytes 417800 | tf_op jit(solution)/shard_map/ppermute | solution.py:385
  27.3 5.0 %collective-permute-start.8 = (bf16[1,256,256]{2,1,0:T(8,128)(2,1)S(1)}, bf16[1,256,256]{2,1,0:T(8,128)(2,1)S(1)}, u32[]{:S(2)}, u32[]{:S(2)}) collective-permute-start(bf16[1,256,256]{2,1,0:T(8,128)(2,1)S(1)} %group_grad.1.refs_0_.refs_3_), channel_id=1, source_target_pairs={{0,16},{8,24},{16,0},{24,8},{1,17},{9,25},{17,1},{25,9},{2,18},{10... | collective-permute-start | bytes 393224 | tf_op jit(solution)/shard_map/ppermute | solution.py:385
  32.3 2.4 %collective-permute-start.9 = (bf16[2,256,512]{2,1,0:T(8,128)(2,1)S(1)}, bf16[2,256,512]{2,1,0:T(8,128)(2,1)S(1)}, u32[]{:S(2)}, u32[]{:S(2)}) collective-permute-start(bf16[2,256,512]{2,1,0:T(8,128)(2,1)S(1)} %pack.2), channel_id=1, source_target_pairs={{0,8},{8,0},{16,24},{24,16},{1,9},{9,1},{17,25},{25,17},{2,10},{10... | collective-permute-start | bytes 1572872 | tf_op jit(solution)/shard_map/ppermute | solution.py:385
  32.4 2.2 %collective-permute-start.10 = (bf16[2,256,256]{2,1,0:T(8,128)(2,1)S(1)}, bf16[2,256,256]{2,1,0:T(8,128)(2,1)S(1)}, u32[]{:S(2)}, u32[]{:S(2)}) collective-permute-start(bf16[2,256,256]{2,1,0:T(8,128)(2,1)S(1)} %pack.3), channel_id=1, source_target_pairs={{0,8},{8,0},{16,24},{24,16},{1,9},{9,1},{17,25},{25,17},{2,10},{10... | collective-permute-start | bytes 786440 | tf_op jit(solution)/shard_map/ppermute | solution.py:385
  35.2 4.8 %collective-permute-start.12 = (bf16[2,64,256]{2,1,0:T(8,128)(2,1)S(1)}, bf16[2,64,256]{2,1,0:T(8,128)(2,1)S(1)}, u32[]{:S(2)}, u32[]{:S(2)}) collective-permute-start(bf16[2,64,256]{2,1,0:T(8,128)(2,1)S(1)} %get-tuple-element.51), channel_id=1, source_target_pairs={{0,1},{1,0},{2,3},{3,2},{4,5},{5,4},{6,7},{7,6},{8,9},{9,8},{10,11... | collective-permute-start | bytes 196616 | tf_op jit(solution)/shard_map/ppermute | solution.py:385
  36.7 6.8 %collective-permute-start.11 = (bf16[2,64,256]{2,1,0:T(8,128)(2,1)S(1)}, bf16[2,64,256]{2,1,0:T(8,128)(2,1)S(1)}, u32[]{:S(2)}, u32[]{:S(2)}) collective-permute-start(bf16[2,64,256]{2,1,0:T(8,128)(2,1)S(1)} %get-tuple-element.48), channel_id=1, source_target_pairs={{0,1},{1,0},{2,3},{3,2},{4,5},{5,4},{6,7},{7,6},{8,9},{9,8},{10,11... | collective-permute-start | bytes 196616 | tf_op jit(solution)/shard_map/ppermute | solution.py:385
  40.0 4.9 %collective-permute-start.13 = (bf16[64,256]{1,0:T(8,128)(2,1)S(1)}, bf16[64,256]{1,0:T(8,128)(2,1)S(1)}, u32[]{:S(2)}, u32[]{:S(2)}) collective-permute-start(bf16[64,256]{1,0:T(8,128)(2,1)S(1)} %get-tuple-element.52), channel_id=1, source_target_pairs={{0,4},{1,5},{2,6},{3,7},{4,0},{5,1},{6,2},{7,3},{8,12},{9,13},{10,... | collective-permute-start | bytes 98312 | tf_op jit(solution)/shard_map/ppermute | solution.py:385
  42.2 5.7 %collective-permute-start.14 = (bf16[64,256]{1,0:T(8,128)(2,1)S(1)}, bf16[64,256]{1,0:T(8,128)(2,1)S(1)}, u32[]{:S(2)}, u32[]{:S(2)}) collective-permute-start(bf16[64,256]{1,0:T(8,128)(2,1)S(1)} %get-tuple-element.53), channel_id=1, source_target_pairs={{0,6},{1,7},{2,4},{3,5},{4,2},{5,3},{6,0},{7,1},{8,14},{9,15},{10,... | collective-permute-start | bytes 98312 | tf_op jit(solution)/shard_map/ppermute | solution.py:385
  43.6 4.4 %collective-permute-start.15 = (bf16[64,256]{1,0:T(8,128)(2,1)S(1)}, bf16[64,256]{1,0:T(8,128)(2,1)S(1)}, u32[]{:S(2)}, u32[]{:S(2)}) collective-permute-start(bf16[64,256]{1,0:T(8,128)(2,1)S(1)} %get-tuple-element.54), channel_id=1, source_target_pairs={{0,2},{1,3},{2,0},{3,1},{4,6},{5,7},{6,4},{7,5},{8,10},{9,11},{10,... | collective-permute-start | bytes 98312 | tf_op jit(solution)/shard_map/ppermute | solution.py:385

commit v15 on v12

--- a/solution.py
+++ b/solution.py
@@ -466,10 +466,7 @@
     far_came = [swap(each, "pool", (half + at) * minor) for at, each in enumerate(far_sums)]
     near_came = [swap(each, "pool", (1 + at) * minor) for at, each in enumerate(near_sums)]
     far_total = add_all(far_came)
-    total = total + far_total
-    for each in near_came:
-        total = total + after(each, far_total).astype(jnp.float32)
-    return total
+    return add_all([total, far_total] + [after(each, far_total) for each in near_came])
 
 
 def solution(mesh):

time: 48.7 us -> 48.7 us (level)
  other arithmetic: 0.64 us -> 0 us
  Pallas kernels: 10.3 us -> 10.9 us
    pallas_call x1 -> x2, Pallas kernels: 0.01 us -> 0.65 us  [add_all(): pl.pallas_call(add_all_kernel, out_shape=jax.ShapeDtypeStruct(pieces[0].s...]
    add x1 -> x0, other arithmetic: 0.64 us -> none  [per_device(): total = total + after(each, far_total).astype(jnp.float32)]
where the time goes in v15:
time: 48.7 us; the launch traced here: 48.5 us
  starting transfers between devices  22 us (45%)
  waiting for transfers between devices  15.5 us (32%)
  Pallas kernels  10.9 us (22%)
    ppermute x16, starting transfers between devices, swap(): return lax.ppermute(value, axis, [(at, at ^ flip) for at in range(size)])  22 us
    ppermute x16, waiting for transfers between devices, swap(): return lax.ppermute(value, axis, [(at, at ^ flip) for at in range(size)])  15.5 us
    pallas_call x4, Pallas kernels, add_pairs(): pl.pallas_call(functools.partial(pairs_kernel, seen, fresh), out_shape=(j...  4.9 us
    pallas_call x1, Pallas kernels, group_grad(): pl.pallas_call(functools.partial(grad_kernel, stages, fresh), out_shape=j...  2.49 us
    pallas_call x1, Pallas kernels, project(): pl.pallas_call(functools.partial(project_kernel, parts), out_shape=(jax.S...  2.27 us
  transfers between devices with their start and end apart: 16, of which 10 were waited for; matrix products, arithmetic and copies ran while one was open for 0% of the time, Pallas kernels for 15%

profile of v15, /device:TPU:0, one launch (start us, length us, event | category | flops | bytes accessed | tf_op | source)
XLA Modules:
  0.0 48.5 jit_solution(3511953141028462522)
XLA Ops:
  0.0 2.3 %project.1 = (bf16[272,256]{1,0:T(8,128)(2,1)S(1)}, f32[256,256]{1,0:T(8,128)S(1)}, f32[256,128]{1,0:T(8,128)S(1)}, bf16[2,256,512]{2,1,0:T(8,128)(2,1)S(1)}, bf16[2,256,512]{2,1,0:T(8,128)(2,1)S(1)}) custom-call(bf16[256,2048]{1,0:T(8,128)(2,1)} %feats_hbm.1, bf16[2048,256]{1,0:T(8,128)(2,1)} %w_hbm.1, s32[1,256]{1,0:T(1,128)} %bitcast.2, s32[1,256]{1,0:T(1,128)} %bitcast.3), custom_call_target="tpu_custom_call" | custom-call | flops 268435456 | bytes 2097152 | tf_op jit(solution)/shard_map/project/pallas_call | solution.py:81
  2.3 3.1 %collective-permute-start.1 = (bf16[272,256]{1,0:T(8,128)(2,1)S(1)}, bf16[272,256]{1,0:T(8,128)(2,1)S(1)}, u32[]{:S(2)}, u32[]{:S(2)}) collective-permute-start(bf16[272,256]{1,0:T(8,128)(2,1)S(1)} %get-tuple-element.32.refs_1_), channel_id=1, source_target_pairs={{0,2},{1,3},{2,0},{3,1},{4,6},{5,7},{6,4},{7,5},{8,10},{9,11},{10,... | collective-permute-start | bytes 417800 | tf_op jit(solution)/shard_map/ppermute | solution.py:380
  5.4 2.6 %collective-permute-start.2 = (bf16[272,256]{1,0:T(8,128)(2,1)S(1)}, bf16[272,256]{1,0:T(8,128)(2,1)S(1)}, u32[]{:S(2)}, u32[]{:S(2)}) collective-permute-start(bf16[272,256]{1,0:T(8,128)(2,1)S(1)} %get-tuple-element.32.refs_1_), channel_id=1, source_target_pairs={{0,4},{1,5},{2,6},{3,7},{4,0},{5,1},{6,2},{7,3},{8,12},{9,13},{10,... | collective-permute-start | bytes 417800 | tf_op jit(solution)/shard_map/ppermute | solution.py:380
  8.0 1.5 %collective-permute-start = (bf16[2,256,512]{2,1,0:T(8,128)(2,1)S(1)}, bf16[2,256,512]{2,1,0:T(8,128)(2,1)S(1)}, u32[]{:S(2)}, u32[]{:S(2)}) collective-permute-start(bf16[2,256,512]{2,1,0:T(8,128)(2,1)S(1)} %get-tuple-element.31), channel_id=1, source_target_pairs={{0,16},{8,24},{16,0},{24,8},{1,17},{9,25},{17,1},{25,9},{2,18},{10... | collective-permute-start | bytes 1572872 | tf_op jit(solution)/shard_map/ppermute | solution.py:380
  9.5 1.5 %collective-permute-start.3 = (bf16[272,256]{1,0:T(8,128)(2,1)S(1)}, bf16[272,256]{1,0:T(8,128)(2,1)S(1)}, u32[]{:S(2)}, u32[]{:S(2)}) collective-permute-start(bf16[272,256]{1,0:T(8,128)(2,1)S(1)} %get-tuple-element.32.refs_1_), channel_id=1, source_target_pairs={{0,1},{1,0},{2,3},{3,2},{4,5},{5,4},{6,7},{7,6},{8,9},{9,8},{10,11... | collective-permute-start | bytes 417800 | tf_op jit(solution)/shard_map/ppermute | solution.py:380
  11.0 0.3 collective-permute-done.1.refs_2_
  11.2 1.8 %collective-permute-start.4 = (bf16[272,256]{1,0:T(8,128)(2,1)S(1)}, bf16[272,256]{1,0:T(8,128)(2,1)S(1)}, u32[]{:S(2)}, u32[]{:S(2)}) collective-permute-start(bf16[272,256]{1,0:T(8,128)(2,1)S(1)} %collective-permute-done.1.refs_2_), channel_id=1, source_target_pairs={{0,1},{1,0},{2,3},{3,2},{4,5},{5,4},{6,7},{7,6},{8,9},{9,8},{10,11... | collective-permute-start | bytes 417800 | tf_op jit(solution)/shard_map/ppermute | solution.py:380
  13.1 1.4 %collective-permute-done.2.refs_3_ = bf16[272,256]{1,0:T(8,128)(2,1)S(1)} collective-permute-done((bf16[272,256]{1,0:T(8,128)(2,1)S(1)}, bf16[272,256]{1,0:T(8,128)(2,1)S(1)}, u32[]{:S(2)}, u32[]{:S(2)}) %collective-permute-start.2) | collective-permute-done | bytes 139296 | tf_op jit(solution)/shard_map/ppermute | solution.py:380
  14.4 0.4 collective-permute-start.5
  14.9 1.5 %collective-permute-start.6 = (bf16[272,256]{1,0:T(8,128)(2,1)S(1)}, bf16[272,256]{1,0:T(8,128)(2,1)S(1)}, u32[]{:S(2)}, u32[]{:S(2)}) collective-permute-start(bf16[272,256]{1,0:T(8,128)(2,1)S(1)} %collective-permute-done.2.refs_3_), channel_id=1, source_target_pairs={{0,1},{1,0},{2,3},{3,2},{4,5},{5,4},{6,7},{7,6},{8,9},{9,8},{10,11... | collective-permute-start | bytes 417800 | tf_op jit(solution)/shard_map/ppermute | solution.py:380
  16.4 1.4 %add_pairs.4 = (f32[4,256]{1,0:T(4,128)S(1)}, f32[256,128]{1,0:T(8,128)S(1)}, f32[4,256,256]{2,1,0:T(8,128)S(1)}) custom-call(s32[4,8]{1,0:T(4,128)S(1)} %copy-done, bf16[272,256]{1,0:T(8,128)(2,1)S(1)} %get-tuple-element.32.refs_1_, bf16[272,256]{1,0:T(8,128)(2,1)S(1)} %collective-permute-done.1.refs_2_, ...), custom_call_target="tpu_custom_call" | custom-call | flops 335544320 | bytes 1572864 | tf_op jit(solution)/shard_map/add_pairs/pallas_call | solution.py:195
  17.8 0.2 collective-permute-done.4.refs_5_
  18.0 1.1 %add_pairs.5 = (f32[5,256]{1,0:T(8,128)S(1)}, f32[256,128]{1,0:T(8,128)S(1)}, f32[1,256,256]{2,1,0:T(8,128)S(1)}) custom-call(s32[4,8]{1,0:T(4,128)S(1)} %copy-done, bf16[272,256]{1,0:T(8,128)(2,1)S(1)} %get-tuple-element.32.refs_1_, bf16[272,256]{1,0:T(8,128)(2,1)S(1)} %collective-permute-done.1.refs_2_, ...), custom_call_target="tpu_custom_call" | custom-call | flops 167772160 | bytes 917504 | tf_op jit(solution)/shard_map/add_pairs/pallas_call | solution.py:195
  19.1 0.4 collective-permute-done.5.value_ref.refs_6_
  19.5 1.6 %collective-permute-start.7 = (bf16[272,256]{1,0:T(8,128)(2,1)S(1)}, bf16[272,256]{1,0:T(8,128)(2,1)S(1)}, u32[]{:S(2)}, u32[]{:S(2)}) collective-permute-start(bf16[272,256]{1,0:T(8,128)(2,1)S(1)} %after.2), channel_id=1, source_target_pairs={{0,1},{1,0},{2,3},{3,2},{4,5},{5,4},{6,7},{7,6},{8,9},{9,8},{10,11... | collective-permute-start | bytes 417800 | tf_op jit(solution)/shard_map/ppermute | solution.py:380
  21.1 1.2 %add_pairs.6 = (f32[6,256]{1,0:T(8,128)S(1)}, f32[256,128]{1,0:T(8,128)S(1)}, f32[1,256,256]{2,1,0:T(8,128)S(1)}) custom-call(s32[4,8]{1,0:T(4,128)S(1)} %copy-done, bf16[272,256]{1,0:T(8,128)(2,1)S(1)} %get-tuple-element.32.refs_1_, bf16[272,256]{1,0:T(8,128)(2,1)S(1)} %collective-permute-done.1.refs_2_, ...), custom_call_target="tpu_custom_call" | custom-call | flops 201326592 | bytes 1048576 | tf_op jit(solution)/shard_map/add_pairs/pallas_call | solution.py:195
  22.3 1.2 %add_pairs.7 = (f32[7,256]{1,0:T(8,128)S(1)}, f32[256,128]{1,0:T(8,128)S(1)}, f32[1,256,256]{2,1,0:T(8,128)S(1)}) custom-call(s32[4,8]{1,0:T(4,128)S(1)} %copy-done, bf16[272,256]{1,0:T(8,128)(2,1)S(1)} %get-tuple-element.32.refs_1_, bf16[272,256]{1,0:T(8,128)(2,1)S(1)} %collective-permute-done.1.refs_2_, ...), custom_call_target="tpu_custom_call" | custom-call | flops 234881024 | bytes 1179648 | tf_op jit(solution)/shard_map/add_pairs/pallas_call | solution.py:195
  23.5 1.2 %collective-permute-done.7.refs_8_ = bf16[272,256]{1,0:T(8,128)(2,1)S(1)} collective-permute-done((bf16[272,256]{1,0:T(8,128)(2,1)S(1)}, bf16[272,256]{1,0:T(8,128)(2,1)S(1)}, u32[]{:S(2)}, u32[]{:S(2)}) %collective-permute-start.7) | collective-permute-done | bytes 139296 | tf_op jit(solution)/shard_map/ppermute | solution.py:380
  24.6 2.5 %group_grad.1.refs_0_.refs_3_ = bf16[1,256,256]{2,1,0:T(8,128)(2,1)S(1)} custom-call(s32[4,8]{1,0:T(4,128)S(1)} %copy-done, bf16[272,256]{1,0:T(8,128)(2,1)S(1)} %get-tuple-element.32.refs_1_, bf16[272,256]{1,0:T(8,128)(2,1)S(1)} %collective-permute-done.1.refs_2_, bf16[272,256]{1,0:T(8,128)(2,1)S(1)} %collective-permute-done.2.refs_3_, ...), custom_call_target="tpu_custom_call" | custom-call | flops 268435456 | bytes 1310720 | tf_op jit(solution)/shard_map/group_grad/pallas_call | solution.py:260
  27.1 1.6 %collective-permute-start.8 = (bf16[1,256,256]{2,1,0:T(8,128)(2,1)S(1)}, bf16[1,256,256]{2,1,0:T(8,128)(2,1)S(1)}, u32[]{:S(2)}, u32[]{:S(2)}) collective-permute-start(bf16[1,256,256]{2,1,0:T(8,128)(2,1)S(1)} %group_grad.1.refs_0_.refs_3_), channel_id=1, source_target_pairs={{0,16},{8,24},{16,0},{24,8},{1,17},{9,25},{17,1},{25,9},{2,18},{10... | collective-permute-start | bytes 393224 | tf_op jit(solution)/shard_map/ppermute | solution.py:380
  28.7 3.4 %collective-permute-done.8.refs_2_.refs_1_.refs_5_ = bf16[1,256,256]{2,1,0:T(8,128)(2,1)S(1)} collective-permute-done((bf16[1,256,256]{2,1,0:T(8,128)(2,1)S(1)}, bf16[1,256,256]{2,1,0:T(8,128)(2,1)S(1)}, u32[]{:S(2)}, u32[]{:S(2)}) %collective-permute-start.8) | collective-permute-done | bytes 131104 | tf_op jit(solution)/shard_map/ppermute | solution.py:380
  32.3 0.6 %collective-permute-start.10 = (bf16[2,256,256]{2,1,0:T(8,128)(2,1)S(1)}, bf16[2,256,256]{2,1,0:T(8,128)(2,1)S(1)}, u32[]{:S(2)}, u32[]{:S(2)}) collective-permute-start(bf16[2,256,256]{2,1,0:T(8,128)(2,1)S(1)} %pack.3), channel_id=1, source_target_pairs={{0,8},{8,0},{16,24},{24,16},{1,9},{9,1},{17,25},{25,17},{2,10},{10... | collective-permute-start | bytes 786440 | tf_op jit(solution)/shard_map/ppermute | solution.py:380
  32.9 1.7 %collective-permute-done.10.refs_4_ = bf16[2,256,256]{2,1,0:T(8,128)(2,1)S(1)} collective-permute-done((bf16[2,256,256]{2,1,0:T(8,128)(2,1)S(1)}, bf16[2,256,256]{2,1,0:T(8,128)(2,1)S(1)}, u32[]{:S(2)}, u32[]{:S(2)}) %collective-permute-start.10) | collective-permute-done | bytes 262176 | tf_op jit(solution)/shard_map/ppermute | solution.py:380
  34.6 0.5 %weight_grad.1 = (f32[2,64,256]{2,1,0:T(8,128)S(1)}, f32[2,64,256]{2,1,0:T(8,128)S(1)}, bf16[2,64,256]{2,1,0:T(8,128)(2,1)S(1)}, bf16[2,64,256]{2,1,0:T(8,128)(2,1)S(1)}) custom-call(bf16[2,256,512]{2,1,0:T(8,128)(2,1)S(1)} %get-tuple-element.30.refs_0_, bf16[2,256,512]{2,1,0:T(8,128)(2,1)S(1)} %collective-permute-done.9.refs_1_, ...), custom_call_target="tpu_custom_call" | custom-call | flops 268435456 | bytes 1048576 | tf_op jit(solution)/shard_map/weight_grad/pallas_call | solution.py:323
  35.1 1.6 %collective-permute-start.12 = (bf16[2,64,256]{2,1,0:T(8,128)(2,1)S(1)}, bf16[2,64,256]{2,1,0:T(8,128)(2,1)S(1)}, u32[]{:S(2)}, u32[]{:S(2)}) collective-permute-start(bf16[2,64,256]{2,1,0:T(8,128)(2,1)S(1)} %get-tuple-element.51), channel_id=1, source_target_pairs={{0,1},{1,0},{2,3},{3,2},{4,5},{5,4},{6,7},{7,6},{8,9},{9,8},{10,11... | collective-permute-start | bytes 196616 | tf_op jit(solution)/shard_map/ppermute | solution.py:380
  36.6 0.5 %collective-permute-start.11 = (bf16[2,64,256]{2,1,0:T(8,128)(2,1)S(1)}, bf16[2,64,256]{2,1,0:T(8,128)(2,1)S(1)}, u32[]{:S(2)}, u32[]{:S(2)}) collective-permute-start(bf16[2,64,256]{2,1,0:T(8,128)(2,1)S(1)} %get-tuple-element.48), channel_id=1, source_target_pairs={{0,1},{1,0},{2,3},{3,2},{4,5},{5,4},{6,7},{7,6},{8,9},{9,8},{10,11... | collective-permute-start | bytes 196616 | tf_op jit(solution)/shard_map/ppermute | solution.py:380
  37.2 2.6 %collective-permute-done.12.refs_0_ = bf16[2,64,256]{2,1,0:T(8,128)(2,1)S(1)} collective-permute-done((bf16[2,64,256]{2,1,0:T(8,128)(2,1)S(1)}, bf16[2,64,256]{2,1,0:T(8,128)(2,1)S(1)}, u32[]{:S(2)}, u32[]{:S(2)}) %collective-permute-start.12) | collective-permute-done | bytes 65568 | tf_op jit(solution)/shard_map/ppermute | solution.py:380
  39.8 2.3 %collective-permute-start.13 = (bf16[64,256]{1,0:T(8,128)(2,1)S(1)}, bf16[64,256]{1,0:T(8,128)(2,1)S(1)}, u32[]{:S(2)}, u32[]{:S(2)}) collective-permute-start(bf16[64,256]{1,0:T(8,128)(2,1)S(1)} %get-tuple-element.52), channel_id=1, source_target_pairs={{0,4},{1,5},{2,6},{3,7},{4,0},{5,1},{6,2},{7,3},{8,12},{9,13},{10,... | collective-permute-start | bytes 98312 | tf_op jit(solution)/shard_map/ppermute | solution.py:380
  42.1 1.3 %collective-permute-start.14 = (bf16[64,256]{1,0:T(8,128)(2,1)S(1)}, bf16[64,256]{1,0:T(8,128)(2,1)S(1)}, u32[]{:S(2)}, u32[]{:S(2)}) collective-permute-start(bf16[64,256]{1,0:T(8,128)(2,1)S(1)} %get-tuple-element.53), channel_id=1, source_target_pairs={{0,6},{1,7},{2,4},{3,5},{4,2},{5,3},{6,0},{7,1},{8,14},{9,15},{10,... | collective-permute-start | bytes 98312 | tf_op jit(solution)/shard_map/ppermute | solution.py:380
  43.5 1.2 %collective-permute-done.13.refs_0_ = bf16[64,256]{1,0:T(8,128)(2,1)S(1)} collective-permute-done((bf16[64,256]{1,0:T(8,128)(2,1)S(1)}, bf16[64,256]{1,0:T(8,128)(2,1)S(1)}, u32[]{:S(2)}, u32[]{:S(2)}) %collective-permute-start.13) | collective-permute-done | bytes 32800 | tf_op jit(solution)/shard_map/ppermute | solution.py:380
  44.7 3.1 %collective-permute-done.14.refs_1_ = bf16[64,256]{1,0:T(8,128)(2,1)S(1)} collective-permute-done((bf16[64,256]{1,0:T(8,128)(2,1)S(1)}, bf16[64,256]{1,0:T(8,128)(2,1)S(1)}, u32[]{:S(2)}, u32[]{:S(2)}) %collective-permute-start.14) | collective-permute-done | bytes 32800 | tf_op jit(solution)/shard_map/ppermute | solution.py:380
  47.9 0.6 %add_all.3 = f32[64,256]{1,0:T(8,128)} custom-call(f32[64,256]{1,0:T(8,128)S(1)} %get-tuple-element.49.refs_0_, f32[64,256]{1,0:T(8,128)S(1)} %add_all.2.refs_0_.refs_1_, bf16[64,256]{1,0:T(8,128)(2,1)S(1)} %after.3.refs_2_), custom_call_target="tpu_custom_call" | custom-call | tf_op jit(solution)/shard_map/add_all/pallas_call | solution.py:368
  (17 shorter events, 0.3 us)
Async XLA Ops:
  2.3 14.1 %copy-start = (s32[4,8]{1,0:T(4,128)S(1)}, s32[4,8]{1,0:T(4,128)}, u32[]{:S(2)}) copy-start(s32[4,8]{1,0:T(4,128)} %refs_0_.9) | copy-start | bytes 388
  2.3 9.0 %collective-permute-start.1 = (bf16[272,256]{1,0:T(8,128)(2,1)S(1)}, bf16[272,256]{1,0:T(8,128)(2,1)S(1)}, u32[]{:S(2)}, u32[]{:S(2)}) collective-permute-start(bf16[272,256]{1,0:T(8,128)(2,1)S(1)} %get-tuple-element.32.refs_1_), channel_id=1, source_target_pairs={{0,2},{1,3},{2,0},{3,1},{4,6},{5,7},{6,4},{7,5},{8,10},{9,11},{10,... | collective-permute-start | bytes 417800 | tf_op jit(solution)/shard_map/ppermute | solution.py:380
  5.4 9.1 %collective-permute-start.2 = (bf16[272,256]{1,0:T(8,128)(2,1)S(1)}, bf16[272,256]{1,0:T(8,128)(2,1)S(1)}, u32[]{:S(2)}, u32[]{:S(2)}) collective-permute-start(bf16[272,256]{1,0:T(8,128)(2,1)S(1)} %get-tuple-element.32.refs_1_), channel_id=1, source_target_pairs={{0,4},{1,5},{2,6},{3,7},{4,0},{5,1},{6,2},{7,3},{8,12},{9,13},{10,... | collective-permute-start | bytes 417800 | tf_op jit(solution)/shard_map/ppermute | solution.py:380
  8.0 20.7 %collective-permute-start = (bf16[2,256,512]{2,1,0:T(8,128)(2,1)S(1)}, bf16[2,256,512]{2,1,0:T(8,128)(2,1)S(1)}, u32[]{:S(2)}, u32[]{:S(2)}) collective-permute-start(bf16[2,256,512]{2,1,0:T(8,128)(2,1)S(1)} %get-tuple-element.31), channel_id=1, source_target_pairs={{0,16},{8,24},{16,0},{24,8},{1,17},{9,25},{17,1},{25,9},{2,18},{10... | collective-permute-start | bytes 1572872 | tf_op jit(solution)/shard_map/ppermute | solution.py:380
  9.5 6.9 %collective-permute-start.3 = (bf16[272,256]{1,0:T(8,128)(2,1)S(1)}, bf16[272,256]{1,0:T(8,128)(2,1)S(1)}, u32[]{:S(2)}, u32[]{:S(2)}) collective-permute-start(bf16[272,256]{1,0:T(8,128)(2,1)S(1)} %get-tuple-element.32.refs_1_), channel_id=1, source_target_pairs={{0,1},{1,0},{2,3},{3,2},{4,5},{5,4},{6,7},{7,6},{8,9},{9,8},{10,11... | collective-permute-start | bytes 417800 | tf_op jit(solution)/shard_map/ppermute | solution.py:380
  11.2 6.7 %collective-permute-start.4 = (bf16[272,256]{1,0:T(8,128)(2,1)S(1)}, bf16[272,256]{1,0:T(8,128)(2,1)S(1)}, u32[]{:S(2)}, u32[]{:S(2)}) collective-permute-start(bf16[272,256]{1,0:T(8,128)(2,1)S(1)} %collective-permute-done.1.refs_2_), channel_id=1, source_target_pairs={{0,1},{1,0},{2,3},{3,2},{4,5},{5,4},{6,7},{7,6},{8,9},{9,8},{10,11... | collective-permute-start | bytes 417800 | tf_op jit(solution)/shard_map/ppermute | solution.py:380
  14.4 5.1 %collective-permute-start.5 = (bf16[272,256]{1,0:T(8,128)(2,1)S(1)}, bf16[272,256]{1,0:T(8,128)(2,1)S(1)}, u32[]{:S(2)}, u32[]{:S(2)}) collective-permute-start(bf16[272,256]{1,0:T(8,128)(2,1)S(1)} %collective-permute-done.2.refs_3_), channel_id=1, source_target_pairs={{0,2},{1,3},{2,0},{3,1},{4,6},{5,7},{6,4},{7,5},{8,10},{9,11},{10,... | collective-permute-start | bytes 417800 | tf_op jit(solution)/shard_map/ppermute | solution.py:380
  14.9 7.4 %collective-permute-start.6 = (bf16[272,256]{1,0:T(8,128)(2,1)S(1)}, bf16[272,256]{1,0:T(8,128)(2,1)S(1)}, u32[]{:S(2)}, u32[]{:S(2)}) collective-permute-start(bf16[272,256]{1,0:T(8,128)(2,1)S(1)} %collective-permute-done.2.refs_3_), channel_id=1, source_target_pairs={{0,1},{1,0},{2,3},{3,2},{4,5},{5,4},{6,7},{7,6},{8,9},{9,8},{10,11... | collective-permute-start | bytes 417800 | tf_op jit(solution)/shard_map/ppermute | solution.py:380
  19.5 5.1 %collective-permute-start.7 = (bf16[272,256]{1,0:T(8,128)(2,1)S(1)}, bf16[272,256]{1,0:T(8,128)(2,1)S(1)}, u32[]{:S(2)}, u32[]{:S(2)}) collective-permute-start(bf16[272,256]{1,0:T(8,128)(2,1)S(1)} %after.2), channel_id=1, source_target_pairs={{0,1},{1,0},{2,3},{3,2},{4,5},{5,4},{6,7},{7,6},{8,9},{9,8},{10,11... | collective-permute-start | bytes 417800 | tf_op jit(solution)/shard_map/ppermute | solution.py:380
  27.1 5.0 %collective-permute-start.8 = (bf16[1,256,256]{2,1,0:T(8,128)(2,1)S(1)}, bf16[1,256,256]{2,1,0:T(8,128)(2,1)S(1)}, u32[]{:S(2)}, u32[]{:S(2)}) collective-permute-start(bf16[1,256,256]{2,1,0:T(8,128)(2,1)S(1)} %group_grad.1.refs_0_.refs_3_), channel_id=1, source_target_pairs={{0,16},{8,24},{16,0},{24,8},{1,17},{9,25},{17,1},{25,9},{2,18},{10... | collective-permute-start | bytes 393224 | tf_op jit(solution)/shard_map/ppermute | solution.py:380
  32.2 2.4 %collective-permute-start.9 = (bf16[2,256,512]{2,1,0:T(8,128)(2,1)S(1)}, bf16[2,256,512]{2,1,0:T(8,128)(2,1)S(1)}, u32[]{:S(2)}, u32[]{:S(2)}) collective-permute-start(bf16[2,256,512]{2,1,0:T(8,128)(2,1)S(1)} %pack.2), channel_id=1, source_target_pairs={{0,8},{8,0},{16,24},{24,16},{1,9},{9,1},{17,25},{25,17},{2,10},{10... | collective-permute-start | bytes 1572872 | tf_op jit(solution)/shard_map/ppermute | solution.py:380
  32.3 2.2 %collective-permute-start.10 = (bf16[2,256,256]{2,1,0:T(8,128)(2,1)S(1)}, bf16[2,256,256]{2,1,0:T(8,128)(2,1)S(1)}, u32[]{:S(2)}, u32[]{:S(2)}) collective-permute-start(bf16[2,256,256]{2,1,0:T(8,128)(2,1)S(1)} %pack.3), channel_id=1, source_target_pairs={{0,8},{8,0},{16,24},{24,16},{1,9},{9,1},{17,25},{25,17},{2,10},{10... | collective-permute-start | bytes 786440 | tf_op jit(solution)/shard_map/ppermute | solution.py:380
  35.1 4.7 %collective-permute-start.12 = (bf16[2,64,256]{2,1,0:T(8,128)(2,1)S(1)}, bf16[2,64,256]{2,1,0:T(8,128)(2,1)S(1)}, u32[]{:S(2)}, u32[]{:S(2)}) collective-permute-start(bf16[2,64,256]{2,1,0:T(8,128)(2,1)S(1)} %get-tuple-element.51), channel_id=1, source_target_pairs={{0,1},{1,0},{2,3},{3,2},{4,5},{5,4},{6,7},{7,6},{8,9},{9,8},{10,11... | collective-permute-start | bytes 196616 | tf_op jit(solution)/shard_map/ppermute | solution.py:380
  36.6 6.8 %collective-permute-start.11 = (bf16[2,64,256]{2,1,0:T(8,128)(2,1)S(1)}, bf16[2,64,256]{2,1,0:T(8,128)(2,1)S(1)}, u32[]{:S(2)}, u32[]{:S(2)}) collective-permute-start(bf16[2,64,256]{2,1,0:T(8,128)(2,1)S(1)} %get-tuple-element.48), channel_id=1, source_target_pairs={{0,1},{1,0},{2,3},{3,2},{4,5},{5,4},{6,7},{7,6},{8,9},{9,8},{10,11... | collective-permute-start | bytes 196616 | tf_op jit(solution)/shard_map/ppermute | solution.py:380
  39.8 4.9 %collective-permute-start.13 = (bf16[64,256]{1,0:T(8,128)(2,1)S(1)}, bf16[64,256]{1,0:T(8,128)(2,1)S(1)}, u32[]{:S(2)}, u32[]{:S(2)}) collective-permute-start(bf16[64,256]{1,0:T(8,128)(2,1)S(1)} %get-tuple-element.52), channel_id=1, source_target_pairs={{0,4},{1,5},{2,6},{3,7},{4,0},{5,1},{6,2},{7,3},{8,12},{9,13},{10,... | collective-permute-start | bytes 98312 | tf_op jit(solution)/shard_map/ppermute | solution.py:380
  42.1 5.7 %collective-permute-start.14 = (bf16[64,256]{1,0:T(8,128)(2,1)S(1)}, bf16[64,256]{1,0:T(8,128)(2,1)S(1)}, u32[]{:S(2)}, u32[]{:S(2)}) collective-permute-start(bf16[64,256]{1,0:T(8,128)(2,1)S(1)} %get-tuple-element.53), channel_id=1, source_target_pairs={{0,6},{1,7},{2,4},{3,5},{4,2},{5,3},{6,0},{7,1},{8,14},{9,15},{10,... | collective-permute-start | bytes 98312 | tf_op jit(solution)/shard_map/ppermute | solution.py:380
  43.4 4.4 %collective-permute-start.15 = (bf16[64,256]{1,0:T(8,128)(2,1)S(1)}, bf16[64,256]{1,0:T(8,128)(2,1)S(1)}, u32[]{:S(2)}, u32[]{:S(2)}) collective-permute-start(bf16[64,256]{1,0:T(8,128)(2,1)S(1)} %get-tuple-element.54), channel_id=1, source_target_pairs={{0,2},{1,3},{2,0},{3,1},{4,6},{5,7},{6,4},{7,5},{8,10},{9,11},{10,... | collective-permute-start | bytes 98312 | tf_op jit(solution)/shard_map/ppermute | solution.py:380

commit v16 on v15

--- a/solution.py
+++ b/solution.py
@@ -143,10 +143,12 @@
         powers = powers_of(0, k)
         if k == 0:
             powers = jnp.where(off_diagonal, powers, 0.0)
-        else:
-            sums[k] = down(powers, own_column)
-        kept_at(k)[...] = powers
-        own_sums = own_sums + folded(powers * weight[k])
+        along, across = powers * weight[k], powers * own_column
+        kept_at(k)[0] = along
+        kept_at(k)[1] = across
+        if k:
+            sums[k] = jnp.sum(across, axis=0, keepdims=True)
+        own_sums = own_sums + folded(along)
     others = [k for k in seen if k]
     for k in fresh:
         if k == 0:
@@ -159,7 +161,7 @@
             sums[other] = sums[other] + down(powers, column)
         sums[k] = sums[k] + rows_to_lanes(mine)
         others.append(k)
-    return sums, own_sums, weight, own_column
+    return sums, own_sums, weight
 
 
 def pairs_kernel(seen, fresh, *refs):
@@ -172,7 +174,7 @@
         sums_ref, own_ref, refs = refs[0], refs[1], refs[2:]
         before = {k: sums_ref[at:at + 1, :] for at, k in enumerate(seen)}
     sums_out, own_out, kept_out = refs
-    sums, own_sums, _, _ = pair_sums(
+    sums, own_sums, _ = pair_sums(
         seen, fresh, counts_ref, msgs, before, own_ref, sums_out, lambda k: kept_out.at[fresh.index(k)]
     )
     own_out[...] = own_sums
@@ -197,7 +199,7 @@
         out_shape=(
             jax.ShapeDtypeStruct((len(known), rows), jnp.float32),
             jax.ShapeDtypeStruct((rows, 128), jnp.float32),
-            jax.ShapeDtypeStruct((len(fresh), rows, rows), jnp.float32),
+            jax.ShapeDtypeStruct((len(fresh), 2, rows, rows), jnp.float32),
         ),
         in_specs=[SMEM] + [VMEM] * (len(known) + len(state)),
         out_specs=(VMEM,) * 3,
@@ -217,7 +219,7 @@
     normed_ref, inv_ref, out_ref, kept = refs[-4:]
     rows, width = normed_ref.shape
     before = {k: sums_ref[at:at + 1, :] for at, k in enumerate(seen)}
-    sums, own_sums, weight, own_weight = pair_sums(
+    sums, own_sums, weight = pair_sums(
         seen, fresh, counts_ref, msgs, before, own_ref, None, lambda k: kept.at[fresh.index(k)]
     )
     sums[0] = rows_to_lanes(own_sums)
@@ -240,9 +242,8 @@
     both = jnp.zeros((2 * rows, width), jnp.float32)
     for k in known:
         columns = (me ^ k) * rows + lanes
-        powers = places[k][...]
-        along = powers * weight[k] * own_recip - jnp.where(own_partner == columns, 1.0, 0.0)
-        across = powers * own_weight * recip[k] - jnp.where(
+        along = places[k][0] * own_recip - jnp.where(own_partner == columns, 1.0, 0.0)
+        across = places[k][1] * recip[k] - jnp.where(
             partner_of(k).astype(jnp.int32) == own_rows, 1.0, 0.0
         )
         coefficients = jnp.concatenate([along.astype(jnp.bfloat16), across.astype(jnp.bfloat16)], axis=0)
@@ -262,7 +263,7 @@
         out_shape=jax.ShapeDtypeStruct((1, rows, width), jnp.bfloat16),
         in_specs=[SMEM] + [VMEM] * (len(known) + len(state) + len(kept) + len(earlier) + 2),
         out_specs=VMEM,
-        scratch_shapes=[pltpu.VMEM((len(fresh), rows, rows), jnp.float32)],
+        scratch_shapes=[pltpu.VMEM((len(fresh), 2, rows, rows), jnp.float32)],
         compiler_params=pltpu.CompilerParams(vmem_limit_bytes=VMEM_LIMIT),
         cost_estimate=pairs_cost(seen, fresh, rows, width),
         name="group_grad",

time: 48.7 us -> 48.5 us (level)
  no operation moved by 1% of the time
where the time goes in v16:
time: 48.5 us; the launch traced here: 48.4 us
  starting transfers between devices  22 us (45%)
  waiting for transfers between devices  15.5 us (32%)
  Pallas kernels  10.8 us (22%)
    ppermute x16, starting transfers between devices, swap(): return lax.ppermute(value, axis, [(at, at ^ flip) for at in range(size)])  22 us
    ppermute x16, waiting for transfers between devices, swap(): return lax.ppermute(value, axis, [(at, at ^ flip) for at in range(size)])  15.5 us
    pallas_call x4, Pallas kernels, add_pairs(): pl.pallas_call(functools.partial(pairs_kernel, seen, fresh), out_shape=(j...  4.94 us
    pallas_call x1, Pallas kernels, project(): pl.pallas_call(functools.partial(project_kernel, parts), out_shape=(jax.S...  2.29 us
    pallas_call x1, Pallas kernels, group_grad(): pl.pallas_call(functools.partial(grad_kernel, stages, fresh), out_shape=j...  2.26 us
  transfers between devices with their start and end apart: 16, of which 10 were waited for; matrix products, arithmetic and copies ran while one was open for 0% of the time, Pallas kernels for 15%

profile of v16, /device:TPU:0, one launch (start us, length us, event | category | flops | bytes accessed | tf_op | source)
XLA Modules:
  0.0 48.4 jit_solution(13020823829474396094)
XLA Ops:
  0.0 2.3 %project.1 = (bf16[272,256]{1,0:T(8,128)(2,1)S(1)}, f32[256,256]{1,0:T(8,128)S(1)}, f32[256,128]{1,0:T(8,128)S(1)}, bf16[2,256,512]{2,1,0:T(8,128)(2,1)S(1)}, bf16[2,256,512]{2,1,0:T(8,128)(2,1)S(1)}) custom-call(bf16[256,2048]{1,0:T(8,128)(2,1)} %feats_hbm.1, bf16[2048,256]{1,0:T(8,128)(2,1)} %w_hbm.1, s32[1,256]{1,0:T(1,128)} %bitcast.2, s32[1,256]{1,0:T(1,128)} %bitcast.3), custom_call_target="tpu_custom_call" | custom-call | flops 268435456 | bytes 2097152 | tf_op jit(solution)/shard_map/project/pallas_call | solution.py:81
  2.3 3.1 %collective-permute-start.1 = (bf16[272,256]{1,0:T(8,128)(2,1)S(1)}, bf16[272,256]{1,0:T(8,128)(2,1)S(1)}, u32[]{:S(2)}, u32[]{:S(2)}) collective-permute-start(bf16[272,256]{1,0:T(8,128)(2,1)S(1)} %get-tuple-element.32.refs_1_), channel_id=1, source_target_pairs={{0,2},{1,3},{2,0},{3,1},{4,6},{5,7},{6,4},{7,5},{8,10},{9,11},{10,... | collective-permute-start | bytes 417800 | tf_op jit(solution)/shard_map/ppermute | solution.py:381
  5.4 2.6 %collective-permute-start.2 = (bf16[272,256]{1,0:T(8,128)(2,1)S(1)}, bf16[272,256]{1,0:T(8,128)(2,1)S(1)}, u32[]{:S(2)}, u32[]{:S(2)}) collective-permute-start(bf16[272,256]{1,0:T(8,128)(2,1)S(1)} %get-tuple-element.32.refs_1_), channel_id=1, source_target_pairs={{0,4},{1,5},{2,6},{3,7},{4,0},{5,1},{6,2},{7,3},{8,12},{9,13},{10,... | collective-permute-start | bytes 417800 | tf_op jit(solution)/shard_map/ppermute | solution.py:381
  8.0 1.5 %collective-permute-start = (bf16[2,256,512]{2,1,0:T(8,128)(2,1)S(1)}, bf16[2,256,512]{2,1,0:T(8,128)(2,1)S(1)}, u32[]{:S(2)}, u32[]{:S(2)}) collective-permute-start(bf16[2,256,512]{2,1,0:T(8,128)(2,1)S(1)} %get-tuple-element.31), channel_id=1, source_target_pairs={{0,16},{8,24},{16,0},{24,8},{1,17},{9,25},{17,1},{25,9},{2,18},{10... | collective-permute-start | bytes 1572872 | tf_op jit(solution)/shard_map/ppermute | solution.py:381
  9.5 1.5 %collective-permute-start.3 = (bf16[272,256]{1,0:T(8,128)(2,1)S(1)}, bf16[272,256]{1,0:T(8,128)(2,1)S(1)}, u32[]{:S(2)}, u32[]{:S(2)}) collective-permute-start(bf16[272,256]{1,0:T(8,128)(2,1)S(1)} %get-tuple-element.32.refs_1_), channel_id=1, source_target_pairs={{0,1},{1,0},{2,3},{3,2},{4,5},{5,4},{6,7},{7,6},{8,9},{9,8},{10,11... | collective-permute-start | bytes 417800 | tf_op jit(solution)/shard_map/ppermute | solution.py:381
  11.0 0.3 collective-permute-done.1.refs_2_
  11.3 1.8 %collective-permute-start.4 = (bf16[272,256]{1,0:T(8,128)(2,1)S(1)}, bf16[272,256]{1,0:T(8,128)(2,1)S(1)}, u32[]{:S(2)}, u32[]{:S(2)}) collective-permute-start(bf16[272,256]{1,0:T(8,128)(2,1)S(1)} %collective-permute-done.1.refs_2_), channel_id=1, source_target_pairs={{0,1},{1,0},{2,3},{3,2},{4,5},{5,4},{6,7},{7,6},{8,9},{9,8},{10,11... | collective-permute-start | bytes 417800 | tf_op jit(solution)/shard_map/ppermute | solution.py:381
  13.1 1.4 %collective-permute-done.2.refs_3_ = bf16[272,256]{1,0:T(8,128)(2,1)S(1)} collective-permute-done((bf16[272,256]{1,0:T(8,128)(2,1)S(1)}, bf16[272,256]{1,0:T(8,128)(2,1)S(1)}, u32[]{:S(2)}, u32[]{:S(2)}) %collective-permute-start.2) | collective-permute-done | bytes 139296 | tf_op jit(solution)/shard_map/ppermute | solution.py:381
  14.5 0.4 collective-permute-start.5
  14.9 1.5 %collective-permute-start.6 = (bf16[272,256]{1,0:T(8,128)(2,1)S(1)}, bf16[272,256]{1,0:T(8,128)(2,1)S(1)}, u32[]{:S(2)}, u32[]{:S(2)}) collective-permute-start(bf16[272,256]{1,0:T(8,128)(2,1)S(1)} %collective-permute-done.2.refs_3_), channel_id=1, source_target_pairs={{0,1},{1,0},{2,3},{3,2},{4,5},{5,4},{6,7},{7,6},{8,9},{9,8},{10,11... | collective-permute-start | bytes 417800 | tf_op jit(solution)/shard_map/ppermute | solution.py:381
  16.4 1.4 %add_pairs.4 = (f32[4,256]{1,0:T(4,128)S(1)}, f32[256,128]{1,0:T(8,128)S(1)}, f32[4,2,256,256]{3,2,1,0:T(8,128)S(1)}) custom-call(s32[4,8]{1,0:T(4,128)S(1)} %copy-done, bf16[272,256]{1,0:T(8,128)(2,1)S(1)} %get-tuple-element.32.refs_1_, bf16[272,256]{1,0:T(8,128)(2,1)S(1)} %collective-permute-done.1.refs_2_, ...), custom_call_target="tpu_custom_call" | custom-call | flops 335544320 | bytes 1572864 | tf_op jit(solution)/shard_map/add_pairs/pallas_call | solution.py:197
  17.8 0.1 collective-permute-done.4.refs_5_
  18.0 1.1 %add_pairs.5 = (f32[5,256]{1,0:T(8,128)S(1)}, f32[256,128]{1,0:T(8,128)S(1)}, f32[1,2,256,256]{3,2,1,0:T(8,128)S(1)}) custom-call(s32[4,8]{1,0:T(4,128)S(1)} %copy-done, bf16[272,256]{1,0:T(8,128)(2,1)S(1)} %get-tuple-element.32.refs_1_, bf16[272,256]{1,0:T(8,128)(2,1)S(1)} %collective-permute-done.1.refs_2_, ...), custom_call_target="tpu_custom_call" | custom-call | flops 167772160 | bytes 917504 | tf_op jit(solution)/shard_map/add_pairs/pallas_call | solution.py:197
  19.1 0.4 collective-permute-done.5.value_ref.refs_6_
  19.5 1.6 %collective-permute-start.7 = (bf16[272,256]{1,0:T(8,128)(2,1)S(1)}, bf16[272,256]{1,0:T(8,128)(2,1)S(1)}, u32[]{:S(2)}, u32[]{:S(2)}) collective-permute-start(bf16[272,256]{1,0:T(8,128)(2,1)S(1)} %after.2), channel_id=1, source_target_pairs={{0,1},{1,0},{2,3},{3,2},{4,5},{5,4},{6,7},{7,6},{8,9},{9,8},{10,11... | collective-permute-start | bytes 417800 | tf_op jit(solution)/shard_map/ppermute | solution.py:381
  21.1 1.2 %add_pairs.6 = (f32[6,256]{1,0:T(8,128)S(1)}, f32[256,128]{1,0:T(8,128)S(1)}, f32[1,2,256,256]{3,2,1,0:T(8,128)S(1)}) custom-call(s32[4,8]{1,0:T(4,128)S(1)} %copy-done, bf16[272,256]{1,0:T(8,128)(2,1)S(1)} %get-tuple-element.32.refs_1_, bf16[272,256]{1,0:T(8,128)(2,1)S(1)} %collective-permute-done.1.refs_2_, ...), custom_call_target="tpu_custom_call" | custom-call | flops 201326592 | bytes 1048576 | tf_op jit(solution)/shard_map/add_pairs/pallas_call | solution.py:197
  22.3 1.2 %add_pairs.7 = (f32[7,256]{1,0:T(8,128)S(1)}, f32[256,128]{1,0:T(8,128)S(1)}, f32[1,2,256,256]{3,2,1,0:T(8,128)S(1)}) custom-call(s32[4,8]{1,0:T(4,128)S(1)} %copy-done, bf16[272,256]{1,0:T(8,128)(2,1)S(1)} %get-tuple-element.32.refs_1_, bf16[272,256]{1,0:T(8,128)(2,1)S(1)} %collective-permute-done.1.refs_2_, ...), custom_call_target="tpu_custom_call" | custom-call | flops 234881024 | bytes 1179648 | tf_op jit(solution)/shard_map/add_pairs/pallas_call | solution.py:197
  23.5 1.2 %collective-permute-done.7.refs_8_ = bf16[272,256]{1,0:T(8,128)(2,1)S(1)} collective-permute-done((bf16[272,256]{1,0:T(8,128)(2,1)S(1)}, bf16[272,256]{1,0:T(8,128)(2,1)S(1)}, u32[]{:S(2)}, u32[]{:S(2)}) %collective-permute-start.7) | collective-permute-done | bytes 139296 | tf_op jit(solution)/shard_map/ppermute | solution.py:381
  24.6 2.3 %group_grad.1.refs_0_.refs_3_ = bf16[1,256,256]{2,1,0:T(8,128)(2,1)S(1)} custom-call(s32[4,8]{1,0:T(4,128)S(1)} %copy-done, bf16[272,256]{1,0:T(8,128)(2,1)S(1)} %get-tuple-element.32.refs_1_, bf16[272,256]{1,0:T(8,128)(2,1)S(1)} %collective-permute-done.1.refs_2_, bf16[272,256]{1,0:T(8,128)(2,1)S(1)} %collective-permute-done.2.refs_3_, ...), custom_call_target="tpu_custom_call" | custom-call | flops 268435456 | bytes 1310720 | tf_op jit(solution)/shard_map/group_grad/pallas_call | solution.py:261
  26.9 1.6 %collective-permute-start.8 = (bf16[1,256,256]{2,1,0:T(8,128)(2,1)S(1)}, bf16[1,256,256]{2,1,0:T(8,128)(2,1)S(1)}, u32[]{:S(2)}, u32[]{:S(2)}) collective-permute-start(bf16[1,256,256]{2,1,0:T(8,128)(2,1)S(1)} %group_grad.1.refs_0_.refs_3_), channel_id=1, source_target_pairs={{0,16},{8,24},{16,0},{24,8},{1,17},{9,25},{17,1},{25,9},{2,18},{10... | collective-permute-start | bytes 393224 | tf_op jit(solution)/shard_map/ppermute | solution.py:381
  28.5 3.4 %collective-permute-done.8.refs_2_.refs_1_.refs_5_ = bf16[1,256,256]{2,1,0:T(8,128)(2,1)S(1)} collective-permute-done((bf16[1,256,256]{2,1,0:T(8,128)(2,1)S(1)}, bf16[1,256,256]{2,1,0:T(8,128)(2,1)S(1)}, u32[]{:S(2)}, u32[]{:S(2)}) %collective-permute-start.8) | collective-permute-done | bytes 131104 | tf_op jit(solution)/shard_map/ppermute | solution.py:381
  32.1 0.6 %collective-permute-start.10 = (bf16[2,256,256]{2,1,0:T(8,128)(2,1)S(1)}, bf16[2,256,256]{2,1,0:T(8,128)(2,1)S(1)}, u32[]{:S(2)}, u32[]{:S(2)}) collective-permute-start(bf16[2,256,256]{2,1,0:T(8,128)(2,1)S(1)} %pack.3), channel_id=1, source_target_pairs={{0,8},{8,0},{16,24},{24,16},{1,9},{9,1},{17,25},{25,17},{2,10},{10... | collective-permute-start | bytes 786440 | tf_op jit(solution)/shard_map/ppermute | solution.py:381
  32.6 1.7 %collective-permute-done.10.refs_4_ = bf16[2,256,256]{2,1,0:T(8,128)(2,1)S(1)} collective-permute-done((bf16[2,256,256]{2,1,0:T(8,128)(2,1)S(1)}, bf16[2,256,256]{2,1,0:T(8,128)(2,1)S(1)}, u32[]{:S(2)}, u32[]{:S(2)}) %collective-permute-start.10) | collective-permute-done | bytes 262176 | tf_op jit(solution)/shard_map/ppermute | solution.py:381
  34.3 0.5 %weight_grad.1 = (f32[2,64,256]{2,1,0:T(8,128)S(1)}, f32[2,64,256]{2,1,0:T(8,128)S(1)}, bf16[2,64,256]{2,1,0:T(8,128)(2,1)S(1)}, bf16[2,64,256]{2,1,0:T(8,128)(2,1)S(1)}) custom-call(bf16[2,256,512]{2,1,0:T(8,128)(2,1)S(1)} %get-tuple-element.30.refs_0_, bf16[2,256,512]{2,1,0:T(8,128)(2,1)S(1)} %collective-permute-done.9.refs_1_, ...), custom_call_target="tpu_custom_call" | custom-call | flops 268435456 | bytes 1048576 | tf_op jit(solution)/shard_map/weight_grad/pallas_call | solution.py:324
  34.9 1.6 %collective-permute-start.12 = (bf16[2,64,256]{2,1,0:T(8,128)(2,1)S(1)}, bf16[2,64,256]{2,1,0:T(8,128)(2,1)S(1)}, u32[]{:S(2)}, u32[]{:S(2)}) collective-permute-start(bf16[2,64,256]{2,1,0:T(8,128)(2,1)S(1)} %get-tuple-element.51), channel_id=1, source_target_pairs={{0,1},{1,0},{2,3},{3,2},{4,5},{5,4},{6,7},{7,6},{8,9},{9,8},{10,11... | collective-permute-start | bytes 196616 | tf_op jit(solution)/shard_map/ppermute | solution.py:381
  36.4 0.5 %collective-permute-start.11 = (bf16[2,64,256]{2,1,0:T(8,128)(2,1)S(1)}, bf16[2,64,256]{2,1,0:T(8,128)(2,1)S(1)}, u32[]{:S(2)}, u32[]{:S(2)}) collective-permute-start(bf16[2,64,256]{2,1,0:T(8,128)(2,1)S(1)} %get-tuple-element.48), channel_id=1, source_target_pairs={{0,1},{1,0},{2,3},{3,2},{4,5},{5,4},{6,7},{7,6},{8,9},{9,8},{10,11... | collective-permute-start | bytes 196616 | tf_op jit(solution)/shard_map/ppermute | solution.py:381
  37.0 2.6 %collective-permute-done.12.refs_0_ = bf16[2,64,256]{2,1,0:T(8,128)(2,1)S(1)} collective-permute-done((bf16[2,64,256]{2,1,0:T(8,128)(2,1)S(1)}, bf16[2,64,256]{2,1,0:T(8,128)(2,1)S(1)}, u32[]{:S(2)}, u32[]{:S(2)}) %collective-permute-start.12) | collective-permute-done | bytes 65568 | tf_op jit(solution)/shard_map/ppermute | solution.py:381
  39.6 2.3 %collective-permute-start.13 = (bf16[64,256]{1,0:T(8,128)(2,1)S(1)}, bf16[64,256]{1,0:T(8,128)(2,1)S(1)}, u32[]{:S(2)}, u32[]{:S(2)}) collective-permute-start(bf16[64,256]{1,0:T(8,128)(2,1)S(1)} %get-tuple-element.52), channel_id=1, source_target_pairs={{0,4},{1,5},{2,6},{3,7},{4,0},{5,1},{6,2},{7,3},{8,12},{9,13},{10,... | collective-permute-start | bytes 98312 | tf_op jit(solution)/shard_map/ppermute | solution.py:381
  42.0 1.3 %collective-permute-start.14 = (bf16[64,256]{1,0:T(8,128)(2,1)S(1)}, bf16[64,256]{1,0:T(8,128)(2,1)S(1)}, u32[]{:S(2)}, u32[]{:S(2)}) collective-permute-start(bf16[64,256]{1,0:T(8,128)(2,1)S(1)} %get-tuple-element.53), channel_id=1, source_target_pairs={{0,6},{1,7},{2,4},{3,5},{4,2},{5,3},{6,0},{7,1},{8,14},{9,15},{10,... | collective-permute-start | bytes 98312 | tf_op jit(solution)/shard_map/ppermute | solution.py:381
  43.4 1.1 %collective-permute-done.13.refs_0_ = bf16[64,256]{1,0:T(8,128)(2,1)S(1)} collective-permute-done((bf16[64,256]{1,0:T(8,128)(2,1)S(1)}, bf16[64,256]{1,0:T(8,128)(2,1)S(1)}, u32[]{:S(2)}, u32[]{:S(2)}) %collective-permute-start.13) | collective-permute-done | bytes 32800 | tf_op jit(solution)/shard_map/ppermute | solution.py:381
  44.5 3.2 %collective-permute-done.14.refs_1_ = bf16[64,256]{1,0:T(8,128)(2,1)S(1)} collective-permute-done((bf16[64,256]{1,0:T(8,128)(2,1)S(1)}, bf16[64,256]{1,0:T(8,128)(2,1)S(1)}, u32[]{:S(2)}, u32[]{:S(2)}) %collective-permute-start.14) | collective-permute-done | bytes 32800 | tf_op jit(solution)/shard_map/ppermute | solution.py:381
  47.7 0.6 %add_all.3 = f32[64,256]{1,0:T(8,128)} custom-call(f32[64,256]{1,0:T(8,128)S(1)} %get-tuple-element.49.refs_0_, f32[64,256]{1,0:T(8,128)S(1)} %add_all.2.refs_0_.refs_1_, bf16[64,256]{1,0:T(8,128)(2,1)S(1)} %after.3.refs_2_), custom_call_target="tpu_custom_call" | custom-call | tf_op jit(solution)/shard_map/add_all/pallas_call | solution.py:369
  (17 shorter events, 0.3 us)
Async XLA Ops:
  0.0 16.4 %copy-start = (s32[4,8]{1,0:T(4,128)S(1)}, s32[4,8]{1,0:T(4,128)}, u32[]{:S(2)}) copy-start(s32[4,8]{1,0:T(4,128)} %refs_0_.9) | copy-start | bytes 388
  2.3 9.0 %collective-permute-start.1 = (bf16[272,256]{1,0:T(8,128)(2,1)S(1)}, bf16[272,256]{1,0:T(8,128)(2,1)S(1)}, u32[]{:S(2)}, u32[]{:S(2)}) collective-permute-start(bf16[272,256]{1,0:T(8,128)(2,1)S(1)} %get-tuple-element.32.refs_1_), channel_id=1, source_target_pairs={{0,2},{1,3},{2,0},{3,1},{4,6},{5,7},{6,4},{7,5},{8,10},{9,11},{10,... | collective-permute-start | bytes 417800 | tf_op jit(solution)/shard_map/ppermute | solution.py:381
  5.4 9.1 %collective-permute-start.2 = (bf16[272,256]{1,0:T(8,128)(2,1)S(1)}, bf16[272,256]{1,0:T(8,128)(2,1)S(1)}, u32[]{:S(2)}, u32[]{:S(2)}) collective-permute-start(bf16[272,256]{1,0:T(8,128)(2,1)S(1)} %get-tuple-element.32.refs_1_), channel_id=1, source_target_pairs={{0,4},{1,5},{2,6},{3,7},{4,0},{5,1},{6,2},{7,3},{8,12},{9,13},{10,... | collective-permute-start | bytes 417800 | tf_op jit(solution)/shard_map/ppermute | solution.py:381
  8.0 20.5 %collective-permute-start = (bf16[2,256,512]{2,1,0:T(8,128)(2,1)S(1)}, bf16[2,256,512]{2,1,0:T(8,128)(2,1)S(1)}, u32[]{:S(2)}, u32[]{:S(2)}) collective-permute-start(bf16[2,256,512]{2,1,0:T(8,128)(2,1)S(1)} %get-tuple-element.31), channel_id=1, source_target_pairs={{0,16},{8,24},{16,0},{24,8},{1,17},{9,25},{17,1},{25,9},{2,18},{10... | collective-permute-start | bytes 1572872 | tf_op jit(solution)/shard_map/ppermute | solution.py:381
  9.5 6.9 %collective-permute-start.3 = (bf16[272,256]{1,0:T(8,128)(2,1)S(1)}, bf16[272,256]{1,0:T(8,128)(2,1)S(1)}, u32[]{:S(2)}, u32[]{:S(2)}) collective-permute-start(bf16[272,256]{1,0:T(8,128)(2,1)S(1)} %get-tuple-element.32.refs_1_), channel_id=1, source_target_pairs={{0,1},{1,0},{2,3},{3,2},{4,5},{5,4},{6,7},{7,6},{8,9},{9,8},{10,11... | collective-permute-start | bytes 417800 | tf_op jit(solution)/shard_map/ppermute | solution.py:381
  11.3 6.7 %collective-permute-start.4 = (bf16[272,256]{1,0:T(8,128)(2,1)S(1)}, bf16[272,256]{1,0:T(8,128)(2,1)S(1)}, u32[]{:S(2)}, u32[]{:S(2)}) collective-permute-start(bf16[272,256]{1,0:T(8,128)(2,1)S(1)} %collective-permute-done.1.refs_2_), channel_id=1, source_target_pairs={{0,1},{1,0},{2,3},{3,2},{4,5},{5,4},{6,7},{7,6},{8,9},{9,8},{10,11... | collective-permute-start | bytes 417800 | tf_op jit(solution)/shard_map/ppermute | solution.py:381
  14.5 5.1 %collective-permute-start.5 = (bf16[272,256]{1,0:T(8,128)(2,1)S(1)}, bf16[272,256]{1,0:T(8,128)(2,1)S(1)}, u32[]{:S(2)}, u32[]{:S(2)}) collective-permute-start(bf16[272,256]{1,0:T(8,128)(2,1)S(1)} %collective-permute-done.2.refs_3_), channel_id=1, source_target_pairs={{0,2},{1,3},{2,0},{3,1},{4,6},{5,7},{6,4},{7,5},{8,10},{9,11},{10,... | collective-permute-start | bytes 417800 | tf_op jit(solution)/shard_map/ppermute | solution.py:381
  14.9 7.3 %collective-permute-start.6 = (bf16[272,256]{1,0:T(8,128)(2,1)S(1)}, bf16[272,256]{1,0:T(8,128)(2,1)S(1)}, u32[]{:S(2)}, u32[]{:S(2)}) collective-permute-start(bf16[272,256]{1,0:T(8,128)(2,1)S(1)} %collective-permute-done.2.refs_3_), channel_id=1, source_target_pairs={{0,1},{1,0},{2,3},{3,2},{4,5},{5,4},{6,7},{7,6},{8,9},{9,8},{10,11... | collective-permute-start | bytes 417800 | tf_op jit(solution)/shard_map/ppermute | solution.py:381
  19.5 5.1 %collective-permute-start.7 = (bf16[272,256]{1,0:T(8,128)(2,1)S(1)}, bf16[272,256]{1,0:T(8,128)(2,1)S(1)}, u32[]{:S(2)}, u32[]{:S(2)}) collective-permute-start(bf16[272,256]{1,0:T(8,128)(2,1)S(1)} %after.2), channel_id=1, source_target_pairs={{0,1},{1,0},{2,3},{3,2},{4,5},{5,4},{6,7},{7,6},{8,9},{9,8},{10,11... | collective-permute-start | bytes 417800 | tf_op jit(solution)/shard_map/ppermute | solution.py:381
  26.9 5.0 %collective-permute-start.8 = (bf16[1,256,256]{2,1,0:T(8,128)(2,1)S(1)}, bf16[1,256,256]{2,1,0:T(8,128)(2,1)S(1)}, u32[]{:S(2)}, u32[]{:S(2)}) collective-permute-start(bf16[1,256,256]{2,1,0:T(8,128)(2,1)S(1)} %group_grad.1.refs_0_.refs_3_), channel_id=1, source_target_pairs={{0,16},{8,24},{16,0},{24,8},{1,17},{9,25},{17,1},{25,9},{2,18},{10... | collective-permute-start | bytes 393224 | tf_op jit(solution)/shard_map/ppermute | solution.py:381
  32.0 2.4 %collective-permute-start.9 = (bf16[2,256,512]{2,1,0:T(8,128)(2,1)S(1)}, bf16[2,256,512]{2,1,0:T(8,128)(2,1)S(1)}, u32[]{:S(2)}, u32[]{:S(2)}) collective-permute-start(bf16[2,256,512]{2,1,0:T(8,128)(2,1)S(1)} %pack.2), channel_id=1, source_target_pairs={{0,8},{8,0},{16,24},{24,16},{1,9},{9,1},{17,25},{25,17},{2,10},{10... | collective-permute-start | bytes 1572872 | tf_op jit(solution)/shard_map/ppermute | solution.py:381
  32.1 2.2 %collective-permute-start.10 = (bf16[2,256,256]{2,1,0:T(8,128)(2,1)S(1)}, bf16[2,256,256]{2,1,0:T(8,128)(2,1)S(1)}, u32[]{:S(2)}, u32[]{:S(2)}) collective-permute-start(bf16[2,256,256]{2,1,0:T(8,128)(2,1)S(1)} %pack.3), channel_id=1, source_target_pairs={{0,8},{8,0},{16,24},{24,16},{1,9},{9,1},{17,25},{25,17},{2,10},{10... | collective-permute-start | bytes 786440 | tf_op jit(solution)/shard_map/ppermute | solution.py:381
  34.9 4.7 %collective-permute-start.12 = (bf16[2,64,256]{2,1,0:T(8,128)(2,1)S(1)}, bf16[2,64,256]{2,1,0:T(8,128)(2,1)S(1)}, u32[]{:S(2)}, u32[]{:S(2)}) collective-permute-start(bf16[2,64,256]{2,1,0:T(8,128)(2,1)S(1)} %get-tuple-element.51), channel_id=1, source_target_pairs={{0,1},{1,0},{2,3},{3,2},{4,5},{5,4},{6,7},{7,6},{8,9},{9,8},{10,11... | collective-permute-start | bytes 196616 | tf_op jit(solution)/shard_map/ppermute | solution.py:381
  36.4 6.8 %collective-permute-start.11 = (bf16[2,64,256]{2,1,0:T(8,128)(2,1)S(1)}, bf16[2,64,256]{2,1,0:T(8,128)(2,1)S(1)}, u32[]{:S(2)}, u32[]{:S(2)}) collective-permute-start(bf16[2,64,256]{2,1,0:T(8,128)(2,1)S(1)} %get-tuple-element.48), channel_id=1, source_target_pairs={{0,1},{1,0},{2,3},{3,2},{4,5},{5,4},{6,7},{7,6},{8,9},{9,8},{10,11... | collective-permute-start | bytes 196616 | tf_op jit(solution)/shard_map/ppermute | solution.py:381
  39.6 4.9 %collective-permute-start.13 = (bf16[64,256]{1,0:T(8,128)(2,1)S(1)}, bf16[64,256]{1,0:T(8,128)(2,1)S(1)}, u32[]{:S(2)}, u32[]{:S(2)}) collective-permute-start(bf16[64,256]{1,0:T(8,128)(2,1)S(1)} %get-tuple-element.52), channel_id=1, source_target_pairs={{0,4},{1,5},{2,6},{3,7},{4,0},{5,1},{6,2},{7,3},{8,12},{9,13},{10,... | collective-permute-start | bytes 98312 | tf_op jit(solution)/shard_map/ppermute | solution.py:381
  42.0 5.7 %collective-permute-start.14 = (bf16[64,256]{1,0:T(8,128)(2,1)S(1)}, bf16[64,256]{1,0:T(8,128)(2,1)S(1)}, u32[]{:S(2)}, u32[]{:S(2)}) collective-permute-start(bf16[64,256]{1,0:T(8,128)(2,1)S(1)} %get-tuple-element.53), channel_id=1, source_target_pairs={{0,6},{1,7},{2,4},{3,5},{4,2},{5,3},{6,0},{7,1},{8,14},{9,15},{10,... | collective-permute-start | bytes 98312 | tf_op jit(solution)/shard_map/ppermute | solution.py:381
  43.3 4.4 %collective-permute-start.15 = (bf16[64,256]{1,0:T(8,128)(2,1)S(1)}, bf16[64,256]{1,0:T(8,128)(2,1)S(1)}, u32[]{:S(2)}, u32[]{:S(2)}) collective-permute-start(bf16[64,256]{1,0:T(8,128)(2,1)S(1)} %get-tuple-element.54), channel_id=1, source_target_pairs={{0,2},{1,3},{2,0},{3,1},{4,6},{5,7},{6,4},{7,5},{8,10},{9,11},{10,... | collective-permute-start | bytes 98312 | tf_op jit(solution)/shard_map/ppermute | solution.py:381

commit v17 on v16

--- a/solution.py
+++ b/solution.py
@@ -43,22 +43,20 @@
     )
     for copy in small:
         copy.start()
-    copies = []
-    for k in range(parts):
-        first = pl.multiple_of((me ^ k) * step, step)
-        cut = pl.ds(first, step)
-        pair = (
-            pltpu.make_async_copy(feats_hbm.at[:, cut], cuts[k], sems.at[0, k]),
-            pltpu.make_async_copy(w_hbm.at[cut, :], w_v.at[pl.ds(k * step, step), :], sems.at[1, k]),
-        )
-        pair[0].start()
-        pair[1].start()
-        copies.append(pair)
+    w_copy = pltpu.make_async_copy(w_hbm, w_v, small_sems.at[2])
+    w_copy.start()
+    firsts = [pl.multiple_of((me ^ k) * step, step) for k in range(parts)]
+    copies = [
+        pltpu.make_async_copy(feats_hbm.at[:, pl.ds(first, step)], cut, sems.at[k])
+        for k, (first, cut) in enumerate(zip(firsts, cuts))
+    ]
+    for copy in copies:
+        copy.start()
+    w_copy.wait()
     projected = jnp.zeros((rows, width), jnp.float32)
-    for k in range(parts):
-        copies[k][0].wait()
-        copies[k][1].wait()
-        projected = projected + f32_dot(cuts[k][...], w_v[pl.ds(k * step, step), :], ((1,), (0,)))
+    for copy, first, cut in zip(copies, firsts, cuts):
+        copy.wait()
+        projected = projected + f32_dot(cut[...], w_v[pl.ds(first, step), :], ((1,), (0,)))
     for copy in small:
         copy.wait()
     partners = partners_ref[...]
@@ -92,8 +90,8 @@
             pltpu.VMEM((din, width), jnp.bfloat16),
             pltpu.VMEM((1, rows), jnp.int32),
             pltpu.VMEM((1, rows), jnp.int32),
-            pltpu.SemaphoreType.DMA((2, parts)),
-            pltpu.SemaphoreType.DMA((2,)),
+            pltpu.SemaphoreType.DMA((parts,)),
+            pltpu.SemaphoreType.DMA((3,)),
         ],
         compiler_params=pltpu.CompilerParams(vmem_limit_bytes=VMEM_LIMIT),
         cost_estimate=pl.CostEstimate(

time: 48.5 us -> 48.8 us (level)
  no operation moved by 1% of the time
where the time goes in v17:
time: 48.8 us; the launch traced here: 48.6 us
  starting transfers between devices  22 us (45%)
  waiting for transfers between devices  15.4 us (32%)
  Pallas kernels  11.1 us (23%)
    ppermute x16, starting transfers between devices, swap(): return lax.ppermute(value, axis, [(at, at ^ flip) for at in range(size)])  22 us
    ppermute x16, waiting for transfers between devices, swap(): return lax.ppermute(value, axis, [(at, at ^ flip) for at in range(size)])  15.4 us
    pallas_call x4, Pallas kernels, add_pairs(): pl.pallas_call(functools.partial(pairs_kernel, seen, fresh), out_shape=(j...  4.95 us
    pallas_call x1, Pallas kernels, project(): pl.pallas_call(functools.partial(project_kernel, parts), out_shape=(jax.S...  2.6 us
    pallas_call x1, Pallas kernels, group_grad(): pl.pallas_call(functools.partial(grad_kernel, stages, fresh), out_shape=j...  2.27 us
  transfers between devices with their start and end apart: 16, of which 10 were waited for; matrix products, arithmetic and copies ran while one was open for 0% of the time, Pallas kernels for 15%

profile of v17, /device:TPU:0, one launch (start us, length us, event | category | flops | bytes accessed | tf_op | source)
XLA Modules:
  0.0 48.6 jit_solution(17002372942219429115)
XLA Ops:
  0.0 2.6 %project.1 = (bf16[272,256]{1,0:T(8,128)(2,1)S(1)}, f32[256,256]{1,0:T(8,128)S(1)}, f32[256,128]{1,0:T(8,128)S(1)}, bf16[2,256,512]{2,1,0:T(8,128)(2,1)S(1)}, bf16[2,256,512]{2,1,0:T(8,128)(2,1)S(1)}) custom-call(bf16[256,2048]{1,0:T(8,128)(2,1)} %feats_hbm.1, bf16[2048,256]{1,0:T(8,128)(2,1)} %w_hbm.1, s32[1,256]{1,0:T(1,128)} %bitcast.2, s32[1,256]{1,0:T(1,128)} %bitcast.3), custom_call_target="tpu_custom_call" | custom-call | flops 268435456 | bytes 2097152 | tf_op jit(solution)/shard_map/project/pallas_call | solution.py:79
  2.6 3.1 %collective-permute-start.1 = (bf16[272,256]{1,0:T(8,128)(2,1)S(1)}, bf16[272,256]{1,0:T(8,128)(2,1)S(1)}, u32[]{:S(2)}, u32[]{:S(2)}) collective-permute-start(bf16[272,256]{1,0:T(8,128)(2,1)S(1)} %get-tuple-element.32.refs_1_), channel_id=1, source_target_pairs={{0,2},{1,3},{2,0},{3,1},{4,6},{5,7},{6,4},{7,5},{8,10},{9,11},{10,... | collective-permute-start | bytes 417800 | tf_op jit(solution)/shard_map/ppermute | solution.py:379
  5.7 2.6 %collective-permute-start.2 = (bf16[272,256]{1,0:T(8,128)(2,1)S(1)}, bf16[272,256]{1,0:T(8,128)(2,1)S(1)}, u32[]{:S(2)}, u32[]{:S(2)}) collective-permute-start(bf16[272,256]{1,0:T(8,128)(2,1)S(1)} %get-tuple-element.32.refs_1_), channel_id=1, source_target_pairs={{0,4},{1,5},{2,6},{3,7},{4,0},{5,1},{6,2},{7,3},{8,12},{9,13},{10,... | collective-permute-start | bytes 417800 | tf_op jit(solution)/shard_map/ppermute | solution.py:379
  8.3 1.5 %collective-permute-start = (bf16[2,256,512]{2,1,0:T(8,128)(2,1)S(1)}, bf16[2,256,512]{2,1,0:T(8,128)(2,1)S(1)}, u32[]{:S(2)}, u32[]{:S(2)}) collective-permute-start(bf16[2,256,512]{2,1,0:T(8,128)(2,1)S(1)} %get-tuple-element.31), channel_id=1, source_target_pairs={{0,16},{8,24},{16,0},{24,8},{1,17},{9,25},{17,1},{25,9},{2,18},{10... | collective-permute-start | bytes 1572872 | tf_op jit(solution)/shard_map/ppermute | solution.py:379
  9.8 1.5 %collective-permute-start.3 = (bf16[272,256]{1,0:T(8,128)(2,1)S(1)}, bf16[272,256]{1,0:T(8,128)(2,1)S(1)}, u32[]{:S(2)}, u32[]{:S(2)}) collective-permute-start(bf16[272,256]{1,0:T(8,128)(2,1)S(1)} %get-tuple-element.32.refs_1_), channel_id=1, source_target_pairs={{0,1},{1,0},{2,3},{3,2},{4,5},{5,4},{6,7},{7,6},{8,9},{9,8},{10,11... | collective-permute-start | bytes 417800 | tf_op jit(solution)/shard_map/ppermute | solution.py:379
  11.3 0.3 collective-permute-done.1.refs_2_
  11.6 1.8 %collective-permute-start.4 = (bf16[272,256]{1,0:T(8,128)(2,1)S(1)}, bf16[272,256]{1,0:T(8,128)(2,1)S(1)}, u32[]{:S(2)}, u32[]{:S(2)}) collective-permute-start(bf16[272,256]{1,0:T(8,128)(2,1)S(1)} %collective-permute-done.1.refs_2_), channel_id=1, source_target_pairs={{0,1},{1,0},{2,3},{3,2},{4,5},{5,4},{6,7},{7,6},{8,9},{9,8},{10,11... | collective-permute-start | bytes 417800 | tf_op jit(solution)/shard_map/ppermute | solution.py:379
  13.4 1.4 %collective-permute-done.2.refs_3_ = bf16[272,256]{1,0:T(8,128)(2,1)S(1)} collective-permute-done((bf16[272,256]{1,0:T(8,128)(2,1)S(1)}, bf16[272,256]{1,0:T(8,128)(2,1)S(1)}, u32[]{:S(2)}, u32[]{:S(2)}) %collective-permute-start.2) | collective-permute-done | bytes 139296 | tf_op jit(solution)/shard_map/ppermute | solution.py:379
  14.8 0.4 collective-permute-start.5
  15.2 1.5 %collective-permute-start.6 = (bf16[272,256]{1,0:T(8,128)(2,1)S(1)}, bf16[272,256]{1,0:T(8,128)(2,1)S(1)}, u32[]{:S(2)}, u32[]{:S(2)}) collective-permute-start(bf16[272,256]{1,0:T(8,128)(2,1)S(1)} %collective-permute-done.2.refs_3_), channel_id=1, source_target_pairs={{0,1},{1,0},{2,3},{3,2},{4,5},{5,4},{6,7},{7,6},{8,9},{9,8},{10,11... | collective-permute-start | bytes 417800 | tf_op jit(solution)/shard_map/ppermute | solution.py:379
  16.7 1.4 %add_pairs.4 = (f32[4,256]{1,0:T(4,128)S(1)}, f32[256,128]{1,0:T(8,128)S(1)}, f32[4,2,256,256]{3,2,1,0:T(8,128)S(1)}) custom-call(s32[4,8]{1,0:T(4,128)S(1)} %copy-done, bf16[272,256]{1,0:T(8,128)(2,1)S(1)} %get-tuple-element.32.refs_1_, bf16[272,256]{1,0:T(8,128)(2,1)S(1)} %collective-permute-done.1.refs_2_, ...), custom_call_target="tpu_custom_call" | custom-call | flops 335544320 | bytes 1572864 | tf_op jit(solution)/shard_map/add_pairs/pallas_call | solution.py:195
  18.1 0.1 collective-permute-done.4.refs_5_
  18.3 1.1 %add_pairs.5 = (f32[5,256]{1,0:T(8,128)S(1)}, f32[256,128]{1,0:T(8,128)S(1)}, f32[1,2,256,256]{3,2,1,0:T(8,128)S(1)}) custom-call(s32[4,8]{1,0:T(4,128)S(1)} %copy-done, bf16[272,256]{1,0:T(8,128)(2,1)S(1)} %get-tuple-element.32.refs_1_, bf16[272,256]{1,0:T(8,128)(2,1)S(1)} %collective-permute-done.1.refs_2_, ...), custom_call_target="tpu_custom_call" | custom-call | flops 167772160 | bytes 917504 | tf_op jit(solution)/shard_map/add_pairs/pallas_call | solution.py:195
  19.4 0.4 collective-permute-done.5.value_ref.refs_6_
  19.8 1.6 %collective-permute-start.7 = (bf16[272,256]{1,0:T(8,128)(2,1)S(1)}, bf16[272,256]{1,0:T(8,128)(2,1)S(1)}, u32[]{:S(2)}, u32[]{:S(2)}) collective-permute-start(bf16[272,256]{1,0:T(8,128)(2,1)S(1)} %after.2), channel_id=1, source_target_pairs={{0,1},{1,0},{2,3},{3,2},{4,5},{5,4},{6,7},{7,6},{8,9},{9,8},{10,11... | collective-permute-start | bytes 417800 | tf_op jit(solution)/shard_map/ppermute | solution.py:379
  21.4 1.2 %add_pairs.6 = (f32[6,256]{1,0:T(8,128)S(1)}, f32[256,128]{1,0:T(8,128)S(1)}, f32[1,2,256,256]{3,2,1,0:T(8,128)S(1)}) custom-call(s32[4,8]{1,0:T(4,128)S(1)} %copy-done, bf16[272,256]{1,0:T(8,128)(2,1)S(1)} %get-tuple-element.32.refs_1_, bf16[272,256]{1,0:T(8,128)(2,1)S(1)} %collective-permute-done.1.refs_2_, ...), custom_call_target="tpu_custom_call" | custom-call | flops 201326592 | bytes 1048576 | tf_op jit(solution)/shard_map/add_pairs/pallas_call | solution.py:195
  22.6 1.2 %add_pairs.7 = (f32[7,256]{1,0:T(8,128)S(1)}, f32[256,128]{1,0:T(8,128)S(1)}, f32[1,2,256,256]{3,2,1,0:T(8,128)S(1)}) custom-call(s32[4,8]{1,0:T(4,128)S(1)} %copy-done, bf16[272,256]{1,0:T(8,128)(2,1)S(1)} %get-tuple-element.32.refs_1_, bf16[272,256]{1,0:T(8,128)(2,1)S(1)} %collective-permute-done.1.refs_2_, ...), custom_call_target="tpu_custom_call" | custom-call | flops 234881024 | bytes 1179648 | tf_op jit(solution)/shard_map/add_pairs/pallas_call | solution.py:195
  23.8 1.1 %collective-permute-done.7.refs_8_ = bf16[272,256]{1,0:T(8,128)(2,1)S(1)} collective-permute-done((bf16[272,256]{1,0:T(8,128)(2,1)S(1)}, bf16[272,256]{1,0:T(8,128)(2,1)S(1)}, u32[]{:S(2)}, u32[]{:S(2)}) %collective-permute-start.7) | collective-permute-done | bytes 139296 | tf_op jit(solution)/shard_map/ppermute | solution.py:379
  25.0 2.3 %group_grad.1.refs_0_.refs_3_ = bf16[1,256,256]{2,1,0:T(8,128)(2,1)S(1)} custom-call(s32[4,8]{1,0:T(4,128)S(1)} %copy-done, bf16[272,256]{1,0:T(8,128)(2,1)S(1)} %get-tuple-element.32.refs_1_, bf16[272,256]{1,0:T(8,128)(2,1)S(1)} %collective-permute-done.1.refs_2_, bf16[272,256]{1,0:T(8,128)(2,1)S(1)} %collective-permute-done.2.refs_3_, ...), custom_call_target="tpu_custom_call" | custom-call | flops 268435456 | bytes 1310720 | tf_op jit(solution)/shard_map/group_grad/pallas_call | solution.py:259
  27.2 1.6 %collective-permute-start.8 = (bf16[1,256,256]{2,1,0:T(8,128)(2,1)S(1)}, bf16[1,256,256]{2,1,0:T(8,128)(2,1)S(1)}, u32[]{:S(2)}, u32[]{:S(2)}) collective-permute-start(bf16[1,256,256]{2,1,0:T(8,128)(2,1)S(1)} %group_grad.1.refs_0_.refs_3_), channel_id=1, source_target_pairs={{0,16},{8,24},{16,0},{24,8},{1,17},{9,25},{17,1},{25,9},{2,18},{10... | collective-permute-start | bytes 393224 | tf_op jit(solution)/shard_map/ppermute | solution.py:379
  28.8 3.4 %collective-permute-done.8.refs_2_.refs_1_.refs_5_ = bf16[1,256,256]{2,1,0:T(8,128)(2,1)S(1)} collective-permute-done((bf16[1,256,256]{2,1,0:T(8,128)(2,1)S(1)}, bf16[1,256,256]{2,1,0:T(8,128)(2,1)S(1)}, u32[]{:S(2)}, u32[]{:S(2)}) %collective-permute-start.8) | collective-permute-done | bytes 131104 | tf_op jit(solution)/shard_map/ppermute | solution.py:379
  32.4 0.6 %collective-permute-start.10 = (bf16[2,256,256]{2,1,0:T(8,128)(2,1)S(1)}, bf16[2,256,256]{2,1,0:T(8,128)(2,1)S(1)}, u32[]{:S(2)}, u32[]{:S(2)}) collective-permute-start(bf16[2,256,256]{2,1,0:T(8,128)(2,1)S(1)} %pack.3), channel_id=1, source_target_pairs={{0,8},{8,0},{16,24},{24,16},{1,9},{9,1},{17,25},{25,17},{2,10},{10... | collective-permute-start | bytes 786440 | tf_op jit(solution)/shard_map/ppermute | solution.py:379
  33.0 1.7 %collective-permute-done.10.refs_4_ = bf16[2,256,256]{2,1,0:T(8,128)(2,1)S(1)} collective-permute-done((bf16[2,256,256]{2,1,0:T(8,128)(2,1)S(1)}, bf16[2,256,256]{2,1,0:T(8,128)(2,1)S(1)}, u32[]{:S(2)}, u32[]{:S(2)}) %collective-permute-start.10) | collective-permute-done | bytes 262176 | tf_op jit(solution)/shard_map/ppermute | solution.py:379
  34.7 0.5 %weight_grad.1 = (f32[2,64,256]{2,1,0:T(8,128)S(1)}, f32[2,64,256]{2,1,0:T(8,128)S(1)}, bf16[2,64,256]{2,1,0:T(8,128)(2,1)S(1)}, bf16[2,64,256]{2,1,0:T(8,128)(2,1)S(1)}) custom-call(bf16[2,256,512]{2,1,0:T(8,128)(2,1)S(1)} %get-tuple-element.30.refs_0_, bf16[2,256,512]{2,1,0:T(8,128)(2,1)S(1)} %collective-permute-done.9.refs_1_, ...), custom_call_target="tpu_custom_call" | custom-call | flops 268435456 | bytes 1048576 | tf_op jit(solution)/shard_map/weight_grad/pallas_call | solution.py:322
  35.2 1.6 %collective-permute-start.12 = (bf16[2,64,256]{2,1,0:T(8,128)(2,1)S(1)}, bf16[2,64,256]{2,1,0:T(8,128)(2,1)S(1)}, u32[]{:S(2)}, u32[]{:S(2)}) collective-permute-start(bf16[2,64,256]{2,1,0:T(8,128)(2,1)S(1)} %get-tuple-element.51), channel_id=1, source_target_pairs={{0,1},{1,0},{2,3},{3,2},{4,5},{5,4},{6,7},{7,6},{8,9},{9,8},{10,11... | collective-permute-start | bytes 196616 | tf_op jit(solution)/shard_map/ppermute | solution.py:379
  36.7 0.5 %collective-permute-start.11 = (bf16[2,64,256]{2,1,0:T(8,128)(2,1)S(1)}, bf16[2,64,256]{2,1,0:T(8,128)(2,1)S(1)}, u32[]{:S(2)}, u32[]{:S(2)}) collective-permute-start(bf16[2,64,256]{2,1,0:T(8,128)(2,1)S(1)} %get-tuple-element.48), channel_id=1, source_target_pairs={{0,1},{1,0},{2,3},{3,2},{4,5},{5,4},{6,7},{7,6},{8,9},{9,8},{10,11... | collective-permute-start | bytes 196616 | tf_op jit(solution)/shard_map/ppermute | solution.py:379
  37.3 2.6 %collective-permute-done.12.refs_0_ = bf16[2,64,256]{2,1,0:T(8,128)(2,1)S(1)} collective-permute-done((bf16[2,64,256]{2,1,0:T(8,128)(2,1)S(1)}, bf16[2,64,256]{2,1,0:T(8,128)(2,1)S(1)}, u32[]{:S(2)}, u32[]{:S(2)}) %collective-permute-start.12) | collective-permute-done | bytes 65568 | tf_op jit(solution)/shard_map/ppermute | solution.py:379
  39.9 2.3 %collective-permute-start.13 = (bf16[64,256]{1,0:T(8,128)(2,1)S(1)}, bf16[64,256]{1,0:T(8,128)(2,1)S(1)}, u32[]{:S(2)}, u32[]{:S(2)}) collective-permute-start(bf16[64,256]{1,0:T(8,128)(2,1)S(1)} %get-tuple-element.52), channel_id=1, source_target_pairs={{0,4},{1,5},{2,6},{3,7},{4,0},{5,1},{6,2},{7,3},{8,12},{9,13},{10,... | collective-permute-start | bytes 98312 | tf_op jit(solution)/shard_map/ppermute | solution.py:379
  42.2 1.3 %collective-permute-start.14 = (bf16[64,256]{1,0:T(8,128)(2,1)S(1)}, bf16[64,256]{1,0:T(8,128)(2,1)S(1)}, u32[]{:S(2)}, u32[]{:S(2)}) collective-permute-start(bf16[64,256]{1,0:T(8,128)(2,1)S(1)} %get-tuple-element.53), channel_id=1, source_target_pairs={{0,6},{1,7},{2,4},{3,5},{4,2},{5,3},{6,0},{7,1},{8,14},{9,15},{10,... | collective-permute-start | bytes 98312 | tf_op jit(solution)/shard_map/ppermute | solution.py:379
  43.7 1.2 %collective-permute-done.13.refs_0_ = bf16[64,256]{1,0:T(8,128)(2,1)S(1)} collective-permute-done((bf16[64,256]{1,0:T(8,128)(2,1)S(1)}, bf16[64,256]{1,0:T(8,128)(2,1)S(1)}, u32[]{:S(2)}, u32[]{:S(2)}) %collective-permute-start.13) | collective-permute-done | bytes 32800 | tf_op jit(solution)/shard_map/ppermute | solution.py:379
  44.8 3.1 %collective-permute-done.14.refs_1_ = bf16[64,256]{1,0:T(8,128)(2,1)S(1)} collective-permute-done((bf16[64,256]{1,0:T(8,128)(2,1)S(1)}, bf16[64,256]{1,0:T(8,128)(2,1)S(1)}, u32[]{:S(2)}, u32[]{:S(2)}) %collective-permute-start.14) | collective-permute-done | bytes 32800 | tf_op jit(solution)/shard_map/ppermute | solution.py:379
  48.0 0.6 %add_all.3 = f32[64,256]{1,0:T(8,128)} custom-call(f32[64,256]{1,0:T(8,128)S(1)} %get-tuple-element.49.refs_0_, f32[64,256]{1,0:T(8,128)S(1)} %add_all.2.refs_0_.refs_1_, bf16[64,256]{1,0:T(8,128)(2,1)S(1)} %after.3.refs_2_), custom_call_target="tpu_custom_call" | custom-call | tf_op jit(solution)/shard_map/add_all/pallas_call | solution.py:367
  (17 shorter events, 0.3 us)
Async XLA Ops:
  0.0 16.7 %copy-start = (s32[4,8]{1,0:T(4,128)S(1)}, s32[4,8]{1,0:T(4,128)}, u32[]{:S(2)}) copy-start(s32[4,8]{1,0:T(4,128)} %refs_0_.9) | copy-start | bytes 388
  2.6 9.0 %collective-permute-start.1 = (bf16[272,256]{1,0:T(8,128)(2,1)S(1)}, bf16[272,256]{1,0:T(8,128)(2,1)S(1)}, u32[]{:S(2)}, u32[]{:S(2)}) collective-permute-start(bf16[272,256]{1,0:T(8,128)(2,1)S(1)} %get-tuple-element.32.refs_1_), channel_id=1, source_target_pairs={{0,2},{1,3},{2,0},{3,1},{4,6},{5,7},{6,4},{7,5},{8,10},{9,11},{10,... | collective-permute-start | bytes 417800 | tf_op jit(solution)/shard_map/ppermute | solution.py:379
  5.7 9.1 %collective-permute-start.2 = (bf16[272,256]{1,0:T(8,128)(2,1)S(1)}, bf16[272,256]{1,0:T(8,128)(2,1)S(1)}, u32[]{:S(2)}, u32[]{:S(2)}) collective-permute-start(bf16[272,256]{1,0:T(8,128)(2,1)S(1)} %get-tuple-element.32.refs_1_), channel_id=1, source_target_pairs={{0,4},{1,5},{2,6},{3,7},{4,0},{5,1},{6,2},{7,3},{8,12},{9,13},{10,... | collective-permute-start | bytes 417800 | tf_op jit(solution)/shard_map/ppermute | solution.py:379
  8.3 20.5 %collective-permute-start = (bf16[2,256,512]{2,1,0:T(8,128)(2,1)S(1)}, bf16[2,256,512]{2,1,0:T(8,128)(2,1)S(1)}, u32[]{:S(2)}, u32[]{:S(2)}) collective-permute-start(bf16[2,256,512]{2,1,0:T(8,128)(2,1)S(1)} %get-tuple-element.31), channel_id=1, source_target_pairs={{0,16},{8,24},{16,0},{24,8},{1,17},{9,25},{17,1},{25,9},{2,18},{10... | collective-permute-start | bytes 1572872 | tf_op jit(solution)/shard_map/ppermute | solution.py:379
  9.8 6.9 %collective-permute-start.3 = (bf16[272,256]{1,0:T(8,128)(2,1)S(1)}, bf16[272,256]{1,0:T(8,128)(2,1)S(1)}, u32[]{:S(2)}, u32[]{:S(2)}) collective-permute-start(bf16[272,256]{1,0:T(8,128)(2,1)S(1)} %get-tuple-element.32.refs_1_), channel_id=1, source_target_pairs={{0,1},{1,0},{2,3},{3,2},{4,5},{5,4},{6,7},{7,6},{8,9},{9,8},{10,11... | collective-permute-start | bytes 417800 | tf_op jit(solution)/shard_map/ppermute | solution.py:379
  11.6 6.7 %collective-permute-start.4 = (bf16[272,256]{1,0:T(8,128)(2,1)S(1)}, bf16[272,256]{1,0:T(8,128)(2,1)S(1)}, u32[]{:S(2)}, u32[]{:S(2)}) collective-permute-start(bf16[272,256]{1,0:T(8,128)(2,1)S(1)} %collective-permute-done.1.refs_2_), channel_id=1, source_target_pairs={{0,1},{1,0},{2,3},{3,2},{4,5},{5,4},{6,7},{7,6},{8,9},{9,8},{10,11... | collective-permute-start | bytes 417800 | tf_op jit(solution)/shard_map/ppermute | solution.py:379
  14.8 5.1 %collective-permute-start.5 = (bf16[272,256]{1,0:T(8,128)(2,1)S(1)}, bf16[272,256]{1,0:T(8,128)(2,1)S(1)}, u32[]{:S(2)}, u32[]{:S(2)}) collective-permute-start(bf16[272,256]{1,0:T(8,128)(2,1)S(1)} %collective-permute-done.2.refs_3_), channel_id=1, source_target_pairs={{0,2},{1,3},{2,0},{3,1},{4,6},{5,7},{6,4},{7,5},{8,10},{9,11},{10,... | collective-permute-start | bytes 417800 | tf_op jit(solution)/shard_map/ppermute | solution.py:379
  15.2 7.3 %collective-permute-start.6 = (bf16[272,256]{1,0:T(8,128)(2,1)S(1)}, bf16[272,256]{1,0:T(8,128)(2,1)S(1)}, u32[]{:S(2)}, u32[]{:S(2)}) collective-permute-start(bf16[272,256]{1,0:T(8,128)(2,1)S(1)} %collective-permute-done.2.refs_3_), channel_id=1, source_target_pairs={{0,1},{1,0},{2,3},{3,2},{4,5},{5,4},{6,7},{7,6},{8,9},{9,8},{10,11... | collective-permute-start | bytes 417800 | tf_op jit(solution)/shard_map/ppermute | solution.py:379
  19.8 5.1 %collective-permute-start.7 = (bf16[272,256]{1,0:T(8,128)(2,1)S(1)}, bf16[272,256]{1,0:T(8,128)(2,1)S(1)}, u32[]{:S(2)}, u32[]{:S(2)}) collective-permute-start(bf16[272,256]{1,0:T(8,128)(2,1)S(1)} %after.2), channel_id=1, source_target_pairs={{0,1},{1,0},{2,3},{3,2},{4,5},{5,4},{6,7},{7,6},{8,9},{9,8},{10,11... | collective-permute-start | bytes 417800 | tf_op jit(solution)/shard_map/ppermute | solution.py:379
  27.2 5.0 %collective-permute-start.8 = (bf16[1,256,256]{2,1,0:T(8,128)(2,1)S(1)}, bf16[1,256,256]{2,1,0:T(8,128)(2,1)S(1)}, u32[]{:S(2)}, u32[]{:S(2)}) collective-permute-start(bf16[1,256,256]{2,1,0:T(8,128)(2,1)S(1)} %group_grad.1.refs_0_.refs_3_), channel_id=1, source_target_pairs={{0,16},{8,24},{16,0},{24,8},{1,17},{9,25},{17,1},{25,9},{2,18},{10... | collective-permute-start | bytes 393224 | tf_op jit(solution)/shard_map/ppermute | solution.py:379
  32.3 2.4 %collective-permute-start.9 = (bf16[2,256,512]{2,1,0:T(8,128)(2,1)S(1)}, bf16[2,256,512]{2,1,0:T(8,128)(2,1)S(1)}, u32[]{:S(2)}, u32[]{:S(2)}) collective-permute-start(bf16[2,256,512]{2,1,0:T(8,128)(2,1)S(1)} %pack.2), channel_id=1, source_target_pairs={{0,8},{8,0},{16,24},{24,16},{1,9},{9,1},{17,25},{25,17},{2,10},{10... | collective-permute-start | bytes 1572872 | tf_op jit(solution)/shard_map/ppermute | solution.py:379
  32.4 2.2 %collective-permute-start.10 = (bf16[2,256,256]{2,1,0:T(8,128)(2,1)S(1)}, bf16[2,256,256]{2,1,0:T(8,128)(2,1)S(1)}, u32[]{:S(2)}, u32[]{:S(2)}) collective-permute-start(bf16[2,256,256]{2,1,0:T(8,128)(2,1)S(1)} %pack.3), channel_id=1, source_target_pairs={{0,8},{8,0},{16,24},{24,16},{1,9},{9,1},{17,25},{25,17},{2,10},{10... | collective-permute-start | bytes 786440 | tf_op jit(solution)/shard_map/ppermute | solution.py:379
  35.2 4.7 %collective-permute-start.12 = (bf16[2,64,256]{2,1,0:T(8,128)(2,1)S(1)}, bf16[2,64,256]{2,1,0:T(8,128)(2,1)S(1)}, u32[]{:S(2)}, u32[]{:S(2)}) collective-permute-start(bf16[2,64,256]{2,1,0:T(8,128)(2,1)S(1)} %get-tuple-element.51), channel_id=1, source_target_pairs={{0,1},{1,0},{2,3},{3,2},{4,5},{5,4},{6,7},{7,6},{8,9},{9,8},{10,11... | collective-permute-start | bytes 196616 | tf_op jit(solution)/shard_map/ppermute | solution.py:379
  36.7 6.8 %collective-permute-start.11 = (bf16[2,64,256]{2,1,0:T(8,128)(2,1)S(1)}, bf16[2,64,256]{2,1,0:T(8,128)(2,1)S(1)}, u32[]{:S(2)}, u32[]{:S(2)}) collective-permute-start(bf16[2,64,256]{2,1,0:T(8,128)(2,1)S(1)} %get-tuple-element.48), channel_id=1, source_target_pairs={{0,1},{1,0},{2,3},{3,2},{4,5},{5,4},{6,7},{7,6},{8,9},{9,8},{10,11... | collective-permute-start | bytes 196616 | tf_op jit(solution)/shard_map/ppermute | solution.py:379
  39.9 4.9 %collective-permute-start.13 = (bf16[64,256]{1,0:T(8,128)(2,1)S(1)}, bf16[64,256]{1,0:T(8,128)(2,1)S(1)}, u32[]{:S(2)}, u32[]{:S(2)}) collective-permute-start(bf16[64,256]{1,0:T(8,128)(2,1)S(1)} %get-tuple-element.52), channel_id=1, source_target_pairs={{0,4},{1,5},{2,6},{3,7},{4,0},{5,1},{6,2},{7,3},{8,12},{9,13},{10,... | collective-permute-start | bytes 98312 | tf_op jit(solution)/shard_map/ppermute | solution.py:379
  42.2 5.7 %collective-permute-start.14 = (bf16[64,256]{1,0:T(8,128)(2,1)S(1)}, bf16[64,256]{1,0:T(8,128)(2,1)S(1)}, u32[]{:S(2)}, u32[]{:S(2)}) collective-permute-start(bf16[64,256]{1,0:T(8,128)(2,1)S(1)} %get-tuple-element.53), channel_id=1, source_target_pairs={{0,6},{1,7},{2,4},{3,5},{4,2},{5,3},{6,0},{7,1},{8,14},{9,15},{10,... | collective-permute-start | bytes 98312 | tf_op jit(solution)/shard_map/ppermute | solution.py:379
  43.6 4.4 %collective-permute-start.15 = (bf16[64,256]{1,0:T(8,128)(2,1)S(1)}, bf16[64,256]{1,0:T(8,128)(2,1)S(1)}, u32[]{:S(2)}, u32[]{:S(2)}) collective-permute-start(bf16[64,256]{1,0:T(8,128)(2,1)S(1)} %get-tuple-element.54), channel_id=1, source_target_pairs={{0,2},{1,3},{2,0},{3,1},{4,6},{5,7},{6,4},{7,5},{8,10},{9,11},{10,... | collective-permute-start | bytes 98312 | tf_op jit(solution)/shard_map/ppermute | solution.py:379

commit v18 on v16

--- a/solution.py
+++ b/solution.py
@@ -464,7 +464,7 @@
     far_sums = add_pieces(own_far, far_came, jnp.bfloat16)
     total, *near_sums = add_pieces(own_near, near_came, jnp.float32)
     half = members // minor // 2
-    far_came = [swap(each, "pool", (half + at) * minor) for at, each in enumerate(far_sums)]
+    far_came = [swap(far_sums[at], "pool", (half + at) * minor) for at in reversed(range(half))]
     near_came = [swap(each, "pool", (1 + at) * minor) for at, each in enumerate(near_sums)]
     far_total = add_all(far_came)
     return add_all([total, far_total] + [after(each, far_total) for each in near_came])

time: 48.5 us -> 47.9 us (0.988)
  waiting for transfers between devices: 15.5 us -> 14.1 us
  starting transfers between devices: 22 us -> 22.8 us
    ppermute x16, waiting for transfers between devices: 15.5 us -> 14.1 us  [swap(): return lax.ppermute(value, axis, [(at, at ^ flip) for at in range(size)])]
    ppermute x16, starting transfers between devices: 22 us -> 22.8 us  [swap(): return lax.ppermute(value, axis, [(at, at ^ flip) for at in range(size)])]
where the time goes in v18:
time: 47.9 us; the launch traced here: 47.8 us
  starting transfers between devices  22.8 us (48%)
  waiting for transfers between devices  14.1 us (29%)
  Pallas kernels  10.8 us (23%)
    ppermute x16, starting transfers between devices, swap(): return lax.ppermute(value, axis, [(at, at ^ flip) for at in range(size)])  22.8 us
    ppermute x16, waiting for transfers between devices, swap(): return lax.ppermute(value, axis, [(at, at ^ flip) for at in range(size)])  14.1 us
    pallas_call x4, Pallas kernels, add_pairs(): pl.pallas_call(functools.partial(pairs_kernel, seen, fresh), out_shape=(j...  4.94 us
    pallas_call x1, Pallas kernels, project(): pl.pallas_call(functools.partial(project_kernel, parts), out_shape=(jax.S...  2.29 us
    pallas_call x1, Pallas kernels, group_grad(): pl.pallas_call(functools.partial(grad_kernel, stages, fresh), out_shape=j...  2.26 us
  transfers between devices with their start and end apart: 16, of which 10 were waited for; matrix products, arithmetic and copies ran while one was open for 0% of the time, Pallas kernels for 15%

profile of v18, /device:TPU:0, one launch (start us, length us, event | category | flops | bytes accessed | tf_op | source)
XLA Modules:
  0.0 47.8 jit_solution(13817065529338208701)
XLA Ops:
  0.0 2.3 %project.1 = (bf16[272,256]{1,0:T(8,128)(2,1)S(1)}, f32[256,256]{1,0:T(8,128)S(1)}, f32[256,128]{1,0:T(8,128)S(1)}, bf16[2,256,512]{2,1,0:T(8,128)(2,1)S(1)}, bf16[2,256,512]{2,1,0:T(8,128)(2,1)S(1)}) custom-call(bf16[256,2048]{1,0:T(8,128)(2,1)} %feats_hbm.1, bf16[2048,256]{1,0:T(8,128)(2,1)} %w_hbm.1, s32[1,256]{1,0:T(1,128)} %bitcast.2, s32[1,256]{1,0:T(1,128)} %bitcast.3), custom_call_target="tpu_custom_call" | custom-call | flops 268435456 | bytes 2097152 | tf_op jit(solution)/shard_map/project/pallas_call | solution.py:81
  2.3 3.1 %collective-permute-start.1 = (bf16[272,256]{1,0:T(8,128)(2,1)S(1)}, bf16[272,256]{1,0:T(8,128)(2,1)S(1)}, u32[]{:S(2)}, u32[]{:S(2)}) collective-permute-start(bf16[272,256]{1,0:T(8,128)(2,1)S(1)} %get-tuple-element.32.refs_1_), channel_id=1, source_target_pairs={{0,2},{1,3},{2,0},{3,1},{4,6},{5,7},{6,4},{7,5},{8,10},{9,11},{10,... | collective-permute-start | bytes 417800 | tf_op jit(solution)/shard_map/ppermute | solution.py:381
  5.4 2.6 %collective-permute-start.2 = (bf16[272,256]{1,0:T(8,128)(2,1)S(1)}, bf16[272,256]{1,0:T(8,128)(2,1)S(1)}, u32[]{:S(2)}, u32[]{:S(2)}) collective-permute-start(bf16[272,256]{1,0:T(8,128)(2,1)S(1)} %get-tuple-element.32.refs_1_), channel_id=1, source_target_pairs={{0,4},{1,5},{2,6},{3,7},{4,0},{5,1},{6,2},{7,3},{8,12},{9,13},{10,... | collective-permute-start | bytes 417800 | tf_op jit(solution)/shard_map/ppermute | solution.py:381
  8.0 1.5 %collective-permute-start = (bf16[2,256,512]{2,1,0:T(8,128)(2,1)S(1)}, bf16[2,256,512]{2,1,0:T(8,128)(2,1)S(1)}, u32[]{:S(2)}, u32[]{:S(2)}) collective-permute-start(bf16[2,256,512]{2,1,0:T(8,128)(2,1)S(1)} %get-tuple-element.31), channel_id=1, source_target_pairs={{0,16},{8,24},{16,0},{24,8},{1,17},{9,25},{17,1},{25,9},{2,18},{10... | collective-permute-start | bytes 1572872 | tf_op jit(solution)/shard_map/ppermute | solution.py:381
  9.5 1.5 %collective-permute-start.3 = (bf16[272,256]{1,0:T(8,128)(2,1)S(1)}, bf16[272,256]{1,0:T(8,128)(2,1)S(1)}, u32[]{:S(2)}, u32[]{:S(2)}) collective-permute-start(bf16[272,256]{1,0:T(8,128)(2,1)S(1)} %get-tuple-element.32.refs_1_), channel_id=1, source_target_pairs={{0,1},{1,0},{2,3},{3,2},{4,5},{5,4},{6,7},{7,6},{8,9},{9,8},{10,11... | collective-permute-start | bytes 417800 | tf_op jit(solution)/shard_map/ppermute | solution.py:381
  11.0 0.3 collective-permute-done.1.refs_2_
  11.3 1.8 %collective-permute-start.4 = (bf16[272,256]{1,0:T(8,128)(2,1)S(1)}, bf16[272,256]{1,0:T(8,128)(2,1)S(1)}, u32[]{:S(2)}, u32[]{:S(2)}) collective-permute-start(bf16[272,256]{1,0:T(8,128)(2,1)S(1)} %collective-permute-done.1.refs_2_), channel_id=1, source_target_pairs={{0,1},{1,0},{2,3},{3,2},{4,5},{5,4},{6,7},{7,6},{8,9},{9,8},{10,11... | collective-permute-start | bytes 417800 | tf_op jit(solution)/shard_map/ppermute | solution.py:381
  13.1 1.4 %collective-permute-done.2.refs_3_ = bf16[272,256]{1,0:T(8,128)(2,1)S(1)} collective-permute-done((bf16[272,256]{1,0:T(8,128)(2,1)S(1)}, bf16[272,256]{1,0:T(8,128)(2,1)S(1)}, u32[]{:S(2)}, u32[]{:S(2)}) %collective-permute-start.2) | collective-permute-done | bytes 139296 | tf_op jit(solution)/shard_map/ppermute | solution.py:381
  14.5 0.4 collective-permute-start.5
  14.9 1.5 %collective-permute-start.6 = (bf16[272,256]{1,0:T(8,128)(2,1)S(1)}, bf16[272,256]{1,0:T(8,128)(2,1)S(1)}, u32[]{:S(2)}, u32[]{:S(2)}) collective-permute-start(bf16[272,256]{1,0:T(8,128)(2,1)S(1)} %collective-permute-done.2.refs_3_), channel_id=1, source_target_pairs={{0,1},{1,0},{2,3},{3,2},{4,5},{5,4},{6,7},{7,6},{8,9},{9,8},{10,11... | collective-permute-start | bytes 417800 | tf_op jit(solution)/shard_map/ppermute | solution.py:381
  16.4 1.4 %add_pairs.4 = (f32[4,256]{1,0:T(4,128)S(1)}, f32[256,128]{1,0:T(8,128)S(1)}, f32[4,2,256,256]{3,2,1,0:T(8,128)S(1)}) custom-call(s32[4,8]{1,0:T(4,128)S(1)} %copy-done, bf16[272,256]{1,0:T(8,128)(2,1)S(1)} %get-tuple-element.32.refs_1_, bf16[272,256]{1,0:T(8,128)(2,1)S(1)} %collective-permute-done.1.refs_2_, ...), custom_call_target="tpu_custom_call" | custom-call | flops 335544320 | bytes 1572864 | tf_op jit(solution)/shard_map/add_pairs/pallas_call | solution.py:197
  18.0 1.1 %add_pairs.5 = (f32[5,256]{1,0:T(8,128)S(1)}, f32[256,128]{1,0:T(8,128)S(1)}, f32[1,2,256,256]{3,2,1,0:T(8,128)S(1)}) custom-call(s32[4,8]{1,0:T(4,128)S(1)} %copy-done, bf16[272,256]{1,0:T(8,128)(2,1)S(1)} %get-tuple-element.32.refs_1_, bf16[272,256]{1,0:T(8,128)(2,1)S(1)} %collective-permute-done.1.refs_2_, ...), custom_call_target="tpu_custom_call" | custom-call | flops 167772160 | bytes 917504 | tf_op jit(solution)/shard_map/add_pairs/pallas_call | solution.py:197
  19.1 0.4 collective-permute-done.5.value_ref.refs_6_
  19.5 1.6 %collective-permute-start.7 = (bf16[272,256]{1,0:T(8,128)(2,1)S(1)}, bf16[272,256]{1,0:T(8,128)(2,1)S(1)}, u32[]{:S(2)}, u32[]{:S(2)}) collective-permute-start(bf16[272,256]{1,0:T(8,128)(2,1)S(1)} %after.2), channel_id=1, source_target_pairs={{0,1},{1,0},{2,3},{3,2},{4,5},{5,4},{6,7},{7,6},{8,9},{9,8},{10,11... | collective-permute-start | bytes 417800 | tf_op jit(solution)/shard_map/ppermute | solution.py:381
  21.1 1.2 %add_pairs.6 = (f32[6,256]{1,0:T(8,128)S(1)}, f32[256,128]{1,0:T(8,128)S(1)}, f32[1,2,256,256]{3,2,1,0:T(8,128)S(1)}) custom-call(s32[4,8]{1,0:T(4,128)S(1)} %copy-done, bf16[272,256]{1,0:T(8,128)(2,1)S(1)} %get-tuple-element.32.refs_1_, bf16[272,256]{1,0:T(8,128)(2,1)S(1)} %collective-permute-done.1.refs_2_, ...), custom_call_target="tpu_custom_call" | custom-call | flops 201326592 | bytes 1048576 | tf_op jit(solution)/shard_map/add_pairs/pallas_call | solution.py:197
  22.3 1.2 %add_pairs.7 = (f32[7,256]{1,0:T(8,128)S(1)}, f32[256,128]{1,0:T(8,128)S(1)}, f32[1,2,256,256]{3,2,1,0:T(8,128)S(1)}) custom-call(s32[4,8]{1,0:T(4,128)S(1)} %copy-done, bf16[272,256]{1,0:T(8,128)(2,1)S(1)} %get-tuple-element.32.refs_1_, bf16[272,256]{1,0:T(8,128)(2,1)S(1)} %collective-permute-done.1.refs_2_, ...), custom_call_target="tpu_custom_call" | custom-call | flops 234881024 | bytes 1179648 | tf_op jit(solution)/shard_map/add_pairs/pallas_call | solution.py:197
  23.5 1.2 %collective-permute-done.7.refs_8_ = bf16[272,256]{1,0:T(8,128)(2,1)S(1)} collective-permute-done((bf16[272,256]{1,0:T(8,128)(2,1)S(1)}, bf16[272,256]{1,0:T(8,128)(2,1)S(1)}, u32[]{:S(2)}, u32[]{:S(2)}) %collective-permute-start.7) | collective-permute-done | bytes 139296 | tf_op jit(solution)/shard_map/ppermute | solution.py:381
  24.6 2.3 %group_grad.1.refs_0_.refs_3_ = bf16[1,256,256]{2,1,0:T(8,128)(2,1)S(1)} custom-call(s32[4,8]{1,0:T(4,128)S(1)} %copy-done, bf16[272,256]{1,0:T(8,128)(2,1)S(1)} %get-tuple-element.32.refs_1_, bf16[272,256]{1,0:T(8,128)(2,1)S(1)} %collective-permute-done.1.refs_2_, bf16[272,256]{1,0:T(8,128)(2,1)S(1)} %collective-permute-done.2.refs_3_, ...), custom_call_target="tpu_custom_call" | custom-call | flops 268435456 | bytes 1310720 | tf_op jit(solution)/shard_map/group_grad/pallas_call | solution.py:261
  26.9 1.6 %collective-permute-start.8 = (bf16[1,256,256]{2,1,0:T(8,128)(2,1)S(1)}, bf16[1,256,256]{2,1,0:T(8,128)(2,1)S(1)}, u32[]{:S(2)}, u32[]{:S(2)}) collective-permute-start(bf16[1,256,256]{2,1,0:T(8,128)(2,1)S(1)} %group_grad.1.refs_0_.refs_3_), channel_id=1, source_target_pairs={{0,16},{8,24},{16,0},{24,8},{1,17},{9,25},{17,1},{25,9},{2,18},{10... | collective-permute-start | bytes 393224 | tf_op jit(solution)/shard_map/ppermute | solution.py:381
  28.5 3.4 %collective-permute-done.8.refs_2_.refs_1_.refs_5_ = bf16[1,256,256]{2,1,0:T(8,128)(2,1)S(1)} collective-permute-done((bf16[1,256,256]{2,1,0:T(8,128)(2,1)S(1)}, bf16[1,256,256]{2,1,0:T(8,128)(2,1)S(1)}, u32[]{:S(2)}, u32[]{:S(2)}) %collective-permute-start.8) | collective-permute-done | bytes 131104 | tf_op jit(solution)/shard_map/ppermute | solution.py:381
  32.1 0.6 %collective-permute-start.10 = (bf16[2,256,256]{2,1,0:T(8,128)(2,1)S(1)}, bf16[2,256,256]{2,1,0:T(8,128)(2,1)S(1)}, u32[]{:S(2)}, u32[]{:S(2)}) collective-permute-start(bf16[2,256,256]{2,1,0:T(8,128)(2,1)S(1)} %pack.3), channel_id=1, source_target_pairs={{0,8},{8,0},{16,24},{24,16},{1,9},{9,1},{17,25},{25,17},{2,10},{10... | collective-permute-start | bytes 786440 | tf_op jit(solution)/shard_map/ppermute | solution.py:381
  32.6 1.7 %collective-permute-done.10.refs_4_ = bf16[2,256,256]{2,1,0:T(8,128)(2,1)S(1)} collective-permute-done((bf16[2,256,256]{2,1,0:T(8,128)(2,1)S(1)}, bf16[2,256,256]{2,1,0:T(8,128)(2,1)S(1)}, u32[]{:S(2)}, u32[]{:S(2)}) %collective-permute-start.10) | collective-permute-done | bytes 262176 | tf_op jit(solution)/shard_map/ppermute | solution.py:381
  34.3 0.5 %weight_grad.1 = (f32[2,64,256]{2,1,0:T(8,128)S(1)}, f32[2,64,256]{2,1,0:T(8,128)S(1)}, bf16[2,64,256]{2,1,0:T(8,128)(2,1)S(1)}, bf16[2,64,256]{2,1,0:T(8,128)(2,1)S(1)}) custom-call(bf16[2,256,512]{2,1,0:T(8,128)(2,1)S(1)} %get-tuple-element.30.refs_0_, bf16[2,256,512]{2,1,0:T(8,128)(2,1)S(1)} %collective-permute-done.9.refs_1_, ...), custom_call_target="tpu_custom_call" | custom-call | flops 268435456 | bytes 1048576 | tf_op jit(solution)/shard_map/weight_grad/pallas_call | solution.py:324
  34.9 1.6 %collective-permute-start.12 = (bf16[2,64,256]{2,1,0:T(8,128)(2,1)S(1)}, bf16[2,64,256]{2,1,0:T(8,128)(2,1)S(1)}, u32[]{:S(2)}, u32[]{:S(2)}) collective-permute-start(bf16[2,64,256]{2,1,0:T(8,128)(2,1)S(1)} %get-tuple-element.51), channel_id=1, source_target_pairs={{0,1},{1,0},{2,3},{3,2},{4,5},{5,4},{6,7},{7,6},{8,9},{9,8},{10,11... | collective-permute-start | bytes 196616 | tf_op jit(solution)/shard_map/ppermute | solution.py:381
  36.4 0.5 %collective-permute-start.11 = (bf16[2,64,256]{2,1,0:T(8,128)(2,1)S(1)}, bf16[2,64,256]{2,1,0:T(8,128)(2,1)S(1)}, u32[]{:S(2)}, u32[]{:S(2)}) collective-permute-start(bf16[2,64,256]{2,1,0:T(8,128)(2,1)S(1)} %get-tuple-element.48), channel_id=1, source_target_pairs={{0,1},{1,0},{2,3},{3,2},{4,5},{5,4},{6,7},{7,6},{8,9},{9,8},{10,11... | collective-permute-start | bytes 196616 | tf_op jit(solution)/shard_map/ppermute | solution.py:381
  37.0 2.6 %collective-permute-done.12.refs_0_ = bf16[2,64,256]{2,1,0:T(8,128)(2,1)S(1)} collective-permute-done((bf16[2,64,256]{2,1,0:T(8,128)(2,1)S(1)}, bf16[2,64,256]{2,1,0:T(8,128)(2,1)S(1)}, u32[]{:S(2)}, u32[]{:S(2)}) %collective-permute-start.12) | collective-permute-done | bytes 65568 | tf_op jit(solution)/shard_map/ppermute | solution.py:381
  39.6 2.5 %collective-permute-start.13 = (bf16[64,256]{1,0:T(8,128)(2,1)S(1)}, bf16[64,256]{1,0:T(8,128)(2,1)S(1)}, u32[]{:S(2)}, u32[]{:S(2)}) collective-permute-start(bf16[64,256]{1,0:T(8,128)(2,1)S(1)} %get-tuple-element.52), channel_id=1, source_target_pairs={{0,6},{1,7},{2,4},{3,5},{4,2},{5,3},{6,0},{7,1},{8,14},{9,15},{10,... | collective-permute-start | bytes 98312 | tf_op jit(solution)/shard_map/ppermute | solution.py:381
  42.1 0.2 collective-permute-start.14
  42.4 1.8 %collective-permute-start.15 = (bf16[64,256]{1,0:T(8,128)(2,1)S(1)}, bf16[64,256]{1,0:T(8,128)(2,1)S(1)}, u32[]{:S(2)}, u32[]{:S(2)}) collective-permute-start(bf16[64,256]{1,0:T(8,128)(2,1)S(1)} %get-tuple-element.54), channel_id=1, source_target_pairs={{0,2},{1,3},{2,0},{3,1},{4,6},{5,7},{6,4},{7,5},{8,10},{9,11},{10,... | collective-permute-start | bytes 98312 | tf_op jit(solution)/shard_map/ppermute | solution.py:381
  44.2 1.4 %collective-permute-done.13.refs_0_ = bf16[64,256]{1,0:T(8,128)(2,1)S(1)} collective-permute-done((bf16[64,256]{1,0:T(8,128)(2,1)S(1)}, bf16[64,256]{1,0:T(8,128)(2,1)S(1)}, u32[]{:S(2)}, u32[]{:S(2)}) %collective-permute-start.13) | collective-permute-done | bytes 32800 | tf_op jit(solution)/shard_map/ppermute | solution.py:381
  45.6 1.6 %collective-permute-done.14.refs_1_ = bf16[64,256]{1,0:T(8,128)(2,1)S(1)} collective-permute-done((bf16[64,256]{1,0:T(8,128)(2,1)S(1)}, bf16[64,256]{1,0:T(8,128)(2,1)S(1)}, u32[]{:S(2)}, u32[]{:S(2)}) %collective-permute-start.14) | collective-permute-done | bytes 32800 | tf_op jit(solution)/shard_map/ppermute | solution.py:381
  47.2 0.6 %add_all.3 = f32[64,256]{1,0:T(8,128)} custom-call(f32[64,256]{1,0:T(8,128)S(1)} %get-tuple-element.49.refs_0_, f32[64,256]{1,0:T(8,128)S(1)} %add_all.2.refs_0_.refs_1_, bf16[64,256]{1,0:T(8,128)(2,1)S(1)} %after.3.refs_2_), custom_call_target="tpu_custom_call" | custom-call | tf_op jit(solution)/shard_map/add_all/pallas_call | solution.py:369
  (17 shorter events, 0.3 us)
Async XLA Ops:
  0.0 16.4 %copy-start = (s32[4,8]{1,0:T(4,128)S(1)}, s32[4,8]{1,0:T(4,128)}, u32[]{:S(2)}) copy-start(s32[4,8]{1,0:T(4,128)} %refs_0_.9) | copy-start | bytes 388
  2.3 9.0 %collective-permute-start.1 = (bf16[272,256]{1,0:T(8,128)(2,1)S(1)}, bf16[272,256]{1,0:T(8,128)(2,1)S(1)}, u32[]{:S(2)}, u32[]{:S(2)}) collective-permute-start(bf16[272,256]{1,0:T(8,128)(2,1)S(1)} %get-tuple-element.32.refs_1_), channel_id=1, source_target_pairs={{0,2},{1,3},{2,0},{3,1},{4,6},{5,7},{6,4},{7,5},{8,10},{9,11},{10,... | collective-permute-start | bytes 417800 | tf_op jit(solution)/shard_map/ppermute | solution.py:381
  5.4 9.1 %collective-permute-start.2 = (bf16[272,256]{1,0:T(8,128)(2,1)S(1)}, bf16[272,256]{1,0:T(8,128)(2,1)S(1)}, u32[]{:S(2)}, u32[]{:S(2)}) collective-permute-start(bf16[272,256]{1,0:T(8,128)(2,1)S(1)} %get-tuple-element.32.refs_1_), channel_id=1, source_target_pairs={{0,4},{1,5},{2,6},{3,7},{4,0},{5,1},{6,2},{7,3},{8,12},{9,13},{10,... | collective-permute-start | bytes 417800 | tf_op jit(solution)/shard_map/ppermute | solution.py:381
  8.0 20.5 %collective-permute-start = (bf16[2,256,512]{2,1,0:T(8,128)(2,1)S(1)}, bf16[2,256,512]{2,1,0:T(8,128)(2,1)S(1)}, u32[]{:S(2)}, u32[]{:S(2)}) collective-permute-start(bf16[2,256,512]{2,1,0:T(8,128)(2,1)S(1)} %get-tuple-element.31), channel_id=1, source_target_pairs={{0,16},{8,24},{16,0},{24,8},{1,17},{9,25},{17,1},{25,9},{2,18},{10... | collective-permute-start | bytes 1572872 | tf_op jit(solution)/shard_map/ppermute | solution.py:381
  9.5 6.9 %collective-permute-start.3 = (bf16[272,256]{1,0:T(8,128)(2,1)S(1)}, bf16[272,256]{1,0:T(8,128)(2,1)S(1)}, u32[]{:S(2)}, u32[]{:S(2)}) collective-permute-start(bf16[272,256]{1,0:T(8,128)(2,1)S(1)} %get-tuple-element.32.refs_1_), channel_id=1, source_target_pairs={{0,1},{1,0},{2,3},{3,2},{4,5},{5,4},{6,7},{7,6},{8,9},{9,8},{10,11... | collective-permute-start | bytes 417800 | tf_op jit(solution)/shard_map/ppermute | solution.py:381
  11.3 6.7 %collective-permute-start.4 = (bf16[272,256]{1,0:T(8,128)(2,1)S(1)}, bf16[272,256]{1,0:T(8,128)(2,1)S(1)}, u32[]{:S(2)}, u32[]{:S(2)}) collective-permute-start(bf16[272,256]{1,0:T(8,128)(2,1)S(1)} %collective-permute-done.1.refs_2_), channel_id=1, source_target_pairs={{0,1},{1,0},{2,3},{3,2},{4,5},{5,4},{6,7},{7,6},{8,9},{9,8},{10,11... | collective-permute-start | bytes 417800 | tf_op jit(solution)/shard_map/ppermute | solution.py:381
  14.5 5.1 %collective-permute-start.5 = (bf16[272,256]{1,0:T(8,128)(2,1)S(1)}, bf16[272,256]{1,0:T(8,128)(2,1)S(1)}, u32[]{:S(2)}, u32[]{:S(2)}) collective-permute-start(bf16[272,256]{1,0:T(8,128)(2,1)S(1)} %collective-permute-done.2.refs_3_), channel_id=1, source_target_pairs={{0,2},{1,3},{2,0},{3,1},{4,6},{5,7},{6,4},{7,5},{8,10},{9,11},{10,... | collective-permute-start | bytes 417800 | tf_op jit(solution)/shard_map/ppermute | solution.py:381
  14.9 7.3 %collective-permute-start.6 = (bf16[272,256]{1,0:T(8,128)(2,1)S(1)}, bf16[272,256]{1,0:T(8,128)(2,1)S(1)}, u32[]{:S(2)}, u32[]{:S(2)}) collective-permute-start(bf16[272,256]{1,0:T(8,128)(2,1)S(1)} %collective-permute-done.2.refs_3_), channel_id=1, source_target_pairs={{0,1},{1,0},{2,3},{3,2},{4,5},{5,4},{6,7},{7,6},{8,9},{9,8},{10,11... | collective-permute-start | bytes 417800 | tf_op jit(solution)/shard_map/ppermute | solution.py:381
  19.5 5.1 %collective-permute-start.7 = (bf16[272,256]{1,0:T(8,128)(2,1)S(1)}, bf16[272,256]{1,0:T(8,128)(2,1)S(1)}, u32[]{:S(2)}, u32[]{:S(2)}) collective-permute-start(bf16[272,256]{1,0:T(8,128)(2,1)S(1)} %after.2), channel_id=1, source_target_pairs={{0,1},{1,0},{2,3},{3,2},{4,5},{5,4},{6,7},{7,6},{8,9},{9,8},{10,11... | collective-permute-start | bytes 417800 | tf_op jit(solution)/shard_map/ppermute | solution.py:381
  26.9 5.0 %collective-permute-start.8 = (bf16[1,256,256]{2,1,0:T(8,128)(2,1)S(1)}, bf16[1,256,256]{2,1,0:T(8,128)(2,1)S(1)}, u32[]{:S(2)}, u32[]{:S(2)}) collective-permute-start(bf16[1,256,256]{2,1,0:T(8,128)(2,1)S(1)} %group_grad.1.refs_0_.refs_3_), channel_id=1, source_target_pairs={{0,16},{8,24},{16,0},{24,8},{1,17},{9,25},{17,1},{25,9},{2,18},{10... | collective-permute-start | bytes 393224 | tf_op jit(solution)/shard_map/ppermute | solution.py:381
  32.0 2.4 %collective-permute-start.9 = (bf16[2,256,512]{2,1,0:T(8,128)(2,1)S(1)}, bf16[2,256,512]{2,1,0:T(8,128)(2,1)S(1)}, u32[]{:S(2)}, u32[]{:S(2)}) collective-permute-start(bf16[2,256,512]{2,1,0:T(8,128)(2,1)S(1)} %pack.2), channel_id=1, source_target_pairs={{0,8},{8,0},{16,24},{24,16},{1,9},{9,1},{17,25},{25,17},{2,10},{10... | collective-permute-start | bytes 1572872 | tf_op jit(solution)/shard_map/ppermute | solution.py:381
  32.1 2.2 %collective-permute-start.10 = (bf16[2,256,256]{2,1,0:T(8,128)(2,1)S(1)}, bf16[2,256,256]{2,1,0:T(8,128)(2,1)S(1)}, u32[]{:S(2)}, u32[]{:S(2)}) collective-permute-start(bf16[2,256,256]{2,1,0:T(8,128)(2,1)S(1)} %pack.3), channel_id=1, source_target_pairs={{0,8},{8,0},{16,24},{24,16},{1,9},{9,1},{17,25},{25,17},{2,10},{10... | collective-permute-start | bytes 786440 | tf_op jit(solution)/shard_map/ppermute | solution.py:381
  34.9 4.7 %collective-permute-start.12 = (bf16[2,64,256]{2,1,0:T(8,128)(2,1)S(1)}, bf16[2,64,256]{2,1,0:T(8,128)(2,1)S(1)}, u32[]{:S(2)}, u32[]{:S(2)}) collective-permute-start(bf16[2,64,256]{2,1,0:T(8,128)(2,1)S(1)} %get-tuple-element.51), channel_id=1, source_target_pairs={{0,1},{1,0},{2,3},{3,2},{4,5},{5,4},{6,7},{7,6},{8,9},{9,8},{10,11... | collective-permute-start | bytes 196616 | tf_op jit(solution)/shard_map/ppermute | solution.py:381
  36.4 5.9 %collective-permute-start.11 = (bf16[2,64,256]{2,1,0:T(8,128)(2,1)S(1)}, bf16[2,64,256]{2,1,0:T(8,128)(2,1)S(1)}, u32[]{:S(2)}, u32[]{:S(2)}) collective-permute-start(bf16[2,64,256]{2,1,0:T(8,128)(2,1)S(1)} %get-tuple-element.48), channel_id=1, source_target_pairs={{0,1},{1,0},{2,3},{3,2},{4,5},{5,4},{6,7},{7,6},{8,9},{9,8},{10,11... | collective-permute-start | bytes 196616 | tf_op jit(solution)/shard_map/ppermute | solution.py:381
  39.6 5.9 %collective-permute-start.13 = (bf16[64,256]{1,0:T(8,128)(2,1)S(1)}, bf16[64,256]{1,0:T(8,128)(2,1)S(1)}, u32[]{:S(2)}, u32[]{:S(2)}) collective-permute-start(bf16[64,256]{1,0:T(8,128)(2,1)S(1)} %get-tuple-element.52), channel_id=1, source_target_pairs={{0,6},{1,7},{2,4},{3,5},{4,2},{5,3},{6,0},{7,1},{8,14},{9,15},{10,... | collective-permute-start | bytes 98312 | tf_op jit(solution)/shard_map/ppermute | solution.py:381
  42.1 5.0 %collective-permute-start.14 = (bf16[64,256]{1,0:T(8,128)(2,1)S(1)}, bf16[64,256]{1,0:T(8,128)(2,1)S(1)}, u32[]{:S(2)}, u32[]{:S(2)}) collective-permute-start(bf16[64,256]{1,0:T(8,128)(2,1)S(1)} %get-tuple-element.53), channel_id=1, source_target_pairs={{0,4},{1,5},{2,6},{3,7},{4,0},{5,1},{6,2},{7,3},{8,12},{9,13},{10,... | collective-permute-start | bytes 98312 | tf_op jit(solution)/shard_map/ppermute | solution.py:381
  42.4 4.8 %collective-permute-start.15 = (bf16[64,256]{1,0:T(8,128)(2,1)S(1)}, bf16[64,256]{1,0:T(8,128)(2,1)S(1)}, u32[]{:S(2)}, u32[]{:S(2)}) collective-permute-start(bf16[64,256]{1,0:T(8,128)(2,1)S(1)} %get-tuple-element.54), channel_id=1, source_target_pairs={{0,2},{1,3},{2,0},{3,1},{4,6},{5,7},{6,4},{7,5},{8,10},{9,11},{10,... | collective-permute-start | bytes 98312 | tf_op jit(solution)/shard_map/ppermute | solution.py:381
